TPU v7x, 128 devices: a whole 4x4x4 slice. The times are simulated.
128 devices in a mesh: image: 8 (over x, z_lo), domain: 16 (over y, z_hi, core).
Axes of the slice: x: 4, y: 4, z: 4 (z_hi: 2, z_lo: 2; z = z_hi * 2 + z_lo), core: 2. Of those that a mesh axis runs over, the one named last changes fastest.
Arguments:
- displacement: float32 [8, 3, 1572864], P('image', None, 'domain'), may hold values from -0.5 to 0.5, as said below
- velocity: float32 [8, 3, 1572864], P('image', None, 'domain'), may hold values from -1.2 to 1.2
Outputs:
- displacement_next: float32 [8, 3, 1572864], P('image', None, 'domain')
- velocity_next: float32 [8, 3, 1572864], P('image', None, 'domain')
Inputs may be any that keep to these rules, and one draw needn't show every extreme that they name: `displacement`: displacements from the lattice sites.
All inputs are finite; a program needn't handle non-finite values.
Results may differ from a plain program's by a relative error of at most 0.0003.
Values sent between devices are 32-bit elements; how exact they have to be, the bound alone decides.
No kernel may reach another device: no remote copies, remote signals or barrier semaphores. Data moves between devices by JAX's collectives and lax.ppermute only.
A program may use at most 128 MiB of HBM per device.

v0:
```python
import functools
import math

import jax
import jax.numpy as jnp
from jax import lax
from jax.experimental import pallas as pl
from jax.experimental.pallas import tpu as pltpu
from jax.sharding import PartitionSpec as P

SIDE = 32
FIRE_STEPS = 2
QUANTITIES = 8
HALO = 2

lattice_const = 3.615
cutoff_sq = 9.61
nearest_sq = 6.533136
pair_scale = 30.0
pair_depth = 0.3
embed_scale = 1.2
bulk_root = 3.605551275463989
spring_const = 2.0
time_step = 0.1
fire_mixing = 0.1
stabilizer = 1e-06

reach_root = math.sqrt(cutoff_sq)
unit_half = 0.5 * lattice_const / reach_root
kappa = cutoff_sq / nearest_sq
dens_shift = (2.0 - kappa) / kappa
pair_shift = (2.5 - 2.0 * kappa) / (2.0 * kappa)
dens_scale = pair_scale * kappa
pair_energy_scale = pair_scale * pair_depth * 2.0 * kappa
dens_slope_shift = 0.75 * dens_shift
pair_slope_shift = 0.75 * pair_shift
dens_slope_scale = -4.0 * dens_scale / cutoff_sq
pair_slope_scale = -4.0 * pair_energy_scale / cutoff_sq
slope_ratio = dens_slope_scale / pair_slope_scale
force_scale = 2.0 * pair_slope_scale * reach_root


def shift_v(field, step, lanes):
    return pltpu.roll(field, (-step) % 128, 1)


def shift_u(field, step, lanes):
    turned = pltpu.roll(field, (-step * SIDE) % 128, 1)
    carried = pltpu.roll(turned, (-step) % 8, 0)
    edge = lanes >= 128 - SIDE if step > 0 else lanes < SIDE
    return jnp.where(edge, carried, turned)


def partners(field, step, lanes):
    along_u = shift_u(field, step, lanes)
    return (shift_v(field, step, lanes), along_u, shift_v(along_u, step, lanes))


def gather_back(at_v, at_u, at_uv, step, lanes):
    return shift_u(at_u + shift_v(at_uv, -step, lanes), -step, lanes) + shift_v(at_v, -step, lanes)


def limits(step, u, v):
    far = jnp.float32(-1e30)
    in_u = (u + step >= 0) & (u + step < SIDE)
    in_v = (v + step >= 0) & (v + step < SIDE)
    one = jnp.ones_like(u, jnp.float32)
    return (
        jnp.where(in_v, one, far),
        jnp.where(in_u, one, far),
        jnp.where(in_u & in_v, one, far),
    )


def force_kernel(own_ref, low_ref, high_ref, force_ref, energy_ref, pos, seps, slopes, rho, embed):
    f32 = jnp.float32
    planes = own_ref.shape[1]
    lanes = lax.broadcasted_iota(jnp.int32, (8, 128), 1)
    subl = lax.broadcasted_iota(jnp.int32, (8, 128), 0)
    site_u = subl * 4 + lanes // SIDE
    site_v = lanes % SIDE
    inverse = f32(1.0 / reach_root)
    pos[:, 0:HALO] = low_ref[...] * inverse
    pos[:, HALO + planes : HALO + planes + HALO] = high_ref[...] * inverse
    pos[:, planes + 2 * HALO :] = jnp.zeros((3, 2, 8, 128), f32)

    def fill(t, carry):
        for j in range(8):
            for axis in range(3):
                pos[axis, HALO + t * 8 + j] = own_ref[axis, t * 8 + j] * inverse
        return carry

    lax.fori_loop(0, planes // 8, fill, 0)

    def separations(e, step):
        h = f32(unit_half)
        sh = f32(step * unit_half)
        own = [pos[axis, e] for axis in range(3)]
        nxt = [pos[axis, e + 1] for axis in range(3)]
        turned = [partners(nxt[axis], step, lanes) for axis in range(3)]
        own_x = own[0] - h
        y_of = (own[1] + sh, own[1], own[1] - sh)
        z_of = (own[2] - sh, own[2], own[2] + sh)
        cross = [
            (nxt[0] - own_x, nxt[1] - y_of[0], nxt[2] - z_of[1]),
            (turned[0][0] - own_x, turned[1][0] - y_of[1], turned[2][0] - z_of[2]),
            (turned[0][1] - own_x, turned[1][1] - y_of[1], turned[2][1] - z_of[0]),
            (turned[0][2] - own_x, turned[1][2] - y_of[2], turned[2][2] - z_of[1]),
        ]
        near_y = nxt[1] - sh
        near_zv = nxt[2] + sh
        near_zu = nxt[2] - sh
        inside = [
            (turned[0][0] - nxt[0], turned[1][0] - near_y, turned[2][0] - near_zv),
            (turned[0][1] - nxt[0], turned[1][1] - near_y, turned[2][1] - near_zu),
        ]
        return cross + inside

    def density(e, step, bounds, carry):
        rho_part, sum_f, sum_c = carry
        one = jnp.ones((8, 128), f32)
        tops = (one, bounds[0], bounds[1], bounds[2], bounds[0], bounds[1])
        dens, cubes = [], []
        for k, sep in enumerate(separations(e, step)):
            y = sep[0] * sep[0] + sep[1] * sep[1] + sep[2] * sep[2]
            c = jnp.maximum(tops[k] - y, 0.0)
            square = c * c
            cube = square * c
            dens.append(cube * (c + f32(dens_shift)))
            cubes.append(cube)
            for axis in range(3):
                seps[e, k, axis] = sep[axis]
            slopes[e, k, 0] = square * (c + f32(pair_slope_shift))
            slopes[e, k, 1] = square * (c + f32(dens_slope_shift))
        cross = (dens[0] + dens[1]) + (dens[2] + dens[3])
        inside = dens[4] + dens[5]
        rho[e] = rho_part + cross
        back = gather_back(dens[1] + dens[4], dens[2] + dens[5], dens[3], step, lanes)
        weight = jnp.where((e >= 1) & (e <= planes), 1.0, 0.0).astype(f32)
        sum_f = sum_f + weight * (cross + inside)
        sum_c = sum_c + weight * (
            ((cubes[0] + cubes[1]) + (cubes[2] + cubes[3])) + (cubes[4] + cubes[5])
        )
        return (dens[0] + inside + back, sum_f, sum_c)

    down = limits(-1, site_u, site_v)
    up = limits(1, site_u, site_v)
    zero = jnp.zeros((8, 128), f32)

    def density_pair(t, carry):
        carry = density(2 * t, -1, down, carry)
        return density(2 * t + 1, 1, up, carry)

    _, sum_f, sum_c = lax.fori_loop(0, planes // 2 + 2, density_pair, (zero, zero, zero))

    def embedding(e):
        w = 1.0 + f32(dens_scale) * rho[e]
        inv = lax.rsqrt(w)
        embed[e] = f32(-0.5 * embed_scale * slope_ratio) * inv
        return w * inv - f32(bulk_root)

    embedding(0)
    embedding(1)
    embedding(HALO + planes)
    embedding(HALO + planes + 1)

    def embed_some(t, total):
        parts = [embedding(HALO + t * 8 + j) for j in range(8)]
        return total + (
            ((parts[0] + parts[1]) + (parts[2] + parts[3]))
            + ((parts[4] + parts[5]) + (parts[6] + parts[7]))
        )

    roots = lax.fori_loop(0, planes // 8, embed_some, zero)
    energy_ref[...] = f32(-embed_scale) * roots + f32(pair_energy_scale) * (
        sum_f + f32(pair_shift - dens_shift) * sum_c
    )

    def force(e, step, carry):
        own = embed[e]
        nxt = embed[e + 1]
        at_v, at_u, at_uv = partners(nxt, step, lanes)
        partner = (own + nxt, own + at_v, own + at_u, own + at_uv, nxt + at_v, nxt + at_u)
        weight = [slopes[e, k, 0] + partner[k] * slopes[e, k, 1] for k in range(6)]
        out = []
        for axis in range(3):
            g = [weight[k] * seps[e, k, axis] for k in range(6)]
            total = carry[axis] + ((g[0] + g[1]) + (g[2] + g[3]))
            force_ref[axis, jnp.maximum(e - HALO, 0)] = f32(force_scale) * total
            back = gather_back(g[1] + g[4], g[2] + g[5], g[3], step, lanes)
            out.append((g[4] + g[5]) - g[0] - back)
        return tuple(out)

    def force_pair(t, carry):
        carry = force(2 * t, -1, carry)
        return force(2 * t + 1, 1, carry)

    lax.fori_loop(0, planes // 2 + 1, force_pair, (zero, zero, zero))


def image_forces(own, low, high):
    vmem = pl.BlockSpec(memory_space=pltpu.VMEM)
    planes = own.shape[1]
    rows = planes + 2 * HALO
    return pl.pallas_call(
        force_kernel,
        out_shape=(
            jax.ShapeDtypeStruct((3, planes, 8, 128), jnp.float32),
            jax.ShapeDtypeStruct((8, 128), jnp.float32),
        ),
        in_specs=[vmem] * 3,
        out_specs=(vmem, vmem),
        scratch_shapes=[
            pltpu.VMEM((3, rows + 2, 8, 128), jnp.float32),
            pltpu.VMEM((rows, 6, 3, 8, 128), jnp.float32),
            pltpu.VMEM((rows, 6, 2, 8, 128), jnp.float32),
            pltpu.VMEM((rows, 8, 128), jnp.float32),
            pltpu.VMEM((rows, 8, 128), jnp.float32),
        ],
        compiler_params=pltpu.CompilerParams(vmem_limit_bytes=32 * 1024 * 1024),
        cost_estimate=pl.CostEstimate(
            flops=40_000_000, bytes_accessed=30_000_000, transcendentals=0
        ),
        name="slab_forces",
    )(own, low, high)


def total_of(tile):
    return jnp.sum(jnp.sum(tile, axis=0, keepdims=True), axis=1, keepdims=True)


def moment_kernel(count, *refs):
    path, forces, speeds = refs[: count + 2], refs[count + 2 : 2 * count + 2], refs[2 * count + 2 : 3 * count + 2]
    energies, out_ref, acc = refs[3 * count + 2 : 4 * count + 2], refs[4 * count + 2], refs[4 * count + 3]
    step = pl.program_id(0)
    planes = path[0].shape[1]
    zero = jnp.zeros((8, 128), jnp.float32)

    @pl.when(step == 0)
    def _():
        acc[...] = jnp.zeros_like(acc)

    def one(p, carry):
        carry = list(carry)
        for axis in range(3):
            at = [ref[axis, p] for ref in path]
            diff = [at[j + 1] - at[j] for j in range(count + 1)]
            square = [d * d for d in diff]
            for j in range(count):
                force, speed = forces[j][axis, p], speeds[j][axis, p]
                terms = (
                    force * force,
                    force * diff[j + 1],
                    force * diff[j],
                    square[j + 1],
                    square[j],
                    diff[j] * diff[j + 1],
                    speed * speed,
                )
                for k, term in enumerate(terms):
                    carry[7 * j + k] = carry[7 * j + k] + term
        return tuple(carry)

    def some(t, carry):
        for j in range(2):
            carry = one(2 * t + j, carry)
        return carry

    sums = lax.fori_loop(0, planes // 2, some, (zero,) * (7 * count))
    for k in range(7 * count):
        acc[k] += sums[k]

    @pl.when(step == pl.num_programs(0) - 1)
    def _():
        lane = lax.broadcasted_iota(jnp.int32, (1, 128), 1)
        row = jnp.zeros((1, 128), jnp.float32)
        for j in range(count):
            row = row + jnp.where(lane == 8 * j, total_of(energies[j][...]), 0.0)
            for k in range(7):
                row = row + jnp.where(lane == 8 * j + 1 + k, total_of(acc[7 * j + k]), 0.0)
        out_ref[...] = jnp.broadcast_to(row, out_ref.shape)


def moments(path, forces, speeds, energies, copies, chunk):
    count = len(forces)
    planes = path[0].shape[1]
    block = pl.BlockSpec((3, chunk, 8, 128), lambda t: (0, t, 0, 0))
    tile = pl.BlockSpec((8, 128), lambda t: (0, 0))
    return pl.pallas_call(
        functools.partial(moment_kernel, count),
        grid=(planes // chunk,),
        out_shape=jax.ShapeDtypeStruct((copies, 128), jnp.float32),
        in_specs=[block] * (3 * count + 2) + [tile] * count,
        out_specs=pl.BlockSpec((copies, 128), lambda t: (0, 0)),
        scratch_shapes=[pltpu.VMEM((7 * count, 8, 128), jnp.float32)],
        compiler_params=pltpu.CompilerParams(vmem_limit_bytes=32 * 1024 * 1024),
        name="path_moments",
    )(*path, *forces, *speeds, *energies)


def path_terms(summary, images):
    lane = lax.broadcasted_iota(jnp.int32, (8, 128), 1)
    image = lax.broadcasted_iota(jnp.int32, (8, 128), 0)

    def column(k):
        picked = jnp.sum(jnp.where(lane == k, summary, 0.0), axis=1, keepdims=True)
        return jnp.broadcast_to(picked, (8, 128))

    e_here, ff, f_fwd, f_bwd, fwd_sq, bwd_sq, fwd_bwd, speed_sq = [column(k) for k in range(8)]
    e_prev = pltpu.roll(e_here, 1, 0)
    e_next = pltpu.roll(e_here, 7, 0)
    inner = (image > 0) & (image < images - 1)
    rise = e_next - e_here
    fall = e_here - e_prev
    larger = jnp.maximum(jnp.abs(rise), jnp.abs(fall))
    smaller = jnp.minimum(jnp.abs(rise), jnp.abs(fall))
    upward = (e_next > e_here) & (e_here > e_prev)
    downward = (e_next < e_here) & (e_here < e_prev)
    toward = e_next > e_prev
    weight_fwd = jnp.where(
        upward, 1.0, jnp.where(downward, 0.0, jnp.where(toward, larger, smaller))
    )
    weight_bwd = jnp.where(
        upward, 0.0, jnp.where(downward, 1.0, jnp.where(toward, smaller, larger))
    )
    tangent_sq = (
        weight_fwd * weight_fwd * fwd_sq
        + 2.0 * weight_fwd * weight_bwd * fwd_bwd
        + weight_bwd * weight_bwd * bwd_sq
    )
    norm_sq = tangent_sq + stabilizer
    force_tan = weight_fwd * f_fwd + weight_bwd * f_bwd
    spring = spring_const * (jnp.sqrt(fwd_sq + stabilizer) - jnp.sqrt(bwd_sq + stabilizer))
    coefficient = -force_tan / norm_sq + spring / jnp.sqrt(norm_sq)
    neb_sq = ff + 2.0 * coefficient * force_tan + coefficient * coefficient * tangent_sq

    def over_inner(value):
        return jnp.sum(jnp.where(inner, value, 0.0), axis=0, keepdims=True)

    force_norm = jnp.sqrt(over_inner(neb_sq) + stabilizer)
    speed_norm = jnp.sqrt(over_inner(speed_sq) + stabilizer)
    gain = jnp.broadcast_to(fire_mixing * (speed_norm / force_norm) + time_step, (8, 128))
    keep = jnp.where(inner, 1.0 - fire_mixing, 0.0)
    push = jnp.where(inner, gain, 0.0)
    along_fwd = jnp.where(inner, gain * coefficient * weight_fwd, 0.0)
    along_bwd = jnp.where(inner, gain * coefficient * weight_bwd, 0.0)
    return keep, push, along_fwd, along_bwd


def update_kernel(count, images, first_ref, gathered_ref, *refs):
    path, forces, speeds = refs[: count + 2], refs[count + 2 : 2 * count + 2], refs[2 * count + 2 : 3 * count + 2]
    moved, new_speeds = refs[3 * count + 2 : 4 * count + 2], refs[4 * count + 2 : 5 * count + 2]
    terms = refs[5 * count + 2]
    planes = path[0].shape[1]

    @pl.when(pl.program_id(0) == 0)
    def _():
        image = lax.broadcasted_iota(jnp.int32, (8, 128), 0)
        lane = lax.broadcasted_iota(jnp.int32, (8, 128), 1)
        summary = jnp.zeros((8, 128), jnp.float32)
        per_group = gathered_ref.shape[0] // (images // count)
        for g in range(images // count):
            rows = gathered_ref[g * per_group : (g + 1) * per_group, :]
            row = jnp.broadcast_to(jnp.sum(rows, axis=0, keepdims=True), (8, 128))
            for j in range(count):
                own_row = row if j == 0 else pltpu.roll(row, 128 - 8 * j, 1)
                summary = jnp.where(image == g * count + j, own_row, summary)
        values = path_terms(summary, images)
        for j in range(count):
            here = image == first_ref[0] + j
            for k, value in enumerate(values):
                own = jnp.sum(jnp.where(here, value, 0.0), axis=0, keepdims=True)
                terms[j, k] = jnp.broadcast_to(own, (8, 128))

    def one(p):
        for axis in range(3):
            at = [ref[axis, p] for ref in path]
            for j in range(count):
                speed = (
                    terms[j, 0] * speeds[j][axis, p]
                    + terms[j, 1] * forces[j][axis, p]
                    + terms[j, 2] * (at[j + 2] - at[j + 1])
                    + terms[j, 3] * (at[j + 1] - at[j])
                )
                new_speeds[j][axis, p] = speed
                moved[j][axis, p] = at[j + 1] + time_step * speed

    def some(t, carry):
        for j in range(2):
            one(2 * t + j)
        return carry

    lax.fori_loop(0, planes // 2, some, 0)


def update(first, gathered, path, forces, speeds, images, chunk):
    count = len(forces)
    planes = path[0].shape[1]
    block = pl.BlockSpec((3, chunk, 8, 128), lambda t: (0, t, 0, 0))
    out = jax.ShapeDtypeStruct((3, planes, 8, 128), jnp.float32)
    results = pl.pallas_call(
        functools.partial(update_kernel, count, images),
        grid=(planes // chunk,),
        out_shape=(out,) * (2 * count),
        in_specs=[
            pl.BlockSpec(memory_space=pltpu.SMEM),
            pl.BlockSpec(gathered.shape, lambda t: (0, 0)),
        ]
        + [block] * (3 * count + 2),
        out_specs=(block,) * (2 * count),
        scratch_shapes=[pltpu.VMEM((count, 4, 8, 128), jnp.float32)],
        compiler_params=pltpu.CompilerParams(vmem_limit_bytes=32 * 1024 * 1024),
        name="fire_update",
    )(first, gathered, *path, *forces, *speeds)
    return results[:count], results[count:]


def local(displacement, velocity):
    planes = displacement.shape[2] // (SIDE * SIDE)
    own_image = lax.axis_index("image")
    images = lax.axis_size("image")
    slabs = lax.axis_size("domain")
    ahead = [(i, (i + 1) % slabs) for i in range(slabs)]
    behind = [(target, source) for source, target in ahead]
    first = own_image.astype(jnp.int32).reshape(1)
    current = displacement.reshape(3, planes, 8, 128)
    moving = velocity.reshape(3, planes, 8, 128)
    for step_index in range(FIRE_STEPS):
        low = lax.ppermute(current[:, -HALO:], "domain", ahead)
        high = lax.ppermute(current[:, :HALO], "domain", behind)
        before = lax.ppermute(current, "image", [(i, i + 1) for i in range(images - 1)])
        after = lax.ppermute(current, "image", [(i + 1, i) for i in range(images - 1)])
        forces, energy = image_forces(current, low, high)
        path = (before, current, after)
        payload = moments(path, (forces,), (moving,), (energy,), images * slabs, 16)
        gathered = lax.all_to_all(payload, ("image", "domain"), 0, 0, tiled=True)
        (current,), (moving,) = update(first, gathered, path, (forces,), (moving,), images, 16)
    return (current.reshape(displacement.shape), moving.reshape(velocity.shape))


def solution(mesh):
    spec = P("image", None, "domain")
    return jax.shard_map(
        local,
        mesh=mesh,
        in_specs=(spec, spec),
        out_specs=(spec, spec),
        check_vma=False,
    )
```

profile of v0, /device:TPU:0, one launch (start us, length us, event | category | flops | bytes accessed | tf_op | source)
XLA Modules:
  0.0 220.5 jit_solution(16772223812065538247)
XLA Ops:
  0.6 1.3 collective-permute-start.1
  1.9 4.6 %collective-permute-start = (f32[3,96,8,128]{3,2,1,0:T(8,128)}, f32[3,96,8,128]{3,2,1,0:T(8,128)S(1)}, u32[]{:S(2)}, u32[]{:S(2)}) collective-permute-start(f32[3,96,8,128]{3,2,1,0:T(8,128)} %bitcast.14), channel_id=1, source_target_pairs={{0,16},{16,32},{32,48},{48,64},{64,80},{80,96},{96,112},{1,17},{17... | collective-permute-start | bytes 3538952 | tf_op jit(solution)/shard_map/ppermute | solution.py:431
  6.6 0.8 fusion.1
  7.3 5.3 %collective-permute-start.3 = (f32[3,2,8,128]{3,2,1,0:T(8,128)S(1)}, f32[3,2,8,128]{3,2,1,0:T(8,128)S(1)}, u32[]{:S(2)}, u32[]{:S(2)}) collective-permute-start(f32[3,2,8,128]{3,2,1,0:T(8,128)S(1)} %get-tuple-element.26), channel_id=1, source_target_pairs={{1,0},{2,1},{3,2},{4,3},{5,4},{6,5},{7,6},{8,7},{9,8},{10,9},{11,1... | collective-permute-start | bytes 73736 | tf_op jit(solution)/shard_map/ppermute | solution.py:430
  12.6 0.0 collective-permute-start.2
  12.6 1.5 collective-permute-done.3.high_ref
  14.1 5.7 %collective-permute-done.2.low_ref = f32[3,2,8,128]{3,2,1,0:T(8,128)S(1)} collective-permute-done((f32[3,2,8,128]{3,2,1,0:T(8,128)S(1)}, f32[3,2,8,128]{3,2,1,0:T(8,128)S(1)}, u32[]{:S(2)}, u32[]{:S(2)}) %collective-permute-start.2) | collective-permute-done | bytes 24608 | tf_op jit(solution)/shard_map/ppermute | solution.py:429
  19.8 0.0 copy-start
  19.8 1.3 copy-done
  21.1 0.0 copy-start.2
  21.1 29.2 %slab_forces.2 = (f32[3,96,8,128]{3,2,1,0:T(8,128)S(1)}, f32[8,128]{1,0:T(8,128)S(1)}) custom-call(f32[3,96,8,128]{3,2,1,0:T(8,128)S(1)} %bitcast.16, f32[3,2,8,128]{3,2,1,0:T(8,128)S(1)} %collective-permute-done.2.low_ref, f32[3,2,8,128]{3,2,1,0:T(8,128)S(1)} %collective-permute-done.3.high_ref), custom_call_target="tpu_custom_call" | custom-call | flops 40000000 | bytes 30000000 | tf_op jit(solution)/shard_map/slab_forces/pallas_call | solution.py:205
  50.2 0.0 copy-start.5
  50.2 0.0 collective-permute-done.1.refs_2_
  50.3 6.3 %collective-permute-done.refs_0_ = f32[3,96,8,128]{3,2,1,0:T(8,128)S(1)} collective-permute-done((f32[3,96,8,128]{3,2,1,0:T(8,128)}, f32[3,96,8,128]{3,2,1,0:T(8,128)S(1)}, u32[]{:S(2)}, u32[]{:S(2)}) %collective-permute-start) | collective-permute-done | bytes 1179680 | tf_op jit(solution)/shard_map/ppermute | solution.py:431
  56.6 0.0 copy-start.3
  56.6 0.0 copy-done.2
  56.6 0.0 copy-start.1
  56.6 1.6 path_moments.2
  58.2 0.0 copy-done.5
  58.2 0.0 copy-done.3
  58.2 0.0 copy-start.7
  58.2 0.6 copy-done.7
  58.8 42.2 %all-to-all-start = ((f32[128,1,128]{2,1,0:T(1,128)}), f32[128,1,128]{2,1,0:T(1,128)}, u32[]{:S(2)}, u32[]{:S(2)}) async-start(f32[128,1,128]{2,1,0:T(1,128)} %bitcast.21), calls=%async_computation | async-start | bytes 131072 | tf_op jit(solution)/shard_map/all_to_all | solution.py:436
  101.0 9.3 %all-to-all-done = f32[128,1,128]{2,1,0:T(1,128)} async-done(((f32[128,1,128]{2,1,0:T(1,128)}), f32[128,1,128]{2,1,0:T(1,128)}, u32[]{:S(2)}, u32[]{:S(2)}) %all-to-all-start) | async-done | bytes 65568 | tf_op jit(solution)/shard_map/all_to_all | solution.py:436
  110.3 0.0 copy-done.1
  110.3 0.0 copy-start.4
  110.3 1.3 copy-done.4
  111.6 0.0 copy-start.6
  111.6 1.3 copy-done.6
  112.8 2.5 %fire_update.2 = (f32[3,96,8,128]{3,2,1,0:T(8,128)S(1)}, f32[3,96,8,128]{3,2,1,0:T(8,128)S(1)}) custom-call(s32[1]{0:T(128)} %bitcast.first_ref, f32[128,128]{1,0:T(8,128)} %bitcast.5.gathered_ref, f32[3,96,8,128]{3,2,1,0:T(8,128)S(1)} %copy-done.4, f32[3,96,8,128]{3,2,1,0:T(8,128)S(1)} %bitcast.18, f32[3,96,8,128]{3,2,1,0:T(8,128)S(1)} %collective-permute-done.1.refs_2_, ...), custom_call_target="tpu_custom_call" | custom-call | tf_op jit(solution)/shard_map/fire_update/pallas_call | solution.py:401
  115.4 1.3 collective-permute-start.5
  116.7 4.6 %collective-permute-start.4 = (f32[3,96,8,128]{3,2,1,0:T(8,128)S(1)}, f32[3,96,8,128]{3,2,1,0:T(8,128)S(1)}, u32[]{:S(2)}, u32[]{:S(2)}) collective-permute-start(f32[3,96,8,128]{3,2,1,0:T(8,128)S(1)} %get-tuple-element.12.own_ref.refs_1_), channel_id=1, source_target_pairs={{0,16},{16,32},{32,48},{48,64},{64,80},{80,96},{96,112},{1,17},{17... | collective-permute-start | bytes 3538952 | tf_op jit(solution)/shard_map/ppermute | solution.py:431
  121.3 0.4 collective-permute-start.7
  121.7 0.2 collective-permute-start.6
  121.9 1.3 collective-permute-done.7.high_ref
  123.2 5.7 %collective-permute-done.6.low_ref = f32[3,2,8,128]{3,2,1,0:T(8,128)S(1)} collective-permute-done((f32[3,2,8,128]{3,2,1,0:T(8,128)S(1)}, f32[3,2,8,128]{3,2,1,0:T(8,128)S(1)}, u32[]{:S(2)}, u32[]{:S(2)}) %collective-permute-start.6) | collective-permute-done | bytes 24608 | tf_op jit(solution)/shard_map/ppermute | solution.py:429
  128.9 29.2 %slab_forces.3 = (f32[3,96,8,128]{3,2,1,0:T(8,128)S(1)}, f32[8,128]{1,0:T(8,128)S(1)}) custom-call(f32[3,96,8,128]{3,2,1,0:T(8,128)S(1)} %get-tuple-element.12.own_ref.refs_1_, f32[3,2,8,128]{3,2,1,0:T(8,128)S(1)} %collective-permute-done.6.low_ref, f32[3,2,8,128]{3,2,1,0:T(8,128)S(1)} %collective-permute-done.7.high_ref), custom_call_target="tpu_custom_call" | custom-call | flops 40000000 | bytes 30000000 | tf_op jit(solution)/shard_map/slab_forces/pallas_call | solution.py:205
  158.0 0.0 collective-permute-done.5.refs_2_
  158.0 11.4 %collective-permute-done.4.refs_0_ = f32[3,96,8,128]{3,2,1,0:T(8,128)S(1)} collective-permute-done((f32[3,96,8,128]{3,2,1,0:T(8,128)S(1)}, f32[3,96,8,128]{3,2,1,0:T(8,128)S(1)}, u32[]{:S(2)}, u32[]{:S(2)}) %collective-permute-start.4) | collective-permute-done | bytes 1179680 | tf_op jit(solution)/shard_map/ppermute | solution.py:431
  169.5 1.6 path_moments.3
  171.0 46.1 %all_to_all.22 = f32[128,1,128]{2,1,0:T(1,128)S(1)} all-to-all(f32[128,1,128]{2,1,0:T(1,128)S(1)} %bitcast.23), channel_id=1, replica_groups=mesh['image'=8,'domain'=16] {'image','domain'}, dimensions={0} | all-to-all | bytes 131072 | tf_op jit(solution)/shard_map/all_to_all | solution.py:436
  217.2 3.3 %fire_update.3 = (f32[3,96,8,128]{3,2,1,0:T(8,128)}, f32[3,96,8,128]{3,2,1,0:T(8,128)}) custom-call(s32[1]{0:T(128)} %bitcast.first_ref, f32[128,128]{1,0:T(8,128)S(1)} %bitcast.22, f32[3,96,8,128]{3,2,1,0:T(8,128)S(1)} %collective-permute-done.4.refs_0_, f32[3,96,8,128]{3,2,1,0:T(8,128)S(1)} %get-tuple-element.12.own_ref.refs_1_, ...), custom_call_target="tpu_custom_call" | custom-call | tf_op jit(solution)/shard_map/fire_update/pallas_call | solution.py:401
  (1 shorter events, 0.0 us)
Async XLA Ops:
  0.6 49.6 %collective-permute-start.1 = (f32[3,96,8,128]{3,2,1,0:T(8,128)}, f32[3,96,8,128]{3,2,1,0:T(8,128)S(1)}, u32[]{:S(2)}, u32[]{:S(2)}) collective-permute-start(f32[3,96,8,128]{3,2,1,0:T(8,128)} %bitcast.13), channel_id=1, source_target_pairs={{16,0},{32,16},{48,32},{64,48},{80,64},{96,80},{112,96},{17,1},{33... | collective-permute-start | bytes 3538952 | tf_op jit(solution)/shard_map/ppermute | solution.py:432
  1.9 54.7 %collective-permute-start = (f32[3,96,8,128]{3,2,1,0:T(8,128)}, f32[3,96,8,128]{3,2,1,0:T(8,128)S(1)}, u32[]{:S(2)}, u32[]{:S(2)}) collective-permute-start(f32[3,96,8,128]{3,2,1,0:T(8,128)} %bitcast.14), channel_id=1, source_target_pairs={{0,16},{16,32},{32,48},{48,64},{64,80},{80,96},{96,112},{1,17},{17... | collective-permute-start | bytes 3538952 | tf_op jit(solution)/shard_map/ppermute | solution.py:431
  7.3 6.8 %collective-permute-start.3 = (f32[3,2,8,128]{3,2,1,0:T(8,128)S(1)}, f32[3,2,8,128]{3,2,1,0:T(8,128)S(1)}, u32[]{:S(2)}, u32[]{:S(2)}) collective-permute-start(f32[3,2,8,128]{3,2,1,0:T(8,128)S(1)} %get-tuple-element.26), channel_id=1, source_target_pairs={{1,0},{2,1},{3,2},{4,3},{5,4},{6,5},{7,6},{8,7},{9,8},{10,9},{11,1... | collective-permute-start | bytes 73736 | tf_op jit(solution)/shard_map/ppermute | solution.py:430
  12.6 7.2 %collective-permute-start.2 = (f32[3,2,8,128]{3,2,1,0:T(8,128)S(1)}, f32[3,2,8,128]{3,2,1,0:T(8,128)S(1)}, u32[]{:S(2)}, u32[]{:S(2)}) collective-permute-start(f32[3,2,8,128]{3,2,1,0:T(8,128)S(1)} %get-tuple-element.27), channel_id=1, source_target_pairs={{0,1},{1,2},{2,3},{3,4},{4,5},{5,6},{6,7},{7,8},{8,9},{9,10},{10,1... | collective-permute-start | bytes 73736 | tf_op jit(solution)/shard_map/ppermute | solution.py:429
  19.8 1.3 copy-start
  21.1 35.5 %copy-start.2 = (f32[1,3,98304]{2,0,1:T(1,128)S(1)}, f32[1,3,98304]{2,0,1:T(1,128)}, u32[]{:S(2)}) copy-start(f32[1,3,98304]{2,0,1:T(1,128)} %param.3) | copy-start | bytes 3538948
  50.2 8.0 %copy-start.5 = (f32[3,96,8,128]{3,2,1,0:T(8,128)}, f32[3,96,8,128]{3,2,1,0:T(8,128)S(1)}, u32[]{:S(2)}) copy-start(f32[3,96,8,128]{3,2,1,0:T(8,128)S(1)} %get-tuple-element.10.refs_3_) | copy-start | bytes 3538948
  56.6 1.6 copy-start.3
  56.6 53.7 %copy-start.1 = (f32[1,3,98304]{2,0,1:T(1,128)S(1)}, f32[1,3,98304]{2,0,1:T(1,128)}, u32[]{:S(2)}) copy-start(f32[1,3,98304]{2,0,1:T(1,128)} %param.2) | copy-start | bytes 3538948
  58.2 0.6 copy-start.7
  58.8 51.5 %all-to-all-start = ((f32[128,1,128]{2,1,0:T(1,128)}), f32[128,1,128]{2,1,0:T(1,128)}, u32[]{:S(2)}, u32[]{:S(2)}) async-start(f32[128,1,128]{2,1,0:T(1,128)} %bitcast.21), calls=%async_computation | async-start | bytes 131072 | tf_op jit(solution)/shard_map/all_to_all | solution.py:436
  110.3 1.3 copy-start.4
  111.6 1.3 copy-start.6
  115.4 42.7 %collective-permute-start.5 = (f32[3,96,8,128]{3,2,1,0:T(8,128)S(1)}, f32[3,96,8,128]{3,2,1,0:T(8,128)S(1)}, u32[]{:S(2)}, u32[]{:S(2)}) collective-permute-start(f32[3,96,8,128]{3,2,1,0:T(8,128)S(1)} %get-tuple-element.12.own_ref.refs_1_), channel_id=1, source_target_pairs={{16,0},{32,16},{48,32},{64,48},{80,64},{96,80},{112,96},{17,1},{33... | collective-permute-start | bytes 3538952 | tf_op jit(solution)/shard_map/ppermute | solution.py:432
  116.7 52.8 %collective-permute-start.4 = (f32[3,96,8,128]{3,2,1,0:T(8,128)S(1)}, f32[3,96,8,128]{3,2,1,0:T(8,128)S(1)}, u32[]{:S(2)}, u32[]{:S(2)}) collective-permute-start(f32[3,96,8,128]{3,2,1,0:T(8,128)S(1)} %get-tuple-element.12.own_ref.refs_1_), channel_id=1, source_target_pairs={{0,16},{16,32},{32,48},{48,64},{64,80},{80,96},{96,112},{1,17},{17... | collective-permute-start | bytes 3538952 | tf_op jit(solution)/shard_map/ppermute | solution.py:431
  121.3 1.9 collective-permute-start.7
  121.7 7.2 %collective-permute-start.6 = (f32[3,2,8,128]{3,2,1,0:T(8,128)S(1)}, f32[3,2,8,128]{3,2,1,0:T(8,128)S(1)}, u32[]{:S(2)}, u32[]{:S(2)}) collective-permute-start(f32[3,2,8,128]{3,2,1,0:T(8,128)S(1)} %get-tuple-element.25), channel_id=1, source_target_pairs={{0,1},{1,2},{2,3},{3,4},{4,5},{5,6},{6,7},{7,8},{8,9},{9,10},{10,1... | collective-permute-start | bytes 73736 | tf_op jit(solution)/shard_map/ppermute | solution.py:429
where the time goes:
time: 221 us; the launch traced here: 220 us
  Pallas kernels  67.3 us (30%)
  starting transfers between devices  59.9 us (27%)
  blocking collectives  46.1 us (21%)
  waiting for transfers between devices  41.2 us (19%)
  local copies, waits for them, and re-layouts  5.21 us (2%)
    pallas_call x2, Pallas kernels, image_forces(): pl.pallas_call(force_kernel, out_shape=(jax.ShapeDtypeStruct((3, planes,...  58.3 us
    all_to_all x1, blocking collectives, local(): gathered = lax.all_to_all(payload, ('image', 'domain'), 0, 0, tiled=True)  46.1 us
    all_to_all x1, starting transfers between devices, local(): gathered = lax.all_to_all(payload, ('image', 'domain'), 0, 0, tiled=True)  42.2 us
    ppermute x2, waiting for transfers between devices, local(): lax.ppermute(current, 'image', [(i, i + 1) for i in range(images - 1)])  17.8 us
    ppermute x2, waiting for transfers between devices, local(): low = lax.ppermute(current[:, -HALO:], 'domain', ahead)  11.3 us
    all_to_all x1, waiting for transfers between devices, local(): gathered = lax.all_to_all(payload, ('image', 'domain'), 0, 0, tiled=True)  9.29 us
    ppermute x2, starting transfers between devices, local(): lax.ppermute(current, 'image', [(i, i + 1) for i in range(images - 1)])  9.25 us
    pallas_call x2, Pallas kernels, update(): pl.pallas_call(functools.partial(update_kernel, count, images), grid=(pla...  5.85 us
  transfers between devices with their start and end apart: 9, of which 7 were waited for; matrix products, arithmetic and copies ran while one was open for 0% of the time, Pallas kernels for 26%

commit v1 on v0

v1 whole, which is shorter than its diff:
```python
import functools
import math

import jax
import jax.numpy as jnp
from jax import lax
from jax.experimental import pallas as pl
from jax.experimental.pallas import tpu as pltpu
from jax.sharding import PartitionSpec as P

SIDE = 32
FIRE_STEPS = 2
QUANTITIES = 8
HALO = 2
PLACE_UNROLL = 16
EMBED_UNROLL = 48
FINISH_UNROLL = 16
CHUNKS = 2
MOMENT_CHUNK = 12
UPDATE_CHUNK = 12

lattice_const = 3.615
cutoff_sq = 9.61
nearest_sq = 6.533136
pair_scale = 30.0
pair_depth = 0.3
embed_scale = 1.2
bulk_root = 3.605551275463989
spring_const = 2.0
time_step = 0.1
fire_mixing = 0.1
stabilizer = 1e-06

reach_root = math.sqrt(cutoff_sq)
unit_half = 0.5 * lattice_const / reach_root
kappa = cutoff_sq / nearest_sq
dens_shift = (2.0 - kappa) / kappa
pair_shift = (2.5 - 2.0 * kappa) / (2.0 * kappa)
dens_scale = pair_scale * kappa
pair_energy_scale = pair_scale * pair_depth * 2.0 * kappa
dens_slope_shift = 0.75 * dens_shift
pair_slope_shift = 0.75 * pair_shift
dens_slope_scale = -4.0 * dens_scale / cutoff_sq
pair_slope_scale = -4.0 * pair_energy_scale / cutoff_sq
slope_ratio = dens_slope_scale / pair_slope_scale
force_scale = 2.0 * pair_slope_scale * reach_root


def shift(field, step_u, step_v, lanes):
    reach = step_u * SIDE + step_v
    turned = pltpu.roll(field, (-reach) % 128, 1)
    if step_u == 0:
        return turned
    carried = pltpu.roll(turned, (-step_u) % 8, 0)
    return jnp.where(lanes >= 128 - reach if reach > 0 else lanes < -reach, carried, turned)


def partners(field, step, lanes):
    return (
        shift(field, 0, step, lanes),
        shift(field, step, 0, lanes),
        shift(field, step, step, lanes),
    )


def gather_back(at_v, at_u, at_uv, step, lanes):
    return (
        shift(at_v, 0, -step, lanes)
        + shift(at_u, -step, 0, lanes)
        + shift(at_uv, -step, -step, lanes)
    )


def limits(step, u, v):
    far = jnp.float32(-1e30)
    in_u = (u + step >= 0) & (u + step < SIDE)
    in_v = (v + step >= 0) & (v + step < SIDE)
    one = jnp.ones_like(u, jnp.float32)
    return (
        jnp.where(in_v, one, far),
        jnp.where(in_u, one, far),
        jnp.where(in_u & in_v, one, far),
    )


def side_of(plane):
    return 1 if plane % 2 == 0 else -1


def force_kernel(
    own_ref, low_ref, high_ref, force_ref, energy_ref, pos, turned, seps, slopes, rho, back, embed, force_back
):
    f32 = jnp.float32
    planes = own_ref.shape[1]
    top = planes + 2 * HALO
    lanes = lax.broadcasted_iota(jnp.int32, (8, 128), 1)
    subl = lax.broadcasted_iota(jnp.int32, (8, 128), 0)
    site_u = subl * 4 + lanes // SIDE
    site_v = lanes % SIDE
    inverse = f32(1.0 / reach_root)
    zero = jnp.zeros((8, 128), f32)

    def place(q, side, values):
        for axis in range(3):
            value = values[axis] * inverse
            pos[axis, q] = value
            for k, seen in enumerate(partners(value, side, lanes)):
                turned[axis, k, q] = seen

    for q in range(HALO):
        place(q, side_of(q), [low_ref[axis, q] for axis in range(3)])
        place(planes + HALO + q, side_of(q), [high_ref[axis, q] for axis in range(3)])

    def place_some(t, carry):
        for j in range(PLACE_UNROLL):
            p = t * PLACE_UNROLL + j
            place(p + HALO, side_of(j), [own_ref[axis, p] for axis in range(3)])
        return carry

    lax.fori_loop(0, planes // PLACE_UNROLL, place_some, 0)

    def separations(e, step):
        h = f32(unit_half)
        sh = f32(step * unit_half)
        own = [pos[axis, e] for axis in range(3)]
        nxt = [pos[axis, e + 1] for axis in range(3)]
        seen = [[turned[axis, k, e + 1] for k in range(3)] for axis in range(3)]
        own_x = own[0] - h
        y_of = (own[1] + sh, own[1], own[1] - sh)
        z_of = (own[2] - sh, own[2], own[2] + sh)
        cross = [
            (nxt[0] - own_x, nxt[1] - y_of[0], nxt[2] - z_of[1]),
            (seen[0][0] - own_x, seen[1][0] - y_of[1], seen[2][0] - z_of[2]),
            (seen[0][1] - own_x, seen[1][1] - y_of[1], seen[2][1] - z_of[0]),
            (seen[0][2] - own_x, seen[1][2] - y_of[2], seen[2][2] - z_of[1]),
        ]
        near_y = nxt[1] - sh
        near_zv = nxt[2] + sh
        near_zu = nxt[2] - sh
        inside = [
            (seen[0][0] - nxt[0], seen[1][0] - near_y, seen[2][0] - near_zv),
            (seen[0][1] - nxt[0], seen[1][1] - near_y, seen[2][1] - near_zu),
        ]
        return cross + inside

    def density(e, step, bounds, carry):
        rho_part, sum_f, sum_c = carry
        one = jnp.ones((8, 128), f32)
        tops = (one, bounds[0], bounds[1], bounds[2], bounds[0], bounds[1])
        dens, cubes = [], []
        for k, sep in enumerate(separations(e, step)):
            y = sep[0] * sep[0] + sep[1] * sep[1] + sep[2] * sep[2]
            c = jnp.maximum(tops[k] - y, 0.0)
            square = c * c
            cube = square * c
            dens.append(cube * (c + f32(dens_shift)))
            cubes.append(cube)
            for axis in range(3):
                seps[e, k, axis] = sep[axis]
            slopes[e, k, 0] = square * (c + f32(pair_slope_shift))
            slopes[e, k, 1] = square * (c + f32(dens_slope_shift))
        cross = (dens[0] + dens[1]) + (dens[2] + dens[3])
        inside = dens[4] + dens[5]
        rho[e] = rho_part + cross
        back[0, e + 1] = dens[1] + dens[4]
        back[1, e + 1] = dens[2] + dens[5]
        back[2, e + 1] = dens[3]
        weight = jnp.where((e >= 1) & (e <= planes), 1.0, 0.0).astype(f32)
        sum_f = sum_f + weight * (cross + inside)
        sum_c = sum_c + weight * (
            ((cubes[0] + cubes[1]) + (cubes[2] + cubes[3])) + (cubes[4] + cubes[5])
        )
        return (dens[0] + inside, sum_f, sum_c)

    down = limits(-1, site_u, site_v)
    up = limits(1, site_u, site_v)

    def density_pair(t, carry):
        carry = density(2 * t, -1, down, carry)
        return density(2 * t + 1, 1, up, carry)

    carry = lax.fori_loop(0, planes // 2 + 1, density_pair, (zero, zero, zero))
    _, sum_f, sum_c = density(planes + 2, -1, down, carry)

    def embedding(q, side):
        total = rho[q] + gather_back(back[0, q], back[1, q], back[2, q], side, lanes)
        w = 1.0 + f32(dens_scale) * total
        inv = lax.rsqrt(w)
        embed[0, q] = f32(-0.5 * embed_scale * slope_ratio) * inv
        return w * inv - f32(bulk_root)

    embedding(1, side_of(1))
    embedding(planes + HALO, side_of(0))

    def embed_some(t, total):
        for j in range(EMBED_UNROLL):
            total = total + embedding(HALO + t * EMBED_UNROLL + j, side_of(j))
        return total

    roots = lax.fori_loop(0, planes // EMBED_UNROLL, embed_some, zero)
    energy_ref[...] = f32(-embed_scale) * roots + f32(pair_energy_scale) * (
        sum_f + f32(pair_shift - dens_shift) * sum_c
    )

    def see(q, side):
        for k, seen in enumerate(partners(embed[0, q], side, lanes)):
            embed[1 + k, q] = seen

    see(planes + HALO, side_of(0))

    def see_some(t, carry):
        for j in range(EMBED_UNROLL):
            see(HALO + t * EMBED_UNROLL + j, side_of(j))
        return carry

    lax.fori_loop(0, planes // EMBED_UNROLL, see_some, 0)

    def force(e, keep, carry):
        own = embed[0, e]
        nxt = embed[0, e + 1]
        at_v, at_u, at_uv = [embed[1 + k, e + 1] for k in range(3)]
        partner = (own + nxt, own + at_v, own + at_u, own + at_uv, nxt + at_v, nxt + at_u)
        weight = [slopes[e, k, 0] + partner[k] * slopes[e, k, 1] for k in range(6)]
        out = []
        for axis in range(3):
            g = [weight[k] * seps[e, k, axis] for k in range(6)]
            if keep:
                force_ref[axis, e - HALO] = carry[axis] + ((g[0] + g[1]) + (g[2] + g[3]))
            force_back[axis, 0, e + 1] = g[1] + g[4]
            force_back[axis, 1, e + 1] = g[2] + g[5]
            force_back[axis, 2, e + 1] = g[3]
            out.append((g[4] + g[5]) - g[0])
        return tuple(out)

    def force_pair(t, carry):
        carry = force(HALO + 2 * t, True, carry)
        return force(HALO + 2 * t + 1, True, carry)

    lax.fori_loop(0, planes // 2, force_pair, force(1, False, (zero, zero, zero)))

    def finish(t, carry):
        for j in range(FINISH_UNROLL):
            p = t * FINISH_UNROLL + j
            for axis in range(3):
                parts = [force_back[axis, k, p + HALO] for k in range(3)]
                force_ref[axis, p] = f32(force_scale) * (
                    force_ref[axis, p] - gather_back(*parts, side_of(j), lanes)
                )
        return carry

    lax.fori_loop(0, planes // FINISH_UNROLL, finish, 0)


def image_forces(own, low, high):
    vmem = pl.BlockSpec(memory_space=pltpu.VMEM)
    planes = own.shape[1]
    rows = planes + 2 * HALO
    return pl.pallas_call(
        force_kernel,
        out_shape=(
            jax.ShapeDtypeStruct((3, planes, 8, 128), jnp.float32),
            jax.ShapeDtypeStruct((8, 128), jnp.float32),
        ),
        in_specs=[vmem] * 3,
        out_specs=(vmem, vmem),
        scratch_shapes=[
            pltpu.VMEM((3, rows, 8, 128), jnp.float32),
            pltpu.VMEM((3, 3, rows, 8, 128), jnp.float32),
            pltpu.VMEM((rows, 6, 3, 8, 128), jnp.float32),
            pltpu.VMEM((rows, 6, 2, 8, 128), jnp.float32),
            pltpu.VMEM((rows, 8, 128), jnp.float32),
            pltpu.VMEM((3, rows, 8, 128), jnp.float32),
            pltpu.VMEM((4, rows, 8, 128), jnp.float32),
            pltpu.VMEM((3, 3, rows, 8, 128), jnp.float32),
        ],
        compiler_params=pltpu.CompilerParams(vmem_limit_bytes=40 * 1024 * 1024),
        cost_estimate=pl.CostEstimate(
            flops=40_000_000, bytes_accessed=30_000_000, transcendentals=0
        ),
        name="slab_forces",
    )(own, low, high)


def total_of(tile):
    return jnp.sum(jnp.sum(tile, axis=0, keepdims=True), axis=1, keepdims=True)


def moment_kernel(side_ref, *refs):
    path, forces, speeds, energies = refs[:4], refs[4:6], refs[6:8], refs[8:10]
    out_ref, acc = refs[10], refs[11]
    step = pl.program_id(0)
    planes = path[0].shape[1]
    zero = jnp.zeros((8, 128), jnp.float32)

    @pl.when(step == 0)
    def _():
        acc[...] = jnp.zeros_like(acc)

    def one(p, carry):
        carry = list(carry)
        for axis in range(3):
            at = [ref[axis, p] for ref in path]
            diff = [at[j + 1] - at[j] for j in range(3)]
            square = [d * d for d in diff]
            for j in range(2):
                force, speed = forces[j][axis, p], speeds[j][axis, p]
                terms = (
                    force * force,
                    force * diff[j + 1],
                    force * diff[j],
                    square[j + 1],
                    square[j],
                    diff[j] * diff[j + 1],
                    speed * speed,
                )
                for k, term in enumerate(terms):
                    carry[7 * j + k] = carry[7 * j + k] + term
        return tuple(carry)

    def some(t, carry):
        for j in range(2):
            carry = one(2 * t + j, carry)
        return carry

    sums = lax.fori_loop(0, planes // 2, some, (zero,) * 14)
    for k in range(14):
        acc[k] += sums[k]

    @pl.when(step == pl.num_programs(0) - 1)
    def _():
        lane = lax.broadcasted_iota(jnp.int32, (1, 128), 1)
        odd = side_ref[0] == 1
        sign = jnp.where(odd, -1.0, 1.0).astype(jnp.float32)
        row = jnp.zeros((1, 128), jnp.float32)
        for j in range(2):
            ahead = [total_of(acc[7 * j + k]) for k in range(7)]
            values = (
                total_of(energies[j][...]),
                ahead[0],
                sign * jnp.where(odd, ahead[2], ahead[1]),
                sign * jnp.where(odd, ahead[1], ahead[2]),
                jnp.where(odd, ahead[4], ahead[3]),
                jnp.where(odd, ahead[3], ahead[4]),
                ahead[5],
                ahead[6],
            )
            for k, value in enumerate(values):
                row = row + jnp.where(lane == 8 * j + k, value, 0.0)
        out_ref[...] = jnp.broadcast_to(row, out_ref.shape)


def moments(side, path, forces, speeds, energies, copies, chunk):
    planes = path[0].shape[1]
    block = pl.BlockSpec((3, chunk, 8, 128), lambda t: (0, t, 0, 0))
    tile = pl.BlockSpec((8, 128), lambda t: (0, 0))
    return pl.pallas_call(
        moment_kernel,
        grid=(planes // chunk,),
        out_shape=jax.ShapeDtypeStruct((copies, 128), jnp.float32),
        in_specs=[pl.BlockSpec(memory_space=pltpu.SMEM)] + [block] * 8 + [tile] * 2,
        out_specs=pl.BlockSpec((copies, 128), lambda t: (0, 0)),
        scratch_shapes=[pltpu.VMEM((14, 8, 128), jnp.float32)],
        compiler_params=pltpu.CompilerParams(vmem_limit_bytes=32 * 1024 * 1024),
        name="path_moments",
    )(side, *path, *forces, *speeds, *energies)


def path_terms(summary, images):
    lane = lax.broadcasted_iota(jnp.int32, (8, 128), 1)
    image = lax.broadcasted_iota(jnp.int32, (8, 128), 0)

    def column(k):
        picked = jnp.sum(jnp.where(lane == k, summary, 0.0), axis=1, keepdims=True)
        return jnp.broadcast_to(picked, (8, 128))

    e_here, ff, f_fwd, f_bwd, fwd_sq, bwd_sq, fwd_bwd, speed_sq = [column(k) for k in range(8)]
    e_prev = pltpu.roll(e_here, 1, 0)
    e_next = pltpu.roll(e_here, 7, 0)
    inner = (image > 0) & (image < images - 1)
    rise = e_next - e_here
    fall = e_here - e_prev
    larger = jnp.maximum(jnp.abs(rise), jnp.abs(fall))
    smaller = jnp.minimum(jnp.abs(rise), jnp.abs(fall))
    upward = (e_next > e_here) & (e_here > e_prev)
    downward = (e_next < e_here) & (e_here < e_prev)
    toward = e_next > e_prev
    weight_fwd = jnp.where(
        upward, 1.0, jnp.where(downward, 0.0, jnp.where(toward, larger, smaller))
    )
    weight_bwd = jnp.where(
        upward, 0.0, jnp.where(downward, 1.0, jnp.where(toward, smaller, larger))
    )
    tangent_sq = (
        weight_fwd * weight_fwd * fwd_sq
        + 2.0 * weight_fwd * weight_bwd * fwd_bwd
        + weight_bwd * weight_bwd * bwd_sq
    )
    norm_sq = tangent_sq + stabilizer
    force_tan = weight_fwd * f_fwd + weight_bwd * f_bwd
    spring = spring_const * (jnp.sqrt(fwd_sq + stabilizer) - jnp.sqrt(bwd_sq + stabilizer))
    coefficient = -force_tan / norm_sq + spring / jnp.sqrt(norm_sq)
    neb_sq = ff + 2.0 * coefficient * force_tan + coefficient * coefficient * tangent_sq

    def over_inner(value):
        return jnp.sum(jnp.where(inner, value, 0.0), axis=0, keepdims=True)

    force_norm = jnp.sqrt(over_inner(neb_sq) + stabilizer)
    speed_norm = jnp.sqrt(over_inner(speed_sq) + stabilizer)
    gain = jnp.broadcast_to(fire_mixing * (speed_norm / force_norm) + time_step, (8, 128))
    keep = jnp.where(inner, 1.0 - fire_mixing, 0.0)
    push = jnp.where(inner, gain, 0.0)
    along_fwd = jnp.where(inner, gain * coefficient * weight_fwd, 0.0)
    along_bwd = jnp.where(inner, gain * coefficient * weight_bwd, 0.0)
    return keep, push, along_fwd, along_bwd


def step_terms(image_ref, gathered_ref, images, terms):
    image = lax.broadcasted_iota(jnp.int32, (8, 128), 0)
    summary = jnp.zeros((8, 128), jnp.float32)
    slabs = gathered_ref.shape[0] // images
    for g in range(images):
        rows = gathered_ref[g * slabs : (g + 1) * slabs, :]
        row = jnp.broadcast_to(jnp.sum(rows, axis=0, keepdims=True), (8, 128))
        summary = summary + jnp.where(image == g, row, 0.0)
        summary = summary + jnp.where(image == (g ^ 1), pltpu.roll(row, 120, 1), 0.0)
    keep, push, along_fwd, along_bwd = path_terms(summary, images)
    here = image_ref[0]
    odd = here % 2 == 1
    values = (keep, push, jnp.where(odd, -along_bwd, along_fwd), jnp.where(odd, -along_fwd, along_bwd))
    for j in range(2):
        at = image == (here + j * (1 - 2 * (here % 2)))
        for k, value in enumerate(values):
            own = jnp.sum(jnp.where(at, value, 0.0), axis=0, keepdims=True)
            terms[j, k] = jnp.broadcast_to(own, (8, 128))


def new_speed(terms, j, speed, force, ahead, behind):
    return terms[j, 0] * speed + terms[j, 1] * force + terms[j, 2] * ahead + terms[j, 3] * behind


def update_kernel(images, image_ref, gathered_ref, *refs):
    path, forces, speeds, moved, new_speeds = refs[:4], refs[4:6], refs[6:8], refs[8:10], refs[10:12]
    terms = refs[12]
    planes = path[0].shape[1]

    @pl.when(pl.program_id(0) == 0)
    def _():
        step_terms(image_ref, gathered_ref, images, terms)

    def some(t, carry):
        for i in range(2):
            p = 2 * t + i
            for axis in range(3):
                at = [ref[axis, p] for ref in path]
                diff = [at[j + 1] - at[j] for j in range(3)]
                for j in range(2):
                    speed = new_speed(terms, j, speeds[j][axis, p], forces[j][axis, p], diff[j + 1], diff[j])
                    new_speeds[j][axis, p] = speed
                    moved[j][axis, p] = at[j + 1] + time_step * speed
        return carry

    lax.fori_loop(0, planes // 2, some, 0)


def update(image, gathered, path, forces, speeds, images, chunk):
    planes = path[0].shape[1]
    block = pl.BlockSpec((3, chunk, 8, 128), lambda t: (0, t, 0, 0))
    out = jax.ShapeDtypeStruct((3, planes, 8, 128), jnp.float32)
    results = pl.pallas_call(
        functools.partial(update_kernel, images),
        grid=(planes // chunk,),
        out_shape=(out,) * 4,
        in_specs=[
            pl.BlockSpec(memory_space=pltpu.SMEM),
            pl.BlockSpec(gathered.shape, lambda t: (0, 0)),
        ]
        + [block] * 8,
        out_specs=(block,) * 4,
        scratch_shapes=[pltpu.VMEM((2, 4, 8, 128), jnp.float32)],
        compiler_params=pltpu.CompilerParams(vmem_limit_bytes=32 * 1024 * 1024),
        name="fire_update",
    )(image, gathered, *path, *forces, *speeds)
    return results[:2], results[2:]


def last_partner_kernel(images, image_ref, gathered_ref, before, here, after, force, speed, new_ref, terms_ref, terms):
    planes = here.shape[1]

    @pl.when(pl.program_id(0) == 0)
    def _():
        step_terms(image_ref, gathered_ref, images, terms)
        terms_ref[...] = terms[...]

    def some(t, carry):
        for i in range(2):
            p = 2 * t + i
            for axis in range(3):
                at = here[axis, p]
                new_ref[axis, p] = new_speed(
                    terms, 1, speed[axis, p], force[axis, p], after[axis, p] - at, at - before[axis, p]
                )
        return carry

    lax.fori_loop(0, planes // 2, some, 0)


def last_partner(image, gathered, path, force, speed, images, chunk):
    planes = force.shape[1]
    block = pl.BlockSpec((3, chunk, 8, 128), lambda t: (0, t, 0, 0))
    return pl.pallas_call(
        functools.partial(last_partner_kernel, images),
        grid=(planes // chunk,),
        out_shape=(
            jax.ShapeDtypeStruct((3, planes, 8, 128), jnp.float32),
            jax.ShapeDtypeStruct((2, 4, 8, 128), jnp.float32),
        ),
        in_specs=[
            pl.BlockSpec(memory_space=pltpu.SMEM),
            pl.BlockSpec(gathered.shape, lambda t: (0, 0)),
        ]
        + [block] * 5,
        out_specs=(block, pl.BlockSpec((2, 4, 8, 128), lambda t: (0, 0, 0, 0))),
        scratch_shapes=[pltpu.VMEM((2, 4, 8, 128), jnp.float32)],
        compiler_params=pltpu.CompilerParams(vmem_limit_bytes=32 * 1024 * 1024),
        name="last_partner",
    )(image, gathered, *path, force, speed)


def last_own_kernel(side_ref, terms, before, here, after, force, speed, moved, new_ref):
    planes = here.shape[1]

    def some(t, carry):
        for i in range(2):
            p = 2 * t + i
            for axis in range(3):
                at = here[axis, p]
                new = new_speed(
                    terms, 0, speed[axis, p], force[axis, p], after[axis, p] - at, at - before[axis, p]
                )
                new_ref[axis, p] = new
                moved[axis, p] = at + time_step * new
        return carry

    lax.fori_loop(0, planes // 2, some, 0)


def last_own(side, terms, path, force, speed, chunk):
    planes = force.shape[1]
    steps = planes // chunk
    block = pl.BlockSpec((3, chunk, 8, 128), lambda t, side_ref: (0, t, 0, 0))
    half = pl.BlockSpec((3, chunk, 8, 128), lambda t, side_ref: (0, side_ref[0] * steps + t, 0, 0))
    out = jax.ShapeDtypeStruct((3, 2 * planes, 8, 128), jnp.float32)
    return pl.pallas_call(
        last_own_kernel,
        grid_spec=pltpu.PrefetchScalarGridSpec(
            num_scalar_prefetch=1,
            grid=(steps,),
            in_specs=[pl.BlockSpec((2, 4, 8, 128), lambda t, side_ref: (0, 0, 0, 0))] + [block] * 5,
            out_specs=(half, half),
        ),
        out_shape=(out, out),
        compiler_params=pltpu.CompilerParams(vmem_limit_bytes=32 * 1024 * 1024),
        name="last_own",
    )(side, terms, *path, force, speed)


def last_join_kernel(side_ref, here, speed, moved_in, speed_in, moved, new_ref):
    planes = here.shape[1]

    def some(t, carry):
        for i in range(4):
            for axis in range(3):
                p = 4 * t + i
                new = speed[axis, p]
                new_ref[axis, p] = new
                moved[axis, p] = here[axis, p] + time_step * new
        return carry

    lax.fori_loop(0, planes // 4, some, 0)


def last_join(side, here, speed, moved, speeds, chunk):
    planes = here.shape[1]
    steps = planes // chunk
    block = pl.BlockSpec((3, chunk, 8, 128), lambda t, side_ref: (0, t, 0, 0))
    half = pl.BlockSpec(
        (3, chunk, 8, 128), lambda t, side_ref: (0, (1 - side_ref[0]) * steps + t, 0, 0)
    )
    out = jax.ShapeDtypeStruct(moved.shape, jnp.float32)
    whole = pl.BlockSpec(memory_space=pl.ANY)
    return pl.pallas_call(
        last_join_kernel,
        grid_spec=pltpu.PrefetchScalarGridSpec(
            num_scalar_prefetch=1,
            grid=(steps,),
            in_specs=[block, block, whole, whole],
            out_specs=(half, half),
        ),
        out_shape=(out, out),
        input_output_aliases={3: 0, 4: 1},
        compiler_params=pltpu.CompilerParams(vmem_limit_bytes=32 * 1024 * 1024),
        name="last_join",
    )(side, here, speed, moved, speeds)


def local(displacement, velocity):
    planes = displacement.shape[2] // (SIDE * SIDE)
    half = planes // 2
    images, slabs = lax.axis_size("image"), lax.axis_size("domain")
    both = ("image", "domain")
    own_image = lax.axis_index("image").astype(jnp.int32)
    side = own_image % 2
    is_low = side == 0
    image_arg, side_arg = own_image.reshape(1), side.reshape(1)
    slab = displacement.reshape(3, planes, 8, 128)
    slab_speed = velocity.reshape(3, planes, 8, 128)

    def at(image, domain):
        return image * slabs + domain % slabs

    everyone = [(i, d) for i in range(images) for d in range(slabs)]
    outer_own = [(at(i, d), at(i, d + 1 - 2 * (i % 2))) for i, d in everyone]
    outer_partner = [(at(i, d), at(i ^ 1, d - 1 + 2 * (i % 2))) for i, d in everyone]
    across = [(i, i ^ 1) for i in range(images)]
    own_out = [(i, i - 2 + 4 * (i % 2)) for i in range(images)]
    own_out = [(a, b) for a, b in own_out if 0 <= b < images]
    partner_out = [(b, a) for a, b in own_out]
    upward = [(at(i, d), at(i ^ 1, d + i % 2)) for i, d in everyone]
    downward = [(b, a) for a, b in upward]

    def planes_from(array, start, count):
        return lax.dynamic_slice_in_dim(array, start, count, axis=1)

    end = planes - HALO
    halo_own = lax.ppermute(planes_from(slab, (1 - side) * end, HALO), both, outer_own)
    halo_partner = lax.ppermute(planes_from(slab, side * end, HALO), both, outer_partner)
    halo_inner = lax.ppermute(planes_from(slab, half - HALO + HALO * side, HALO), "image", across)
    own = planes_from(slab, half * side, half)
    own_speed = planes_from(slab_speed, half * side, half)
    piece = half // CHUNKS
    pieces = [
        lax.ppermute(planes_from(slab, half * (1 - side) + c * piece, piece), "image", across)
        for c in range(CHUNKS)
    ]
    beyond_own = lax.ppermute(own, "image", own_out)
    beyond_partner = jnp.concatenate(
        [lax.ppermute(part, "image", partner_out) for part in pieces], axis=1
    )
    partner = jnp.concatenate(pieces, axis=1)
    partner_speed = lax.ppermute(planes_from(slab_speed, half * (1 - side), half), "image", across)
    near_low, near_high = slab[:, half - HALO : half], slab[:, half : half + HALO]
    own_halo = (jnp.where(is_low, halo_own, near_low), jnp.where(is_low, near_high, halo_own))
    partner_halo = (
        jnp.where(is_low, halo_partner, halo_inner),
        jnp.where(is_low, halo_inner, halo_partner),
    )

    path = (beyond_partner, own, partner, beyond_own)
    speeds = (own_speed, partner_speed)
    halos = (own_halo, partner_halo)
    for step_index in range(FIRE_STEPS):
        results = [image_forces(part, *halo) for part, halo in zip(path[1:3], halos)]
        forces, energies = zip(*results)
        payload = moments(side_arg, path, forces, speeds, energies, images * slabs, MOMENT_CHUNK)
        gathered = lax.all_to_all(payload, both, 0, 0, tiled=True)
        if step_index == FIRE_STEPS - 1:
            break
        moved, speeds = update(image_arg, gathered, path, forces, speeds, images, UPDATE_CHUNK)
        tops = jnp.stack([part[:, half - HALO :] for part in moved])
        bottoms = jnp.stack([part[:, :HALO] for part in moved])
        low = lax.ppermute(tops, both, upward)
        high = lax.ppermute(bottoms, both, downward)
        halos = ((low[1], high[1]), (low[0], high[0]))
        path = (
            lax.ppermute(moved[1], "image", partner_out),
            moved[0],
            moved[1],
            lax.ppermute(moved[0], "image", own_out),
        )
        returned = lax.ppermute(moved[1], "image", across)
    last_speed, terms = last_partner(
        image_arg, gathered, path[1:], forces[1], speeds[1], images, UPDATE_CHUNK
    )
    returned_speed = lax.ppermute(last_speed, "image", across)
    moved, new_speeds = last_own(side_arg, terms, path[:3], forces[0], speeds[0], UPDATE_CHUNK)
    moved, new_speeds = last_join(side_arg, returned, returned_speed, moved, new_speeds, UPDATE_CHUNK)
    return (moved.reshape(displacement.shape), new_speeds.reshape(velocity.shape))


def solution(mesh):
    spec = P("image", None, "domain")
    return jax.shard_map(
        local,
        mesh=mesh,
        in_specs=(spec, spec),
        out_specs=(spec, spec),
        check_vma=False,
    )
```

time: 221 us -> 124 us (0.56)
  Pallas kernels: 67.3 us -> 25.3 us
  blocking collectives: 46.1 us -> 20.4 us
  starting transfers between devices: 59.9 us -> 40.8 us
  waiting for transfers between devices: 41.2 us -> 27.9 us
    pallas_call x2 -> x4, Pallas kernels: 58.3 us -> 13.9 us  [image_forces(): pl.pallas_call(force_kernel, out_shape=(jax.ShapeDtypeStruct((3, planes,...]
    all_to_all x1, starting transfers between devices: 42.2 us -> 7.83 us  [local(): gathered = lax.all_to_all(payload, both, 0, 0, tiled=True)]
    all_to_all x1, blocking collectives: 46.1 us -> 20.4 us  [local(): gathered = lax.all_to_all(payload, both, 0, 0, tiled=True)]
    ppermute x8 -> x15, starting transfers between devices: 17.7 us -> 32.9 us  [the longest x2 6.9 us: local(): lax.ppermute(planes_from(slab, half * (1 - side) + c * piece, piece), 'im...]
    ppermute x8 -> x15, waiting for transfers between devices: 31.9 us -> 19.7 us  [the longest x1 11.6 us: local(): returned_speed = lax.ppermute(last_speed, 'image', across)]
    dynamic_slice x0 -> x4, local copies, waits for them, and re-layouts: none -> 3.57 us  [planes_from(): return lax.dynamic_slice_in_dim(array, start, count, axis=1)]
    pallas_call x4 -> x6, Pallas kernels: 8.99 us -> 11.4 us  [the longest x1 3.32 us: last_join(): pl.pallas_call(last_join_kernel, grid_spec=pltpu.PrefetchScalarGridSpec(n...]
  transfers between devices with their start and end apart: 9 -> 16, of which waited for: 7 -> 6; matrix products, arithmetic and copies ran while one was open for 0% -> 4% of each run, Pallas kernels for 26% -> 14%
where the time goes in v1:
time: 124 us; the launch traced here: 123 us
  starting transfers between devices  40.8 us (33%)
  waiting for transfers between devices  27.9 us (22%)
  Pallas kernels  25.3 us (20%)
  blocking collectives  20.4 us (16%)
  local copies, waits for them, and re-layouts  7.29 us (6%)
    all_to_all x1, blocking collectives, local(): gathered = lax.all_to_all(payload, both, 0, 0, tiled=True)  20.4 us
    pallas_call x4, Pallas kernels, image_forces(): pl.pallas_call(force_kernel, out_shape=(jax.ShapeDtypeStruct((3, planes,...  13.9 us
    ppermute x1, waiting for transfers between devices, local(): returned_speed = lax.ppermute(last_speed, 'image', across)  11.6 us
    all_to_all x1, waiting for transfers between devices, local(): gathered = lax.all_to_all(payload, both, 0, 0, tiled=True)  8.21 us
    all_to_all x1, starting transfers between devices, local(): gathered = lax.all_to_all(payload, both, 0, 0, tiled=True)  7.83 us
    ppermute x2, starting transfers between devices, local(): lax.ppermute(planes_from(slab, half * (1 - side) + c * piece, piece), 'im...  6.9 us
    ppermute x2, starting transfers between devices, local(): lax.ppermute(part, 'image', partner_out)  6.8 us
    ppermute x1, starting transfers between devices, local(): high = lax.ppermute(bottoms, both, downward)  5.04 us
  transfers between devices with their start and end apart: 16, of which 6 were waited for; matrix products, arithmetic and copies ran while one was open for 4% of the time, Pallas kernels for 14%

profile of v1, /device:TPU:0, one launch (start us, length us, event | category | flops | bytes accessed | tf_op | source)
XLA Modules:
  0.0 123.4 jit_solution(8725660709181399458)
XLA Ops:
  0.6 0.0 copy-start.5
  0.7 1.5 %constant_dynamic-slice_fusion.4 = f32[3,2,8,128]{3,2,1,0:T(8,128)} fusion(f32[3,96,8,128]{3,2,1,0:T(8,128)} %bitcast.33, s32[]{:T(128)S(6)} %select_n.52), kind=kLoop, calls=%fused_computation.22 | loop fusion | bytes 49156 | tf_op jit(solution)/shard_map/dynamic_slice | solution.py:632
  2.1 0.0 collective-permute-start.5
  2.1 0.0 copy-start.6
  2.1 2.0 %constant_dynamic-slice_fusion.6 = (f32[3,24,8,128]{3,2,1,0:T(8,128)}, f32[3,24,8,128]{3,2,1,0:T(8,128)}) fusion(f32[3,96,8,128]{3,2,1,0:T(8,128)} %bitcast.34, s32[]{:T(128)S(6)} %select_n.49, s32[]{:T(128)S(6)} %select_n.48), kind=kLoop, calls=%fused_computation.24 | loop fusion | bytes 1179656 | tf_op jit(solution)/shard_map/dynamic_slice | solution.py:632
  4.1 6.9 %collective-permute-start.2 = (f32[3,24,8,128]{3,2,1,0:T(8,128)}, f32[3,24,8,128]{3,2,1,0:T(8,128)}, u32[]{:S(2)}, u32[]{:S(2)}) collective-permute-start(f32[3,24,8,128]{3,2,1,0:T(8,128)} %get-tuple-element.52), channel_id=1, source_target_pairs={{0,16},{16,0},{32,48},{48,32},{64,80},{80,64},{96,112},{112,96},{1... | collective-permute-start | bytes 884744 | tf_op jit(solution)/shard_map/ppermute | solution.py:642
  11.0 0.0 collective-permute-start
  11.0 0.0 copy-done.5
  11.1 1.3 %collective-permute-start.4 = (f32[3,48,8,128]{3,2,1,0:T(8,128)S(1)}, f32[3,48,8,128]{3,2,1,0:T(8,128)S(1)}, u32[]{:S(2)}, u32[]{:S(2)}) collective-permute-start(f32[3,48,8,128]{3,2,1,0:T(8,128)S(1)} %constant_dynamic-slice_fusion.5.own_ref.refs_1_), channel_id=1, source_target_pairs={{16,48},{32,0},{48,80},{64,32},{80,112},{96,64},{17,49},{33,1},{49... | collective-permute-start | bytes 1769480 | tf_op jit(solution)/shard_map/ppermute | solution.py:645
  12.4 0.0 collective-permute-done.5
  12.4 0.8 constant_dynamic-slice_fusion.2
  13.1 4.2 %collective-permute-start.7 = (f32[3,2,8,128]{3,2,1,0:T(8,128)S(1)}, f32[3,2,8,128]{3,2,1,0:T(8,128)S(1)}, u32[]{:S(2)}, u32[]{:S(2)}) collective-permute-start(f32[3,2,8,128]{3,2,1,0:T(8,128)S(1)} %get-tuple-element.48), channel_id=1, source_target_pairs={{0,16},{16,0},{32,48},{48,32},{64,80},{80,64},{96,112},{112,96},{1... | collective-permute-start | bytes 73736 | tf_op jit(solution)/shard_map/ppermute | solution.py:637
  17.3 0.0 collective-permute-start.6
  17.3 0.0 copy-done.6
  17.3 0.1 constant_dynamic-slice_fusion
  17.4 3.5 %slab_forces.4 = (f32[3,48,8,128]{3,2,1,0:T(8,128)S(1)}, f32[8,128]{1,0:T(8,128)S(1)}) custom-call(f32[3,48,8,128]{3,2,1,0:T(8,128)S(1)} %constant_dynamic-slice_fusion.5.own_ref.refs_1_, f32[3,2,8,128]{3,2,1,0:T(8,128)S(1)} %get-tuple-element.50.low_ref, f32[3,2,8,128]{3,2,1,0:T(8,128)S(1)} %get-tuple-element.51.high_ref), custom_call_target="tpu_custom_call" | custom-call | flops 40000000 | bytes 30000000 | tf_op jit(solution)/shard_map/slab_forces/pallas_call | solution.py:258
  20.9 3.2 %collective-permute-done.7 = f32[3,2,8,128]{3,2,1,0:T(8,128)S(1)} collective-permute-done((f32[3,2,8,128]{3,2,1,0:T(8,128)S(1)}, f32[3,2,8,128]{3,2,1,0:T(8,128)S(1)}, u32[]{:S(2)}, u32[]{:S(2)}) %collective-permute-start.7) | collective-permute-done | bytes 24608 | tf_op jit(solution)/shard_map/ppermute | solution.py:637
  24.2 0.5 collective-permute-start.8
  24.7 0.0 collective-permute-done
  24.7 3.4 %collective-permute-start.1 = (f32[3,24,8,128]{3,2,1,0:T(8,128)}, f32[3,24,8,128]{3,2,1,0:T(8,128)S(1)}, u32[]{:S(2)}, u32[]{:S(2)}) collective-permute-start(f32[3,24,8,128]{3,2,1,0:T(8,128)} %collective-permute-done), channel_id=1, source_target_pairs={{48,16},{0,32},{80,48},{32,64},{112,80},{64,96},{49,17},{1,33},{81... | collective-permute-start | bytes 884744 | tf_op jit(solution)/shard_map/ppermute | solution.py:647
  28.1 0.0 collective-permute-done.6
  28.1 0.0 collective-permute-done.2
  28.2 3.4 %collective-permute-start.3 = (f32[3,24,8,128]{3,2,1,0:T(8,128)}, f32[3,24,8,128]{3,2,1,0:T(8,128)S(1)}, u32[]{:S(2)}, u32[]{:S(2)}) collective-permute-start(f32[3,24,8,128]{3,2,1,0:T(8,128)} %collective-permute-done.2), channel_id=1, source_target_pairs={{48,16},{0,32},{80,48},{32,64},{112,80},{64,96},{49,17},{1,33},{81... | collective-permute-start | bytes 884744 | tf_op jit(solution)/shard_map/ppermute | solution.py:647
  31.6 1.0 constant_dynamic-update-slice_fusion.3
  32.5 1.0 constant_dynamic-update-slice_fusion.2.own_ref.refs_2_
  33.5 3.5 %slab_forces.5 = (f32[3,48,8,128]{3,2,1,0:T(8,128)S(1)}, f32[8,128]{1,0:T(8,128)S(1)}) custom-call(f32[3,48,8,128]{3,2,1,0:T(8,128)S(1)} %constant_dynamic-update-slice_fusion.2.own_ref.refs_2_, f32[3,2,8,128]{3,2,1,0:T(8,128)S(1)} %get-tuple-element.63.low_ref, f32[3,2,8,128]{3,2,1,0:T(8,128)S(1)} %get-tuple-element.62.high_ref), custom_call_target="tpu_custom_call" | custom-call | flops 40000000 | bytes 30000000 | tf_op jit(solution)/shard_map/slab_forces/pallas_call | solution.py:258
  37.0 0.0 collective-permute-done.1
  37.1 2.0 %collective-permute-done.3 = f32[3,24,8,128]{3,2,1,0:T(8,128)S(1)} collective-permute-done((f32[3,24,8,128]{3,2,1,0:T(8,128)}, f32[3,24,8,128]{3,2,1,0:T(8,128)S(1)}, u32[]{:S(2)}, u32[]{:S(2)}) %collective-permute-start.3) | collective-permute-done | bytes 294944 | tf_op jit(solution)/shard_map/ppermute | solution.py:647
  39.0 0.0 collective-permute-done.4.refs_3_
  39.1 0.0 collective-permute-done.8.refs_7_
  39.1 1.3 %path_moments.2 = f32[128,128]{1,0:T(8,128)S(1)} custom-call(s32[1]{0:T(128)} %bitcast.side_ref, f32[3,48,8,128]{3,2,1,0:T(8,128)S(1)} %constant_dynamic-update-slice_fusion.refs_0_, f32[3,48,8,128]{3,2,1,0:T(8,128)S(1)} %constant_dynamic-slice_fusion.5.own_ref.refs_1_, f32[3,48,8,128]{3,2,1,0:T(8,128)S(1)} %constant_dynamic-update-slice_fusion.2.own_ref.refs_2_, ...), custom_call_target="tpu_custom_call" | custom-call | tf_op jit(solution)/shard_map/path_moments/pallas_call | solution.py:356
  40.4 20.4 %all_to_all.22 = f32[128,1,128]{2,1,0:T(1,128)S(1)} all-to-all(f32[128,1,128]{2,1,0:T(1,128)S(1)} %bitcast.32), channel_id=1, replica_groups=mesh['image'=8,'domain'=16] {'image','domain'}, dimensions={0} | all-to-all | bytes 131072 | tf_op jit(solution)/shard_map/all_to_all | solution.py:665
  60.8 1.6 %fire_update.1 = (f32[3,48,8,128]{3,2,1,0:T(8,128)S(1)}, f32[3,48,8,128]{3,2,1,0:T(8,128)S(1)}, f32[3,48,8,128]{3,2,1,0:T(8,128)S(1)}, f32[3,48,8,128]{3,2,1,0:T(8,128)S(1)}) custom-call(s32[1]{0:T(128)} %bitcast.1.image_ref, f32[128,128]{1,0:T(8,128)S(1)} %bitcast.30, f32[3,48,8,128]{3,2,1,0:T(8,128)S(1)} %constant_dynamic-update-slice_fusion.refs_0_, ...), custom_call_target="tpu_custom_call" | custom-call | tf_op jit(solution)/shard_map/fire_update/pallas_call | solution.py:469
  62.4 1.3 %collective-permute-start.11 = (f32[3,48,8,128]{3,2,1,0:T(8,128)S(1)}, f32[3,48,8,128]{3,2,1,0:T(8,128)S(1)}, u32[]{:S(2)}, u32[]{:S(2)}) collective-permute-start(f32[3,48,8,128]{3,2,1,0:T(8,128)S(1)} %get-tuple-element.25.own_ref.refs_1_.before.here), channel_id=1, source_target_pairs={{16,48},{32,0},{48,80},{64,32},{80,112},{96,64},{17,49},{33,1},{49... | collective-permute-start | bytes 1769480 | tf_op jit(solution)/shard_map/ppermute | solution.py:678
  63.7 4.6 %collective-permute-start.10 = (f32[3,48,8,128]{3,2,1,0:T(8,128)S(1)}, f32[3,48,8,128]{3,2,1,0:T(8,128)S(1)}, u32[]{:S(2)}, u32[]{:S(2)}) collective-permute-start(f32[3,48,8,128]{3,2,1,0:T(8,128)S(1)} %get-tuple-element.24.own_ref.refs_2_.here.after), channel_id=1, source_target_pairs={{48,16},{0,32},{80,48},{32,64},{112,80},{64,96},{49,17},{1,33},{81... | collective-permute-start | bytes 1769480 | tf_op jit(solution)/shard_map/ppermute | solution.py:675
  68.3 0.1 collective-permute-start.12
  68.4 5.0 %collective-permute-start.13 = (f32[2,3,2,8,128]{4,3,2,1,0:T(8,128)S(1)}, f32[2,3,2,8,128]{4,3,2,1,0:T(8,128)S(1)}, u32[]{:S(2)}, u32[]{:S(2)}) collective-permute-start(f32[2,3,2,8,128]{4,3,2,1,0:T(8,128)S(1)} %pad_maximum_fusion.1), channel_id=1, source_target_pairs={{16,0},{17,1},{18,2},{19,3},{20,4},{21,5},{22,6},{23,7},{24,8},{25... | collective-permute-start | bytes 147464 | tf_op jit(solution)/shard_map/ppermute | solution.py:672
  73.5 1.8 %collective-permute-done.12 = f32[2,3,2,8,128]{4,3,2,1,0:T(8,128)S(1)} collective-permute-done((f32[2,3,2,8,128]{4,3,2,1,0:T(8,128)S(1)}, f32[2,3,2,8,128]{4,3,2,1,0:T(8,128)S(1)}, u32[]{:S(2)}, u32[]{:S(2)}) %collective-permute-start.12) | collective-permute-done | bytes 49184 | tf_op jit(solution)/shard_map/ppermute | solution.py:671
  75.2 0.0 collective-permute-done.13
  75.3 3.5 %slab_forces.7 = (f32[3,48,8,128]{3,2,1,0:T(8,128)S(1)}, f32[8,128]{1,0:T(8,128)S(1)}) custom-call(f32[3,48,8,128]{3,2,1,0:T(8,128)S(1)} %get-tuple-element.24.own_ref.refs_2_.here.after, f32[3,2,8,128]{3,2,1,0:T(8,128)S(1)} %get-tuple-element.60.low_ref, f32[3,2,8,128]{3,2,1,0:T(8,128)S(1)} %get-tuple-element.58.high_ref), custom_call_target="tpu_custom_call" | custom-call | flops 40000000 | bytes 30000000 | tf_op jit(solution)/shard_map/slab_forces/pallas_call | solution.py:258
  78.7 0.0 copy-start.2
  78.8 3.5 %slab_forces.6 = (f32[3,48,8,128]{3,2,1,0:T(8,128)S(1)}, f32[8,128]{1,0:T(8,128)S(1)}) custom-call(f32[3,48,8,128]{3,2,1,0:T(8,128)S(1)} %get-tuple-element.25.own_ref.refs_1_.before.here, f32[3,2,8,128]{3,2,1,0:T(8,128)S(1)} %get-tuple-element.61.low_ref, f32[3,2,8,128]{3,2,1,0:T(8,128)S(1)} %get-tuple-element.59.high_ref), custom_call_target="tpu_custom_call" | custom-call | flops 40000000 | bytes 30000000 | tf_op jit(solution)/shard_map/slab_forces/pallas_call | solution.py:258
  82.2 0.0 copy-start
  82.2 0.0 collective-permute-done.11.refs_3_.after
  82.3 0.0 collective-permute-done.10.refs_0_.before
  82.3 1.3 %path_moments.3 = f32[128,128]{1,0:T(8,128)S(1)} custom-call(s32[1]{0:T(128)} %bitcast.side_ref, f32[3,48,8,128]{3,2,1,0:T(8,128)S(1)} %collective-permute-done.10.refs_0_.before, f32[3,48,8,128]{3,2,1,0:T(8,128)S(1)} %get-tuple-element.25.own_ref.refs_1_.before.here, f32[3,48,8,128]{3,2,1,0:T(8,128)S(1)} %get-tuple-element.24.own_ref.refs_2_.here.after, ...), custom_call_target="tpu_custom_call" | custom-call | tf_op jit(solution)/shard_map/path_moments/pallas_call | solution.py:356
  83.6 0.0 copy-done.2
  83.6 0.0 copy-done
  83.6 0.0 copy-start.4
  83.6 0.6 copy-done.4
  84.2 7.8 %all-to-all-start.1 = ((f32[128,1,128]{2,1,0:T(1,128)}), f32[128,1,128]{2,1,0:T(1,128)}, u32[]{:S(2)}, u32[]{:S(2)}) async-start(f32[128,1,128]{2,1,0:T(1,128)} %bitcast.31), calls=%async_computation.1 | async-start | bytes 131072 | tf_op jit(solution)/shard_map/all_to_all | solution.py:665
  92.1 1.1 collective-permute-start.9
  93.2 8.2 %all-to-all-done.1 = f32[128,1,128]{2,1,0:T(1,128)} async-done(((f32[128,1,128]{2,1,0:T(1,128)}), f32[128,1,128]{2,1,0:T(1,128)}, u32[]{:S(2)}, u32[]{:S(2)}) %all-to-all-start.1) | async-done | bytes 65568 | tf_op jit(solution)/shard_map/all_to_all | solution.py:665
  101.4 0.0 copy-start.3
  101.4 1.1 copy-done.3
  102.4 0.0 copy-start.1
  102.4 1.8 %last_partner.1 = (f32[3,48,8,128]{3,2,1,0:T(8,128)S(1)}, f32[2,4,8,128]{3,2,1,0:T(8,128)S(1)}) custom-call(s32[1]{0:T(128)} %bitcast.1.image_ref, f32[128,128]{1,0:T(8,128)} %bitcast.17.gathered_ref, f32[3,48,8,128]{3,2,1,0:T(8,128)S(1)} %get-tuple-element.25.own_ref.refs_1_.before.here, f32[3,48,8,128]{3,2,1,0:T(8,128)S(1)} %get-tuple-element.24.own_ref.refs_2_.here.after, ...), custom_call_target="tpu_custom_call" | custom-call | tf_op jit(solution)/shard_map/last_partner/pallas_call | solution.py:510
  104.2 1.1 collective-permute-start.14
  105.3 0.0 copy-done.1
  105.3 2.0 %last_own.1 = (f32[3,96,8,128]{3,2,1,0:T(8,128)}, f32[3,96,8,128]{3,2,1,0:T(8,128)}) custom-call(s32[1]{0:T(128)} %bitcast.side_ref, f32[2,4,8,128]{3,2,1,0:T(8,128)S(1)} %get-tuple-element.33.terms, f32[3,48,8,128]{3,2,1,0:T(8,128)S(1)} %collective-permute-done.10.refs_0_.before, f32[3,48,8,128]{3,2,1,0:T(8,128)S(1)} %get-tuple-element.25.own_ref.refs_1_.before.here, ...), custom_call_target="tpu_custom_call" | custom-call | tf_op jit(solution)/shard_map/last_own/pallas_call | solution.py:553
  107.4 1.1 collective-permute-done.9.here
  108.5 11.6 %collective-permute-done.14.speed = f32[3,48,8,128]{3,2,1,0:T(8,128)S(1)} collective-permute-done((f32[3,48,8,128]{3,2,1,0:T(8,128)S(1)}, f32[3,48,8,128]{3,2,1,0:T(8,128)S(1)}, u32[]{:S(2)}, u32[]{:S(2)}) %collective-permute-start.14) | collective-permute-done | bytes 589856 | tf_op jit(solution)/shard_map/ppermute | solution.py:684
  120.1 3.3 %last_join.1 = (f32[3,96,8,128]{3,2,1,0:T(8,128)}, f32[3,96,8,128]{3,2,1,0:T(8,128)}) custom-call(s32[1]{0:T(128)} %bitcast.side_ref, f32[3,48,8,128]{3,2,1,0:T(8,128)} %collective-permute-done.9.here, f32[3,48,8,128]{3,2,1,0:T(8,128)S(1)} %collective-permute-done.14.speed, ...), custom_call_target="tpu_custom_call", output_to_operand_aliasing={{0}: (3, {}), {1}: (4, {})} | custom-call | tf_op jit(solution)/shard_map/last_join/pallas_call | solution.py:591
  (9 shorter events, 0.1 us)
Async XLA Ops:
  0.6 10.4 %copy-start.5 = (f32[1,3,98304]{2,0,1:T(1,128)S(1)}, f32[1,3,98304]{2,0,1:T(1,128)}, u32[]{:S(2)}) copy-start(f32[1,3,98304]{2,0,1:T(1,128)} %param.2) | copy-start | bytes 3538948
  2.1 10.3 %collective-permute-start.5 = (f32[3,2,8,128]{3,2,1,0:T(8,128)}, f32[3,2,8,128]{3,2,1,0:T(8,128)}, u32[]{:S(2)}, u32[]{:S(2)}) collective-permute-start(f32[3,2,8,128]{3,2,1,0:T(8,128)} %constant_dynamic-slice_fusion.4), channel_id=1, source_target_pairs={{0,1},{1,2},{2,3},{3,4},{4,5},{5,6},{6,7},{7,8},{8,9},{9,10},{10,1... | collective-permute-start | bytes 73736 | tf_op jit(solution)/shard_map/ppermute | solution.py:635
  2.1 15.2 %copy-start.6 = (f32[1,3,98304]{2,0,1:T(1,128)S(1)}, f32[1,3,98304]{2,0,1:T(1,128)}, u32[]{:S(2)}) copy-start(f32[1,3,98304]{2,0,1:T(1,128)} %param.3) | copy-start | bytes 3538948
  4.1 24.0 %collective-permute-start.2 = (f32[3,24,8,128]{3,2,1,0:T(8,128)}, f32[3,24,8,128]{3,2,1,0:T(8,128)}, u32[]{:S(2)}, u32[]{:S(2)}) collective-permute-start(f32[3,24,8,128]{3,2,1,0:T(8,128)} %get-tuple-element.52), channel_id=1, source_target_pairs={{0,16},{16,0},{32,48},{48,32},{64,80},{80,64},{96,112},{112,96},{1... | collective-permute-start | bytes 884744 | tf_op jit(solution)/shard_map/ppermute | solution.py:642
  11.0 13.7 %collective-permute-start = (f32[3,24,8,128]{3,2,1,0:T(8,128)}, f32[3,24,8,128]{3,2,1,0:T(8,128)}, u32[]{:S(2)}, u32[]{:S(2)}) collective-permute-start(f32[3,24,8,128]{3,2,1,0:T(8,128)} %get-tuple-element.53), channel_id=1, source_target_pairs={{0,16},{16,0},{32,48},{48,32},{64,80},{80,64},{96,112},{112,96},{1... | collective-permute-start | bytes 884744 | tf_op jit(solution)/shard_map/ppermute | solution.py:642
  11.1 28.0 %collective-permute-start.4 = (f32[3,48,8,128]{3,2,1,0:T(8,128)S(1)}, f32[3,48,8,128]{3,2,1,0:T(8,128)S(1)}, u32[]{:S(2)}, u32[]{:S(2)}) collective-permute-start(f32[3,48,8,128]{3,2,1,0:T(8,128)S(1)} %constant_dynamic-slice_fusion.5.own_ref.refs_1_), channel_id=1, source_target_pairs={{16,48},{32,0},{48,80},{64,32},{80,112},{96,64},{17,49},{33,1},{49... | collective-permute-start | bytes 1769480 | tf_op jit(solution)/shard_map/ppermute | solution.py:645
  13.1 11.0 %collective-permute-start.7 = (f32[3,2,8,128]{3,2,1,0:T(8,128)S(1)}, f32[3,2,8,128]{3,2,1,0:T(8,128)S(1)}, u32[]{:S(2)}, u32[]{:S(2)}) collective-permute-start(f32[3,2,8,128]{3,2,1,0:T(8,128)S(1)} %get-tuple-element.48), channel_id=1, source_target_pairs={{0,16},{16,0},{32,48},{48,32},{64,80},{80,64},{96,112},{112,96},{1... | collective-permute-start | bytes 73736 | tf_op jit(solution)/shard_map/ppermute | solution.py:637
  17.3 10.8 %collective-permute-start.6 = (f32[3,2,8,128]{3,2,1,0:T(8,128)S(1)}, f32[3,2,8,128]{3,2,1,0:T(8,128)S(1)}, u32[]{:S(2)}, u32[]{:S(2)}) collective-permute-start(f32[3,2,8,128]{3,2,1,0:T(8,128)S(1)} %get-tuple-element.49), channel_id=1, source_target_pairs={{0,31},{1,16},{2,17},{3,18},{4,19},{5,20},{6,21},{7,22},{8,23},{9,... | collective-permute-start | bytes 73736 | tf_op jit(solution)/shard_map/ppermute | solution.py:636
  24.2 14.9 %collective-permute-start.8 = (f32[3,48,8,128]{3,2,1,0:T(8,128)S(1)}, f32[3,48,8,128]{3,2,1,0:T(8,128)S(1)}, u32[]{:S(2)}, u32[]{:S(2)}) collective-permute-start(f32[3,48,8,128]{3,2,1,0:T(8,128)S(1)} %get-tuple-element.46), channel_id=1, source_target_pairs={{0,16},{16,0},{32,48},{48,32},{64,80},{80,64},{96,112},{112,96},{1... | collective-permute-start | bytes 1769480 | tf_op jit(solution)/shard_map/ppermute | solution.py:650
  24.7 12.3 %collective-permute-start.1 = (f32[3,24,8,128]{3,2,1,0:T(8,128)}, f32[3,24,8,128]{3,2,1,0:T(8,128)S(1)}, u32[]{:S(2)}, u32[]{:S(2)}) collective-permute-start(f32[3,24,8,128]{3,2,1,0:T(8,128)} %collective-permute-done), channel_id=1, source_target_pairs={{48,16},{0,32},{80,48},{32,64},{112,80},{64,96},{49,17},{1,33},{81... | collective-permute-start | bytes 884744 | tf_op jit(solution)/shard_map/ppermute | solution.py:647
  28.2 10.9 %collective-permute-start.3 = (f32[3,24,8,128]{3,2,1,0:T(8,128)}, f32[3,24,8,128]{3,2,1,0:T(8,128)S(1)}, u32[]{:S(2)}, u32[]{:S(2)}) collective-permute-start(f32[3,24,8,128]{3,2,1,0:T(8,128)} %collective-permute-done.2), channel_id=1, source_target_pairs={{48,16},{0,32},{80,48},{32,64},{112,80},{64,96},{49,17},{1,33},{81... | collective-permute-start | bytes 884744 | tf_op jit(solution)/shard_map/ppermute | solution.py:647
  62.4 19.9 %collective-permute-start.11 = (f32[3,48,8,128]{3,2,1,0:T(8,128)S(1)}, f32[3,48,8,128]{3,2,1,0:T(8,128)S(1)}, u32[]{:S(2)}, u32[]{:S(2)}) collective-permute-start(f32[3,48,8,128]{3,2,1,0:T(8,128)S(1)} %get-tuple-element.25.own_ref.refs_1_.before.here), channel_id=1, source_target_pairs={{16,48},{32,0},{48,80},{64,32},{80,112},{96,64},{17,49},{33,1},{49... | collective-permute-start | bytes 1769480 | tf_op jit(solution)/shard_map/ppermute | solution.py:678
  63.7 18.5 %collective-permute-start.10 = (f32[3,48,8,128]{3,2,1,0:T(8,128)S(1)}, f32[3,48,8,128]{3,2,1,0:T(8,128)S(1)}, u32[]{:S(2)}, u32[]{:S(2)}) collective-permute-start(f32[3,48,8,128]{3,2,1,0:T(8,128)S(1)} %get-tuple-element.24.own_ref.refs_2_.here.after), channel_id=1, source_target_pairs={{48,16},{0,32},{80,48},{32,64},{112,80},{64,96},{49,17},{1,33},{81... | collective-permute-start | bytes 1769480 | tf_op jit(solution)/shard_map/ppermute | solution.py:675
  68.3 6.9 %collective-permute-start.12 = (f32[2,3,2,8,128]{4,3,2,1,0:T(8,128)S(1)}, f32[2,3,2,8,128]{4,3,2,1,0:T(8,128)S(1)}, u32[]{:S(2)}, u32[]{:S(2)}) collective-permute-start(f32[2,3,2,8,128]{4,3,2,1,0:T(8,128)S(1)} %pad_maximum_fusion), channel_id=1, source_target_pairs={{0,16},{1,17},{2,18},{3,19},{4,20},{5,21},{6,22},{7,23},{8,24},{9,... | collective-permute-start | bytes 147464 | tf_op jit(solution)/shard_map/ppermute | solution.py:671
  68.4 6.8 %collective-permute-start.13 = (f32[2,3,2,8,128]{4,3,2,1,0:T(8,128)S(1)}, f32[2,3,2,8,128]{4,3,2,1,0:T(8,128)S(1)}, u32[]{:S(2)}, u32[]{:S(2)}) collective-permute-start(f32[2,3,2,8,128]{4,3,2,1,0:T(8,128)S(1)} %pad_maximum_fusion.1), channel_id=1, source_target_pairs={{16,0},{17,1},{18,2},{19,3},{20,4},{21,5},{22,6},{23,7},{24,8},{25... | collective-permute-start | bytes 147464 | tf_op jit(solution)/shard_map/ppermute | solution.py:672
  78.7 4.9 %copy-start.2 = (f32[3,48,8,128]{3,2,1,0:T(8,128)}, f32[3,48,8,128]{3,2,1,0:T(8,128)S(1)}, u32[]{:S(2)}) copy-start(f32[3,48,8,128]{3,2,1,0:T(8,128)S(1)} %get-tuple-element.27.refs_5_.force) | copy-start | bytes 1769476
  82.2 1.4 %copy-start = (f32[3,48,8,128]{3,2,1,0:T(8,128)}, f32[3,48,8,128]{3,2,1,0:T(8,128)S(1)}, u32[]{:S(2)}) copy-start(f32[3,48,8,128]{3,2,1,0:T(8,128)S(1)} %get-tuple-element.26.refs_4_.force) | copy-start | bytes 1769476
  83.6 0.6 copy-start.4
  84.2 17.1 %all-to-all-start.1 = ((f32[128,1,128]{2,1,0:T(1,128)}), f32[128,1,128]{2,1,0:T(1,128)}, u32[]{:S(2)}, u32[]{:S(2)}) async-start(f32[128,1,128]{2,1,0:T(1,128)} %bitcast.31), calls=%async_computation.1 | async-start | bytes 131072 | tf_op jit(solution)/shard_map/all_to_all | solution.py:665
  92.1 16.4 %collective-permute-start.9 = (f32[3,48,8,128]{3,2,1,0:T(8,128)S(1)}, f32[3,48,8,128]{3,2,1,0:T(8,128)}, u32[]{:S(2)}, u32[]{:S(2)}) collective-permute-start(f32[3,48,8,128]{3,2,1,0:T(8,128)S(1)} %get-tuple-element.24.own_ref.refs_2_.here.after), channel_id=1, source_target_pairs={{0,16},{16,0},{32,48},{48,32},{64,80},{80,64},{96,112},{112,96},{1... | collective-permute-start | bytes 1769480 | tf_op jit(solution)/shard_map/ppermute | solution.py:680
  101.4 1.1 copy-start.3
  102.4 2.9 %copy-start.1 = (f32[3,48,8,128]{3,2,1,0:T(8,128)S(1)}, f32[3,48,8,128]{3,2,1,0:T(8,128)}, u32[]{:S(2)}) copy-start(f32[3,48,8,128]{3,2,1,0:T(8,128)} %copy-done) | copy-start | bytes 1769476
  104.2 15.9 %collective-permute-start.14 = (f32[3,48,8,128]{3,2,1,0:T(8,128)S(1)}, f32[3,48,8,128]{3,2,1,0:T(8,128)S(1)}, u32[]{:S(2)}, u32[]{:S(2)}) collective-permute-start(f32[3,48,8,128]{3,2,1,0:T(8,128)S(1)} %get-tuple-element.32), channel_id=1, source_target_pairs={{0,16},{16,0},{32,48},{48,32},{64,80},{80,64},{96,112},{112,96},{1... | collective-permute-start | bytes 1769480 | tf_op jit(solution)/shard_map/ppermute | solution.py:684

commit v2 on v1

--- a/solution.py
+++ b/solution.py
@@ -15,9 +15,8 @@
 PLACE_UNROLL = 16
 EMBED_UNROLL = 48
 FINISH_UNROLL = 16
-CHUNKS = 2
-MOMENT_CHUNK = 12
-UPDATE_CHUNK = 12
+REGIONS = 2
+JOIN_STEPS = 2
 
 lattice_const = 3.615
 cutoff_sq = 9.61
@@ -87,12 +86,12 @@
     return 1 if plane % 2 == 0 else -1
 
 
-def force_kernel(
-    own_ref, low_ref, high_ref, force_ref, energy_ref, pos, turned, seps, slopes, rho, back, embed, force_back
-):
+def force_kernel(starts, slots, side_ref, *refs):
+    count = len(starts)
+    sources = [ref if slot is None else ref.at[slot] for ref, slot in zip(refs, slots)]
+    force_ref, energy_ref, pos, turned, seps, slopes, rho, back, embed, force_back = refs[count:]
     f32 = jnp.float32
-    planes = own_ref.shape[1]
-    top = planes + 2 * HALO
+    planes = force_ref.shape[1]
     lanes = lax.broadcasted_iota(jnp.int32, (8, 128), 1)
     subl = lax.broadcasted_iota(jnp.int32, (8, 128), 0)
     site_u = subl * 4 + lanes // SIDE
@@ -107,17 +106,17 @@
             for k, seen in enumerate(partners(value, side, lanes)):
                 turned[axis, k, q] = seen
 
-    for q in range(HALO):
-        place(q, side_of(q), [low_ref[axis, q] for axis in range(3)])
-        place(planes + HALO + q, side_of(q), [high_ref[axis, q] for axis in range(3)])
-
-    def place_some(t, carry):
-        for j in range(PLACE_UNROLL):
-            p = t * PLACE_UNROLL + j
-            place(p + HALO, side_of(j), [own_ref[axis, p] for axis in range(3)])
-        return carry
-
-    lax.fori_loop(0, planes // PLACE_UNROLL, place_some, 0)
+    for k, source in enumerate(sources):
+        rows = source.shape[1]
+        unroll = rows if rows <= 24 else PLACE_UNROLL
+
+        def place_some(t, carry, source=source, start=at_side(starts[k], side_ref), unroll=unroll):
+            for j in range(unroll):
+                p = t * unroll + j
+                place(start + p, side_of(j), [source[axis, p] for axis in range(3)])
+            return carry
+
+        lax.fori_loop(0, rows // unroll, place_some, 0)
 
     def separations(e, step):
         h = f32(unit_half)
@@ -251,17 +250,17 @@
     lax.fori_loop(0, planes // FINISH_UNROLL, finish, 0)
 
 
-def image_forces(own, low, high):
+def image_forces(side, planes, sources):
+    arrays, slots, starts = zip(*sources)
     vmem = pl.BlockSpec(memory_space=pltpu.VMEM)
-    planes = own.shape[1]
     rows = planes + 2 * HALO
     return pl.pallas_call(
-        force_kernel,
+        functools.partial(force_kernel, starts, slots),
         out_shape=(
             jax.ShapeDtypeStruct((3, planes, 8, 128), jnp.float32),
             jax.ShapeDtypeStruct((8, 128), jnp.float32),
         ),
-        in_specs=[vmem] * 3,
+        in_specs=[pl.BlockSpec(memory_space=pltpu.SMEM)] + [vmem] * len(arrays),
         out_specs=(vmem, vmem),
         scratch_shapes=[
             pltpu.VMEM((3, rows, 8, 128), jnp.float32),
@@ -275,94 +274,112 @@
         ],
         compiler_params=pltpu.CompilerParams(vmem_limit_bytes=40 * 1024 * 1024),
         cost_estimate=pl.CostEstimate(
-            flops=40_000_000, bytes_accessed=30_000_000, transcendentals=0
+            flops=20_000_000, bytes_accessed=15_000_000, transcendentals=0
         ),
         name="slab_forces",
-    )(own, low, high)
+    )(side, *arrays)
 
 
 def total_of(tile):
     return jnp.sum(jnp.sum(tile, axis=0, keepdims=True), axis=1, keepdims=True)
 
 
-def moment_kernel(side_ref, *refs):
-    path, forces, speeds, energies = refs[:4], refs[4:6], refs[6:8], refs[8:10]
-    out_ref, acc = refs[10], refs[11]
-    step = pl.program_id(0)
-    planes = path[0].shape[1]
+def piece_of(pieces, region):
+    rows = sum(piece.shape[1] for piece in pieces) // REGIONS
+    at = region * rows
+    for piece in pieces:
+        if at < piece.shape[1]:
+            return piece, at, rows
+        at -= piece.shape[1]
+
+
+def over_planes(body, rows, unroll, carry=0):
+    def some(t, carry):
+        for j in range(unroll):
+            carry = body(t * unroll + j, carry)
+        return carry
+
+    return lax.fori_loop(0, rows // unroll, some, carry)
+
+
+def groups(refs, counts):
+    out, at = [], 0
+    for count in counts:
+        out.append(refs[at : at + count])
+        at += count
+    return out, refs[at:]
+
+
+def moment_kernel(counts, side_ref, *refs):
+    path, refs = groups(refs, counts)
+    forces, speeds, energies, out_ref = refs[:2], refs[2:4], refs[4:6], refs[6]
     zero = jnp.zeros((8, 128), jnp.float32)
-
-    @pl.when(step == 0)
-    def _():
-        acc[...] = jnp.zeros_like(acc)
-
-    def one(p, carry):
-        carry = list(carry)
-        for axis in range(3):
-            at = [ref[axis, p] for ref in path]
-            diff = [at[j + 1] - at[j] for j in range(3)]
-            square = [d * d for d in diff]
-            for j in range(2):
-                force, speed = forces[j][axis, p], speeds[j][axis, p]
-                terms = (
-                    force * force,
-                    force * diff[j + 1],
-                    force * diff[j],
-                    square[j + 1],
-                    square[j],
-                    diff[j] * diff[j + 1],
-                    speed * speed,
-                )
-                for k, term in enumerate(terms):
-                    carry[7 * j + k] = carry[7 * j + k] + term
-        return tuple(carry)
-
-    def some(t, carry):
-        for j in range(2):
-            carry = one(2 * t + j, carry)
-        return carry
-
-    sums = lax.fori_loop(0, planes // 2, some, (zero,) * 14)
-    for k in range(14):
-        acc[k] += sums[k]
-
-    @pl.when(step == pl.num_programs(0) - 1)
-    def _():
-        lane = lax.broadcasted_iota(jnp.int32, (1, 128), 1)
-        odd = side_ref[0] == 1
-        sign = jnp.where(odd, -1.0, 1.0).astype(jnp.float32)
-        row = jnp.zeros((1, 128), jnp.float32)
-        for j in range(2):
-            ahead = [total_of(acc[7 * j + k]) for k in range(7)]
-            values = (
-                total_of(energies[j][...]),
-                ahead[0],
-                sign * jnp.where(odd, ahead[2], ahead[1]),
-                sign * jnp.where(odd, ahead[1], ahead[2]),
-                jnp.where(odd, ahead[4], ahead[3]),
-                jnp.where(odd, ahead[3], ahead[4]),
-                ahead[5],
-                ahead[6],
-            )
-            for k, value in enumerate(values):
-                row = row + jnp.where(lane == 8 * j + k, value, 0.0)
-        out_ref[...] = jnp.broadcast_to(row, out_ref.shape)
-
-
-def moments(side, path, forces, speeds, energies, copies, chunk):
-    planes = path[0].shape[1]
-    block = pl.BlockSpec((3, chunk, 8, 128), lambda t: (0, t, 0, 0))
-    tile = pl.BlockSpec((8, 128), lambda t: (0, 0))
+    sums = (zero,) * 14
+    for region in range(REGIONS):
+        held = [piece_of(pieces, region) for pieces in path]
+        rows = held[0][2]
+
+        def one(p, carry):
+            carry = list(carry)
+            for axis in range(3):
+                at = [ref[axis, start + p] for ref, start, _ in held]
+                diff = [at[j + 1] - at[j] for j in range(3)]
+                square = [d * d for d in diff]
+                for j in range(2):
+                    force = forces[j][axis, region * rows + p]
+                    speed = speeds[j][axis, region * rows + p]
+                    terms = (
+                        force * force,
+                        force * diff[j + 1],
+                        force * diff[j],
+                        square[j + 1],
+                        square[j],
+                        diff[j] * diff[j + 1],
+                        speed * speed,
+                    )
+                    for k, term in enumerate(terms):
+                        carry[7 * j + k] = carry[7 * j + k] + term
+            return tuple(carry)
+
+        sums = over_planes(one, rows, 2, sums)
+
+    lane = lax.broadcasted_iota(jnp.int32, (1, 128), 1)
+    odd = side_ref[0] == 1
+    sign = jnp.where(odd, -1.0, 1.0).astype(jnp.float32)
+    row = jnp.zeros((1, 128), jnp.float32)
+    for j in range(2):
+        ahead = [total_of(sums[7 * j + k]) for k in range(7)]
+        values = (
+            total_of(energies[j][...]),
+            ahead[0],
+            sign * jnp.where(odd, ahead[2], ahead[1]),
+            sign * jnp.where(odd, ahead[1], ahead[2]),
+            jnp.where(odd, ahead[4], ahead[3]),
+            jnp.where(odd, ahead[3], ahead[4]),
+            ahead[5],
+            ahead[6],
+        )
+        for k, value in enumerate(values):
+            row = row + jnp.where(lane == 8 * j + k, value, 0.0)
+    out_ref[...] = jnp.broadcast_to(row, out_ref.shape)
+
+
+VMEM = pl.BlockSpec(memory_space=pltpu.VMEM)
+SMEM = pl.BlockSpec(memory_space=pltpu.SMEM)
+PARAMS = pltpu.CompilerParams(vmem_limit_bytes=32 * 1024 * 1024)
+
+
+def moments(side, path, forces, speeds, energies, copies):
+    counts = [len(pieces) for pieces in path]
+    arrays = [piece for pieces in path for piece in pieces] + [*forces, *speeds, *energies]
     return pl.pallas_call(
-        moment_kernel,
-        grid=(planes // chunk,),
+        functools.partial(moment_kernel, counts),
         out_shape=jax.ShapeDtypeStruct((copies, 128), jnp.float32),
-        in_specs=[pl.BlockSpec(memory_space=pltpu.SMEM)] + [block] * 8 + [tile] * 2,
-        out_specs=pl.BlockSpec((copies, 128), lambda t: (0, 0)),
-        scratch_shapes=[pltpu.VMEM((14, 8, 128), jnp.float32)],
-        compiler_params=pltpu.CompilerParams(vmem_limit_bytes=32 * 1024 * 1024),
+        in_specs=[SMEM] + [VMEM] * len(arrays),
+        out_specs=VMEM,
+        compiler_params=PARAMS,
         name="path_moments",
-    )(side, *path, *forces, *speeds, *energies)
+    )(side, *arrays)
 
 
 def path_terms(summary, images):
@@ -438,153 +455,134 @@
     return terms[j, 0] * speed + terms[j, 1] * force + terms[j, 2] * ahead + terms[j, 3] * behind
 
 
-def update_kernel(images, image_ref, gathered_ref, *refs):
-    path, forces, speeds, moved, new_speeds = refs[:4], refs[4:6], refs[6:8], refs[8:10], refs[10:12]
-    terms = refs[12]
-    planes = path[0].shape[1]
-
-    @pl.when(pl.program_id(0) == 0)
-    def _():
-        step_terms(image_ref, gathered_ref, images, terms)
-
-    def some(t, carry):
-        for i in range(2):
-            p = 2 * t + i
+def update_kernel(counts, images, image_ref, gathered_ref, *refs):
+    path, refs = groups(refs, counts)
+    forces, speeds, moved, new_speeds = refs[:2], refs[2:4], refs[4:6], refs[6:8]
+    tops, bottoms, terms = refs[8:11]
+    step_terms(image_ref, gathered_ref, images, terms)
+    for region in range(REGIONS):
+        held = [piece_of(pieces, region) for pieces in path]
+        rows = held[0][2]
+
+        def one(p, carry):
             for axis in range(3):
-                at = [ref[axis, p] for ref in path]
+                at = [ref[axis, start + p] for ref, start, _ in held]
                 diff = [at[j + 1] - at[j] for j in range(3)]
                 for j in range(2):
-                    speed = new_speed(terms, j, speeds[j][axis, p], forces[j][axis, p], diff[j + 1], diff[j])
-                    new_speeds[j][axis, p] = speed
-                    moved[j][axis, p] = at[j + 1] + time_step * speed
-        return carry
-
-    lax.fori_loop(0, planes // 2, some, 0)
-
-
-def update(image, gathered, path, forces, speeds, images, chunk):
-    planes = path[0].shape[1]
-    block = pl.BlockSpec((3, chunk, 8, 128), lambda t: (0, t, 0, 0))
-    out = jax.ShapeDtypeStruct((3, planes, 8, 128), jnp.float32)
+                    q = region * rows + p
+                    speed = new_speed(terms, j, speeds[j][axis, q], forces[j][axis, q], diff[j + 1], diff[j])
+                    new_speeds[j][axis, q] = speed
+                    moved[j][axis, q] = at[j + 1] + time_step * speed
+            return carry
+
+        over_planes(one, rows, 2)
+    planes = moved[0].shape[1]
+    for j in range(2):
+        tops[j] = moved[j][:, planes - HALO :]
+        bottoms[j] = moved[j][:, :HALO]
+
+
+def update(image, gathered, path, forces, speeds, images):
+    counts = [len(pieces) for pieces in path]
+    arrays = [piece for pieces in path for piece in pieces] + [*forces, *speeds]
+    out = jax.ShapeDtypeStruct(forces[0].shape, jnp.float32)
+    edge = jax.ShapeDtypeStruct((2, 3, HALO, 8, 128), jnp.float32)
     results = pl.pallas_call(
-        functools.partial(update_kernel, images),
-        grid=(planes // chunk,),
-        out_shape=(out,) * 4,
-        in_specs=[
-            pl.BlockSpec(memory_space=pltpu.SMEM),
-            pl.BlockSpec(gathered.shape, lambda t: (0, 0)),
-        ]
-        + [block] * 8,
-        out_specs=(block,) * 4,
+        functools.partial(update_kernel, counts, images),
+        out_shape=(out,) * 4 + (edge,) * 2,
+        in_specs=[SMEM] + [VMEM] * (1 + len(arrays)),
+        out_specs=(VMEM,) * 6,
         scratch_shapes=[pltpu.VMEM((2, 4, 8, 128), jnp.float32)],
-        compiler_params=pltpu.CompilerParams(vmem_limit_bytes=32 * 1024 * 1024),
+        compiler_params=PARAMS,
         name="fire_update",
-    )(image, gathered, *path, *forces, *speeds)
-    return results[:2], results[2:]
-
-
-def last_partner_kernel(images, image_ref, gathered_ref, before, here, after, force, speed, new_ref, terms_ref, terms):
-    planes = here.shape[1]
-
-    @pl.when(pl.program_id(0) == 0)
-    def _():
-        step_terms(image_ref, gathered_ref, images, terms)
-        terms_ref[...] = terms[...]
-
-    def some(t, carry):
-        for i in range(2):
-            p = 2 * t + i
+    )(image, gathered, *arrays)
+    return results[:2], results[2:4], results[4], results[5]
+
+
+def last_partner_kernel(images, image_ref, gathered_ref, before, here, after, force, speed, *outs):
+    parts, terms_ref = outs[:-1], outs[-1]
+    step_terms(image_ref, gathered_ref, images, terms_ref)
+    for region, part in enumerate(parts):
+        rows = part.shape[1]
+
+        def one(p, carry):
+            q = region * rows + p
             for axis in range(3):
-                at = here[axis, p]
-                new_ref[axis, p] = new_speed(
-                    terms, 1, speed[axis, p], force[axis, p], after[axis, p] - at, at - before[axis, p]
+                at = here[axis, q]
+                part[axis, p] = new_speed(
+                    terms_ref, 1, speed[axis, q], force[axis, q], after[axis, q] - at, at - before[axis, q]
                 )
-        return carry
-
-    lax.fori_loop(0, planes // 2, some, 0)
-
-
-def last_partner(image, gathered, path, force, speed, images, chunk):
-    planes = force.shape[1]
-    block = pl.BlockSpec((3, chunk, 8, 128), lambda t: (0, t, 0, 0))
+            return carry
+
+        over_planes(one, rows, 2)
+
+
+def last_partner(image, gathered, path, force, speed, images):
+    part = jax.ShapeDtypeStruct((3, force.shape[1] // REGIONS, 8, 128), jnp.float32)
     return pl.pallas_call(
         functools.partial(last_partner_kernel, images),
-        grid=(planes // chunk,),
-        out_shape=(
-            jax.ShapeDtypeStruct((3, planes, 8, 128), jnp.float32),
-            jax.ShapeDtypeStruct((2, 4, 8, 128), jnp.float32),
-        ),
-        in_specs=[
-            pl.BlockSpec(memory_space=pltpu.SMEM),
-            pl.BlockSpec(gathered.shape, lambda t: (0, 0)),
-        ]
-        + [block] * 5,
-        out_specs=(block, pl.BlockSpec((2, 4, 8, 128), lambda t: (0, 0, 0, 0))),
-        scratch_shapes=[pltpu.VMEM((2, 4, 8, 128), jnp.float32)],
-        compiler_params=pltpu.CompilerParams(vmem_limit_bytes=32 * 1024 * 1024),
+        out_shape=(part,) * REGIONS + (jax.ShapeDtypeStruct((2, 4, 8, 128), jnp.float32),),
+        in_specs=[SMEM] + [VMEM] * 6,
+        out_specs=(VMEM,) * (REGIONS + 1),
+        compiler_params=PARAMS,
         name="last_partner",
     )(image, gathered, *path, force, speed)
 
 
 def last_own_kernel(side_ref, terms, before, here, after, force, speed, moved, new_ref):
-    planes = here.shape[1]
-
-    def some(t, carry):
-        for i in range(2):
-            p = 2 * t + i
-            for axis in range(3):
-                at = here[axis, p]
-                new = new_speed(
-                    terms, 0, speed[axis, p], force[axis, p], after[axis, p] - at, at - before[axis, p]
-                )
-                new_ref[axis, p] = new
-                moved[axis, p] = at + time_step * new
+    def one(p, carry):
+        for axis in range(3):
+            at = here[axis, p]
+            new = new_speed(
+                terms, 0, speed[axis, p], force[axis, p], after[axis, p] - at, at - before[axis, p]
+            )
+            new_ref[axis, p] = new
+            moved[axis, p] = at + time_step * new
         return carry
 
-    lax.fori_loop(0, planes // 2, some, 0)
-
-
-def last_own(side, terms, path, force, speed, chunk):
+    over_planes(one, here.shape[1], 2)
+
+
+def last_own(side, terms, path, force, speed):
     planes = force.shape[1]
-    steps = planes // chunk
+    chunk = planes // REGIONS
     block = pl.BlockSpec((3, chunk, 8, 128), lambda t, side_ref: (0, t, 0, 0))
-    half = pl.BlockSpec((3, chunk, 8, 128), lambda t, side_ref: (0, side_ref[0] * steps + t, 0, 0))
+    half = pl.BlockSpec((3, chunk, 8, 128), lambda t, side_ref: (0, side_ref[0] * REGIONS + t, 0, 0))
     out = jax.ShapeDtypeStruct((3, 2 * planes, 8, 128), jnp.float32)
     return pl.pallas_call(
         last_own_kernel,
         grid_spec=pltpu.PrefetchScalarGridSpec(
             num_scalar_prefetch=1,
-            grid=(steps,),
+            grid=(REGIONS,),
             in_specs=[pl.BlockSpec((2, 4, 8, 128), lambda t, side_ref: (0, 0, 0, 0))] + [block] * 5,
             out_specs=(half, half),
         ),
         out_shape=(out, out),
-        compiler_params=pltpu.CompilerParams(vmem_limit_bytes=32 * 1024 * 1024),
+        compiler_params=PARAMS,
         name="last_own",
     )(side, terms, *path, force, speed)
 
 
 def last_join_kernel(side_ref, here, speed, moved_in, speed_in, moved, new_ref):
-    planes = here.shape[1]
-
-    def some(t, carry):
-        for i in range(4):
-            for axis in range(3):
-                p = 4 * t + i
-                new = speed[axis, p]
-                new_ref[axis, p] = new
-                moved[axis, p] = here[axis, p] + time_step * new
+    def one(p, carry):
+        for axis in range(3):
+            new = speed[axis, p]
+            new_ref[axis, p] = new
+            moved[axis, p] = here[axis, p] + time_step * new
         return carry
 
-    lax.fori_loop(0, planes // 4, some, 0)
-
-
-def last_join(side, here, speed, moved, speeds, chunk):
-    planes = here.shape[1]
-    steps = planes // chunk
+    over_planes(one, speed.shape[1], 4)
+
+
+def last_join(side, region, here, speed, moved, speeds):
+    rows = speed.shape[1]
+    chunk = rows // JOIN_STEPS
+    first = region * JOIN_STEPS
     block = pl.BlockSpec((3, chunk, 8, 128), lambda t, side_ref: (0, t, 0, 0))
+    here_block = pl.BlockSpec((3, chunk, 8, 128), lambda t, side_ref: (0, first + t, 0, 0))
     half = pl.BlockSpec(
-        (3, chunk, 8, 128), lambda t, side_ref: (0, (1 - side_ref[0]) * steps + t, 0, 0)
+        (3, chunk, 8, 128),
+        lambda t, side_ref: (0, (1 - side_ref[0]) * REGIONS * JOIN_STEPS + first + t, 0, 0),
     )
     out = jax.ShapeDtypeStruct(moved.shape, jnp.float32)
     whole = pl.BlockSpec(memory_space=pl.ANY)
@@ -592,15 +590,46 @@
         last_join_kernel,
         grid_spec=pltpu.PrefetchScalarGridSpec(
             num_scalar_prefetch=1,
-            grid=(steps,),
-            in_specs=[block, block, whole, whole],
+            grid=(JOIN_STEPS,),
+            in_specs=[here_block, block, whole, whole],
             out_specs=(half, half),
         ),
         out_shape=(out, out),
         input_output_aliases={3: 0, 4: 1},
-        compiler_params=pltpu.CompilerParams(vmem_limit_bytes=32 * 1024 * 1024),
+        compiler_params=PARAMS,
         name="last_join",
     )(side, here, speed, moved, speeds)
+
+
+def cut_kernel(starts, side_ref, *refs):
+    count = len(starts)
+    source, outs, sems = refs[0], refs[1 : 1 + count], refs[1 + count]
+    copies = []
+    for k, out in enumerate(outs):
+        rows = source.at[:, pl.ds(at_side(starts[k], side_ref), out.shape[1])]
+        copies.append(pltpu.make_async_copy(rows, out, sems.at[k]))
+    for copy in copies:
+        copy.start()
+    for copy in copies:
+        copy.wait()
+
+
+def at_side(pair, side_ref):
+    even, odd = pair
+    return even if even == odd else even + (odd - even) * side_ref[0]
+
+
+def cut(side, array, starts, sizes):
+    count = len(sizes)
+    return pl.pallas_call(
+        functools.partial(cut_kernel, starts),
+        out_shape=tuple(jax.ShapeDtypeStruct((3, size, 8, 128), jnp.float32) for size in sizes),
+        in_specs=[SMEM, pl.BlockSpec(memory_space=pltpu.HBM)],
+        out_specs=(VMEM,) * count,
+        scratch_shapes=[pltpu.SemaphoreType.DMA((count,))],
+        compiler_params=PARAMS,
+        name="cut",
+    )(side, array)
 
 
 def local(displacement, velocity):
@@ -610,7 +639,6 @@
     both = ("image", "domain")
     own_image = lax.axis_index("image").astype(jnp.int32)
     side = own_image % 2
-    is_low = side == 0
     image_arg, side_arg = own_image.reshape(1), side.reshape(1)
     slab = displacement.reshape(3, planes, 8, 128)
     slab_speed = velocity.reshape(3, planes, 8, 128)
@@ -628,62 +656,77 @@
     upward = [(at(i, d), at(i ^ 1, d + i % 2)) for i, d in everyone]
     downward = [(b, a) for a, b in upward]
 
-    def planes_from(array, start, count):
-        return lax.dynamic_slice_in_dim(array, start, count, axis=1)
-
-    end = planes - HALO
-    halo_own = lax.ppermute(planes_from(slab, (1 - side) * end, HALO), both, outer_own)
-    halo_partner = lax.ppermute(planes_from(slab, side * end, HALO), both, outer_partner)
-    halo_inner = lax.ppermute(planes_from(slab, half - HALO + HALO * side, HALO), "image", across)
-    own = planes_from(slab, half * side, half)
-    own_speed = planes_from(slab_speed, half * side, half)
-    piece = half // CHUNKS
-    pieces = [
-        lax.ppermute(planes_from(slab, half * (1 - side) + c * piece, piece), "image", across)
-        for c in range(CHUNKS)
-    ]
+    end, top = planes - HALO, half + HALO
+    piece = half // REGIONS
+    edge_own, edge_partner, edge_inner, near_inner, own, *far_pieces = cut(
+        side_arg,
+        slab,
+        ((end, 0), (0, end), (half - HALO, half), (half, half - HALO), (0, half))
+        + tuple((half + c * piece, c * piece) for c in range(REGIONS)),
+        (HALO,) * 4 + (half,) + (piece,) * REGIONS,
+    )
+    halo_own = lax.ppermute(edge_own, both, outer_own)
+    halo_partner = lax.ppermute(edge_partner, both, outer_partner)
+    halo_inner = lax.ppermute(edge_inner, "image", across)
+    *far_pieces, halo_own, halo_partner, halo_inner = lax.optimization_barrier(
+        (*far_pieces, halo_own, halo_partner, halo_inner)
+    )
+    partner = [lax.ppermute(part, "image", across) for part in far_pieces]
     beyond_own = lax.ppermute(own, "image", own_out)
-    beyond_partner = jnp.concatenate(
-        [lax.ppermute(part, "image", partner_out) for part in pieces], axis=1
-    )
-    partner = jnp.concatenate(pieces, axis=1)
-    partner_speed = lax.ppermute(planes_from(slab_speed, half * (1 - side), half), "image", across)
-    near_low, near_high = slab[:, half - HALO : half], slab[:, half : half + HALO]
-    own_halo = (jnp.where(is_low, halo_own, near_low), jnp.where(is_low, near_high, halo_own))
-    partner_halo = (
-        jnp.where(is_low, halo_partner, halo_inner),
-        jnp.where(is_low, halo_inner, halo_partner),
-    )
-
-    path = (beyond_partner, own, partner, beyond_own)
+    outer, inner = (0, top), (top, 0)
+    own_force, own_energy = image_forces(
+        side_arg,
+        half,
+        ((own, None, (HALO, HALO)), (halo_own, None, outer), (near_inner, None, inner)),
+    )
+    own_speed, far_speed = cut(side_arg, slab_speed, ((0, half), (half, 0)), (half, half))
+    far_speed, _ = lax.optimization_barrier((far_speed, own_energy))
+    *partner[1:], _ = lax.optimization_barrier((*partner[1:], own_energy))
+    beyond_partner = [lax.ppermute(part, "image", partner_out) for part in partner]
+    halo_inner, beyond_partner[0] = lax.optimization_barrier((halo_inner, beyond_partner[0]))
+    partner_speed = lax.ppermute(far_speed, "image", across)
+
+    partner_sources = tuple(
+        (part, None, (HALO + c * piece,) * 2) for c, part in enumerate(partner)
+    ) + ((halo_partner, None, outer), (halo_inner, None, inner))
+    path = (beyond_partner, [own], partner, [beyond_own])
     speeds = (own_speed, partner_speed)
-    halos = (own_halo, partner_halo)
+    results = [(own_force, own_energy), image_forces(side_arg, half, partner_sources)]
     for step_index in range(FIRE_STEPS):
-        results = [image_forces(part, *halo) for part, halo in zip(path[1:3], halos)]
+        if step_index > 0:
+            results = [image_forces(side_arg, half, held) for held in sources]
         forces, energies = zip(*results)
-        payload = moments(side_arg, path, forces, speeds, energies, images * slabs, MOMENT_CHUNK)
+        payload = moments(side_arg, path, forces, speeds, energies, images * slabs)
         gathered = lax.all_to_all(payload, both, 0, 0, tiled=True)
         if step_index == FIRE_STEPS - 1:
             break
-        moved, speeds = update(image_arg, gathered, path, forces, speeds, images, UPDATE_CHUNK)
-        tops = jnp.stack([part[:, half - HALO :] for part in moved])
-        bottoms = jnp.stack([part[:, :HALO] for part in moved])
+        moved, speeds, tops, bottoms = update(image_arg, gathered, path, forces, speeds, images)
         low = lax.ppermute(tops, both, upward)
         high = lax.ppermute(bottoms, both, downward)
-        halos = ((low[1], high[1]), (low[0], high[0]))
+        sources = [
+            (
+                (moved[j], None, (HALO, HALO)),
+                (low, 1 - j, (0, 0)),
+                (high, 1 - j, (top, top)),
+            )
+            for j in range(2)
+        ]
         path = (
-            lax.ppermute(moved[1], "image", partner_out),
-            moved[0],
-            moved[1],
-            lax.ppermute(moved[0], "image", own_out),
+            [lax.ppermute(moved[1], "image", partner_out)],
+            [moved[0]],
+            [moved[1]],
+            [lax.ppermute(moved[0], "image", own_out)],
         )
-        returned = lax.ppermute(moved[1], "image", across)
-    last_speed, terms = last_partner(
-        image_arg, gathered, path[1:], forces[1], speeds[1], images, UPDATE_CHUNK
-    )
-    returned_speed = lax.ppermute(last_speed, "image", across)
-    moved, new_speeds = last_own(side_arg, terms, path[:3], forces[0], speeds[0], UPDATE_CHUNK)
-    moved, new_speeds = last_join(side_arg, returned, returned_speed, moved, new_speeds, UPDATE_CHUNK)
+        back_home, _ = lax.optimization_barrier((moved[1], low))
+        returned = lax.ppermute(back_home, "image", across)
+    whole = [pieces[0] for pieces in path]
+    *last_speeds, terms = last_partner(
+        image_arg, gathered, whole[1:], forces[1], speeds[1], images
+    )
+    last_speeds = [lax.ppermute(part, "image", across) for part in last_speeds]
+    moved, new_speeds = last_own(side_arg, terms, whole[:3], forces[0], speeds[0])
+    for region, part in enumerate(last_speeds):
+        moved, new_speeds = last_join(side_arg, region, returned, part, moved, new_speeds)
     return (moved.reshape(displacement.shape), new_speeds.reshape(velocity.shape))
 
 

time: 124 us -> 123 us (level)
  waiting for transfers between devices: 27.9 us -> 41.8 us
  starting transfers between devices: 40.8 us -> 27.1 us
  blocking collectives: 20.4 us -> 30.7 us
  local copies, waits for them, and re-layouts: 7.29 us -> 1.27 us
  Pallas kernels: 25.3 us -> 20.5 us
    ppermute x1, waiting for transfers between devices: 0.01 us -> 12.3 us  [local(): high = lax.ppermute(bottoms, both, downward)]
    all_to_all x1 -> x2, blocking collectives: 20.4 us -> 30.7 us  [local(): gathered = lax.all_to_all(payload, both, 0, 0, tiled=True)]
    all_to_all x1 -> x0, waiting for transfers between devices: 8.21 us -> none  [local(): gathered = lax.all_to_all(payload, both, 0, 0, tiled=True)]
    all_to_all x1 -> x0, starting transfers between devices: 7.83 us -> none  [local(): gathered = lax.all_to_all(payload, both, 0, 0, tiled=True)]
    ppermute x8 -> x9, waiting for transfers between devices: 16 us -> 21.8 us  [the longest x2 10.3 us: local(): last_speeds = [lax.ppermute(part, 'image', across) for part in last_speeds]]
    ppermute x1, waiting for transfers between devices: 1.76 us -> 6.82 us  [local(): low = lax.ppermute(tops, both, upward)]
    ppermute x1, starting transfers between devices: 5.04 us -> 0.01 us  [local(): high = lax.ppermute(bottoms, both, downward)]
    dynamic_slice x4 -> x0, local copies, waits for them, and re-layouts: 3.57 us -> none  [planes_from(): return lax.dynamic_slice_in_dim(array, start, count, axis=1)]
  transfers between devices with their start and end apart: 16 -> 16, of which waited for: 6 -> 9; matrix products, arithmetic and copies ran while one was open for 4% -> 0% of each run, Pallas kernels for 14% -> 14%
where the time goes in v2:
time: 123 us; the launch traced here: 122 us
  waiting for transfers between devices  41.8 us (34%)
  blocking collectives  30.7 us (25%)
  starting transfers between devices  27.1 us (22%)
  Pallas kernels  20.5 us (17%)
  local copies, waits for them, and re-layouts  1.27 us (1%)
    all_to_all x2, blocking collectives, local(): gathered = lax.all_to_all(payload, both, 0, 0, tiled=True)  30.7 us
    pallas_call x4, Pallas kernels, image_forces(): pl.pallas_call(functools.partial(force_kernel, starts, slots), out_shape=...  13.7 us
    ppermute x1, waiting for transfers between devices, local(): high = lax.ppermute(bottoms, both, downward)  12.3 us
    ppermute x2, waiting for transfers between devices, local(): last_speeds = [lax.ppermute(part, 'image', across) for part in last_speeds]  10.3 us
    ppermute x1, waiting for transfers between devices, local(): low = lax.ppermute(tops, both, upward)  6.82 us
    ppermute x2, starting transfers between devices, local(): lax.ppermute(part, 'image', partner_out)  6.81 us
    ppermute x1, starting transfers between devices, local(): halo_partner = lax.ppermute(edge_partner, both, outer_partner)  6.67 us
    ppermute x2, waiting for transfers between devices, local(): partner = [lax.ppermute(part, 'image', across) for part in far_pieces]  5.36 us
  transfers between devices with their start and end apart: 16, of which 9 were waited for; matrix products, arithmetic and copies ran while one was open for 0% of the time, Pallas kernels for 14%

profile of v2, /device:TPU:0, one launch (start us, length us, event | category | flops | bytes accessed | tf_op | source)
XLA Modules:
  0.0 122.2 jit_solution(4122414044156489475)
XLA Ops:
  0.6 0.0 copy-start
  0.7 1.3 %copy-done = f32[1,3,98304]{2,0,1:T(1,128)S(1)} copy-done((f32[1,3,98304]{2,0,1:T(1,128)S(1)}, f32[1,3,98304]{2,0,1:T(1,128)}, u32[]{:S(2)}) %copy-start) | copy-done | bytes 1179672
  1.9 0.0 copy-start.1
  1.9 0.2 cut.2
  2.1 0.1 collective-permute-start
  2.2 6.7 %collective-permute-start.1 = (f32[3,2,8,128]{3,2,1,0:T(8,128)S(1)}, f32[3,2,8,128]{3,2,1,0:T(8,128)S(1)}, u32[]{:S(2)}, u32[]{:S(2)}) collective-permute-start(f32[3,2,8,128]{3,2,1,0:T(8,128)S(1)} %get-tuple-element.47), channel_id=1, source_target_pairs={{0,31},{1,16},{2,17},{3,18},{4,19},{5,20},{6,21},{7,22},{8,23},{9,... | collective-permute-start | bytes 73736 | tf_op jit(solution)/shard_map/ppermute | solution.py:669
  8.9 0.2 collective-permute-start.2
  9.1 1.3 %collective-permute-start.7 = (f32[3,48,8,128]{3,2,1,0:T(8,128)S(1)}, f32[3,48,8,128]{3,2,1,0:T(8,128)S(1)}, u32[]{:S(2)}, u32[]{:S(2)}) collective-permute-start(f32[3,48,8,128]{3,2,1,0:T(8,128)S(1)} %get-tuple-element.53.refs_0_.refs_2_), channel_id=1, source_target_pairs={{16,48},{32,0},{48,80},{64,32},{80,112},{96,64},{17,49},{33,1},{49... | collective-permute-start | bytes 1769480 | tf_op jit(solution)/shard_map/ppermute | solution.py:675
  10.4 0.0 copy-done.1
  10.4 0.1 cut.3
  10.5 0.0 collective-permute-done.refs_1_
  10.5 0.0 collective-permute-done.1.refs_2_
  10.5 2.2 %collective-permute-done.2.refs_3_ = f32[3,2,8,128]{3,2,1,0:T(8,128)S(1)} collective-permute-done((f32[3,2,8,128]{3,2,1,0:T(8,128)S(1)}, f32[3,2,8,128]{3,2,1,0:T(8,128)S(1)}, u32[]{:S(2)}, u32[]{:S(2)}) %collective-permute-start.2) | collective-permute-done | bytes 24608 | tf_op jit(solution)/shard_map/ppermute | solution.py:670
  12.7 1.9 %collective-permute-start.3 = (f32[3,24,8,128]{3,2,1,0:T(8,128)S(1)}, f32[3,24,8,128]{3,2,1,0:T(8,128)S(1)}, u32[]{:S(2)}, u32[]{:S(2)}) collective-permute-start(f32[3,24,8,128]{3,2,1,0:T(8,128)S(1)} %get-tuple-element.50), channel_id=1, source_target_pairs={{0,16},{16,0},{32,48},{48,32},{64,80},{80,64},{96,112},{112,96},{1... | collective-permute-start | bytes 884744 | tf_op jit(solution)/shard_map/ppermute | solution.py:674
  14.6 0.2 collective-permute-start.5
  14.7 3.5 %slab_forces.4 = (f32[3,48,8,128]{3,2,1,0:T(8,128)S(1)}, f32[8,128]{1,0:T(8,128)S(1)}) custom-call(s32[1]{0:T(128)} %bitcast.side_ref, f32[3,48,8,128]{3,2,1,0:T(8,128)S(1)} %get-tuple-element.53.refs_0_.refs_2_, f32[3,2,8,128]{3,2,1,0:T(8,128)S(1)} %collective-permute-done.refs_1_, f32[3,2,8,128]{3,2,1,0:T(8,128)S(1)} %get-tuple-element.55.refs_2_), custom_call_target="tpu_custom_call" | custom-call | flops 20000000 | bytes 15000000 | tf_op jit(solution)/shard_map/slab_forces/pallas_call | solution.py:257
  18.2 1.9 %collective-permute-start.8 = (f32[3,48,8,128]{3,2,1,0:T(8,128)S(1)}, f32[3,48,8,128]{3,2,1,0:T(8,128)S(1)}, u32[]{:S(2)}, u32[]{:S(2)}) collective-permute-start(f32[3,48,8,128]{3,2,1,0:T(8,128)S(1)} %get-tuple-element.64), channel_id=1, source_target_pairs={{0,16},{16,0},{32,48},{48,32},{64,80},{80,64},{96,112},{112,96},{1... | collective-permute-start | bytes 1769480 | tf_op jit(solution)/shard_map/ppermute | solution.py:687
  20.1 2.5 %collective-permute-done.3.refs_0_.refs_3_ = f32[3,24,8,128]{3,2,1,0:T(8,128)S(1)} collective-permute-done((f32[3,24,8,128]{3,2,1,0:T(8,128)S(1)}, f32[3,24,8,128]{3,2,1,0:T(8,128)S(1)}, u32[]{:S(2)}, u32[]{:S(2)}) %collective-permute-start.3) | collective-permute-done | bytes 294944 | tf_op jit(solution)/shard_map/ppermute | solution.py:674
  22.6 3.4 %collective-permute-start.4 = (f32[3,24,8,128]{3,2,1,0:T(8,128)S(1)}, f32[3,24,8,128]{3,2,1,0:T(8,128)S(1)}, u32[]{:S(2)}, u32[]{:S(2)}) collective-permute-start(f32[3,24,8,128]{3,2,1,0:T(8,128)S(1)} %collective-permute-done.3.refs_0_.refs_3_), channel_id=1, source_target_pairs={{48,16},{0,32},{80,48},{32,64},{112,80},{64,96},{49,17},{1,33},{81... | collective-permute-start | bytes 884744 | tf_op jit(solution)/shard_map/ppermute | solution.py:685
  26.0 2.9 %collective-permute-done.5.refs_1_.refs_4_ = f32[3,24,8,128]{3,2,1,0:T(8,128)S(1)} collective-permute-done((f32[3,24,8,128]{3,2,1,0:T(8,128)S(1)}, f32[3,24,8,128]{3,2,1,0:T(8,128)S(1)}, u32[]{:S(2)}, u32[]{:S(2)}) %collective-permute-start.5) | collective-permute-done | bytes 294944 | tf_op jit(solution)/shard_map/ppermute | solution.py:674
  28.9 3.4 %collective-permute-start.6 = (f32[3,24,8,128]{3,2,1,0:T(8,128)S(1)}, f32[3,24,8,128]{3,2,1,0:T(8,128)S(1)}, u32[]{:S(2)}, u32[]{:S(2)}) collective-permute-start(f32[3,24,8,128]{3,2,1,0:T(8,128)S(1)} %collective-permute-done.5.refs_1_.refs_4_), channel_id=1, source_target_pairs={{48,16},{0,32},{80,48},{32,64},{112,80},{64,96},{49,17},{1,33},{81... | collective-permute-start | bytes 884744 | tf_op jit(solution)/shard_map/ppermute | solution.py:685
  32.3 0.0 collective-permute-done.4.refs_0_
  32.3 3.3 %slab_forces.5 = (f32[3,48,8,128]{3,2,1,0:T(8,128)S(1)}, f32[8,128]{1,0:T(8,128)S(1)}) custom-call(s32[1]{0:T(128)} %bitcast.side_ref, f32[3,24,8,128]{3,2,1,0:T(8,128)S(1)} %collective-permute-done.3.refs_0_.refs_3_, f32[3,24,8,128]{3,2,1,0:T(8,128)S(1)} %collective-permute-done.5.refs_1_.refs_4_, f32[3,2,8,128]{3,2,1,0:T(8,128)S(1)} %collective-permute-done.1.refs_2_, ...), custom_call_target="tpu_custom_call" | custom-call | flops 20000000 | bytes 15000000 | tf_op jit(solution)/shard_map/slab_forces/pallas_call | solution.py:257
  35.6 0.0 collective-permute-done.7.refs_5_
  35.6 0.9 collective-permute-done.6.refs_1_
  36.5 3.9 %collective-permute-done.8.refs_9_ = f32[3,48,8,128]{3,2,1,0:T(8,128)S(1)} collective-permute-done((f32[3,48,8,128]{3,2,1,0:T(8,128)S(1)}, f32[3,48,8,128]{3,2,1,0:T(8,128)S(1)}, u32[]{:S(2)}, u32[]{:S(2)}) %collective-permute-start.8) | collective-permute-done | bytes 589856 | tf_op jit(solution)/shard_map/ppermute | solution.py:687
  40.4 0.8 path_moments.2
  41.2 15.7 %all_to_all.22 = f32[128,1,128]{2,1,0:T(1,128)S(1)} all-to-all(f32[128,1,128]{2,1,0:T(1,128)S(1)} %bitcast.17), channel_id=1, replica_groups=mesh['image'=8,'domain'=16] {'image','domain'}, dimensions={0} | all-to-all | bytes 131072 | tf_op jit(solution)/shard_map/all_to_all | solution.py:700
  56.9 0.9 fire_update.1
  57.8 1.3 %collective-permute-start.12 = (f32[3,48,8,128]{3,2,1,0:T(8,128)S(1)}, f32[3,48,8,128]{3,2,1,0:T(8,128)S(1)}, u32[]{:S(2)}, u32[]{:S(2)}) collective-permute-start(f32[3,48,8,128]{3,2,1,0:T(8,128)S(1)} %get-tuple-element.69.refs_0_.refs_1_.before.here), channel_id=1, source_target_pairs={{16,48},{32,0},{48,80},{64,32},{80,112},{96,64},{17,49},{33,1},{49... | collective-permute-start | bytes 1769480 | tf_op jit(solution)/shard_map/ppermute | solution.py:718
  59.1 4.6 %collective-permute-start.11 = (f32[3,48,8,128]{3,2,1,0:T(8,128)S(1)}, f32[3,48,8,128]{3,2,1,0:T(8,128)S(1)}, u32[]{:S(2)}, u32[]{:S(2)}) collective-permute-start(f32[3,48,8,128]{3,2,1,0:T(8,128)S(1)} %get-tuple-element.68.refs_0_.refs_2_.here.after), channel_id=1, source_target_pairs={{48,16},{0,32},{80,48},{32,64},{112,80},{64,96},{49,17},{1,33},{81... | collective-permute-start | bytes 1769480 | tf_op jit(solution)/shard_map/ppermute | solution.py:715
  63.7 0.1 collective-permute-start.9
  63.8 6.8 %collective-permute-done.9.refs_1_ = f32[2,3,2,8,128]{4,3,2,1,0:T(8,128)S(1)} collective-permute-done((f32[2,3,2,8,128]{4,3,2,1,0:T(8,128)S(1)}, f32[2,3,2,8,128]{4,3,2,1,0:T(8,128)S(1)}, u32[]{:S(2)}, u32[]{:S(2)}) %collective-permute-start.9) | collective-permute-done | bytes 49184 | tf_op jit(solution)/shard_map/ppermute | solution.py:704
  70.6 0.0 collective-permute-start.10
  70.6 0.0 collective-permute-start.13
  70.6 12.3 %collective-permute-done.13.refs_2_ = f32[2,3,2,8,128]{4,3,2,1,0:T(8,128)S(1)} collective-permute-done((f32[2,3,2,8,128]{4,3,2,1,0:T(8,128)S(1)}, f32[2,3,2,8,128]{4,3,2,1,0:T(8,128)S(1)}, u32[]{:S(2)}, u32[]{:S(2)}) %collective-permute-start.13) | collective-permute-done | bytes 49184 | tf_op jit(solution)/shard_map/ppermute | solution.py:705
  82.9 3.5 %slab_forces.7 = (f32[3,48,8,128]{3,2,1,0:T(8,128)S(1)}, f32[8,128]{1,0:T(8,128)S(1)}) custom-call(s32[1]{0:T(128)} %bitcast.side_ref, f32[3,48,8,128]{3,2,1,0:T(8,128)S(1)} %get-tuple-element.68.refs_0_.refs_2_.here.after, f32[2,3,2,8,128]{4,3,2,1,0:T(8,128)S(1)} %collective-permute-done.9.refs_1_, f32[2,3,2,8,128]{4,3,2,1,0:T(8,128)S(1)} %collective-permute-done.13.refs_2_), custom_call_target="tpu_custom_call" | custom-call | flops 20000000 | bytes 15000000 | tf_op jit(solution)/shard_map/slab_forces/pallas_call | solution.py:257
  86.4 3.5 %slab_forces.6 = (f32[3,48,8,128]{3,2,1,0:T(8,128)S(1)}, f32[8,128]{1,0:T(8,128)S(1)}) custom-call(s32[1]{0:T(128)} %bitcast.side_ref, f32[3,48,8,128]{3,2,1,0:T(8,128)S(1)} %get-tuple-element.69.refs_0_.refs_1_.before.here, f32[2,3,2,8,128]{4,3,2,1,0:T(8,128)S(1)} %collective-permute-done.9.refs_1_, f32[2,3,2,8,128]{4,3,2,1,0:T(8,128)S(1)} %collective-permute-done.13.refs_2_), custom_call_target="tpu_custom_call" | custom-call | flops 20000000 | bytes 15000000 | tf_op jit(solution)/shard_map/slab_forces/pallas_call | solution.py:257
  89.9 0.0 collective-permute-done.12.refs_3_.after
  89.9 0.0 collective-permute-done.11.refs_0_.before
  89.9 0.8 path_moments.3
  90.8 15.0 %all_to_all.23 = f32[128,1,128]{2,1,0:T(1,128)S(1)} all-to-all(f32[128,1,128]{2,1,0:T(1,128)S(1)} %bitcast.18), channel_id=1, replica_groups=mesh['image'=8,'domain'=16] {'image','domain'}, dimensions={0} | all-to-all | bytes 131072 | tf_op jit(solution)/shard_map/all_to_all | solution.py:700
  105.8 0.6 last_partner.1
  106.4 0.9 collective-permute-start.15
  107.3 1.2 collective-permute-start.14
  108.5 1.6 %last_own.1 = (f32[3,96,8,128]{3,2,1,0:T(8,128)}, f32[3,96,8,128]{3,2,1,0:T(8,128)}) custom-call(s32[1]{0:T(128)} %bitcast.side_ref, f32[2,4,8,128]{3,2,1,0:T(8,128)S(1)} %get-tuple-element.79.terms, f32[3,48,8,128]{3,2,1,0:T(8,128)S(1)} %collective-permute-done.11.refs_0_.before, f32[3,48,8,128]{3,2,1,0:T(8,128)S(1)} %get-tuple-element.69.refs_0_.refs_1_.before.here, ...), custom_call_target="tpu_custom_call" | custom-call | tf_op jit(solution)/shard_map/last_own/pallas_call | solution.py:552
  110.1 0.0 collective-permute-done.10.here
  110.1 6.3 %collective-permute-done.15.speed = f32[3,24,8,128]{3,2,1,0:T(8,128)S(1)} collective-permute-done((f32[3,24,8,128]{3,2,1,0:T(8,128)S(1)}, f32[3,24,8,128]{3,2,1,0:T(8,128)S(1)}, u32[]{:S(2)}, u32[]{:S(2)}) %collective-permute-start.15) | collective-permute-done | bytes 294944 | tf_op jit(solution)/shard_map/ppermute | solution.py:726
  116.4 0.9 last_join.2
  117.3 4.0 %collective-permute-done.14.speed = f32[3,24,8,128]{3,2,1,0:T(8,128)S(1)} collective-permute-done((f32[3,24,8,128]{3,2,1,0:T(8,128)S(1)}, f32[3,24,8,128]{3,2,1,0:T(8,128)S(1)}, u32[]{:S(2)}, u32[]{:S(2)}) %collective-permute-start.14) | collective-permute-done | bytes 294944 | tf_op jit(solution)/shard_map/ppermute | solution.py:726
  121.3 0.9 last_join.3
Async XLA Ops:
  0.6 1.3 %copy-start = (f32[1,3,98304]{2,0,1:T(1,128)S(1)}, f32[1,3,98304]{2,0,1:T(1,128)}, u32[]{:S(2)}) copy-start(f32[1,3,98304]{2,0,1:T(1,128)} %param.2) | copy-start | bytes 3538948
  1.9 8.5 %copy-start.1 = (f32[1,3,98304]{2,0,1:T(1,128)S(1)}, f32[1,3,98304]{2,0,1:T(1,128)}, u32[]{:S(2)}) copy-start(f32[1,3,98304]{2,0,1:T(1,128)} %param.3) | copy-start | bytes 3538948
  2.1 8.4 %collective-permute-start = (f32[3,2,8,128]{3,2,1,0:T(8,128)S(1)}, f32[3,2,8,128]{3,2,1,0:T(8,128)S(1)}, u32[]{:S(2)}, u32[]{:S(2)}) collective-permute-start(f32[3,2,8,128]{3,2,1,0:T(8,128)S(1)} %get-tuple-element.46), channel_id=1, source_target_pairs={{0,1},{1,2},{2,3},{3,4},{4,5},{5,6},{6,7},{7,8},{8,9},{9,10},{10,1... | collective-permute-start | bytes 73736 | tf_op jit(solution)/shard_map/ppermute | solution.py:668
  2.2 8.3 %collective-permute-start.1 = (f32[3,2,8,128]{3,2,1,0:T(8,128)S(1)}, f32[3,2,8,128]{3,2,1,0:T(8,128)S(1)}, u32[]{:S(2)}, u32[]{:S(2)}) collective-permute-start(f32[3,2,8,128]{3,2,1,0:T(8,128)S(1)} %get-tuple-element.47), channel_id=1, source_target_pairs={{0,31},{1,16},{2,17},{3,18},{4,19},{5,20},{6,21},{7,22},{8,23},{9,... | collective-permute-start | bytes 73736 | tf_op jit(solution)/shard_map/ppermute | solution.py:669
  8.9 3.8 %collective-permute-start.2 = (f32[3,2,8,128]{3,2,1,0:T(8,128)S(1)}, f32[3,2,8,128]{3,2,1,0:T(8,128)S(1)}, u32[]{:S(2)}, u32[]{:S(2)}) collective-permute-start(f32[3,2,8,128]{3,2,1,0:T(8,128)S(1)} %get-tuple-element.48), channel_id=1, source_target_pairs={{0,16},{16,0},{32,48},{48,32},{64,80},{80,64},{96,112},{112,96},{1... | collective-permute-start | bytes 73736 | tf_op jit(solution)/shard_map/ppermute | solution.py:670
  9.1 26.5 %collective-permute-start.7 = (f32[3,48,8,128]{3,2,1,0:T(8,128)S(1)}, f32[3,48,8,128]{3,2,1,0:T(8,128)S(1)}, u32[]{:S(2)}, u32[]{:S(2)}) collective-permute-start(f32[3,48,8,128]{3,2,1,0:T(8,128)S(1)} %get-tuple-element.53.refs_0_.refs_2_), channel_id=1, source_target_pairs={{16,48},{32,0},{48,80},{64,32},{80,112},{96,64},{17,49},{33,1},{49... | collective-permute-start | bytes 1769480 | tf_op jit(solution)/shard_map/ppermute | solution.py:675
  12.7 9.9 %collective-permute-start.3 = (f32[3,24,8,128]{3,2,1,0:T(8,128)S(1)}, f32[3,24,8,128]{3,2,1,0:T(8,128)S(1)}, u32[]{:S(2)}, u32[]{:S(2)}) collective-permute-start(f32[3,24,8,128]{3,2,1,0:T(8,128)S(1)} %get-tuple-element.50), channel_id=1, source_target_pairs={{0,16},{16,0},{32,48},{48,32},{64,80},{80,64},{96,112},{112,96},{1... | collective-permute-start | bytes 884744 | tf_op jit(solution)/shard_map/ppermute | solution.py:674
  14.6 14.3 %collective-permute-start.5 = (f32[3,24,8,128]{3,2,1,0:T(8,128)S(1)}, f32[3,24,8,128]{3,2,1,0:T(8,128)S(1)}, u32[]{:S(2)}, u32[]{:S(2)}) collective-permute-start(f32[3,24,8,128]{3,2,1,0:T(8,128)S(1)} %get-tuple-element.52), channel_id=1, source_target_pairs={{0,16},{16,0},{32,48},{48,32},{64,80},{80,64},{96,112},{112,96},{1... | collective-permute-start | bytes 884744 | tf_op jit(solution)/shard_map/ppermute | solution.py:674
  18.2 22.2 %collective-permute-start.8 = (f32[3,48,8,128]{3,2,1,0:T(8,128)S(1)}, f32[3,48,8,128]{3,2,1,0:T(8,128)S(1)}, u32[]{:S(2)}, u32[]{:S(2)}) collective-permute-start(f32[3,48,8,128]{3,2,1,0:T(8,128)S(1)} %get-tuple-element.64), channel_id=1, source_target_pairs={{0,16},{16,0},{32,48},{48,32},{64,80},{80,64},{96,112},{112,96},{1... | collective-permute-start | bytes 1769480 | tf_op jit(solution)/shard_map/ppermute | solution.py:687
  22.6 9.7 %collective-permute-start.4 = (f32[3,24,8,128]{3,2,1,0:T(8,128)S(1)}, f32[3,24,8,128]{3,2,1,0:T(8,128)S(1)}, u32[]{:S(2)}, u32[]{:S(2)}) collective-permute-start(f32[3,24,8,128]{3,2,1,0:T(8,128)S(1)} %collective-permute-done.3.refs_0_.refs_3_), channel_id=1, source_target_pairs={{48,16},{0,32},{80,48},{32,64},{112,80},{64,96},{49,17},{1,33},{81... | collective-permute-start | bytes 884744 | tf_op jit(solution)/shard_map/ppermute | solution.py:685
  28.9 7.6 %collective-permute-start.6 = (f32[3,24,8,128]{3,2,1,0:T(8,128)S(1)}, f32[3,24,8,128]{3,2,1,0:T(8,128)S(1)}, u32[]{:S(2)}, u32[]{:S(2)}) collective-permute-start(f32[3,24,8,128]{3,2,1,0:T(8,128)S(1)} %collective-permute-done.5.refs_1_.refs_4_), channel_id=1, source_target_pairs={{48,16},{0,32},{80,48},{32,64},{112,80},{64,96},{49,17},{1,33},{81... | collective-permute-start | bytes 884744 | tf_op jit(solution)/shard_map/ppermute | solution.py:685
  57.8 32.1 %collective-permute-start.12 = (f32[3,48,8,128]{3,2,1,0:T(8,128)S(1)}, f32[3,48,8,128]{3,2,1,0:T(8,128)S(1)}, u32[]{:S(2)}, u32[]{:S(2)}) collective-permute-start(f32[3,48,8,128]{3,2,1,0:T(8,128)S(1)} %get-tuple-element.69.refs_0_.refs_1_.before.here), channel_id=1, source_target_pairs={{16,48},{32,0},{48,80},{64,32},{80,112},{96,64},{17,49},{33,1},{49... | collective-permute-start | bytes 1769480 | tf_op jit(solution)/shard_map/ppermute | solution.py:718
  59.1 30.8 %collective-permute-start.11 = (f32[3,48,8,128]{3,2,1,0:T(8,128)S(1)}, f32[3,48,8,128]{3,2,1,0:T(8,128)S(1)}, u32[]{:S(2)}, u32[]{:S(2)}) collective-permute-start(f32[3,48,8,128]{3,2,1,0:T(8,128)S(1)} %get-tuple-element.68.refs_0_.refs_2_.here.after), channel_id=1, source_target_pairs={{48,16},{0,32},{80,48},{32,64},{112,80},{64,96},{49,17},{1,33},{81... | collective-permute-start | bytes 1769480 | tf_op jit(solution)/shard_map/ppermute | solution.py:715
  63.7 6.9 %collective-permute-start.9 = (f32[2,3,2,8,128]{4,3,2,1,0:T(8,128)S(1)}, f32[2,3,2,8,128]{4,3,2,1,0:T(8,128)S(1)}, u32[]{:S(2)}, u32[]{:S(2)}) collective-permute-start(f32[2,3,2,8,128]{4,3,2,1,0:T(8,128)S(1)} %get-tuple-element.67), channel_id=1, source_target_pairs={{0,16},{1,17},{2,18},{3,19},{4,20},{5,21},{6,22},{7,23},{8,24},{9,... | collective-permute-start | bytes 147464 | tf_op jit(solution)/shard_map/ppermute | solution.py:704
  70.6 39.4 %collective-permute-start.10 = (f32[3,48,8,128]{3,2,1,0:T(8,128)S(1)}, f32[3,48,8,128]{3,2,1,0:T(8,128)S(1)}, u32[]{:S(2)}, u32[]{:S(2)}) collective-permute-start(f32[3,48,8,128]{3,2,1,0:T(8,128)S(1)} %get-tuple-element.68.refs_0_.refs_2_.here.after), channel_id=1, source_target_pairs={{0,16},{16,0},{32,48},{48,32},{64,80},{80,64},{96,112},{112,96},{1... | collective-permute-start | bytes 1769480 | tf_op jit(solution)/shard_map/ppermute | solution.py:721
  70.6 12.3 %collective-permute-start.13 = (f32[2,3,2,8,128]{4,3,2,1,0:T(8,128)S(1)}, f32[2,3,2,8,128]{4,3,2,1,0:T(8,128)S(1)}, u32[]{:S(2)}, u32[]{:S(2)}) collective-permute-start(f32[2,3,2,8,128]{4,3,2,1,0:T(8,128)S(1)} %get-tuple-element.70), channel_id=1, source_target_pairs={{16,0},{17,1},{18,2},{19,3},{20,4},{21,5},{22,6},{23,7},{24,8},{25... | collective-permute-start | bytes 147464 | tf_op jit(solution)/shard_map/ppermute | solution.py:705
  106.4 10.0 %collective-permute-start.15 = (f32[3,24,8,128]{3,2,1,0:T(8,128)S(1)}, f32[3,24,8,128]{3,2,1,0:T(8,128)S(1)}, u32[]{:S(2)}, u32[]{:S(2)}) collective-permute-start(f32[3,24,8,128]{3,2,1,0:T(8,128)S(1)} %get-tuple-element.78), channel_id=1, source_target_pairs={{0,16},{16,0},{32,48},{48,32},{64,80},{80,64},{96,112},{112,96},{1... | collective-permute-start | bytes 884744 | tf_op jit(solution)/shard_map/ppermute | solution.py:726
  107.3 14.0 %collective-permute-start.14 = (f32[3,24,8,128]{3,2,1,0:T(8,128)S(1)}, f32[3,24,8,128]{3,2,1,0:T(8,128)S(1)}, u32[]{:S(2)}, u32[]{:S(2)}) collective-permute-start(f32[3,24,8,128]{3,2,1,0:T(8,128)S(1)} %get-tuple-element.77), channel_id=1, source_target_pairs={{0,16},{16,0},{32,48},{48,32},{64,80},{80,64},{96,112},{112,96},{1... | collective-permute-start | bytes 884744 | tf_op jit(solution)/shard_map/ppermute | solution.py:726

commit v3 on v2

--- a/solution.py
+++ b/solution.py
@@ -312,9 +312,9 @@
 
 def moment_kernel(counts, side_ref, *refs):
     path, refs = groups(refs, counts)
-    forces, speeds, energies, out_ref = refs[:2], refs[2:4], refs[4:6], refs[6]
+    forces, energies, speed_sq, out_ref = refs[:2], refs[2:4], refs[4:6], refs[6]
     zero = jnp.zeros((8, 128), jnp.float32)
-    sums = (zero,) * 14
+    sums = (zero,) * 12
     for region in range(REGIONS):
         held = [piece_of(pieces, region) for pieces in path]
         rows = held[0][2]
@@ -327,7 +327,6 @@
                 square = [d * d for d in diff]
                 for j in range(2):
                     force = forces[j][axis, region * rows + p]
-                    speed = speeds[j][axis, region * rows + p]
                     terms = (
                         force * force,
                         force * diff[j + 1],
@@ -335,10 +334,9 @@
                         square[j + 1],
                         square[j],
                         diff[j] * diff[j + 1],
-                        speed * speed,
                     )
                     for k, term in enumerate(terms):
-                        carry[7 * j + k] = carry[7 * j + k] + term
+                        carry[6 * j + k] = carry[6 * j + k] + term
             return tuple(carry)
 
         sums = over_planes(one, rows, 2, sums)
@@ -348,7 +346,7 @@
     sign = jnp.where(odd, -1.0, 1.0).astype(jnp.float32)
     row = jnp.zeros((1, 128), jnp.float32)
     for j in range(2):
-        ahead = [total_of(sums[7 * j + k]) for k in range(7)]
+        ahead = [total_of(sums[6 * j + k]) for k in range(6)]
         values = (
             total_of(energies[j][...]),
             ahead[0],
@@ -357,7 +355,7 @@
             jnp.where(odd, ahead[4], ahead[3]),
             jnp.where(odd, ahead[3], ahead[4]),
             ahead[5],
-            ahead[6],
+            total_of(speed_sq[j][...]),
         )
         for k, value in enumerate(values):
             row = row + jnp.where(lane == 8 * j + k, value, 0.0)
@@ -367,11 +365,12 @@
 VMEM = pl.BlockSpec(memory_space=pltpu.VMEM)
 SMEM = pl.BlockSpec(memory_space=pltpu.SMEM)
 PARAMS = pltpu.CompilerParams(vmem_limit_bytes=32 * 1024 * 1024)
-
-
-def moments(side, path, forces, speeds, energies, copies):
+TILE = jax.ShapeDtypeStruct((8, 128), jnp.float32)
+
+
+def moments(side, path, forces, energies, speed_sq, copies):
     counts = [len(pieces) for pieces in path]
-    arrays = [piece for pieces in path for piece in pieces] + [*forces, *speeds, *energies]
+    arrays = [piece for pieces in path for piece in pieces] + [*forces, *energies, *speed_sq]
     return pl.pallas_call(
         functools.partial(moment_kernel, counts),
         out_shape=jax.ShapeDtypeStruct((copies, 128), jnp.float32),
@@ -458,13 +457,15 @@
 def update_kernel(counts, images, image_ref, gathered_ref, *refs):
     path, refs = groups(refs, counts)
     forces, speeds, moved, new_speeds = refs[:2], refs[2:4], refs[4:6], refs[6:8]
-    tops, bottoms, terms = refs[8:11]
+    tops, bottoms, speed_sq, terms = refs[8], refs[9], refs[10:12], refs[12]
     step_terms(image_ref, gathered_ref, images, terms)
+    sums = (jnp.zeros((8, 128), jnp.float32),) * 2
     for region in range(REGIONS):
         held = [piece_of(pieces, region) for pieces in path]
         rows = held[0][2]
 
         def one(p, carry):
+            carry = list(carry)
             for axis in range(3):
                 at = [ref[axis, start + p] for ref, start, _ in held]
                 diff = [at[j + 1] - at[j] for j in range(3)]
@@ -473,9 +474,11 @@
                     speed = new_speed(terms, j, speeds[j][axis, q], forces[j][axis, q], diff[j + 1], diff[j])
                     new_speeds[j][axis, q] = speed
                     moved[j][axis, q] = at[j + 1] + time_step * speed
-            return carry
-
-        over_planes(one, rows, 2)
+                    carry[j] = carry[j] + speed * speed
+            return tuple(carry)
+
+        sums = over_planes(one, rows, 2, sums)
+    speed_sq[0][...], speed_sq[1][...] = sums
     planes = moved[0].shape[1]
     for j in range(2):
         tops[j] = moved[j][:, planes - HALO :]
@@ -489,14 +492,14 @@
     edge = jax.ShapeDtypeStruct((2, 3, HALO, 8, 128), jnp.float32)
     results = pl.pallas_call(
         functools.partial(update_kernel, counts, images),
-        out_shape=(out,) * 4 + (edge,) * 2,
+        out_shape=(out,) * 4 + (edge,) * 2 + (TILE,) * 2,
         in_specs=[SMEM] + [VMEM] * (1 + len(arrays)),
-        out_specs=(VMEM,) * 6,
+        out_specs=(VMEM,) * 8,
         scratch_shapes=[pltpu.VMEM((2, 4, 8, 128), jnp.float32)],
         compiler_params=PARAMS,
         name="fire_update",
     )(image, gathered, *arrays)
-    return results[:2], results[2:4], results[4], results[5]
+    return results[:2], results[2:4], results[4], results[5], results[6:]
 
 
 def last_partner_kernel(images, image_ref, gathered_ref, before, here, after, force, speed, *outs):
@@ -601,9 +604,9 @@
     )(side, here, speed, moved, speeds)
 
 
-def cut_kernel(starts, side_ref, *refs):
+def cut_kernel(starts, squares, side_ref, *refs):
     count = len(starts)
-    source, outs, sems = refs[0], refs[1 : 1 + count], refs[1 + count]
+    source, outs, sems = refs[0], refs[1 : 1 + count], refs[-1]
     copies = []
     for k, out in enumerate(outs):
         rows = source.at[:, pl.ds(at_side(starts[k], side_ref), out.shape[1])]
@@ -612,6 +615,15 @@
         copy.start()
     for copy in copies:
         copy.wait()
+    if squares:
+        total = jnp.zeros((8, 128), jnp.float32)
+        for out in outs:
+
+            def one(p, total, out=out):
+                return total + sum(out[axis, p] * out[axis, p] for axis in range(3))
+
+            total = over_planes(one, out.shape[1], 4, total)
+        refs[1 + count][...] = total
 
 
 def at_side(pair, side_ref):
@@ -619,13 +631,14 @@
     return even if even == odd else even + (odd - even) * side_ref[0]
 
 
-def cut(side, array, starts, sizes):
+def cut(side, array, starts, sizes, squares=False):
     count = len(sizes)
     return pl.pallas_call(
-        functools.partial(cut_kernel, starts),
-        out_shape=tuple(jax.ShapeDtypeStruct((3, size, 8, 128), jnp.float32) for size in sizes),
+        functools.partial(cut_kernel, starts, squares),
+        out_shape=tuple(jax.ShapeDtypeStruct((3, size, 8, 128), jnp.float32) for size in sizes)
+        + (TILE,) * squares,
         in_specs=[SMEM, pl.BlockSpec(memory_space=pltpu.HBM)],
-        out_specs=(VMEM,) * count,
+        out_specs=(VMEM,) * (count + squares),
         scratch_shapes=[pltpu.SemaphoreType.DMA((count,))],
         compiler_params=PARAMS,
         name="cut",
@@ -668,8 +681,8 @@
     halo_own = lax.ppermute(edge_own, both, outer_own)
     halo_partner = lax.ppermute(edge_partner, both, outer_partner)
     halo_inner = lax.ppermute(edge_inner, "image", across)
-    *far_pieces, halo_own, halo_partner, halo_inner = lax.optimization_barrier(
-        (*far_pieces, halo_own, halo_partner, halo_inner)
+    *far_pieces[1:], halo_own, halo_partner, halo_inner = lax.optimization_barrier(
+        (*far_pieces[1:], halo_own, halo_partner, halo_inner)
     )
     partner = [lax.ppermute(part, "image", across) for part in far_pieces]
     beyond_own = lax.ppermute(own, "image", own_out)
@@ -679,7 +692,9 @@
         half,
         ((own, None, (HALO, HALO)), (halo_own, None, outer), (near_inner, None, inner)),
     )
-    own_speed, far_speed = cut(side_arg, slab_speed, ((0, half), (half, 0)), (half, half))
+    own_speed, far_speed, slab_sq = cut(
+        side_arg, slab_speed, ((0, half), (half, 0)), (half, half), True
+    )
     far_speed, _ = lax.optimization_barrier((far_speed, own_energy))
     *partner[1:], _ = lax.optimization_barrier((*partner[1:], own_energy))
     beyond_partner = [lax.ppermute(part, "image", partner_out) for part in partner]
@@ -691,16 +706,19 @@
     ) + ((halo_partner, None, outer), (halo_inner, None, inner))
     path = (beyond_partner, [own], partner, [beyond_own])
     speeds = (own_speed, partner_speed)
+    speed_sq = (slab_sq, jnp.zeros_like(slab_sq))
     results = [(own_force, own_energy), image_forces(side_arg, half, partner_sources)]
     for step_index in range(FIRE_STEPS):
         if step_index > 0:
             results = [image_forces(side_arg, half, held) for held in sources]
+            back_home, _ = lax.optimization_barrier((back_home, results[0][1]))
+            returned = lax.ppermute(back_home, "image", across)
         forces, energies = zip(*results)
-        payload = moments(side_arg, path, forces, speeds, energies, images * slabs)
+        payload = moments(side_arg, path, forces, energies, speed_sq, images * slabs)
         gathered = lax.all_to_all(payload, both, 0, 0, tiled=True)
         if step_index == FIRE_STEPS - 1:
             break
-        moved, speeds, tops, bottoms = update(image_arg, gathered, path, forces, speeds, images)
+        moved, speeds, tops, bottoms, speed_sq = update(image_arg, gathered, path, forces, speeds, images)
         low = lax.ppermute(tops, both, upward)
         high = lax.ppermute(bottoms, both, downward)
         sources = [
@@ -717,8 +735,7 @@
             [moved[1]],
             [lax.ppermute(moved[0], "image", own_out)],
         )
-        back_home, _ = lax.optimization_barrier((moved[1], low))
-        returned = lax.ppermute(back_home, "image", across)
+        back_home = moved[1]
     whole = [pieces[0] for pieces in path]
     *last_speeds, terms = last_partner(
         image_arg, gathered, whole[1:], forces[1], speeds[1], images

time: 123 us -> 116 us (0.943)
  starting transfers between devices: 27.1 us -> 42.6 us
  waiting for transfers between devices: 41.8 us -> 27.8 us
  blocking collectives: 30.7 us -> 17.9 us
  local copies, waits for them, and re-layouts: 1.27 us -> 3.75 us
  Pallas kernels: 20.5 us -> 22.5 us
    all_to_all x2 -> x1, blocking collectives: 30.7 us -> 17.9 us  [local(): gathered = lax.all_to_all(payload, both, 0, 0, tiled=True)]
    ppermute x1, waiting for transfers between devices: 12.3 us -> 0.01 us  [local(): high = lax.ppermute(bottoms, both, downward)]
    all_to_all x0 -> x1, waiting for transfers between devices: none -> 9.29 us  [local(): gathered = lax.all_to_all(payload, both, 0, 0, tiled=True)]
    all_to_all x0 -> x1, starting transfers between devices: none -> 8.64 us  [local(): gathered = lax.all_to_all(payload, both, 0, 0, tiled=True)]
    ppermute x2, waiting for transfers between devices: 5.36 us -> 0.01 us  [local(): partner = [lax.ppermute(part, 'image', across) for part in far_pieces]]
    ppermute x1, waiting for transfers between devices: 6.82 us -> 1.77 us  [local(): low = lax.ppermute(tops, both, upward)]
    ppermute x1, starting transfers between devices: 0.01 us -> 5.05 us  [local(): high = lax.ppermute(bottoms, both, downward)]
    ppermute x1, waiting for transfers between devices: 3.9 us -> 0.01 us  [local(): partner_speed = lax.ppermute(far_speed, 'image', across)]
  transfers between devices with their start and end apart: 16 -> 17, of which waited for: 9 -> 7; matrix products, arithmetic and copies ran while one was open for 0% -> 0% of each run, Pallas kernels for 14% -> 17%
where the time goes in v3:
time: 116 us; the launch traced here: 115 us
  starting transfers between devices  42.6 us (37%)
  waiting for transfers between devices  27.8 us (24%)
  Pallas kernels  22.5 us (19%)
  blocking collectives  17.9 us (15%)
  local copies, waits for them, and re-layouts  3.75 us (3%)
    all_to_all x1, blocking collectives, local(): gathered = lax.all_to_all(payload, both, 0, 0, tiled=True)  17.9 us
    pallas_call x4, Pallas kernels, image_forces(): pl.pallas_call(functools.partial(force_kernel, starts, slots), out_shape=...  13.7 us
    ppermute x2, waiting for transfers between devices, local(): last_speeds = [lax.ppermute(part, 'image', across) for part in last_speeds]  10.3 us
    all_to_all x1, waiting for transfers between devices, local(): gathered = lax.all_to_all(payload, both, 0, 0, tiled=True)  9.29 us
    all_to_all x1, starting transfers between devices, local(): gathered = lax.all_to_all(payload, both, 0, 0, tiled=True)  8.64 us
    ppermute x1, starting transfers between devices, local(): halo_partner = lax.ppermute(edge_partner, both, outer_partner)  6.67 us
    ppermute x2, starting transfers between devices, local(): lax.ppermute(part, 'image', partner_out)  6.48 us
    ppermute x1, starting transfers between devices, local(): high = lax.ppermute(bottoms, both, downward)  5.05 us
  transfers between devices with their start and end apart: 17, of which 7 were waited for; matrix products, arithmetic and copies ran while one was open for 0% of the time, Pallas kernels for 17%

profile of v3, /device:TPU:0, one launch (start us, length us, event | category | flops | bytes accessed | tf_op | source)
XLA Modules:
  0.0 115.5 jit_solution(13146589355415316291)
XLA Ops:
  0.6 0.0 copy-start
  0.7 1.3 %copy-done = f32[1,3,98304]{2,0,1:T(1,128)S(1)} copy-done((f32[1,3,98304]{2,0,1:T(1,128)S(1)}, f32[1,3,98304]{2,0,1:T(1,128)}, u32[]{:S(2)}) %copy-start) | copy-done | bytes 1179672
  1.9 0.0 copy-start.1
  1.9 0.2 cut.2
  2.1 0.1 collective-permute-start
  2.2 6.7 %collective-permute-start.1 = (f32[3,2,8,128]{3,2,1,0:T(8,128)S(1)}, f32[3,2,8,128]{3,2,1,0:T(8,128)S(1)}, u32[]{:S(2)}, u32[]{:S(2)}) collective-permute-start(f32[3,2,8,128]{3,2,1,0:T(8,128)S(1)} %get-tuple-element.48), channel_id=1, source_target_pairs={{0,31},{1,16},{2,17},{3,18},{4,19},{5,20},{6,21},{7,22},{8,23},{9,... | collective-permute-start | bytes 73736 | tf_op jit(solution)/shard_map/ppermute | solution.py:682
  8.9 0.2 collective-permute-start.2
  9.1 1.8 %collective-permute-start.3 = (f32[3,24,8,128]{3,2,1,0:T(8,128)S(1)}, f32[3,24,8,128]{3,2,1,0:T(8,128)S(1)}, u32[]{:S(2)}, u32[]{:S(2)}) collective-permute-start(f32[3,24,8,128]{3,2,1,0:T(8,128)S(1)} %get-tuple-element.51), channel_id=1, source_target_pairs={{0,16},{16,0},{32,48},{48,32},{64,80},{80,64},{96,112},{112,96},{1... | collective-permute-start | bytes 884744 | tf_op jit(solution)/shard_map/ppermute | solution.py:687
  10.9 0.0 collective-permute-done.refs_1_
  10.9 0.0 collective-permute-done.1.refs_2_
  10.9 2.0 %collective-permute-done.2.refs_3_ = f32[3,2,8,128]{3,2,1,0:T(8,128)S(1)} collective-permute-done((f32[3,2,8,128]{3,2,1,0:T(8,128)S(1)}, f32[3,2,8,128]{3,2,1,0:T(8,128)S(1)}, u32[]{:S(2)}, u32[]{:S(2)}) %collective-permute-start.2) | collective-permute-done | bytes 24608 | tf_op jit(solution)/shard_map/ppermute | solution.py:683
  12.9 0.0 collective-permute-start.5
  12.9 1.3 %collective-permute-start.7 = (f32[3,48,8,128]{3,2,1,0:T(8,128)S(1)}, f32[3,48,8,128]{3,2,1,0:T(8,128)S(1)}, u32[]{:S(2)}, u32[]{:S(2)}) collective-permute-start(f32[3,48,8,128]{3,2,1,0:T(8,128)S(1)} %get-tuple-element.54.refs_0_.refs_2_), channel_id=1, source_target_pairs={{16,48},{32,0},{48,80},{64,32},{80,112},{96,64},{17,49},{33,1},{49... | collective-permute-start | bytes 1769480 | tf_op jit(solution)/shard_map/ppermute | solution.py:688
  14.2 0.0 copy-done.1
  14.2 1.2 %cut.3 = (f32[3,48,8,128]{3,2,1,0:T(8,128)S(1)}, f32[3,48,8,128]{3,2,1,0:T(8,128)}, f32[8,128]{1,0:T(8,128)S(1)}) custom-call(s32[1]{0:T(128)} %bitcast.side_ref, f32[3,96,8,128]{3,2,1,0:T(8,128)S(1)} %bitcast.15), custom_call_target="tpu_custom_call" | custom-call | tf_op jit(solution)/shard_map/cut/pallas_call | solution.py:636
  15.4 0.0 copy-start.2
  15.4 0.8 copy-done.2
  16.2 3.5 %slab_forces.4 = (f32[3,48,8,128]{3,2,1,0:T(8,128)S(1)}, f32[8,128]{1,0:T(8,128)S(1)}) custom-call(s32[1]{0:T(128)} %bitcast.side_ref, f32[3,48,8,128]{3,2,1,0:T(8,128)S(1)} %get-tuple-element.54.refs_0_.refs_2_, f32[3,2,8,128]{3,2,1,0:T(8,128)S(1)} %collective-permute-done.refs_1_, f32[3,2,8,128]{3,2,1,0:T(8,128)S(1)} %get-tuple-element.56.refs_2_), custom_call_target="tpu_custom_call" | custom-call | flops 20000000 | bytes 15000000 | tf_op jit(solution)/shard_map/slab_forces/pallas_call | solution.py:257
  19.7 4.2 %collective-permute-start.8 = (f32[3,48,8,128]{3,2,1,0:T(8,128)}, f32[3,48,8,128]{3,2,1,0:T(8,128)}, u32[]{:S(2)}, u32[]{:S(2)}) collective-permute-start(f32[3,48,8,128]{3,2,1,0:T(8,128)} %get-tuple-element.67), channel_id=1, source_target_pairs={{0,16},{16,0},{32,48},{48,32},{64,80},{80,64},{96,112},{112,96},{1... | collective-permute-start | bytes 1769480 | tf_op jit(solution)/shard_map/ppermute | solution.py:702
  23.9 0.0 collective-permute-done.3.refs_0_.refs_3_
  23.9 3.4 %collective-permute-start.4 = (f32[3,24,8,128]{3,2,1,0:T(8,128)S(1)}, f32[3,24,8,128]{3,2,1,0:T(8,128)S(1)}, u32[]{:S(2)}, u32[]{:S(2)}) collective-permute-start(f32[3,24,8,128]{3,2,1,0:T(8,128)S(1)} %collective-permute-done.3.refs_0_.refs_3_), channel_id=1, source_target_pairs={{48,16},{0,32},{80,48},{32,64},{112,80},{64,96},{49,17},{1,33},{81... | collective-permute-start | bytes 884744 | tf_op jit(solution)/shard_map/ppermute | solution.py:700
  27.3 0.0 collective-permute-done.5.refs_1_.refs_4_
  27.3 3.1 %collective-permute-start.6 = (f32[3,24,8,128]{3,2,1,0:T(8,128)S(1)}, f32[3,24,8,128]{3,2,1,0:T(8,128)S(1)}, u32[]{:S(2)}, u32[]{:S(2)}) collective-permute-start(f32[3,24,8,128]{3,2,1,0:T(8,128)S(1)} %collective-permute-done.5.refs_1_.refs_4_), channel_id=1, source_target_pairs={{48,16},{0,32},{80,48},{32,64},{112,80},{64,96},{49,17},{1,33},{81... | collective-permute-start | bytes 884744 | tf_op jit(solution)/shard_map/ppermute | solution.py:700
  30.4 4.3 %collective-permute-done.4.refs_0_ = f32[3,24,8,128]{3,2,1,0:T(8,128)S(1)} collective-permute-done((f32[3,24,8,128]{3,2,1,0:T(8,128)S(1)}, f32[3,24,8,128]{3,2,1,0:T(8,128)S(1)}, u32[]{:S(2)}, u32[]{:S(2)}) %collective-permute-start.4) | collective-permute-done | bytes 294944 | tf_op jit(solution)/shard_map/ppermute | solution.py:700
  34.7 3.3 %slab_forces.5 = (f32[3,48,8,128]{3,2,1,0:T(8,128)S(1)}, f32[8,128]{1,0:T(8,128)S(1)}) custom-call(s32[1]{0:T(128)} %bitcast.side_ref, f32[3,24,8,128]{3,2,1,0:T(8,128)S(1)} %collective-permute-done.3.refs_0_.refs_3_, f32[3,24,8,128]{3,2,1,0:T(8,128)S(1)} %collective-permute-done.5.refs_1_.refs_4_, f32[3,2,8,128]{3,2,1,0:T(8,128)S(1)} %collective-permute-done.1.refs_2_, ...), custom_call_target="tpu_custom_call" | custom-call | flops 20000000 | bytes 15000000 | tf_op jit(solution)/shard_map/slab_forces/pallas_call | solution.py:257
  38.0 0.0 collective-permute-done.7.refs_5_
  38.0 0.1 collective-permute-done.6.refs_1_
  38.1 0.7 path_moments.2
  38.8 0.0 copy-start.4
  38.8 0.6 copy-done.4
  39.4 8.6 %all-to-all-start = ((f32[128,1,128]{2,1,0:T(1,128)}), f32[128,1,128]{2,1,0:T(1,128)}, u32[]{:S(2)}, u32[]{:S(2)}) async-start(f32[128,1,128]{2,1,0:T(1,128)} %bitcast.16), calls=%async_computation | async-start | bytes 131072 | tf_op jit(solution)/shard_map/all_to_all | solution.py:718
  48.1 0.0 collective-permute-done.8.refs_9_
  48.1 9.3 %all-to-all-done = f32[128,1,128]{2,1,0:T(1,128)} async-done(((f32[128,1,128]{2,1,0:T(1,128)}), f32[128,1,128]{2,1,0:T(1,128)}, u32[]{:S(2)}, u32[]{:S(2)}) %all-to-all-start) | async-done | bytes 65568 | tf_op jit(solution)/shard_map/all_to_all | solution.py:718
  57.4 0.0 copy-start.3
  57.4 1.1 copy-done.3
  58.5 2.0 %fire_update.1 = (f32[3,48,8,128]{3,2,1,0:T(8,128)S(1)}, f32[3,48,8,128]{3,2,1,0:T(8,128)S(1)}, f32[3,48,8,128]{3,2,1,0:T(8,128)S(1)}, f32[3,48,8,128]{3,2,1,0:T...) custom-call(s32[1]{0:T(128)} %bitcast.1.image_ref, ...), custom_call_target="tpu_custom_call" | custom-call | tf_op jit(solution)/shard_map/fire_update/pallas_call | solution.py:493
  60.5 1.3 %collective-permute-start.13 = (f32[3,48,8,128]{3,2,1,0:T(8,128)S(1)}, f32[3,48,8,128]{3,2,1,0:T(8,128)S(1)}, u32[]{:S(2)}, u32[]{:S(2)}) collective-permute-start(f32[3,48,8,128]{3,2,1,0:T(8,128)S(1)} %get-tuple-element.69.refs_0_.refs_1_.before.here), channel_id=1, source_target_pairs={{16,48},{32,0},{48,80},{64,32},{80,112},{96,64},{17,49},{33,1},{49... | collective-permute-start | bytes 1769480 | tf_op jit(solution)/shard_map/ppermute | solution.py:736
  61.8 4.6 %collective-permute-start.12 = (f32[3,48,8,128]{3,2,1,0:T(8,128)S(1)}, f32[3,48,8,128]{3,2,1,0:T(8,128)S(1)}, u32[]{:S(2)}, u32[]{:S(2)}) collective-permute-start(f32[3,48,8,128]{3,2,1,0:T(8,128)S(1)} %get-tuple-element.73.refs_0_.refs_2_.here.after), channel_id=1, source_target_pairs={{48,16},{0,32},{80,48},{32,64},{112,80},{64,96},{49,17},{1,33},{81... | collective-permute-start | bytes 1769480 | tf_op jit(solution)/shard_map/ppermute | solution.py:733
  66.4 0.1 collective-permute-start.9
  66.5 5.1 %collective-permute-start.10 = (f32[2,3,2,8,128]{4,3,2,1,0:T(8,128)S(1)}, f32[2,3,2,8,128]{4,3,2,1,0:T(8,128)S(1)}, u32[]{:S(2)}, u32[]{:S(2)}) collective-permute-start(f32[2,3,2,8,128]{4,3,2,1,0:T(8,128)S(1)} %get-tuple-element.71), channel_id=1, source_target_pairs={{16,0},{17,1},{18,2},{19,3},{20,4},{21,5},{22,6},{23,7},{24,8},{25... | collective-permute-start | bytes 147464 | tf_op jit(solution)/shard_map/ppermute | solution.py:723
  71.5 1.8 %collective-permute-done.9.refs_1_ = f32[2,3,2,8,128]{4,3,2,1,0:T(8,128)S(1)} collective-permute-done((f32[2,3,2,8,128]{4,3,2,1,0:T(8,128)S(1)}, f32[2,3,2,8,128]{4,3,2,1,0:T(8,128)S(1)}, u32[]{:S(2)}, u32[]{:S(2)}) %collective-permute-start.9) | collective-permute-done | bytes 49184 | tf_op jit(solution)/shard_map/ppermute | solution.py:722
  73.3 0.0 collective-permute-done.10.refs_2_
  73.3 3.5 %slab_forces.6 = (f32[3,48,8,128]{3,2,1,0:T(8,128)S(1)}, f32[8,128]{1,0:T(8,128)S(1)}) custom-call(s32[1]{0:T(128)} %bitcast.side_ref, f32[3,48,8,128]{3,2,1,0:T(8,128)S(1)} %get-tuple-element.69.refs_0_.refs_1_.before.here, f32[2,3,2,8,128]{4,3,2,1,0:T(8,128)S(1)} %collective-permute-done.9.refs_1_, f32[2,3,2,8,128]{4,3,2,1,0:T(8,128)S(1)} %collective-permute-done.10.refs_2_), custom_call_target="tpu_custom_call" | custom-call | flops 20000000 | bytes 15000000 | tf_op jit(solution)/shard_map/slab_forces/pallas_call | solution.py:257
  76.8 0.1 collective-permute-start.11
  76.9 3.5 %slab_forces.7 = (f32[3,48,8,128]{3,2,1,0:T(8,128)S(1)}, f32[8,128]{1,0:T(8,128)S(1)}) custom-call(s32[1]{0:T(128)} %bitcast.side_ref, f32[3,48,8,128]{3,2,1,0:T(8,128)S(1)} %get-tuple-element.73.refs_0_.refs_2_.here.after, f32[2,3,2,8,128]{4,3,2,1,0:T(8,128)S(1)} %collective-permute-done.9.refs_1_, f32[2,3,2,8,128]{4,3,2,1,0:T(8,128)S(1)} %collective-permute-done.10.refs_2_), custom_call_target="tpu_custom_call" | custom-call | flops 20000000 | bytes 15000000 | tf_op jit(solution)/shard_map/slab_forces/pallas_call | solution.py:257
  80.3 0.0 collective-permute-done.13.refs_3_.after
  80.4 0.0 collective-permute-done.12.refs_0_.before
  80.4 0.7 path_moments.3
  81.1 17.9 %all_to_all.22 = f32[128,1,128]{2,1,0:T(1,128)S(1)} all-to-all(f32[128,1,128]{2,1,0:T(1,128)S(1)} %bitcast.17), channel_id=1, replica_groups=mesh['image'=8,'domain'=16] {'image','domain'}, dimensions={0} | all-to-all | bytes 131072 | tf_op jit(solution)/shard_map/all_to_all | solution.py:718
  99.0 0.6 last_partner.1
  99.6 0.9 collective-permute-start.15
  100.5 1.2 %collective-permute-start.14 = (f32[3,24,8,128]{3,2,1,0:T(8,128)S(1)}, f32[3,24,8,128]{3,2,1,0:T(8,128)S(1)}, u32[]{:S(2)}, u32[]{:S(2)}) collective-permute-start(f32[3,24,8,128]{3,2,1,0:T(8,128)S(1)} %get-tuple-element.80), channel_id=1, source_target_pairs={{0,16},{16,0},{32,48},{48,32},{64,80},{80,64},{96,112},{112,96},{1... | collective-permute-start | bytes 884744 | tf_op jit(solution)/shard_map/ppermute | solution.py:743
  101.7 1.6 %last_own.1 = (f32[3,96,8,128]{3,2,1,0:T(8,128)}, f32[3,96,8,128]{3,2,1,0:T(8,128)}) custom-call(s32[1]{0:T(128)} %bitcast.side_ref, f32[2,4,8,128]{3,2,1,0:T(8,128)S(1)} %get-tuple-element.82.terms, f32[3,48,8,128]{3,2,1,0:T(8,128)S(1)} %collective-permute-done.12.refs_0_.before, f32[3,48,8,128]{3,2,1,0:T(8,128)S(1)} %get-tuple-element.69.refs_0_.refs_1_.before.here, ...), custom_call_target="tpu_custom_call" | custom-call | tf_op jit(solution)/shard_map/last_own/pallas_call | solution.py:555
  103.3 0.0 collective-permute-done.11.here
  103.3 6.3 %collective-permute-done.15.speed = f32[3,24,8,128]{3,2,1,0:T(8,128)S(1)} collective-permute-done((f32[3,24,8,128]{3,2,1,0:T(8,128)S(1)}, f32[3,24,8,128]{3,2,1,0:T(8,128)S(1)}, u32[]{:S(2)}, u32[]{:S(2)}) %collective-permute-start.15) | collective-permute-done | bytes 294944 | tf_op jit(solution)/shard_map/ppermute | solution.py:743
  109.6 0.9 last_join.2
  110.6 4.0 %collective-permute-done.14.speed = f32[3,24,8,128]{3,2,1,0:T(8,128)S(1)} collective-permute-done((f32[3,24,8,128]{3,2,1,0:T(8,128)S(1)}, f32[3,24,8,128]{3,2,1,0:T(8,128)S(1)}, u32[]{:S(2)}, u32[]{:S(2)}) %collective-permute-start.14) | collective-permute-done | bytes 294944 | tf_op jit(solution)/shard_map/ppermute | solution.py:743
  114.5 0.9 last_join.3
  (1 shorter events, 0.0 us)
Async XLA Ops:
  0.6 1.3 %copy-start = (f32[1,3,98304]{2,0,1:T(1,128)S(1)}, f32[1,3,98304]{2,0,1:T(1,128)}, u32[]{:S(2)}) copy-start(f32[1,3,98304]{2,0,1:T(1,128)} %param.2) | copy-start | bytes 3538948
  1.9 12.3 %copy-start.1 = (f32[1,3,98304]{2,0,1:T(1,128)S(1)}, f32[1,3,98304]{2,0,1:T(1,128)}, u32[]{:S(2)}) copy-start(f32[1,3,98304]{2,0,1:T(1,128)} %param.3) | copy-start | bytes 3538948
  2.1 8.8 %collective-permute-start = (f32[3,2,8,128]{3,2,1,0:T(8,128)S(1)}, f32[3,2,8,128]{3,2,1,0:T(8,128)S(1)}, u32[]{:S(2)}, u32[]{:S(2)}) collective-permute-start(f32[3,2,8,128]{3,2,1,0:T(8,128)S(1)} %get-tuple-element.47), channel_id=1, source_target_pairs={{0,1},{1,2},{2,3},{3,4},{4,5},{5,6},{6,7},{7,8},{8,9},{9,10},{10,1... | collective-permute-start | bytes 73736 | tf_op jit(solution)/shard_map/ppermute | solution.py:681
  2.2 8.7 %collective-permute-start.1 = (f32[3,2,8,128]{3,2,1,0:T(8,128)S(1)}, f32[3,2,8,128]{3,2,1,0:T(8,128)S(1)}, u32[]{:S(2)}, u32[]{:S(2)}) collective-permute-start(f32[3,2,8,128]{3,2,1,0:T(8,128)S(1)} %get-tuple-element.48), channel_id=1, source_target_pairs={{0,31},{1,16},{2,17},{3,18},{4,19},{5,20},{6,21},{7,22},{8,23},{9,... | collective-permute-start | bytes 73736 | tf_op jit(solution)/shard_map/ppermute | solution.py:682
  8.9 4.0 %collective-permute-start.2 = (f32[3,2,8,128]{3,2,1,0:T(8,128)S(1)}, f32[3,2,8,128]{3,2,1,0:T(8,128)S(1)}, u32[]{:S(2)}, u32[]{:S(2)}) collective-permute-start(f32[3,2,8,128]{3,2,1,0:T(8,128)S(1)} %get-tuple-element.49), channel_id=1, source_target_pairs={{0,16},{16,0},{32,48},{48,32},{64,80},{80,64},{96,112},{112,96},{1... | collective-permute-start | bytes 73736 | tf_op jit(solution)/shard_map/ppermute | solution.py:683
  9.1 14.8 %collective-permute-start.3 = (f32[3,24,8,128]{3,2,1,0:T(8,128)S(1)}, f32[3,24,8,128]{3,2,1,0:T(8,128)S(1)}, u32[]{:S(2)}, u32[]{:S(2)}) collective-permute-start(f32[3,24,8,128]{3,2,1,0:T(8,128)S(1)} %get-tuple-element.51), channel_id=1, source_target_pairs={{0,16},{16,0},{32,48},{48,32},{64,80},{80,64},{96,112},{112,96},{1... | collective-permute-start | bytes 884744 | tf_op jit(solution)/shard_map/ppermute | solution.py:687
  12.9 14.4 %collective-permute-start.5 = (f32[3,24,8,128]{3,2,1,0:T(8,128)S(1)}, f32[3,24,8,128]{3,2,1,0:T(8,128)S(1)}, u32[]{:S(2)}, u32[]{:S(2)}) collective-permute-start(f32[3,24,8,128]{3,2,1,0:T(8,128)S(1)} %get-tuple-element.53), channel_id=1, source_target_pairs={{0,16},{16,0},{32,48},{48,32},{64,80},{80,64},{96,112},{112,96},{1... | collective-permute-start | bytes 884744 | tf_op jit(solution)/shard_map/ppermute | solution.py:687
  12.9 25.1 %collective-permute-start.7 = (f32[3,48,8,128]{3,2,1,0:T(8,128)S(1)}, f32[3,48,8,128]{3,2,1,0:T(8,128)S(1)}, u32[]{:S(2)}, u32[]{:S(2)}) collective-permute-start(f32[3,48,8,128]{3,2,1,0:T(8,128)S(1)} %get-tuple-element.54.refs_0_.refs_2_), channel_id=1, source_target_pairs={{16,48},{32,0},{48,80},{64,32},{80,112},{96,64},{17,49},{33,1},{49... | collective-permute-start | bytes 1769480 | tf_op jit(solution)/shard_map/ppermute | solution.py:688
  15.4 0.8 copy-start.2
  19.7 28.4 %collective-permute-start.8 = (f32[3,48,8,128]{3,2,1,0:T(8,128)}, f32[3,48,8,128]{3,2,1,0:T(8,128)}, u32[]{:S(2)}, u32[]{:S(2)}) collective-permute-start(f32[3,48,8,128]{3,2,1,0:T(8,128)} %get-tuple-element.67), channel_id=1, source_target_pairs={{0,16},{16,0},{32,48},{48,32},{64,80},{80,64},{96,112},{112,96},{1... | collective-permute-start | bytes 1769480 | tf_op jit(solution)/shard_map/ppermute | solution.py:702
  23.9 10.8 %collective-permute-start.4 = (f32[3,24,8,128]{3,2,1,0:T(8,128)S(1)}, f32[3,24,8,128]{3,2,1,0:T(8,128)S(1)}, u32[]{:S(2)}, u32[]{:S(2)}) collective-permute-start(f32[3,24,8,128]{3,2,1,0:T(8,128)S(1)} %collective-permute-done.3.refs_0_.refs_3_), channel_id=1, source_target_pairs={{48,16},{0,32},{80,48},{32,64},{112,80},{64,96},{49,17},{1,33},{81... | collective-permute-start | bytes 884744 | tf_op jit(solution)/shard_map/ppermute | solution.py:700
  27.3 10.8 %collective-permute-start.6 = (f32[3,24,8,128]{3,2,1,0:T(8,128)S(1)}, f32[3,24,8,128]{3,2,1,0:T(8,128)S(1)}, u32[]{:S(2)}, u32[]{:S(2)}) collective-permute-start(f32[3,24,8,128]{3,2,1,0:T(8,128)S(1)} %collective-permute-done.5.refs_1_.refs_4_), channel_id=1, source_target_pairs={{48,16},{0,32},{80,48},{32,64},{112,80},{64,96},{49,17},{1,33},{81... | collective-permute-start | bytes 884744 | tf_op jit(solution)/shard_map/ppermute | solution.py:700
  38.8 0.6 copy-start.4
  39.4 17.9 %all-to-all-start = ((f32[128,1,128]{2,1,0:T(1,128)}), f32[128,1,128]{2,1,0:T(1,128)}, u32[]{:S(2)}, u32[]{:S(2)}) async-start(f32[128,1,128]{2,1,0:T(1,128)} %bitcast.16), calls=%async_computation | async-start | bytes 131072 | tf_op jit(solution)/shard_map/all_to_all | solution.py:718
  57.4 1.1 copy-start.3
  60.5 19.9 %collective-permute-start.13 = (f32[3,48,8,128]{3,2,1,0:T(8,128)S(1)}, f32[3,48,8,128]{3,2,1,0:T(8,128)S(1)}, u32[]{:S(2)}, u32[]{:S(2)}) collective-permute-start(f32[3,48,8,128]{3,2,1,0:T(8,128)S(1)} %get-tuple-element.69.refs_0_.refs_1_.before.here), channel_id=1, source_target_pairs={{16,48},{32,0},{48,80},{64,32},{80,112},{96,64},{17,49},{33,1},{49... | collective-permute-start | bytes 1769480 | tf_op jit(solution)/shard_map/ppermute | solution.py:736
  61.8 18.6 %collective-permute-start.12 = (f32[3,48,8,128]{3,2,1,0:T(8,128)S(1)}, f32[3,48,8,128]{3,2,1,0:T(8,128)S(1)}, u32[]{:S(2)}, u32[]{:S(2)}) collective-permute-start(f32[3,48,8,128]{3,2,1,0:T(8,128)S(1)} %get-tuple-element.73.refs_0_.refs_2_.here.after), channel_id=1, source_target_pairs={{48,16},{0,32},{80,48},{32,64},{112,80},{64,96},{49,17},{1,33},{81... | collective-permute-start | bytes 1769480 | tf_op jit(solution)/shard_map/ppermute | solution.py:733
  66.4 6.9 %collective-permute-start.9 = (f32[2,3,2,8,128]{4,3,2,1,0:T(8,128)S(1)}, f32[2,3,2,8,128]{4,3,2,1,0:T(8,128)S(1)}, u32[]{:S(2)}, u32[]{:S(2)}) collective-permute-start(f32[2,3,2,8,128]{4,3,2,1,0:T(8,128)S(1)} %get-tuple-element.70), channel_id=1, source_target_pairs={{0,16},{1,17},{2,18},{3,19},{4,20},{5,21},{6,22},{7,23},{8,24},{9,... | collective-permute-start | bytes 147464 | tf_op jit(solution)/shard_map/ppermute | solution.py:722
  66.5 6.8 %collective-permute-start.10 = (f32[2,3,2,8,128]{4,3,2,1,0:T(8,128)S(1)}, f32[2,3,2,8,128]{4,3,2,1,0:T(8,128)S(1)}, u32[]{:S(2)}, u32[]{:S(2)}) collective-permute-start(f32[2,3,2,8,128]{4,3,2,1,0:T(8,128)S(1)} %get-tuple-element.71), channel_id=1, source_target_pairs={{16,0},{17,1},{18,2},{19,3},{20,4},{21,5},{22,6},{23,7},{24,8},{25... | collective-permute-start | bytes 147464 | tf_op jit(solution)/shard_map/ppermute | solution.py:723
  76.8 26.5 %collective-permute-start.11 = (f32[3,48,8,128]{3,2,1,0:T(8,128)S(1)}, f32[3,48,8,128]{3,2,1,0:T(8,128)S(1)}, u32[]{:S(2)}, u32[]{:S(2)}) collective-permute-start(f32[3,48,8,128]{3,2,1,0:T(8,128)S(1)} %get-tuple-element.73.refs_0_.refs_2_.here.after), channel_id=1, source_target_pairs={{0,16},{16,0},{32,48},{48,32},{64,80},{80,64},{96,112},{112,96},{1... | collective-permute-start | bytes 1769480 | tf_op jit(solution)/shard_map/ppermute | solution.py:715
  99.6 10.0 %collective-permute-start.15 = (f32[3,24,8,128]{3,2,1,0:T(8,128)S(1)}, f32[3,24,8,128]{3,2,1,0:T(8,128)S(1)}, u32[]{:S(2)}, u32[]{:S(2)}) collective-permute-start(f32[3,24,8,128]{3,2,1,0:T(8,128)S(1)} %get-tuple-element.81), channel_id=1, source_target_pairs={{0,16},{16,0},{32,48},{48,32},{64,80},{80,64},{96,112},{112,96},{1... | collective-permute-start | bytes 884744 | tf_op jit(solution)/shard_map/ppermute | solution.py:743
  100.5 14.0 %collective-permute-start.14 = (f32[3,24,8,128]{3,2,1,0:T(8,128)S(1)}, f32[3,24,8,128]{3,2,1,0:T(8,128)S(1)}, u32[]{:S(2)}, u32[]{:S(2)}) collective-permute-start(f32[3,24,8,128]{3,2,1,0:T(8,128)S(1)} %get-tuple-element.80), channel_id=1, source_target_pairs={{0,16},{16,0},{32,48},{48,32},{64,80},{80,64},{96,112},{112,96},{1... | collective-permute-start | bytes 884744 | tf_op jit(solution)/shard_map/ppermute | solution.py:743

commit v4 on v3

--- a/solution.py
+++ b/solution.py
@@ -272,7 +272,7 @@
             pltpu.VMEM((4, rows, 8, 128), jnp.float32),
             pltpu.VMEM((3, 3, rows, 8, 128), jnp.float32),
         ],
-        compiler_params=pltpu.CompilerParams(vmem_limit_bytes=40 * 1024 * 1024),
+        compiler_params=pltpu.CompilerParams(vmem_limit_bytes=20 * 1024 * 1024),
         cost_estimate=pl.CostEstimate(
             flops=20_000_000, bytes_accessed=15_000_000, transcendentals=0
         ),
@@ -364,7 +364,7 @@
 
 VMEM = pl.BlockSpec(memory_space=pltpu.VMEM)
 SMEM = pl.BlockSpec(memory_space=pltpu.SMEM)
-PARAMS = pltpu.CompilerParams(vmem_limit_bytes=32 * 1024 * 1024)
+PARAMS = pltpu.CompilerParams(vmem_limit_bytes=16 * 1024 * 1024)
 TILE = jax.ShapeDtypeStruct((8, 128), jnp.float32)
 
 
@@ -454,11 +454,18 @@
     return terms[j, 0] * speed + terms[j, 1] * force + terms[j, 2] * ahead + terms[j, 3] * behind
 
 
-def update_kernel(counts, images, image_ref, gathered_ref, *refs):
+def update_kernel(counts, images, image_ref, gathered_ref, slab_speed, *refs):
     path, refs = groups(refs, counts)
-    forces, speeds, moved, new_speeds = refs[:2], refs[2:4], refs[4:6], refs[6:8]
-    tops, bottoms, speed_sq, terms = refs[8], refs[9], refs[10:12], refs[12]
+    forces, partner_speed, moved, new_speeds = refs[:2], refs[2], refs[3:5], refs[5:7]
+    tops, bottoms, speed_sq, (terms, own_speed, sem) = refs[7], refs[8], refs[9:11], refs[11:]
+    speeds = (own_speed, partner_speed)
+    half = own_speed.shape[1]
+    copy = pltpu.make_async_copy(
+        slab_speed.at[:, pl.ds(image_ref[0] % 2 * half, half)], own_speed, sem
+    )
+    copy.start()
     step_terms(image_ref, gathered_ref, images, terms)
+    copy.wait()
     sums = (jnp.zeros((8, 128), jnp.float32),) * 2
     for region in range(REGIONS):
         held = [piece_of(pieces, region) for pieces in path]
@@ -485,20 +492,24 @@
         bottoms[j] = moved[j][:, :HALO]
 
 
-def update(image, gathered, path, forces, speeds, images):
+def update(image, gathered, path, forces, slab_speed, partner_speed, images):
     counts = [len(pieces) for pieces in path]
-    arrays = [piece for pieces in path for piece in pieces] + [*forces, *speeds]
+    arrays = [piece for pieces in path for piece in pieces] + [*forces, partner_speed]
     out = jax.ShapeDtypeStruct(forces[0].shape, jnp.float32)
     edge = jax.ShapeDtypeStruct((2, 3, HALO, 8, 128), jnp.float32)
     results = pl.pallas_call(
         functools.partial(update_kernel, counts, images),
         out_shape=(out,) * 4 + (edge,) * 2 + (TILE,) * 2,
-        in_specs=[SMEM] + [VMEM] * (1 + len(arrays)),
+        in_specs=[SMEM, VMEM, pl.BlockSpec(memory_space=pltpu.HBM)] + [VMEM] * len(arrays),
         out_specs=(VMEM,) * 8,
-        scratch_shapes=[pltpu.VMEM((2, 4, 8, 128), jnp.float32)],
+        scratch_shapes=[
+            pltpu.VMEM((2, 4, 8, 128), jnp.float32),
+            pltpu.VMEM(forces[0].shape, jnp.float32),
+            pltpu.SemaphoreType.DMA,
+        ],
         compiler_params=PARAMS,
         name="fire_update",
-    )(image, gathered, *arrays)
+    )(image, gathered, slab_speed, *arrays)
     return results[:2], results[2:4], results[4], results[5], results[6:]
 
 
@@ -616,14 +627,11 @@
     for copy in copies:
         copy.wait()
     if squares:
-        total = jnp.zeros((8, 128), jnp.float32)
-        for out in outs:
-
-            def one(p, total, out=out):
-                return total + sum(out[axis, p] * out[axis, p] for axis in range(3))
-
-            total = over_planes(one, out.shape[1], 4, total)
-        refs[1 + count][...] = total
+
+        def one(p, total):
+            return total + sum(source[axis, p] * source[axis, p] for axis in range(3))
+
+        refs[1 + count][...] = over_planes(one, source.shape[1], 4, jnp.zeros((8, 128), jnp.float32))
 
 
 def at_side(pair, side_ref):
@@ -637,7 +645,7 @@
         functools.partial(cut_kernel, starts, squares),
         out_shape=tuple(jax.ShapeDtypeStruct((3, size, 8, 128), jnp.float32) for size in sizes)
         + (TILE,) * squares,
-        in_specs=[SMEM, pl.BlockSpec(memory_space=pltpu.HBM)],
+        in_specs=[SMEM, VMEM if squares else pl.BlockSpec(memory_space=pltpu.HBM)],
         out_specs=(VMEM,) * (count + squares),
         scratch_shapes=[pltpu.SemaphoreType.DMA((count,))],
         compiler_params=PARAMS,
@@ -687,27 +695,29 @@
     partner = [lax.ppermute(part, "image", across) for part in far_pieces]
     beyond_own = lax.ppermute(own, "image", own_out)
     outer, inner = (0, top), (top, 0)
+    beyond_partner = [lax.ppermute(part, "image", partner_out) for part in partner]
+    partner_force, partner_energy = image_forces(
+        side_arg,
+        half,
+        tuple((part, None, (HALO + c * piece,) * 2) for c, part in enumerate(partner))
+        + ((halo_partner, None, outer), (halo_inner, None, inner)),
+    )
+    held, near_inner, beyond_partner[0], _ = lax.optimization_barrier(
+        (own, near_inner, beyond_partner[0], partner_energy)
+    )
     own_force, own_energy = image_forces(
         side_arg,
         half,
-        ((own, None, (HALO, HALO)), (halo_own, None, outer), (near_inner, None, inner)),
-    )
-    own_speed, far_speed, slab_sq = cut(
-        side_arg, slab_speed, ((0, half), (half, 0)), (half, half), True
-    )
-    far_speed, _ = lax.optimization_barrier((far_speed, own_energy))
-    *partner[1:], _ = lax.optimization_barrier((*partner[1:], own_energy))
-    beyond_partner = [lax.ppermute(part, "image", partner_out) for part in partner]
-    halo_inner, beyond_partner[0] = lax.optimization_barrier((halo_inner, beyond_partner[0]))
+        ((held, None, (HALO, HALO)), (halo_own, None, outer), (near_inner, None, inner)),
+    )
+    far_speed, slab_sq = cut(side_arg, slab_speed, ((half, 0),), (half,), True)
+    far_speed, _ = lax.optimization_barrier((far_speed, beyond_partner[0]))
     partner_speed = lax.ppermute(far_speed, "image", across)
 
-    partner_sources = tuple(
-        (part, None, (HALO + c * piece,) * 2) for c, part in enumerate(partner)
-    ) + ((halo_partner, None, outer), (halo_inner, None, inner))
     path = (beyond_partner, [own], partner, [beyond_own])
-    speeds = (own_speed, partner_speed)
+    speeds = (slab_speed, partner_speed)
     speed_sq = (slab_sq, jnp.zeros_like(slab_sq))
-    results = [(own_force, own_energy), image_forces(side_arg, half, partner_sources)]
+    results = [(own_force, own_energy), (partner_force, partner_energy)]
     for step_index in range(FIRE_STEPS):
         if step_index > 0:
             results = [image_forces(side_arg, half, held) for held in sources]
@@ -718,7 +728,9 @@
         gathered = lax.all_to_all(payload, both, 0, 0, tiled=True)
         if step_index == FIRE_STEPS - 1:
             break
-        moved, speeds, tops, bottoms, speed_sq = update(image_arg, gathered, path, forces, speeds, images)
+        moved, speeds, tops, bottoms, speed_sq = update(
+            image_arg, gathered, path, forces, *speeds, images
+        )
         low = lax.ppermute(tops, both, upward)
         high = lax.ppermute(bottoms, both, downward)
         sources = [

time: 116 us -> 111 us (0.957)
  blocking collectives: 17.9 us -> 35.7 us
  starting transfers between devices: 42.6 us -> 31.4 us
  waiting for transfers between devices: 27.8 us -> 20.9 us
  local copies, waits for them, and re-layouts: 3.75 us -> 1.36 us
  Pallas kernels: 22.5 us -> 20.7 us
    all_to_all x1 -> x2, blocking collectives: 17.9 us -> 35.7 us  [local(): gathered = lax.all_to_all(payload, both, 0, 0, tiled=True)]
    all_to_all x1 -> x0, waiting for transfers between devices: 9.29 us -> none  [local(): gathered = lax.all_to_all(payload, both, 0, 0, tiled=True)]
    all_to_all x1 -> x0, starting transfers between devices: 8.64 us -> none  [local(): gathered = lax.all_to_all(payload, both, 0, 0, tiled=True)]
    ppermute x2, waiting for transfers between devices: 0.01 us -> 2.79 us  [local(): partner = [lax.ppermute(part, 'image', across) for part in far_pieces]]
    ppermute x2, waiting for transfers between devices: 4.4 us -> 1.64 us  [local(): lax.ppermute(part, 'image', partner_out)]
    ppermute x1, starting transfers between devices: 4.24 us -> 1.82 us  [local(): partner_speed = lax.ppermute(far_speed, 'image', across)]
    unnamed x10 -> x4, local copies, waits for them, and re-layouts: 3.75 us -> 1.36 us
    ppermute x1, waiting for transfers between devices: 0.01 us -> 1.64 us  [local(): halo_own = lax.ppermute(edge_own, both, outer_own)]
  transfers between devices with their start and end apart: 17 -> 16, of which waited for: 7 -> 8; matrix products, arithmetic and copies ran while one was open for 0% -> 0% of each run, Pallas kernels for 17% -> 17%
where the time goes in v4:
time: 111 us
  blocking collectives  35.7 us (32%)
  starting transfers between devices  31.4 us (28%)
  waiting for transfers between devices  20.9 us (19%)
  Pallas kernels  20.7 us (19%)
  local copies, waits for them, and re-layouts  1.36 us (1%)
    all_to_all x2, blocking collectives, local(): gathered = lax.all_to_all(payload, both, 0, 0, tiled=True)  35.7 us
    pallas_call x4, Pallas kernels, image_forces(): pl.pallas_call(functools.partial(force_kernel, starts, slots), out_shape=...  13.7 us
    ppermute x2, waiting for transfers between devices, local(): last_speeds = [lax.ppermute(part, 'image', across) for part in last_speeds]  10.3 us
    ppermute x2, starting transfers between devices, local(): lax.ppermute(part, 'image', partner_out)  6.82 us
    ppermute x1, starting transfers between devices, local(): halo_partner = lax.ppermute(edge_partner, both, outer_partner)  5.09 us
    ppermute x1, starting transfers between devices, local(): high = lax.ppermute(bottoms, both, downward)  5.05 us
    ppermute x1, starting transfers between devices, local(): lax.ppermute(moved[1], 'image', partner_out)  4.58 us
    ppermute x2, starting transfers between devices, local(): partner = [lax.ppermute(part, 'image', across) for part in far_pieces]  2.97 us
  transfers between devices with their start and end apart: 16, of which 8 were waited for; matrix products, arithmetic and copies ran while one was open for 0% of the time, Pallas kernels for 17%

profile of v4, /device:TPU:0, one launch (start us, length us, event | category | flops | bytes accessed | tf_op | source)
XLA Modules:
  0.0 111.0 jit_solution(10307348488628188246)
XLA Ops:
  0.6 0.0 copy-start
  0.7 0.0 copy-start.1
  0.7 1.4 %copy-done.1 = f32[1,3,98304]{2,0,1:T(1,128)S(1)} copy-done((f32[1,3,98304]{2,0,1:T(1,128)S(1)}, f32[1,3,98304]{2,0,1:T(1,128)}, u32[]{:S(2)}) %copy-start.1) | copy-done | bytes 1179672
  2.0 0.2 cut.2
  2.2 2.1 %collective-permute-start = (f32[3,24,8,128]{3,2,1,0:T(8,128)S(1)}, f32[3,24,8,128]{3,2,1,0:T(8,128)S(1)}, u32[]{:S(2)}, u32[]{:S(2)}) collective-permute-start(f32[3,24,8,128]{3,2,1,0:T(8,128)S(1)} %get-tuple-element.47), channel_id=1, source_target_pairs={{0,16},{16,0},{32,48},{48,32},{64,80},{80,64},{96,112},{112,96},{1... | collective-permute-start | bytes 884744 | tf_op jit(solution)/shard_map/ppermute | solution.py:695
  4.3 0.0 collective-permute-start.2
  4.3 5.1 %collective-permute-start.3 = (f32[3,2,8,128]{3,2,1,0:T(8,128)S(1)}, f32[3,2,8,128]{3,2,1,0:T(8,128)S(1)}, u32[]{:S(2)}, u32[]{:S(2)}) collective-permute-start(f32[3,2,8,128]{3,2,1,0:T(8,128)S(1)} %get-tuple-element.50), channel_id=1, source_target_pairs={{0,31},{1,16},{2,17},{3,18},{4,19},{5,20},{6,21},{7,22},{8,23},{9,... | collective-permute-start | bytes 73736 | tf_op jit(solution)/shard_map/ppermute | solution.py:690
  9.4 0.2 collective-permute-start.4
  9.6 1.6 %collective-permute-done.2.refs_1_ = f32[3,2,8,128]{3,2,1,0:T(8,128)S(1)} collective-permute-done((f32[3,2,8,128]{3,2,1,0:T(8,128)S(1)}, f32[3,2,8,128]{3,2,1,0:T(8,128)S(1)}, u32[]{:S(2)}, u32[]{:S(2)}) %collective-permute-start.2) | collective-permute-done | bytes 24608 | tf_op jit(solution)/shard_map/ppermute | solution.py:689
  11.3 0.0 collective-permute-done.3.refs_2_
  11.3 1.9 %collective-permute-done.4.refs_3_ = f32[3,2,8,128]{3,2,1,0:T(8,128)S(1)} collective-permute-done((f32[3,2,8,128]{3,2,1,0:T(8,128)S(1)}, f32[3,2,8,128]{3,2,1,0:T(8,128)S(1)}, u32[]{:S(2)}, u32[]{:S(2)}) %collective-permute-start.4) | collective-permute-done | bytes 24608 | tf_op jit(solution)/shard_map/ppermute | solution.py:691
  13.2 0.9 collective-permute-start.5
  14.1 0.0 collective-permute-done.refs_0_.refs_3_
  14.1 3.4 %collective-permute-start.1 = (f32[3,24,8,128]{3,2,1,0:T(8,128)S(1)}, f32[3,24,8,128]{3,2,1,0:T(8,128)S(1)}, u32[]{:S(2)}, u32[]{:S(2)}) collective-permute-start(f32[3,24,8,128]{3,2,1,0:T(8,128)S(1)} %collective-permute-done.refs_0_.refs_3_), channel_id=1, source_target_pairs={{48,16},{0,32},{80,48},{32,64},{112,80},{64,96},{49,17},{1,33},{81... | collective-permute-start | bytes 884744 | tf_op jit(solution)/shard_map/ppermute | solution.py:698
  17.5 1.3 %collective-permute-start.7 = (f32[3,48,8,128]{3,2,1,0:T(8,128)S(1)}, f32[3,48,8,128]{3,2,1,0:T(8,128)S(1)}, u32[]{:S(2)}, u32[]{:S(2)}) collective-permute-start(f32[3,48,8,128]{3,2,1,0:T(8,128)S(1)} %get-tuple-element.57.refs_0_.refs_2_), channel_id=1, source_target_pairs={{16,48},{32,0},{48,80},{64,32},{80,112},{96,64},{17,49},{33,1},{49... | collective-permute-start | bytes 1769480 | tf_op jit(solution)/shard_map/ppermute | solution.py:696
  18.8 0.0 copy-done
  18.8 0.3 cut.3
  19.1 2.8 %collective-permute-done.5.refs_1_.refs_4_ = f32[3,24,8,128]{3,2,1,0:T(8,128)S(1)} collective-permute-done((f32[3,24,8,128]{3,2,1,0:T(8,128)S(1)}, f32[3,24,8,128]{3,2,1,0:T(8,128)S(1)}, u32[]{:S(2)}, u32[]{:S(2)}) %collective-permute-start.5) | collective-permute-done | bytes 294944 | tf_op jit(solution)/shard_map/ppermute | solution.py:695
  21.9 3.3 %slab_forces.4 = (f32[3,48,8,128]{3,2,1,0:T(8,128)S(1)}, f32[8,128]{1,0:T(8,128)S(1)}) custom-call(s32[1]{0:T(128)} %bitcast.side_ref, f32[3,24,8,128]{3,2,1,0:T(8,128)S(1)} %collective-permute-done.refs_0_.refs_3_, f32[3,24,8,128]{3,2,1,0:T(8,128)S(1)} %collective-permute-done.5.refs_1_.refs_4_, f32[3,2,8,128]{3,2,1,0:T(8,128)S(1)} %collective-permute-done.3.refs_2_, ...), custom_call_target="tpu_custom_call" | custom-call | flops 20000000 | bytes 15000000 | tf_op jit(solution)/shard_map/slab_forces/pallas_call | solution.py:257
  25.2 0.0 collective-permute-done.1.refs_0_
  25.2 1.8 %collective-permute-start.8 = (f32[3,48,8,128]{3,2,1,0:T(8,128)S(1)}, f32[3,48,8,128]{3,2,1,0:T(8,128)S(1)}, u32[]{:S(2)}, u32[]{:S(2)}) collective-permute-start(f32[3,48,8,128]{3,2,1,0:T(8,128)S(1)} %get-tuple-element.65), channel_id=1, source_target_pairs={{0,16},{16,0},{32,48},{48,32},{64,80},{80,64},{96,112},{112,96},{1... | collective-permute-start | bytes 1769480 | tf_op jit(solution)/shard_map/ppermute | solution.py:715
  27.0 3.4 %collective-permute-start.6 = (f32[3,24,8,128]{3,2,1,0:T(8,128)S(1)}, f32[3,24,8,128]{3,2,1,0:T(8,128)S(1)}, u32[]{:S(2)}, u32[]{:S(2)}) collective-permute-start(f32[3,24,8,128]{3,2,1,0:T(8,128)S(1)} %collective-permute-done.5.refs_1_.refs_4_), channel_id=1, source_target_pairs={{48,16},{0,32},{80,48},{32,64},{112,80},{64,96},{49,17},{1,33},{81... | collective-permute-start | bytes 884744 | tf_op jit(solution)/shard_map/ppermute | solution.py:698
  30.5 3.5 %slab_forces.5 = (f32[3,48,8,128]{3,2,1,0:T(8,128)S(1)}, f32[8,128]{1,0:T(8,128)S(1)}) custom-call(s32[1]{0:T(128)} %bitcast.side_ref, f32[3,48,8,128]{3,2,1,0:T(8,128)S(1)} %get-tuple-element.57.refs_0_.refs_2_, f32[3,2,8,128]{3,2,1,0:T(8,128)S(1)} %collective-permute-done.2.refs_1_, f32[3,2,8,128]{3,2,1,0:T(8,128)S(1)} %get-tuple-element.59.refs_2_), custom_call_target="tpu_custom_call" | custom-call | flops 20000000 | bytes 15000000 | tf_op jit(solution)/shard_map/slab_forces/pallas_call | solution.py:257
  33.9 0.8 collective-permute-done.7.refs_5_
  34.7 1.6 %collective-permute-done.6.refs_1_ = f32[3,24,8,128]{3,2,1,0:T(8,128)S(1)} collective-permute-done((f32[3,24,8,128]{3,2,1,0:T(8,128)S(1)}, f32[3,24,8,128]{3,2,1,0:T(8,128)S(1)}, u32[]{:S(2)}, u32[]{:S(2)}) %collective-permute-start.6) | collective-permute-done | bytes 294944 | tf_op jit(solution)/shard_map/ppermute | solution.py:698
  36.4 0.7 path_moments.2
  37.1 18.0 %all_to_all.22 = f32[128,1,128]{2,1,0:T(1,128)S(1)} all-to-all(f32[128,1,128]{2,1,0:T(1,128)S(1)} %bitcast.18), channel_id=1, replica_groups=mesh['image'=8,'domain'=16] {'image','domain'}, dimensions={0} | all-to-all | bytes 131072 | tf_op jit(solution)/shard_map/all_to_all | solution.py:728
  55.1 0.0 collective-permute-done.8.refs_8_
  55.1 1.0 fire_update.1
  56.1 1.3 %collective-permute-start.13 = (f32[3,48,8,128]{3,2,1,0:T(8,128)S(1)}, f32[3,48,8,128]{3,2,1,0:T(8,128)S(1)}, u32[]{:S(2)}, u32[]{:S(2)}) collective-permute-start(f32[3,48,8,128]{3,2,1,0:T(8,128)S(1)} %get-tuple-element.67.refs_0_.refs_1_.before.here), channel_id=1, source_target_pairs={{16,48},{32,0},{48,80},{64,32},{80,112},{96,64},{17,49},{33,1},{49... | collective-permute-start | bytes 1769480 | tf_op jit(solution)/shard_map/ppermute | solution.py:748
  57.4 4.6 %collective-permute-start.12 = (f32[3,48,8,128]{3,2,1,0:T(8,128)S(1)}, f32[3,48,8,128]{3,2,1,0:T(8,128)S(1)}, u32[]{:S(2)}, u32[]{:S(2)}) collective-permute-start(f32[3,48,8,128]{3,2,1,0:T(8,128)S(1)} %get-tuple-element.71.refs_0_.refs_2_.here.after), channel_id=1, source_target_pairs={{48,16},{0,32},{80,48},{32,64},{112,80},{64,96},{49,17},{1,33},{81... | collective-permute-start | bytes 1769480 | tf_op jit(solution)/shard_map/ppermute | solution.py:745
  62.0 0.1 collective-permute-start.9
  62.1 5.1 %collective-permute-start.10 = (f32[2,3,2,8,128]{4,3,2,1,0:T(8,128)S(1)}, f32[2,3,2,8,128]{4,3,2,1,0:T(8,128)S(1)}, u32[]{:S(2)}, u32[]{:S(2)}) collective-permute-start(f32[2,3,2,8,128]{4,3,2,1,0:T(8,128)S(1)} %get-tuple-element.69), channel_id=1, source_target_pairs={{16,0},{17,1},{18,2},{19,3},{20,4},{21,5},{22,6},{23,7},{24,8},{25... | collective-permute-start | bytes 147464 | tf_op jit(solution)/shard_map/ppermute | solution.py:735
  67.1 1.8 %collective-permute-done.9.refs_1_ = f32[2,3,2,8,128]{4,3,2,1,0:T(8,128)S(1)} collective-permute-done((f32[2,3,2,8,128]{4,3,2,1,0:T(8,128)S(1)}, f32[2,3,2,8,128]{4,3,2,1,0:T(8,128)S(1)}, u32[]{:S(2)}, u32[]{:S(2)}) %collective-permute-start.9) | collective-permute-done | bytes 49184 | tf_op jit(solution)/shard_map/ppermute | solution.py:734
  68.9 0.0 collective-permute-done.10.refs_2_
  68.9 3.5 %slab_forces.6 = (f32[3,48,8,128]{3,2,1,0:T(8,128)S(1)}, f32[8,128]{1,0:T(8,128)S(1)}) custom-call(s32[1]{0:T(128)} %bitcast.side_ref, f32[3,48,8,128]{3,2,1,0:T(8,128)S(1)} %get-tuple-element.67.refs_0_.refs_1_.before.here, f32[2,3,2,8,128]{4,3,2,1,0:T(8,128)S(1)} %collective-permute-done.9.refs_1_, f32[2,3,2,8,128]{4,3,2,1,0:T(8,128)S(1)} %collective-permute-done.10.refs_2_), custom_call_target="tpu_custom_call" | custom-call | flops 20000000 | bytes 15000000 | tf_op jit(solution)/shard_map/slab_forces/pallas_call | solution.py:257
  72.4 0.1 collective-permute-start.11
  72.5 3.5 %slab_forces.7 = (f32[3,48,8,128]{3,2,1,0:T(8,128)S(1)}, f32[8,128]{1,0:T(8,128)S(1)}) custom-call(s32[1]{0:T(128)} %bitcast.side_ref, f32[3,48,8,128]{3,2,1,0:T(8,128)S(1)} %get-tuple-element.71.refs_0_.refs_2_.here.after, f32[2,3,2,8,128]{4,3,2,1,0:T(8,128)S(1)} %collective-permute-done.9.refs_1_, f32[2,3,2,8,128]{4,3,2,1,0:T(8,128)S(1)} %collective-permute-done.10.refs_2_), custom_call_target="tpu_custom_call" | custom-call | flops 20000000 | bytes 15000000 | tf_op jit(solution)/shard_map/slab_forces/pallas_call | solution.py:257
  76.0 0.0 collective-permute-done.13.refs_3_.after
  76.0 0.0 collective-permute-done.12.refs_0_.before
  76.0 0.7 path_moments.3
  76.7 17.8 %all_to_all.23 = f32[128,1,128]{2,1,0:T(1,128)S(1)} all-to-all(f32[128,1,128]{2,1,0:T(1,128)S(1)} %bitcast.19), channel_id=1, replica_groups=mesh['image'=8,'domain'=16] {'image','domain'}, dimensions={0} | all-to-all | bytes 131072 | tf_op jit(solution)/shard_map/all_to_all | solution.py:728
  94.5 0.6 last_partner.1
  95.1 0.9 collective-permute-start.15
  96.0 1.2 %collective-permute-start.14 = (f32[3,24,8,128]{3,2,1,0:T(8,128)S(1)}, f32[3,24,8,128]{3,2,1,0:T(8,128)S(1)}, u32[]{:S(2)}, u32[]{:S(2)}) collective-permute-start(f32[3,24,8,128]{3,2,1,0:T(8,128)S(1)} %get-tuple-element.78), channel_id=1, source_target_pairs={{0,16},{16,0},{32,48},{48,32},{64,80},{80,64},{96,112},{112,96},{1... | collective-permute-start | bytes 884744 | tf_op jit(solution)/shard_map/ppermute | solution.py:755
  97.2 1.6 %last_own.1 = (f32[3,96,8,128]{3,2,1,0:T(8,128)}, f32[3,96,8,128]{3,2,1,0:T(8,128)}) custom-call(s32[1]{0:T(128)} %bitcast.side_ref, f32[2,4,8,128]{3,2,1,0:T(8,128)S(1)} %get-tuple-element.80.terms, f32[3,48,8,128]{3,2,1,0:T(8,128)S(1)} %collective-permute-done.12.refs_0_.before, f32[3,48,8,128]{3,2,1,0:T(8,128)S(1)} %get-tuple-element.67.refs_0_.refs_1_.before.here, ...), custom_call_target="tpu_custom_call" | custom-call | tf_op jit(solution)/shard_map/last_own/pallas_call | solution.py:566
  98.8 0.0 collective-permute-done.11.here
  98.8 6.3 %collective-permute-done.15.speed = f32[3,24,8,128]{3,2,1,0:T(8,128)S(1)} collective-permute-done((f32[3,24,8,128]{3,2,1,0:T(8,128)S(1)}, f32[3,24,8,128]{3,2,1,0:T(8,128)S(1)}, u32[]{:S(2)}, u32[]{:S(2)}) %collective-permute-start.15) | collective-permute-done | bytes 294944 | tf_op jit(solution)/shard_map/ppermute | solution.py:755
  105.1 0.9 last_join.2
  106.0 4.0 %collective-permute-done.14.speed = f32[3,24,8,128]{3,2,1,0:T(8,128)S(1)} collective-permute-done((f32[3,24,8,128]{3,2,1,0:T(8,128)S(1)}, f32[3,24,8,128]{3,2,1,0:T(8,128)S(1)}, u32[]{:S(2)}, u32[]{:S(2)}) %collective-permute-start.14) | collective-permute-done | bytes 294944 | tf_op jit(solution)/shard_map/ppermute | solution.py:755
  110.0 0.9 last_join.3
  (1 shorter events, 0.0 us)
Async XLA Ops:
  0.6 18.2 %copy-start = (f32[1,3,98304]{2,0,1:T(1,128)S(1)}, f32[1,3,98304]{2,0,1:T(1,128)}, u32[]{:S(2)}) copy-start(f32[1,3,98304]{2,0,1:T(1,128)} %param.3) | copy-start | bytes 3538948
  0.7 1.4 %copy-start.1 = (f32[1,3,98304]{2,0,1:T(1,128)S(1)}, f32[1,3,98304]{2,0,1:T(1,128)}, u32[]{:S(2)}) copy-start(f32[1,3,98304]{2,0,1:T(1,128)} %param.2) | copy-start | bytes 3538948
  2.2 11.9 %collective-permute-start = (f32[3,24,8,128]{3,2,1,0:T(8,128)S(1)}, f32[3,24,8,128]{3,2,1,0:T(8,128)S(1)}, u32[]{:S(2)}, u32[]{:S(2)}) collective-permute-start(f32[3,24,8,128]{3,2,1,0:T(8,128)S(1)} %get-tuple-element.47), channel_id=1, source_target_pairs={{0,16},{16,0},{32,48},{48,32},{64,80},{80,64},{96,112},{112,96},{1... | collective-permute-start | bytes 884744 | tf_op jit(solution)/shard_map/ppermute | solution.py:695
  4.3 7.0 %collective-permute-start.2 = (f32[3,2,8,128]{3,2,1,0:T(8,128)S(1)}, f32[3,2,8,128]{3,2,1,0:T(8,128)S(1)}, u32[]{:S(2)}, u32[]{:S(2)}) collective-permute-start(f32[3,2,8,128]{3,2,1,0:T(8,128)S(1)} %get-tuple-element.49), channel_id=1, source_target_pairs={{0,1},{1,2},{2,3},{3,4},{4,5},{5,6},{6,7},{7,8},{8,9},{9,10},{10,1... | collective-permute-start | bytes 73736 | tf_op jit(solution)/shard_map/ppermute | solution.py:689
  4.3 7.0 %collective-permute-start.3 = (f32[3,2,8,128]{3,2,1,0:T(8,128)S(1)}, f32[3,2,8,128]{3,2,1,0:T(8,128)S(1)}, u32[]{:S(2)}, u32[]{:S(2)}) collective-permute-start(f32[3,2,8,128]{3,2,1,0:T(8,128)S(1)} %get-tuple-element.50), channel_id=1, source_target_pairs={{0,31},{1,16},{2,17},{3,18},{4,19},{5,20},{6,21},{7,22},{8,23},{9,... | collective-permute-start | bytes 73736 | tf_op jit(solution)/shard_map/ppermute | solution.py:690
  9.4 3.8 %collective-permute-start.4 = (f32[3,2,8,128]{3,2,1,0:T(8,128)S(1)}, f32[3,2,8,128]{3,2,1,0:T(8,128)S(1)}, u32[]{:S(2)}, u32[]{:S(2)}) collective-permute-start(f32[3,2,8,128]{3,2,1,0:T(8,128)S(1)} %get-tuple-element.51), channel_id=1, source_target_pairs={{0,16},{16,0},{32,48},{48,32},{64,80},{80,64},{96,112},{112,96},{1... | collective-permute-start | bytes 73736 | tf_op jit(solution)/shard_map/ppermute | solution.py:691
  13.2 8.7 %collective-permute-start.5 = (f32[3,24,8,128]{3,2,1,0:T(8,128)S(1)}, f32[3,24,8,128]{3,2,1,0:T(8,128)S(1)}, u32[]{:S(2)}, u32[]{:S(2)}) collective-permute-start(f32[3,24,8,128]{3,2,1,0:T(8,128)S(1)} %get-tuple-element.52), channel_id=1, source_target_pairs={{0,16},{16,0},{32,48},{48,32},{64,80},{80,64},{96,112},{112,96},{1... | collective-permute-start | bytes 884744 | tf_op jit(solution)/shard_map/ppermute | solution.py:695
  14.1 11.1 %collective-permute-start.1 = (f32[3,24,8,128]{3,2,1,0:T(8,128)S(1)}, f32[3,24,8,128]{3,2,1,0:T(8,128)S(1)}, u32[]{:S(2)}, u32[]{:S(2)}) collective-permute-start(f32[3,24,8,128]{3,2,1,0:T(8,128)S(1)} %collective-permute-done.refs_0_.refs_3_), channel_id=1, source_target_pairs={{48,16},{0,32},{80,48},{32,64},{112,80},{64,96},{49,17},{1,33},{81... | collective-permute-start | bytes 884744 | tf_op jit(solution)/shard_map/ppermute | solution.py:698
  17.5 17.2 %collective-permute-start.7 = (f32[3,48,8,128]{3,2,1,0:T(8,128)S(1)}, f32[3,48,8,128]{3,2,1,0:T(8,128)S(1)}, u32[]{:S(2)}, u32[]{:S(2)}) collective-permute-start(f32[3,48,8,128]{3,2,1,0:T(8,128)S(1)} %get-tuple-element.57.refs_0_.refs_2_), channel_id=1, source_target_pairs={{16,48},{32,0},{48,80},{64,32},{80,112},{96,64},{17,49},{33,1},{49... | collective-permute-start | bytes 1769480 | tf_op jit(solution)/shard_map/ppermute | solution.py:696
  25.2 29.8 %collective-permute-start.8 = (f32[3,48,8,128]{3,2,1,0:T(8,128)S(1)}, f32[3,48,8,128]{3,2,1,0:T(8,128)S(1)}, u32[]{:S(2)}, u32[]{:S(2)}) collective-permute-start(f32[3,48,8,128]{3,2,1,0:T(8,128)S(1)} %get-tuple-element.65), channel_id=1, source_target_pairs={{0,16},{16,0},{32,48},{48,32},{64,80},{80,64},{96,112},{112,96},{1... | collective-permute-start | bytes 1769480 | tf_op jit(solution)/shard_map/ppermute | solution.py:715
  27.0 9.3 %collective-permute-start.6 = (f32[3,24,8,128]{3,2,1,0:T(8,128)S(1)}, f32[3,24,8,128]{3,2,1,0:T(8,128)S(1)}, u32[]{:S(2)}, u32[]{:S(2)}) collective-permute-start(f32[3,24,8,128]{3,2,1,0:T(8,128)S(1)} %collective-permute-done.5.refs_1_.refs_4_), channel_id=1, source_target_pairs={{48,16},{0,32},{80,48},{32,64},{112,80},{64,96},{49,17},{1,33},{81... | collective-permute-start | bytes 884744 | tf_op jit(solution)/shard_map/ppermute | solution.py:698
  56.1 19.9 %collective-permute-start.13 = (f32[3,48,8,128]{3,2,1,0:T(8,128)S(1)}, f32[3,48,8,128]{3,2,1,0:T(8,128)S(1)}, u32[]{:S(2)}, u32[]{:S(2)}) collective-permute-start(f32[3,48,8,128]{3,2,1,0:T(8,128)S(1)} %get-tuple-element.67.refs_0_.refs_1_.before.here), channel_id=1, source_target_pairs={{16,48},{32,0},{48,80},{64,32},{80,112},{96,64},{17,49},{33,1},{49... | collective-permute-start | bytes 1769480 | tf_op jit(solution)/shard_map/ppermute | solution.py:748
  57.4 18.6 %collective-permute-start.12 = (f32[3,48,8,128]{3,2,1,0:T(8,128)S(1)}, f32[3,48,8,128]{3,2,1,0:T(8,128)S(1)}, u32[]{:S(2)}, u32[]{:S(2)}) collective-permute-start(f32[3,48,8,128]{3,2,1,0:T(8,128)S(1)} %get-tuple-element.71.refs_0_.refs_2_.here.after), channel_id=1, source_target_pairs={{48,16},{0,32},{80,48},{32,64},{112,80},{64,96},{49,17},{1,33},{81... | collective-permute-start | bytes 1769480 | tf_op jit(solution)/shard_map/ppermute | solution.py:745
  62.0 6.9 %collective-permute-start.9 = (f32[2,3,2,8,128]{4,3,2,1,0:T(8,128)S(1)}, f32[2,3,2,8,128]{4,3,2,1,0:T(8,128)S(1)}, u32[]{:S(2)}, u32[]{:S(2)}) collective-permute-start(f32[2,3,2,8,128]{4,3,2,1,0:T(8,128)S(1)} %get-tuple-element.68), channel_id=1, source_target_pairs={{0,16},{1,17},{2,18},{3,19},{4,20},{5,21},{6,22},{7,23},{8,24},{9,... | collective-permute-start | bytes 147464 | tf_op jit(solution)/shard_map/ppermute | solution.py:734
  62.1 6.8 %collective-permute-start.10 = (f32[2,3,2,8,128]{4,3,2,1,0:T(8,128)S(1)}, f32[2,3,2,8,128]{4,3,2,1,0:T(8,128)S(1)}, u32[]{:S(2)}, u32[]{:S(2)}) collective-permute-start(f32[2,3,2,8,128]{4,3,2,1,0:T(8,128)S(1)} %get-tuple-element.69), channel_id=1, source_target_pairs={{16,0},{17,1},{18,2},{19,3},{20,4},{21,5},{22,6},{23,7},{24,8},{25... | collective-permute-start | bytes 147464 | tf_op jit(solution)/shard_map/ppermute | solution.py:735
  72.4 26.4 %collective-permute-start.11 = (f32[3,48,8,128]{3,2,1,0:T(8,128)S(1)}, f32[3,48,8,128]{3,2,1,0:T(8,128)S(1)}, u32[]{:S(2)}, u32[]{:S(2)}) collective-permute-start(f32[3,48,8,128]{3,2,1,0:T(8,128)S(1)} %get-tuple-element.71.refs_0_.refs_2_.here.after), channel_id=1, source_target_pairs={{0,16},{16,0},{32,48},{48,32},{64,80},{80,64},{96,112},{112,96},{1... | collective-permute-start | bytes 1769480 | tf_op jit(solution)/shard_map/ppermute | solution.py:725
  95.1 10.0 %collective-permute-start.15 = (f32[3,24,8,128]{3,2,1,0:T(8,128)S(1)}, f32[3,24,8,128]{3,2,1,0:T(8,128)S(1)}, u32[]{:S(2)}, u32[]{:S(2)}) collective-permute-start(f32[3,24,8,128]{3,2,1,0:T(8,128)S(1)} %get-tuple-element.79), channel_id=1, source_target_pairs={{0,16},{16,0},{32,48},{48,32},{64,80},{80,64},{96,112},{112,96},{1... | collective-permute-start | bytes 884744 | tf_op jit(solution)/shard_map/ppermute | solution.py:755
  96.0 14.0 %collective-permute-start.14 = (f32[3,24,8,128]{3,2,1,0:T(8,128)S(1)}, f32[3,24,8,128]{3,2,1,0:T(8,128)S(1)}, u32[]{:S(2)}, u32[]{:S(2)}) collective-permute-start(f32[3,24,8,128]{3,2,1,0:T(8,128)S(1)} %get-tuple-element.78), channel_id=1, source_target_pairs={{0,16},{16,0},{32,48},{48,32},{64,80},{80,64},{96,112},{112,96},{1... | collective-permute-start | bytes 884744 | tf_op jit(solution)/shard_map/ppermute | solution.py:755

commit v5 on v4

--- a/solution.py
+++ b/solution.py
@@ -12,10 +12,10 @@
 FIRE_STEPS = 2
 QUANTITIES = 8
 HALO = 2
-PLACE_UNROLL = 16
 EMBED_UNROLL = 48
 FINISH_UNROLL = 16
 REGIONS = 2
+PIECES = (16, 32)
 JOIN_STEPS = 2
 
 lattice_const = 3.615
@@ -86,10 +86,21 @@
     return 1 if plane % 2 == 0 else -1
 
 
-def force_kernel(starts, slots, side_ref, *refs):
-    count = len(starts)
-    sources = [ref if slot is None else ref.at[slot] for ref, slot in zip(refs, slots)]
-    force_ref, energy_ref, pos, turned, seps, slopes, rho, back, embed, force_back = refs[count:]
+def force_kernel(layouts, side_ref, *refs):
+    count = sum(len(layout) for layout in layouts)
+    images = len(layouts)
+    arrays, outs, scratch = refs[:count], refs[count : count + 2 * images], refs[count + 2 * images :]
+    at = 0
+    for j, layout in enumerate(layouts):
+        sources = [
+            (ref if slot is None else ref.at[slot], row, size, at_side(start, side_ref))
+            for ref, (slot, row, size, start) in zip(arrays[at:], layout)
+        ]
+        at += len(layout)
+        slab_forces(sources, outs[2 * j], outs[2 * j + 1], *scratch)
+
+
+def slab_forces(sources, force_ref, energy_ref, pos, turned, seps, slopes, rho, back, embed, force_back):
     f32 = jnp.float32
     planes = force_ref.shape[1]
     lanes = lax.broadcasted_iota(jnp.int32, (8, 128), 1)
@@ -106,17 +117,16 @@
             for k, seen in enumerate(partners(value, side, lanes)):
                 turned[axis, k, q] = seen
 
-    for k, source in enumerate(sources):
-        rows = source.shape[1]
-        unroll = rows if rows <= 24 else PLACE_UNROLL
-
-        def place_some(t, carry, source=source, start=at_side(starts[k], side_ref), unroll=unroll):
+    for source, row, size, start in sources:
+        unroll = max(n for n in range(2, 25, 2) if size % n == 0)
+
+        def place_some(t, carry, source=source, row=row, start=start, unroll=unroll):
             for j in range(unroll):
                 p = t * unroll + j
-                place(start + p, side_of(j), [source[axis, p] for axis in range(3)])
+                place(start + p, side_of(j), [source[axis, row + p] for axis in range(3)])
             return carry
 
-        lax.fori_loop(0, rows // unroll, place_some, 0)
+        lax.fori_loop(0, size // unroll, place_some, 0)
 
     def separations(e, step):
         h = f32(unit_half)
@@ -250,18 +260,20 @@
     lax.fori_loop(0, planes // FINISH_UNROLL, finish, 0)
 
 
-def image_forces(side, planes, sources):
-    arrays, slots, starts = zip(*sources)
+def image_forces(side, planes, images):
     vmem = pl.BlockSpec(memory_space=pltpu.VMEM)
     rows = planes + 2 * HALO
-    return pl.pallas_call(
-        functools.partial(force_kernel, starts, slots),
+    arrays = [source[0] for sources in images for source in sources]
+    layouts = [[source[1:] for source in sources] for sources in images]
+    results = pl.pallas_call(
+        functools.partial(force_kernel, layouts),
         out_shape=(
             jax.ShapeDtypeStruct((3, planes, 8, 128), jnp.float32),
             jax.ShapeDtypeStruct((8, 128), jnp.float32),
-        ),
+        )
+        * len(images),
         in_specs=[pl.BlockSpec(memory_space=pltpu.SMEM)] + [vmem] * len(arrays),
-        out_specs=(vmem, vmem),
+        out_specs=(vmem,) * (2 * len(images)),
         scratch_shapes=[
             pltpu.VMEM((3, rows, 8, 128), jnp.float32),
             pltpu.VMEM((3, 3, rows, 8, 128), jnp.float32),
@@ -274,23 +286,22 @@
         ],
         compiler_params=pltpu.CompilerParams(vmem_limit_bytes=20 * 1024 * 1024),
         cost_estimate=pl.CostEstimate(
-            flops=20_000_000, bytes_accessed=15_000_000, transcendentals=0
+            flops=40_000_000, bytes_accessed=30_000_000, transcendentals=0
         ),
         name="slab_forces",
     )(side, *arrays)
+    return results[::2], results[1::2]
 
 
 def total_of(tile):
     return jnp.sum(jnp.sum(tile, axis=0, keepdims=True), axis=1, keepdims=True)
 
 
-def piece_of(pieces, region):
-    rows = sum(piece.shape[1] for piece in pieces) // REGIONS
-    at = region * rows
-    for piece in pieces:
-        if at < piece.shape[1]:
-            return piece, at, rows
-        at -= piece.shape[1]
+def regions_of(path):
+    at = 0
+    for k, rows in enumerate(PIECES):
+        yield at, rows, [(pieces[k], 0) if len(pieces) > 1 else (pieces[0], at) for pieces in path]
+        at += rows
 
 
 def over_planes(body, rows, unroll, carry=0):
@@ -315,18 +326,16 @@
     forces, energies, speed_sq, out_ref = refs[:2], refs[2:4], refs[4:6], refs[6]
     zero = jnp.zeros((8, 128), jnp.float32)
     sums = (zero,) * 12
-    for region in range(REGIONS):
-        held = [piece_of(pieces, region) for pieces in path]
-        rows = held[0][2]
+    for first, rows, held in regions_of(path):
 
         def one(p, carry):
             carry = list(carry)
             for axis in range(3):
-                at = [ref[axis, start + p] for ref, start, _ in held]
+                at = [ref[axis, start + p] for ref, start in held]
                 diff = [at[j + 1] - at[j] for j in range(3)]
                 square = [d * d for d in diff]
                 for j in range(2):
-                    force = forces[j][axis, region * rows + p]
+                    force = forces[j][axis, first + p]
                     terms = (
                         force * force,
                         force * diff[j + 1],
@@ -467,17 +476,15 @@
     step_terms(image_ref, gathered_ref, images, terms)
     copy.wait()
     sums = (jnp.zeros((8, 128), jnp.float32),) * 2
-    for region in range(REGIONS):
-        held = [piece_of(pieces, region) for pieces in path]
-        rows = held[0][2]
+    for first, rows, held in regions_of(path):
 
         def one(p, carry):
             carry = list(carry)
             for axis in range(3):
-                at = [ref[axis, start + p] for ref, start, _ in held]
+                at = [ref[axis, start + p] for ref, start in held]
                 diff = [at[j + 1] - at[j] for j in range(3)]
                 for j in range(2):
-                    q = region * rows + p
+                    q = first + p
                     speed = new_speed(terms, j, speeds[j][axis, q], forces[j][axis, q], diff[j + 1], diff[j])
                     new_speeds[j][axis, q] = speed
                     moved[j][axis, q] = at[j + 1] + time_step * speed
@@ -615,13 +622,18 @@
     )(side, here, speed, moved, speeds)
 
 
-def cut_kernel(starts, squares, side_ref, *refs):
-    count = len(starts)
+def cut_kernel(blocks, squares, side_ref, *refs):
+    count = len(blocks)
     source, outs, sems = refs[0], refs[1 : 1 + count], refs[-1]
     copies = []
     for k, out in enumerate(outs):
-        rows = source.at[:, pl.ds(at_side(starts[k], side_ref), out.shape[1])]
-        copies.append(pltpu.make_async_copy(rows, out, sems.at[k]))
+        at = 0
+        for start, size in blocks[k]:
+            rows = source.at[:, pl.ds(at_side(start, side_ref), size)]
+            copies.append(
+                pltpu.make_async_copy(rows, out.at[:, pl.ds(at, size)], sems.at[len(copies)])
+            )
+            at += size
     for copy in copies:
         copy.start()
     for copy in copies:
@@ -639,15 +651,16 @@
     return even if even == odd else even + (odd - even) * side_ref[0]
 
 
-def cut(side, array, starts, sizes, squares=False):
-    count = len(sizes)
+def cut(side, array, blocks, squares=False):
+    count = len(blocks)
+    sizes = [sum(size for _, size in block) for block in blocks]
     return pl.pallas_call(
-        functools.partial(cut_kernel, starts, squares),
+        functools.partial(cut_kernel, blocks, squares),
         out_shape=tuple(jax.ShapeDtypeStruct((3, size, 8, 128), jnp.float32) for size in sizes)
         + (TILE,) * squares,
         in_specs=[SMEM, VMEM if squares else pl.BlockSpec(memory_space=pltpu.HBM)],
         out_specs=(VMEM,) * (count + squares),
-        scratch_shapes=[pltpu.SemaphoreType.DMA((count,))],
+        scratch_shapes=[pltpu.SemaphoreType.DMA((sum(len(block) for block in blocks),))],
         compiler_params=PARAMS,
         name="cut",
     )(side, array)
@@ -668,8 +681,7 @@
         return image * slabs + domain % slabs
 
     everyone = [(i, d) for i in range(images) for d in range(slabs)]
-    outer_own = [(at(i, d), at(i, d + 1 - 2 * (i % 2))) for i, d in everyone]
-    outer_partner = [(at(i, d), at(i ^ 1, d - 1 + 2 * (i % 2))) for i, d in everyone]
+    outward = [(at(i, d), at(i, d + 1 - 2 * (i % 2))) for i, d in everyone]
     across = [(i, i ^ 1) for i in range(images)]
     own_out = [(i, i - 2 + 4 * (i % 2)) for i in range(images)]
     own_out = [(a, b) for a, b in own_out if 0 <= b < images]
@@ -678,52 +690,46 @@
     downward = [(b, a) for a, b in upward]
 
     end, top = planes - HALO, half + HALO
-    piece = half // REGIONS
-    edge_own, edge_partner, edge_inner, near_inner, own, *far_pieces = cut(
+    piece = PIECES[0]
+    outer, inner = (0, top), (top, 0)
+    edge_own, near_inner, own, lead, rest = cut(
         side_arg,
         slab,
-        ((end, 0), (0, end), (half - HALO, half), (half, half - HALO), (0, half))
-        + tuple((half + c * piece, c * piece) for c in range(REGIONS)),
-        (HALO,) * 4 + (half,) + (piece,) * REGIONS,
-    )
-    halo_own = lax.ppermute(edge_own, both, outer_own)
-    halo_partner = lax.ppermute(edge_partner, both, outer_partner)
-    halo_inner = lax.ppermute(edge_inner, "image", across)
-    *far_pieces[1:], halo_own, halo_partner, halo_inner = lax.optimization_barrier(
-        (*far_pieces[1:], halo_own, halo_partner, halo_inner)
-    )
-    partner = [lax.ppermute(part, "image", across) for part in far_pieces]
+        (
+            (((end, 0), HALO),),
+            (((half, half - HALO), HALO),),
+            (((0, half), half),),
+            (((half, 0), piece), ((half - HALO, half), HALO), ((0, end), HALO)),
+            (((half + piece, piece), PIECES[1]),),
+        ),
+    )
+    partner = [lax.ppermute(part, "image", across) for part in (lead, rest)]
     beyond_own = lax.ppermute(own, "image", own_out)
-    outer, inner = (0, top), (top, 0)
+    edges = jnp.concatenate([edge_own, partner[0][:, piece + HALO :]], axis=1)
+    halo = lax.ppermute(edges, both, outward)
     beyond_partner = [lax.ppermute(part, "image", partner_out) for part in partner]
-    partner_force, partner_energy = image_forces(
-        side_arg,
-        half,
-        tuple((part, None, (HALO + c * piece,) * 2) for c, part in enumerate(partner))
-        + ((halo_partner, None, outer), (halo_inner, None, inner)),
-    )
-    held, near_inner, beyond_partner[0], _ = lax.optimization_barrier(
-        (own, near_inner, beyond_partner[0], partner_energy)
-    )
-    own_force, own_energy = image_forces(
-        side_arg,
-        half,
-        ((held, None, (HALO, HALO)), (halo_own, None, outer), (near_inner, None, inner)),
-    )
-    far_speed, slab_sq = cut(side_arg, slab_speed, ((half, 0),), (half,), True)
-    far_speed, _ = lax.optimization_barrier((far_speed, beyond_partner[0]))
+    own_source = (
+        (own, None, 0, half, (HALO, HALO)),
+        (halo, None, 0, HALO, outer),
+        (near_inner, None, 0, HALO, inner),
+    )
+    partner_source = (
+        (partner[0], None, 0, piece, (HALO, HALO)),
+        (partner[0], None, piece, HALO, inner),
+        (partner[1], None, 0, PIECES[1], (HALO + piece,) * 2),
+        (halo, None, HALO, HALO, outer),
+    )
+    forces, energies = image_forces(side_arg, half, (own_source, partner_source))
+    far_speed, slab_sq = cut(side_arg, slab_speed, ((((half, 0), half),),), True)
+    far_speed, *_ = lax.optimization_barrier((far_speed, halo, beyond_partner[0]))
     partner_speed = lax.ppermute(far_speed, "image", across)
 
     path = (beyond_partner, [own], partner, [beyond_own])
     speeds = (slab_speed, partner_speed)
     speed_sq = (slab_sq, jnp.zeros_like(slab_sq))
-    results = [(own_force, own_energy), (partner_force, partner_energy)]
     for step_index in range(FIRE_STEPS):
         if step_index > 0:
-            results = [image_forces(side_arg, half, held) for held in sources]
-            back_home, _ = lax.optimization_barrier((back_home, results[0][1]))
-            returned = lax.ppermute(back_home, "image", across)
-        forces, energies = zip(*results)
+            forces, energies = image_forces(side_arg, half, sources)
         payload = moments(side_arg, path, forces, energies, speed_sq, images * slabs)
         gathered = lax.all_to_all(payload, both, 0, 0, tiled=True)
         if step_index == FIRE_STEPS - 1:
@@ -735,9 +741,9 @@
         high = lax.ppermute(bottoms, both, downward)
         sources = [
             (
-                (moved[j], None, (HALO, HALO)),
-                (low, 1 - j, (0, 0)),
-                (high, 1 - j, (top, top)),
+                (moved[j], None, 0, half, (HALO, HALO)),
+                (low, 1 - j, 0, HALO, (0, 0)),
+                (high, 1 - j, 0, HALO, (top, top)),
             )
             for j in range(2)
         ]
@@ -747,7 +753,8 @@
             [moved[1]],
             [lax.ppermute(moved[0], "image", own_out)],
         )
-        back_home = moved[1]
+        back_home, _, _ = lax.optimization_barrier((moved[1], low, high))
+        returned = lax.ppermute(back_home, "image", across)
     whole = [pieces[0] for pieces in path]
     *last_speeds, terms = last_partner(
         image_arg, gathered, whole[1:], forces[1], speeds[1], images

time: 111 us -> 113 us (1.018)
  starting transfers between devices: 31.4 us -> 24.7 us
  waiting for transfers between devices: 20.9 us -> 26.6 us
  blocking collectives: 35.7 us -> 38 us
    ppermute x5 -> x3, waiting for transfers between devices: 6.37 us -> 13.5 us  [the longest x1 6.8 us: local(): halo = lax.ppermute(edges, both, outward)]
    ppermute x5 -> x3, starting transfers between devices: 8.29 us -> 2.25 us  [the longest x2 2.17 us: local(): partner = [lax.ppermute(part, 'image', across) for part in (lead, rest)]]
    all_to_all x2, blocking collectives: 35.7 us -> 38 us  [local(): gathered = lax.all_to_all(payload, both, 0, 0, tiled=True)]
    ppermute x1, starting transfers between devices: 1.82 us -> 0.02 us  [local(): partner_speed = lax.ppermute(far_speed, 'image', across)]
    ppermute x2, starting transfers between devices: 6.82 us -> 8.05 us  [local(): lax.ppermute(part, 'image', partner_out)]
    pallas_call x6 -> x4, Pallas kernels: 14.2 us -> 14.2 us  [the longest x2 13.6 us: image_forces(): pl.pallas_call(functools.partial(force_kernel, layouts), out_shape=(jax.S...]
  transfers between devices with their start and end apart: 16 -> 14, of which waited for: 8 -> 6; matrix products, arithmetic and copies ran while one was open for 0% -> 0% of each run, Pallas kernels for 17% -> 16%
where the time goes in v5:
time: 113 us; the launch traced here: 112 us
  blocking collectives  38 us (34%)
  waiting for transfers between devices  26.6 us (24%)
  starting transfers between devices  24.7 us (22%)
  Pallas kernels  20.7 us (18%)
  local copies, waits for them, and re-layouts  1.37 us (1%)
    all_to_all x2, blocking collectives, local(): gathered = lax.all_to_all(payload, both, 0, 0, tiled=True)  38 us
    pallas_call x2, Pallas kernels, image_forces(): pl.pallas_call(functools.partial(force_kernel, layouts), out_shape=(jax.S...  13.6 us
    ppermute x2, waiting for transfers between devices, local(): last_speeds = [lax.ppermute(part, 'image', across) for part in last_speeds]  10.3 us
    ppermute x2, starting transfers between devices, local(): lax.ppermute(part, 'image', partner_out)  8.05 us
    ppermute x1, waiting for transfers between devices, local(): halo = lax.ppermute(edges, both, outward)  6.8 us
    ppermute x2, waiting for transfers between devices, local(): partner = [lax.ppermute(part, 'image', across) for part in (lead, rest)]  6.71 us
    ppermute x1, starting transfers between devices, local(): high = lax.ppermute(bottoms, both, downward)  5.05 us
    ppermute x1, starting transfers between devices, local(): lax.ppermute(moved[1], 'image', partner_out)  4.58 us
  transfers between devices with their start and end apart: 14, of which 6 were waited for; matrix products, arithmetic and copies ran while one was open for 0% of the time, Pallas kernels for 16%

profile of v5, /device:TPU:0, one launch (start us, length us, event | category | flops | bytes accessed | tf_op | source)
XLA Modules:
  0.0 112.3 jit_solution(15887418712476819734)
XLA Ops:
  0.6 0.0 copy-start
  0.7 0.0 copy-start.1
  0.7 1.4 %copy-done.1 = f32[1,3,98304]{2,0,1:T(1,128)S(1)} copy-done((f32[1,3,98304]{2,0,1:T(1,128)S(1)}, f32[1,3,98304]{2,0,1:T(1,128)}, u32[]{:S(2)}) %copy-start.1) | copy-done | bytes 1179672
  2.0 0.3 cut.2
  2.3 2.1 %collective-permute-start = (f32[3,20,8,128]{3,2,1,0:T(8,128)S(1)}, f32[3,20,8,128]{3,2,1,0:T(8,128)S(1)}, u32[]{:S(2)}, u32[]{:S(2)}) collective-permute-start(f32[3,20,8,128]{3,2,1,0:T(8,128)S(1)} %get-tuple-element.36), channel_id=1, source_target_pairs={{0,16},{16,0},{32,48},{48,32},{64,80},{80,64},{96,112},{112,96},{1... | collective-permute-start | bytes 737288 | tf_op jit(solution)/shard_map/ppermute | solution.py:706
  4.4 0.1 collective-permute-start.2
  4.5 6.7 %collective-permute-done.refs_3_.refs_4_ = f32[3,20,8,128]{3,2,1,0:T(8,128)S(1)} collective-permute-done((f32[3,20,8,128]{3,2,1,0:T(8,128)S(1)}, f32[3,20,8,128]{3,2,1,0:T(8,128)S(1)}, u32[]{:S(2)}, u32[]{:S(2)}) %collective-permute-start) | collective-permute-done | bytes 245792 | tf_op jit(solution)/shard_map/ppermute | solution.py:706
  11.2 3.5 %collective-permute-start.1 = (f32[3,20,8,128]{3,2,1,0:T(8,128)S(1)}, f32[3,20,8,128]{3,2,1,0:T(8,128)S(1)}, u32[]{:S(2)}, u32[]{:S(2)}) collective-permute-start(f32[3,20,8,128]{3,2,1,0:T(8,128)S(1)} %collective-permute-done.refs_3_.refs_4_), channel_id=1, source_target_pairs={{48,16},{0,32},{80,48},{32,64},{112,80},{64,96},{49,17},{1,33},{81... | collective-permute-start | bytes 737288 | tf_op jit(solution)/shard_map/ppermute | solution.py:710
  14.7 1.3 %collective-permute-start.4 = (f32[3,48,8,128]{3,2,1,0:T(8,128)S(1)}, f32[3,48,8,128]{3,2,1,0:T(8,128)S(1)}, u32[]{:S(2)}, u32[]{:S(2)}) collective-permute-start(f32[3,48,8,128]{3,2,1,0:T(8,128)S(1)} %get-tuple-element.38.refs_0_.refs_2_), channel_id=1, source_target_pairs={{16,48},{32,0},{48,80},{64,32},{80,112},{96,64},{17,49},{33,1},{49... | collective-permute-start | bytes 1769480 | tf_op jit(solution)/shard_map/ppermute | solution.py:707
  16.0 0.1 collective-permute-start.5
  16.1 0.0 copy-done
  16.1 0.3 cut.3
  16.4 6.8 %collective-permute-done.5.refs_1_.refs_6_ = f32[3,4,8,128]{3,2,1,0:T(8,128)S(1)} collective-permute-done((f32[3,4,8,128]{3,2,1,0:T(8,128)S(1)}, f32[3,4,8,128]{3,2,1,0:T(8,128)S(1)}, u32[]{:S(2)}, u32[]{:S(2)}) %collective-permute-start.5) | collective-permute-done | bytes 49184 | tf_op jit(solution)/shard_map/ppermute | solution.py:709
  23.2 0.0 collective-permute-done.1.refs_0_
  23.2 0.0 collective-permute-start.6
  23.3 0.0 collective-permute-done.2.refs_5_.refs_4_
  23.3 4.6 %collective-permute-start.3 = (f32[3,32,8,128]{3,2,1,0:T(8,128)S(1)}, f32[3,32,8,128]{3,2,1,0:T(8,128)S(1)}, u32[]{:S(2)}, u32[]{:S(2)}) collective-permute-start(f32[3,32,8,128]{3,2,1,0:T(8,128)S(1)} %collective-permute-done.2.refs_5_.refs_4_), channel_id=1, source_target_pairs={{48,16},{0,32},{80,48},{32,64},{112,80},{64,96},{49,17},{1,33},{81... | collective-permute-start | bytes 1179656 | tf_op jit(solution)/shard_map/ppermute | solution.py:710
  27.8 6.8 %slab_forces.2 = (f32[3,48,8,128]{3,2,1,0:T(8,128)S(1)}, f32[8,128]{1,0:T(8,128)S(1)}, f32[3,48,8,128]{3,2,1,0:T(8,128)S(1)}, f32[8,128]{1,0:T(8,128)S(1)}) custom-call(s32[1]{0:T(128)} %bitcast.side_ref, f32[3,48,8,128]{3,2,1,0:T(8,128)S(1)} %get-tuple-element.38.refs_0_.refs_2_, f32[3,4,8,128]{3,2,1,0:T(8,128)S(1)} %collective-permute-done.5.refs_1_.refs_6_, ...), custom_call_target="tpu_custom_call" | custom-call | flops 40000000 | bytes 30000000 | tf_op jit(solution)/shard_map/slab_forces/pallas_call | solution.py:268
  34.7 0.0 collective-permute-done.4.refs_5_
  34.7 1.0 collective-permute-done.3.refs_1_
  35.7 0.7 path_moments.2
  36.4 20.2 %all_to_all.22 = f32[128,1,128]{2,1,0:T(1,128)S(1)} all-to-all(f32[128,1,128]{2,1,0:T(1,128)S(1)} %bitcast.18), channel_id=1, replica_groups=mesh['image'=8,'domain'=16] {'image','domain'}, dimensions={0} | all-to-all | bytes 131072 | tf_op jit(solution)/shard_map/all_to_all | solution.py:734
  56.7 0.0 collective-permute-done.6.refs_8_
  56.7 1.0 fire_update.1
  57.7 1.3 %collective-permute-start.11 = (f32[3,48,8,128]{3,2,1,0:T(8,128)S(1)}, f32[3,48,8,128]{3,2,1,0:T(8,128)S(1)}, u32[]{:S(2)}, u32[]{:S(2)}) collective-permute-start(f32[3,48,8,128]{3,2,1,0:T(8,128)S(1)} %get-tuple-element.52.refs_0_.refs_1_.before.here), channel_id=1, source_target_pairs={{16,48},{32,0},{48,80},{64,32},{80,112},{96,64},{17,49},{33,1},{49... | collective-permute-start | bytes 1769480 | tf_op jit(solution)/shard_map/ppermute | solution.py:754
  59.0 4.6 %collective-permute-start.10 = (f32[3,48,8,128]{3,2,1,0:T(8,128)S(1)}, f32[3,48,8,128]{3,2,1,0:T(8,128)S(1)}, u32[]{:S(2)}, u32[]{:S(2)}) collective-permute-start(f32[3,48,8,128]{3,2,1,0:T(8,128)S(1)} %get-tuple-element.51.refs_3_.refs_2_.here.after), channel_id=1, source_target_pairs={{48,16},{0,32},{80,48},{32,64},{112,80},{64,96},{49,17},{1,33},{81... | collective-permute-start | bytes 1769480 | tf_op jit(solution)/shard_map/ppermute | solution.py:751
  63.6 0.1 collective-permute-start.7
  63.7 5.1 %collective-permute-start.8 = (f32[2,3,2,8,128]{4,3,2,1,0:T(8,128)S(1)}, f32[2,3,2,8,128]{4,3,2,1,0:T(8,128)S(1)}, u32[]{:S(2)}, u32[]{:S(2)}) collective-permute-start(f32[2,3,2,8,128]{4,3,2,1,0:T(8,128)S(1)} %get-tuple-element.50), channel_id=1, source_target_pairs={{16,0},{17,1},{18,2},{19,3},{20,4},{21,5},{22,6},{23,7},{24,8},{25... | collective-permute-start | bytes 147464 | tf_op jit(solution)/shard_map/ppermute | solution.py:741
  68.7 1.8 %collective-permute-done.7.refs_1_.refs_4_ = f32[2,3,2,8,128]{4,3,2,1,0:T(8,128)S(1)} collective-permute-done((f32[2,3,2,8,128]{4,3,2,1,0:T(8,128)S(1)}, f32[2,3,2,8,128]{4,3,2,1,0:T(8,128)S(1)}, u32[]{:S(2)}, u32[]{:S(2)}) %collective-permute-start.7) | collective-permute-done | bytes 49184 | tf_op jit(solution)/shard_map/ppermute | solution.py:740
  70.5 0.0 collective-permute-done.8.refs_2_.refs_5_
  70.5 0.0 collective-permute-start.9
  70.5 6.8 %slab_forces.3 = (f32[3,48,8,128]{3,2,1,0:T(8,128)S(1)}, f32[8,128]{1,0:T(8,128)S(1)}, f32[3,48,8,128]{3,2,1,0:T(8,128)S(1)}, f32[8,128]{1,0:T(8,128)S(1)}) custom-call(s32[1]{0:T(128)} %bitcast.side_ref, f32[3,48,8,128]{3,2,1,0:T(8,128)S(1)} %get-tuple-element.52.refs_0_.refs_1_.before.here, ...), custom_call_target="tpu_custom_call" | custom-call | flops 40000000 | bytes 30000000 | tf_op jit(solution)/shard_map/slab_forces/pallas_call | solution.py:268
  77.3 0.0 collective-permute-done.11.refs_3_.after
  77.3 0.0 collective-permute-done.10.refs_0_.before
  77.3 0.7 path_moments.3
  78.1 17.8 %all_to_all.23 = f32[128,1,128]{2,1,0:T(1,128)S(1)} all-to-all(f32[128,1,128]{2,1,0:T(1,128)S(1)} %bitcast.19), channel_id=1, replica_groups=mesh['image'=8,'domain'=16] {'image','domain'}, dimensions={0} | all-to-all | bytes 131072 | tf_op jit(solution)/shard_map/all_to_all | solution.py:734
  95.9 0.6 last_partner.1
  96.5 0.9 collective-permute-start.13
  97.4 1.2 %collective-permute-start.12 = (f32[3,24,8,128]{3,2,1,0:T(8,128)S(1)}, f32[3,24,8,128]{3,2,1,0:T(8,128)S(1)}, u32[]{:S(2)}, u32[]{:S(2)}) collective-permute-start(f32[3,24,8,128]{3,2,1,0:T(8,128)S(1)} %get-tuple-element.60), channel_id=1, source_target_pairs={{0,16},{16,0},{32,48},{48,32},{64,80},{80,64},{96,112},{112,96},{1... | collective-permute-start | bytes 884744 | tf_op jit(solution)/shard_map/ppermute | solution.py:762
  98.6 1.6 %last_own.1 = (f32[3,96,8,128]{3,2,1,0:T(8,128)}, f32[3,96,8,128]{3,2,1,0:T(8,128)}) custom-call(s32[1]{0:T(128)} %bitcast.side_ref, f32[2,4,8,128]{3,2,1,0:T(8,128)S(1)} %get-tuple-element.62.terms, f32[3,48,8,128]{3,2,1,0:T(8,128)S(1)} %collective-permute-done.10.refs_0_.before, f32[3,48,8,128]{3,2,1,0:T(8,128)S(1)} %get-tuple-element.52.refs_0_.refs_1_.before.here, ...), custom_call_target="tpu_custom_call" | custom-call | tf_op jit(solution)/shard_map/last_own/pallas_call | solution.py:573
  100.1 0.0 collective-permute-done.9.here
  100.1 6.3 %collective-permute-done.13.speed = f32[3,24,8,128]{3,2,1,0:T(8,128)S(1)} collective-permute-done((f32[3,24,8,128]{3,2,1,0:T(8,128)S(1)}, f32[3,24,8,128]{3,2,1,0:T(8,128)S(1)}, u32[]{:S(2)}, u32[]{:S(2)}) %collective-permute-start.13) | collective-permute-done | bytes 294944 | tf_op jit(solution)/shard_map/ppermute | solution.py:762
  106.5 0.9 last_join.2
  107.4 4.0 %collective-permute-done.12.speed = f32[3,24,8,128]{3,2,1,0:T(8,128)S(1)} collective-permute-done((f32[3,24,8,128]{3,2,1,0:T(8,128)S(1)}, f32[3,24,8,128]{3,2,1,0:T(8,128)S(1)}, u32[]{:S(2)}, u32[]{:S(2)}) %collective-permute-start.12) | collective-permute-done | bytes 294944 | tf_op jit(solution)/shard_map/ppermute | solution.py:762
  111.4 0.9 last_join.3
  (3 shorter events, 0.0 us)
Async XLA Ops:
  0.6 15.5 %copy-start = (f32[1,3,98304]{2,0,1:T(1,128)S(1)}, f32[1,3,98304]{2,0,1:T(1,128)}, u32[]{:S(2)}) copy-start(f32[1,3,98304]{2,0,1:T(1,128)} %param.3) | copy-start | bytes 3538948
  0.7 1.4 %copy-start.1 = (f32[1,3,98304]{2,0,1:T(1,128)S(1)}, f32[1,3,98304]{2,0,1:T(1,128)}, u32[]{:S(2)}) copy-start(f32[1,3,98304]{2,0,1:T(1,128)} %param.2) | copy-start | bytes 3538948
  2.3 8.9 %collective-permute-start = (f32[3,20,8,128]{3,2,1,0:T(8,128)S(1)}, f32[3,20,8,128]{3,2,1,0:T(8,128)S(1)}, u32[]{:S(2)}, u32[]{:S(2)}) collective-permute-start(f32[3,20,8,128]{3,2,1,0:T(8,128)S(1)} %get-tuple-element.36), channel_id=1, source_target_pairs={{0,16},{16,0},{32,48},{48,32},{64,80},{80,64},{96,112},{112,96},{1... | collective-permute-start | bytes 737288 | tf_op jit(solution)/shard_map/ppermute | solution.py:706
  4.4 18.9 %collective-permute-start.2 = (f32[3,32,8,128]{3,2,1,0:T(8,128)S(1)}, f32[3,32,8,128]{3,2,1,0:T(8,128)S(1)}, u32[]{:S(2)}, u32[]{:S(2)}) collective-permute-start(f32[3,32,8,128]{3,2,1,0:T(8,128)S(1)} %get-tuple-element.37), channel_id=1, source_target_pairs={{0,16},{16,0},{32,48},{48,32},{64,80},{80,64},{96,112},{112,96},{1... | collective-permute-start | bytes 1179656 | tf_op jit(solution)/shard_map/ppermute | solution.py:706
  11.2 12.0 %collective-permute-start.1 = (f32[3,20,8,128]{3,2,1,0:T(8,128)S(1)}, f32[3,20,8,128]{3,2,1,0:T(8,128)S(1)}, u32[]{:S(2)}, u32[]{:S(2)}) collective-permute-start(f32[3,20,8,128]{3,2,1,0:T(8,128)S(1)} %collective-permute-done.refs_3_.refs_4_), channel_id=1, source_target_pairs={{48,16},{0,32},{80,48},{32,64},{112,80},{64,96},{49,17},{1,33},{81... | collective-permute-start | bytes 737288 | tf_op jit(solution)/shard_map/ppermute | solution.py:710
  14.7 20.0 %collective-permute-start.4 = (f32[3,48,8,128]{3,2,1,0:T(8,128)S(1)}, f32[3,48,8,128]{3,2,1,0:T(8,128)S(1)}, u32[]{:S(2)}, u32[]{:S(2)}) collective-permute-start(f32[3,48,8,128]{3,2,1,0:T(8,128)S(1)} %get-tuple-element.38.refs_0_.refs_2_), channel_id=1, source_target_pairs={{16,48},{32,0},{48,80},{64,32},{80,112},{96,64},{17,49},{33,1},{49... | collective-permute-start | bytes 1769480 | tf_op jit(solution)/shard_map/ppermute | solution.py:707
  16.0 7.2 %collective-permute-start.5 = (f32[3,4,8,128]{3,2,1,0:T(8,128)S(1)}, f32[3,4,8,128]{3,2,1,0:T(8,128)S(1)}, u32[]{:S(2)}, u32[]{:S(2)}) collective-permute-start(f32[3,4,8,128]{3,2,1,0:T(8,128)S(1)} %pad_maximum_fusion), channel_id=1, source_target_pairs={{0,1},{1,2},{2,3},{3,4},{4,5},{5,6},{6,7},{7,8},{8,9},{9,10},{10,1... | collective-permute-start | bytes 147464 | tf_op jit(solution)/shard_map/ppermute | solution.py:709
  23.2 33.4 %collective-permute-start.6 = (f32[3,48,8,128]{3,2,1,0:T(8,128)S(1)}, f32[3,48,8,128]{3,2,1,0:T(8,128)S(1)}, u32[]{:S(2)}, u32[]{:S(2)}) collective-permute-start(f32[3,48,8,128]{3,2,1,0:T(8,128)S(1)} %get-tuple-element.47), channel_id=1, source_target_pairs={{0,16},{16,0},{32,48},{48,32},{64,80},{80,64},{96,112},{112,96},{1... | collective-permute-start | bytes 1769480 | tf_op jit(solution)/shard_map/ppermute | solution.py:725
  23.3 12.4 %collective-permute-start.3 = (f32[3,32,8,128]{3,2,1,0:T(8,128)S(1)}, f32[3,32,8,128]{3,2,1,0:T(8,128)S(1)}, u32[]{:S(2)}, u32[]{:S(2)}) collective-permute-start(f32[3,32,8,128]{3,2,1,0:T(8,128)S(1)} %collective-permute-done.2.refs_5_.refs_4_), channel_id=1, source_target_pairs={{48,16},{0,32},{80,48},{32,64},{112,80},{64,96},{49,17},{1,33},{81... | collective-permute-start | bytes 1179656 | tf_op jit(solution)/shard_map/ppermute | solution.py:710
  57.7 19.6 %collective-permute-start.11 = (f32[3,48,8,128]{3,2,1,0:T(8,128)S(1)}, f32[3,48,8,128]{3,2,1,0:T(8,128)S(1)}, u32[]{:S(2)}, u32[]{:S(2)}) collective-permute-start(f32[3,48,8,128]{3,2,1,0:T(8,128)S(1)} %get-tuple-element.52.refs_0_.refs_1_.before.here), channel_id=1, source_target_pairs={{16,48},{32,0},{48,80},{64,32},{80,112},{96,64},{17,49},{33,1},{49... | collective-permute-start | bytes 1769480 | tf_op jit(solution)/shard_map/ppermute | solution.py:754
  59.0 18.3 %collective-permute-start.10 = (f32[3,48,8,128]{3,2,1,0:T(8,128)S(1)}, f32[3,48,8,128]{3,2,1,0:T(8,128)S(1)}, u32[]{:S(2)}, u32[]{:S(2)}) collective-permute-start(f32[3,48,8,128]{3,2,1,0:T(8,128)S(1)} %get-tuple-element.51.refs_3_.refs_2_.here.after), channel_id=1, source_target_pairs={{48,16},{0,32},{80,48},{32,64},{112,80},{64,96},{49,17},{1,33},{81... | collective-permute-start | bytes 1769480 | tf_op jit(solution)/shard_map/ppermute | solution.py:751
  63.6 6.9 %collective-permute-start.7 = (f32[2,3,2,8,128]{4,3,2,1,0:T(8,128)S(1)}, f32[2,3,2,8,128]{4,3,2,1,0:T(8,128)S(1)}, u32[]{:S(2)}, u32[]{:S(2)}) collective-permute-start(f32[2,3,2,8,128]{4,3,2,1,0:T(8,128)S(1)} %get-tuple-element.49), channel_id=1, source_target_pairs={{0,16},{1,17},{2,18},{3,19},{4,20},{5,21},{6,22},{7,23},{8,24},{9,... | collective-permute-start | bytes 147464 | tf_op jit(solution)/shard_map/ppermute | solution.py:740
  63.7 6.8 %collective-permute-start.8 = (f32[2,3,2,8,128]{4,3,2,1,0:T(8,128)S(1)}, f32[2,3,2,8,128]{4,3,2,1,0:T(8,128)S(1)}, u32[]{:S(2)}, u32[]{:S(2)}) collective-permute-start(f32[2,3,2,8,128]{4,3,2,1,0:T(8,128)S(1)} %get-tuple-element.50), channel_id=1, source_target_pairs={{16,0},{17,1},{18,2},{19,3},{20,4},{21,5},{22,6},{23,7},{24,8},{25... | collective-permute-start | bytes 147464 | tf_op jit(solution)/shard_map/ppermute | solution.py:741
  70.5 29.6 %collective-permute-start.9 = (f32[3,48,8,128]{3,2,1,0:T(8,128)S(1)}, f32[3,48,8,128]{3,2,1,0:T(8,128)S(1)}, u32[]{:S(2)}, u32[]{:S(2)}) collective-permute-start(f32[3,48,8,128]{3,2,1,0:T(8,128)S(1)} %get-tuple-element.51.refs_3_.refs_2_.here.after), channel_id=1, source_target_pairs={{0,16},{16,0},{32,48},{48,32},{64,80},{80,64},{96,112},{112,96},{1... | collective-permute-start | bytes 1769480 | tf_op jit(solution)/shard_map/ppermute | solution.py:757
  96.5 10.0 %collective-permute-start.13 = (f32[3,24,8,128]{3,2,1,0:T(8,128)S(1)}, f32[3,24,8,128]{3,2,1,0:T(8,128)S(1)}, u32[]{:S(2)}, u32[]{:S(2)}) collective-permute-start(f32[3,24,8,128]{3,2,1,0:T(8,128)S(1)} %get-tuple-element.61), channel_id=1, source_target_pairs={{0,16},{16,0},{32,48},{48,32},{64,80},{80,64},{96,112},{112,96},{1... | collective-permute-start | bytes 884744 | tf_op jit(solution)/shard_map/ppermute | solution.py:762
  97.4 14.0 %collective-permute-start.12 = (f32[3,24,8,128]{3,2,1,0:T(8,128)S(1)}, f32[3,24,8,128]{3,2,1,0:T(8,128)S(1)}, u32[]{:S(2)}, u32[]{:S(2)}) collective-permute-start(f32[3,24,8,128]{3,2,1,0:T(8,128)S(1)} %get-tuple-element.60), channel_id=1, source_target_pairs={{0,16},{16,0},{32,48},{48,32},{64,80},{80,64},{96,112},{112,96},{1... | collective-permute-start | bytes 884744 | tf_op jit(solution)/shard_map/ppermute | solution.py:762

commit v6 on v5

--- a/solution.py
+++ b/solution.py
@@ -721,7 +721,7 @@
     )
     forces, energies = image_forces(side_arg, half, (own_source, partner_source))
     far_speed, slab_sq = cut(side_arg, slab_speed, ((((half, 0), half),),), True)
-    far_speed, *_ = lax.optimization_barrier((far_speed, halo, beyond_partner[0]))
+    far_speed, *_ = lax.optimization_barrier((far_speed, halo, beyond_partner[0], beyond_own))
     partner_speed = lax.ppermute(far_speed, "image", across)
 
     path = (beyond_partner, [own], partner, [beyond_own])

time: 113 us -> 112 us (level)
  blocking collectives: 38 us -> 36.5 us
    ppermute x2, starting transfers between devices: 2.17 us -> 4.31 us  [local(): partner = [lax.ppermute(part, 'image', across) for part in (lead, rest)]]
    ppermute x2, starting transfers between devices: 8.05 us -> 6.48 us  [local(): lax.ppermute(part, 'image', partner_out)]
    all_to_all x2, blocking collectives: 38 us -> 36.5 us  [local(): gathered = lax.all_to_all(payload, both, 0, 0, tiled=True)]
where the time goes in v6:
time: 112 us
  blocking collectives  36.5 us (33%)
  waiting for transfers between devices  27.3 us (24%)
  starting transfers between devices  25.3 us (23%)
  Pallas kernels  20.7 us (18%)
  local copies, waits for them, and re-layouts  1.37 us (1%)
    all_to_all x2, blocking collectives, local(): gathered = lax.all_to_all(payload, both, 0, 0, tiled=True)  36.5 us
    pallas_call x2, Pallas kernels, image_forces(): pl.pallas_call(functools.partial(force_kernel, layouts), out_shape=(jax.S...  13.6 us
    ppermute x2, waiting for transfers between devices, local(): last_speeds = [lax.ppermute(part, 'image', across) for part in last_speeds]  10.3 us
    ppermute x1, waiting for transfers between devices, local(): halo = lax.ppermute(edges, both, outward)  6.91 us
    ppermute x2, waiting for transfers between devices, local(): partner = [lax.ppermute(part, 'image', across) for part in (lead, rest)]  6.73 us
    ppermute x2, starting transfers between devices, local(): lax.ppermute(part, 'image', partner_out)  6.48 us
    ppermute x1, starting transfers between devices, local(): high = lax.ppermute(bottoms, both, downward)  5.05 us
    ppermute x1, starting transfers between devices, local(): lax.ppermute(moved[1], 'image', partner_out)  4.58 us
  transfers between devices with their start and end apart: 14, of which 6 were waited for; matrix products, arithmetic and copies ran while one was open for 0% of the time, Pallas kernels for 16%

profile of v6, /device:TPU:0, one launch (start us, length us, event | category | flops | bytes accessed | tf_op | source)
XLA Modules:
  0.0 112.0 jit_solution(10115996065982805990)
XLA Ops:
  0.6 0.0 copy-start
  0.7 0.0 copy-start.1
  0.7 1.4 %copy-done.1 = f32[1,3,98304]{2,0,1:T(1,128)S(1)} copy-done((f32[1,3,98304]{2,0,1:T(1,128)S(1)}, f32[1,3,98304]{2,0,1:T(1,128)}, u32[]{:S(2)}) %copy-start.1) | copy-done | bytes 1179672
  2.0 0.3 cut.2
  2.3 1.3 %collective-permute-start.4 = (f32[3,48,8,128]{3,2,1,0:T(8,128)S(1)}, f32[3,48,8,128]{3,2,1,0:T(8,128)S(1)}, u32[]{:S(2)}, u32[]{:S(2)}) collective-permute-start(f32[3,48,8,128]{3,2,1,0:T(8,128)S(1)} %get-tuple-element.38.refs_0_.refs_2_), channel_id=1, source_target_pairs={{16,48},{32,0},{48,80},{64,32},{80,112},{96,64},{17,49},{33,1},{49... | collective-permute-start | bytes 1769480 | tf_op jit(solution)/shard_map/ppermute | solution.py:707
  3.6 4.2 %collective-permute-start = (f32[3,20,8,128]{3,2,1,0:T(8,128)S(1)}, f32[3,20,8,128]{3,2,1,0:T(8,128)S(1)}, u32[]{:S(2)}, u32[]{:S(2)}) collective-permute-start(f32[3,20,8,128]{3,2,1,0:T(8,128)S(1)} %get-tuple-element.36), channel_id=1, source_target_pairs={{0,16},{16,0},{32,48},{48,32},{64,80},{80,64},{96,112},{112,96},{1... | collective-permute-start | bytes 737288 | tf_op jit(solution)/shard_map/ppermute | solution.py:706
  7.8 0.1 collective-permute-start.2
  7.9 6.7 %collective-permute-done.refs_3_.refs_4_ = f32[3,20,8,128]{3,2,1,0:T(8,128)S(1)} collective-permute-done((f32[3,20,8,128]{3,2,1,0:T(8,128)S(1)}, f32[3,20,8,128]{3,2,1,0:T(8,128)S(1)}, u32[]{:S(2)}, u32[]{:S(2)}) %collective-permute-start) | collective-permute-done | bytes 245792 | tf_op jit(solution)/shard_map/ppermute | solution.py:706
  14.7 3.4 %collective-permute-start.1 = (f32[3,20,8,128]{3,2,1,0:T(8,128)S(1)}, f32[3,20,8,128]{3,2,1,0:T(8,128)S(1)}, u32[]{:S(2)}, u32[]{:S(2)}) collective-permute-start(f32[3,20,8,128]{3,2,1,0:T(8,128)S(1)} %collective-permute-done.refs_3_.refs_4_), channel_id=1, source_target_pairs={{48,16},{0,32},{80,48},{32,64},{112,80},{64,96},{49,17},{1,33},{81... | collective-permute-start | bytes 737288 | tf_op jit(solution)/shard_map/ppermute | solution.py:710
  18.1 0.1 collective-permute-start.5
  18.1 0.0 copy-done
  18.1 0.3 cut.3
  18.5 6.9 %collective-permute-done.5.refs_1_.refs_6_ = f32[3,4,8,128]{3,2,1,0:T(8,128)S(1)} collective-permute-done((f32[3,4,8,128]{3,2,1,0:T(8,128)S(1)}, f32[3,4,8,128]{3,2,1,0:T(8,128)S(1)}, u32[]{:S(2)}, u32[]{:S(2)}) %collective-permute-start.5) | collective-permute-done | bytes 49184 | tf_op jit(solution)/shard_map/ppermute | solution.py:709
  25.4 0.0 collective-permute-done.1.refs_0_
  25.4 0.0 collective-permute-done.4.refs_5_
  25.4 0.0 collective-permute-start.6
  25.4 0.0 collective-permute-done.2.refs_5_.refs_4_
  25.4 3.1 %collective-permute-start.3 = (f32[3,32,8,128]{3,2,1,0:T(8,128)S(1)}, f32[3,32,8,128]{3,2,1,0:T(8,128)S(1)}, u32[]{:S(2)}, u32[]{:S(2)}) collective-permute-start(f32[3,32,8,128]{3,2,1,0:T(8,128)S(1)} %collective-permute-done.2.refs_5_.refs_4_), channel_id=1, source_target_pairs={{48,16},{0,32},{80,48},{32,64},{112,80},{64,96},{49,17},{1,33},{81... | collective-permute-start | bytes 1179656 | tf_op jit(solution)/shard_map/ppermute | solution.py:710
  28.5 6.8 %slab_forces.2 = (f32[3,48,8,128]{3,2,1,0:T(8,128)S(1)}, f32[8,128]{1,0:T(8,128)S(1)}, f32[3,48,8,128]{3,2,1,0:T(8,128)S(1)}, f32[8,128]{1,0:T(8,128)S(1)}) custom-call(s32[1]{0:T(128)} %bitcast.side_ref, f32[3,48,8,128]{3,2,1,0:T(8,128)S(1)} %get-tuple-element.38.refs_0_.refs_2_, f32[3,4,8,128]{3,2,1,0:T(8,128)S(1)} %collective-permute-done.5.refs_1_.refs_6_, ...), custom_call_target="tpu_custom_call" | custom-call | flops 40000000 | bytes 30000000 | tf_op jit(solution)/shard_map/slab_forces/pallas_call | solution.py:268
  35.4 1.5 %collective-permute-done.3.refs_1_ = f32[3,32,8,128]{3,2,1,0:T(8,128)S(1)} collective-permute-done((f32[3,32,8,128]{3,2,1,0:T(8,128)S(1)}, f32[3,32,8,128]{3,2,1,0:T(8,128)S(1)}, u32[]{:S(2)}, u32[]{:S(2)}) %collective-permute-start.3) | collective-permute-done | bytes 393248 | tf_op jit(solution)/shard_map/ppermute | solution.py:710
  36.9 0.7 path_moments.2
  37.6 18.7 %all_to_all.22 = f32[128,1,128]{2,1,0:T(1,128)S(1)} all-to-all(f32[128,1,128]{2,1,0:T(1,128)S(1)} %bitcast.18), channel_id=1, replica_groups=mesh['image'=8,'domain'=16] {'image','domain'}, dimensions={0} | all-to-all | bytes 131072 | tf_op jit(solution)/shard_map/all_to_all | solution.py:734
  56.3 0.0 collective-permute-done.6.refs_8_
  56.3 1.0 fire_update.1
  57.4 1.3 %collective-permute-start.11 = (f32[3,48,8,128]{3,2,1,0:T(8,128)S(1)}, f32[3,48,8,128]{3,2,1,0:T(8,128)S(1)}, u32[]{:S(2)}, u32[]{:S(2)}) collective-permute-start(f32[3,48,8,128]{3,2,1,0:T(8,128)S(1)} %get-tuple-element.52.refs_0_.refs_1_.before.here), channel_id=1, source_target_pairs={{16,48},{32,0},{48,80},{64,32},{80,112},{96,64},{17,49},{33,1},{49... | collective-permute-start | bytes 1769480 | tf_op jit(solution)/shard_map/ppermute | solution.py:754
  58.7 4.6 %collective-permute-start.10 = (f32[3,48,8,128]{3,2,1,0:T(8,128)S(1)}, f32[3,48,8,128]{3,2,1,0:T(8,128)S(1)}, u32[]{:S(2)}, u32[]{:S(2)}) collective-permute-start(f32[3,48,8,128]{3,2,1,0:T(8,128)S(1)} %get-tuple-element.51.refs_3_.refs_2_.here.after), channel_id=1, source_target_pairs={{48,16},{0,32},{80,48},{32,64},{112,80},{64,96},{49,17},{1,33},{81... | collective-permute-start | bytes 1769480 | tf_op jit(solution)/shard_map/ppermute | solution.py:751
  63.3 0.1 collective-permute-start.7
  63.4 5.1 %collective-permute-start.8 = (f32[2,3,2,8,128]{4,3,2,1,0:T(8,128)S(1)}, f32[2,3,2,8,128]{4,3,2,1,0:T(8,128)S(1)}, u32[]{:S(2)}, u32[]{:S(2)}) collective-permute-start(f32[2,3,2,8,128]{4,3,2,1,0:T(8,128)S(1)} %get-tuple-element.50), channel_id=1, source_target_pairs={{16,0},{17,1},{18,2},{19,3},{20,4},{21,5},{22,6},{23,7},{24,8},{25... | collective-permute-start | bytes 147464 | tf_op jit(solution)/shard_map/ppermute | solution.py:741
  68.4 1.8 %collective-permute-done.7.refs_1_.refs_4_ = f32[2,3,2,8,128]{4,3,2,1,0:T(8,128)S(1)} collective-permute-done((f32[2,3,2,8,128]{4,3,2,1,0:T(8,128)S(1)}, f32[2,3,2,8,128]{4,3,2,1,0:T(8,128)S(1)}, u32[]{:S(2)}, u32[]{:S(2)}) %collective-permute-start.7) | collective-permute-done | bytes 49184 | tf_op jit(solution)/shard_map/ppermute | solution.py:740
  70.2 0.0 collective-permute-done.8.refs_2_.refs_5_
  70.2 0.0 collective-permute-start.9
  70.2 6.8 %slab_forces.3 = (f32[3,48,8,128]{3,2,1,0:T(8,128)S(1)}, f32[8,128]{1,0:T(8,128)S(1)}, f32[3,48,8,128]{3,2,1,0:T(8,128)S(1)}, f32[8,128]{1,0:T(8,128)S(1)}) custom-call(s32[1]{0:T(128)} %bitcast.side_ref, f32[3,48,8,128]{3,2,1,0:T(8,128)S(1)} %get-tuple-element.52.refs_0_.refs_1_.before.here, ...), custom_call_target="tpu_custom_call" | custom-call | flops 40000000 | bytes 30000000 | tf_op jit(solution)/shard_map/slab_forces/pallas_call | solution.py:268
  77.0 0.0 collective-permute-done.11.refs_3_.after
  77.0 0.0 collective-permute-done.10.refs_0_.before
  77.0 0.7 path_moments.3
  77.7 17.8 %all_to_all.23 = f32[128,1,128]{2,1,0:T(1,128)S(1)} all-to-all(f32[128,1,128]{2,1,0:T(1,128)S(1)} %bitcast.19), channel_id=1, replica_groups=mesh['image'=8,'domain'=16] {'image','domain'}, dimensions={0} | all-to-all | bytes 131072 | tf_op jit(solution)/shard_map/all_to_all | solution.py:734
  95.5 0.6 last_partner.1
  96.1 0.9 collective-permute-start.13
  97.0 1.2 %collective-permute-start.12 = (f32[3,24,8,128]{3,2,1,0:T(8,128)S(1)}, f32[3,24,8,128]{3,2,1,0:T(8,128)S(1)}, u32[]{:S(2)}, u32[]{:S(2)}) collective-permute-start(f32[3,24,8,128]{3,2,1,0:T(8,128)S(1)} %get-tuple-element.60), channel_id=1, source_target_pairs={{0,16},{16,0},{32,48},{48,32},{64,80},{80,64},{96,112},{112,96},{1... | collective-permute-start | bytes 884744 | tf_op jit(solution)/shard_map/ppermute | solution.py:762
  98.2 1.6 %last_own.1 = (f32[3,96,8,128]{3,2,1,0:T(8,128)}, f32[3,96,8,128]{3,2,1,0:T(8,128)}) custom-call(s32[1]{0:T(128)} %bitcast.side_ref, f32[2,4,8,128]{3,2,1,0:T(8,128)S(1)} %get-tuple-element.62.terms, f32[3,48,8,128]{3,2,1,0:T(8,128)S(1)} %collective-permute-done.10.refs_0_.before, f32[3,48,8,128]{3,2,1,0:T(8,128)S(1)} %get-tuple-element.52.refs_0_.refs_1_.before.here, ...), custom_call_target="tpu_custom_call" | custom-call | tf_op jit(solution)/shard_map/last_own/pallas_call | solution.py:573
  99.8 0.0 collective-permute-done.9.here
  99.8 6.3 %collective-permute-done.13.speed = f32[3,24,8,128]{3,2,1,0:T(8,128)S(1)} collective-permute-done((f32[3,24,8,128]{3,2,1,0:T(8,128)S(1)}, f32[3,24,8,128]{3,2,1,0:T(8,128)S(1)}, u32[]{:S(2)}, u32[]{:S(2)}) %collective-permute-start.13) | collective-permute-done | bytes 294944 | tf_op jit(solution)/shard_map/ppermute | solution.py:762
  106.1 0.9 last_join.2
  107.1 4.0 %collective-permute-done.12.speed = f32[3,24,8,128]{3,2,1,0:T(8,128)S(1)} collective-permute-done((f32[3,24,8,128]{3,2,1,0:T(8,128)S(1)}, f32[3,24,8,128]{3,2,1,0:T(8,128)S(1)}, u32[]{:S(2)}, u32[]{:S(2)}) %collective-permute-start.12) | collective-permute-done | bytes 294944 | tf_op jit(solution)/shard_map/ppermute | solution.py:762
  111.1 0.9 last_join.3
  (3 shorter events, 0.0 us)
Async XLA Ops:
  0.6 17.5 %copy-start = (f32[1,3,98304]{2,0,1:T(1,128)S(1)}, f32[1,3,98304]{2,0,1:T(1,128)}, u32[]{:S(2)}) copy-start(f32[1,3,98304]{2,0,1:T(1,128)} %param.3) | copy-start | bytes 3538948
  0.7 1.4 %copy-start.1 = (f32[1,3,98304]{2,0,1:T(1,128)S(1)}, f32[1,3,98304]{2,0,1:T(1,128)}, u32[]{:S(2)}) copy-start(f32[1,3,98304]{2,0,1:T(1,128)} %param.2) | copy-start | bytes 3538948
  2.3 23.1 %collective-permute-start.4 = (f32[3,48,8,128]{3,2,1,0:T(8,128)S(1)}, f32[3,48,8,128]{3,2,1,0:T(8,128)S(1)}, u32[]{:S(2)}, u32[]{:S(2)}) collective-permute-start(f32[3,48,8,128]{3,2,1,0:T(8,128)S(1)} %get-tuple-element.38.refs_0_.refs_2_), channel_id=1, source_target_pairs={{16,48},{32,0},{48,80},{64,32},{80,112},{96,64},{17,49},{33,1},{49... | collective-permute-start | bytes 1769480 | tf_op jit(solution)/shard_map/ppermute | solution.py:707
  3.6 11.0 %collective-permute-start = (f32[3,20,8,128]{3,2,1,0:T(8,128)S(1)}, f32[3,20,8,128]{3,2,1,0:T(8,128)S(1)}, u32[]{:S(2)}, u32[]{:S(2)}) collective-permute-start(f32[3,20,8,128]{3,2,1,0:T(8,128)S(1)} %get-tuple-element.36), channel_id=1, source_target_pairs={{0,16},{16,0},{32,48},{48,32},{64,80},{80,64},{96,112},{112,96},{1... | collective-permute-start | bytes 737288 | tf_op jit(solution)/shard_map/ppermute | solution.py:706
  7.8 17.5 %collective-permute-start.2 = (f32[3,32,8,128]{3,2,1,0:T(8,128)S(1)}, f32[3,32,8,128]{3,2,1,0:T(8,128)S(1)}, u32[]{:S(2)}, u32[]{:S(2)}) collective-permute-start(f32[3,32,8,128]{3,2,1,0:T(8,128)S(1)} %get-tuple-element.37), channel_id=1, source_target_pairs={{0,16},{16,0},{32,48},{48,32},{64,80},{80,64},{96,112},{112,96},{1... | collective-permute-start | bytes 1179656 | tf_op jit(solution)/shard_map/ppermute | solution.py:706
  14.7 10.7 %collective-permute-start.1 = (f32[3,20,8,128]{3,2,1,0:T(8,128)S(1)}, f32[3,20,8,128]{3,2,1,0:T(8,128)S(1)}, u32[]{:S(2)}, u32[]{:S(2)}) collective-permute-start(f32[3,20,8,128]{3,2,1,0:T(8,128)S(1)} %collective-permute-done.refs_3_.refs_4_), channel_id=1, source_target_pairs={{48,16},{0,32},{80,48},{32,64},{112,80},{64,96},{49,17},{1,33},{81... | collective-permute-start | bytes 737288 | tf_op jit(solution)/shard_map/ppermute | solution.py:710
  18.1 7.3 %collective-permute-start.5 = (f32[3,4,8,128]{3,2,1,0:T(8,128)S(1)}, f32[3,4,8,128]{3,2,1,0:T(8,128)S(1)}, u32[]{:S(2)}, u32[]{:S(2)}) collective-permute-start(f32[3,4,8,128]{3,2,1,0:T(8,128)S(1)} %pad_maximum_fusion), channel_id=1, source_target_pairs={{0,1},{1,2},{2,3},{3,4},{4,5},{5,6},{6,7},{7,8},{8,9},{9,10},{10,1... | collective-permute-start | bytes 147464 | tf_op jit(solution)/shard_map/ppermute | solution.py:709
  25.4 31.0 %collective-permute-start.6 = (f32[3,48,8,128]{3,2,1,0:T(8,128)S(1)}, f32[3,48,8,128]{3,2,1,0:T(8,128)S(1)}, u32[]{:S(2)}, u32[]{:S(2)}) collective-permute-start(f32[3,48,8,128]{3,2,1,0:T(8,128)S(1)} %get-tuple-element.47), channel_id=1, source_target_pairs={{0,16},{16,0},{32,48},{48,32},{64,80},{80,64},{96,112},{112,96},{1... | collective-permute-start | bytes 1769480 | tf_op jit(solution)/shard_map/ppermute | solution.py:725
  25.4 11.5 %collective-permute-start.3 = (f32[3,32,8,128]{3,2,1,0:T(8,128)S(1)}, f32[3,32,8,128]{3,2,1,0:T(8,128)S(1)}, u32[]{:S(2)}, u32[]{:S(2)}) collective-permute-start(f32[3,32,8,128]{3,2,1,0:T(8,128)S(1)} %collective-permute-done.2.refs_5_.refs_4_), channel_id=1, source_target_pairs={{48,16},{0,32},{80,48},{32,64},{112,80},{64,96},{49,17},{1,33},{81... | collective-permute-start | bytes 1179656 | tf_op jit(solution)/shard_map/ppermute | solution.py:710
  57.4 19.6 %collective-permute-start.11 = (f32[3,48,8,128]{3,2,1,0:T(8,128)S(1)}, f32[3,48,8,128]{3,2,1,0:T(8,128)S(1)}, u32[]{:S(2)}, u32[]{:S(2)}) collective-permute-start(f32[3,48,8,128]{3,2,1,0:T(8,128)S(1)} %get-tuple-element.52.refs_0_.refs_1_.before.here), channel_id=1, source_target_pairs={{16,48},{32,0},{48,80},{64,32},{80,112},{96,64},{17,49},{33,1},{49... | collective-permute-start | bytes 1769480 | tf_op jit(solution)/shard_map/ppermute | solution.py:754
  58.7 18.3 %collective-permute-start.10 = (f32[3,48,8,128]{3,2,1,0:T(8,128)S(1)}, f32[3,48,8,128]{3,2,1,0:T(8,128)S(1)}, u32[]{:S(2)}, u32[]{:S(2)}) collective-permute-start(f32[3,48,8,128]{3,2,1,0:T(8,128)S(1)} %get-tuple-element.51.refs_3_.refs_2_.here.after), channel_id=1, source_target_pairs={{48,16},{0,32},{80,48},{32,64},{112,80},{64,96},{49,17},{1,33},{81... | collective-permute-start | bytes 1769480 | tf_op jit(solution)/shard_map/ppermute | solution.py:751
  63.3 6.9 %collective-permute-start.7 = (f32[2,3,2,8,128]{4,3,2,1,0:T(8,128)S(1)}, f32[2,3,2,8,128]{4,3,2,1,0:T(8,128)S(1)}, u32[]{:S(2)}, u32[]{:S(2)}) collective-permute-start(f32[2,3,2,8,128]{4,3,2,1,0:T(8,128)S(1)} %get-tuple-element.49), channel_id=1, source_target_pairs={{0,16},{1,17},{2,18},{3,19},{4,20},{5,21},{6,22},{7,23},{8,24},{9,... | collective-permute-start | bytes 147464 | tf_op jit(solution)/shard_map/ppermute | solution.py:740
  63.4 6.8 %collective-permute-start.8 = (f32[2,3,2,8,128]{4,3,2,1,0:T(8,128)S(1)}, f32[2,3,2,8,128]{4,3,2,1,0:T(8,128)S(1)}, u32[]{:S(2)}, u32[]{:S(2)}) collective-permute-start(f32[2,3,2,8,128]{4,3,2,1,0:T(8,128)S(1)} %get-tuple-element.50), channel_id=1, source_target_pairs={{16,0},{17,1},{18,2},{19,3},{20,4},{21,5},{22,6},{23,7},{24,8},{25... | collective-permute-start | bytes 147464 | tf_op jit(solution)/shard_map/ppermute | solution.py:741
  70.2 29.6 %collective-permute-start.9 = (f32[3,48,8,128]{3,2,1,0:T(8,128)S(1)}, f32[3,48,8,128]{3,2,1,0:T(8,128)S(1)}, u32[]{:S(2)}, u32[]{:S(2)}) collective-permute-start(f32[3,48,8,128]{3,2,1,0:T(8,128)S(1)} %get-tuple-element.51.refs_3_.refs_2_.here.after), channel_id=1, source_target_pairs={{0,16},{16,0},{32,48},{48,32},{64,80},{80,64},{96,112},{112,96},{1... | collective-permute-start | bytes 1769480 | tf_op jit(solution)/shard_map/ppermute | solution.py:757
  96.1 10.0 %collective-permute-start.13 = (f32[3,24,8,128]{3,2,1,0:T(8,128)S(1)}, f32[3,24,8,128]{3,2,1,0:T(8,128)S(1)}, u32[]{:S(2)}, u32[]{:S(2)}) collective-permute-start(f32[3,24,8,128]{3,2,1,0:T(8,128)S(1)} %get-tuple-element.61), channel_id=1, source_target_pairs={{0,16},{16,0},{32,48},{48,32},{64,80},{80,64},{96,112},{112,96},{1... | collective-permute-start | bytes 884744 | tf_op jit(solution)/shard_map/ppermute | solution.py:762
  97.0 14.0 %collective-permute-start.12 = (f32[3,24,8,128]{3,2,1,0:T(8,128)S(1)}, f32[3,24,8,128]{3,2,1,0:T(8,128)S(1)}, u32[]{:S(2)}, u32[]{:S(2)}) collective-permute-start(f32[3,24,8,128]{3,2,1,0:T(8,128)S(1)} %get-tuple-element.60), channel_id=1, source_target_pairs={{0,16},{16,0},{32,48},{48,32},{64,80},{80,64},{96,112},{112,96},{1... | collective-permute-start | bytes 884744 | tf_op jit(solution)/shard_map/ppermute | solution.py:762

commit v7 on v6

--- a/solution.py
+++ b/solution.py
@@ -15,7 +15,7 @@
 EMBED_UNROLL = 48
 FINISH_UNROLL = 16
 REGIONS = 2
-PIECES = (16, 32)
+PIECES = (24, 24)
 JOIN_STEPS = 2
 
 lattice_const = 3.615
@@ -681,7 +681,8 @@
         return image * slabs + domain % slabs
 
     everyone = [(i, d) for i in range(images) for d in range(slabs)]
-    outward = [(at(i, d), at(i, d + 1 - 2 * (i % 2))) for i, d in everyone]
+    outer_own = [(at(i, d), at(i, d + 1 - 2 * (i % 2))) for i, d in everyone]
+    outer_partner = [(at(i, d), at(i ^ 1, d - 1 + 2 * (i % 2))) for i, d in everyone]
     across = [(i, i ^ 1) for i in range(images)]
     own_out = [(i, i - 2 + 4 * (i % 2)) for i in range(images)]
     own_out = [(a, b) for a, b in own_out if 0 <= b < images]
@@ -692,36 +693,40 @@
     end, top = planes - HALO, half + HALO
     piece = PIECES[0]
     outer, inner = (0, top), (top, 0)
-    edge_own, near_inner, own, lead, rest = cut(
+    edge_own, edge_partner, near_inner, own, lead, rest = cut(
         side_arg,
         slab,
         (
             (((end, 0), HALO),),
+            (((0, end), HALO),),
             (((half, half - HALO), HALO),),
             (((0, half), half),),
-            (((half, 0), piece), ((half - HALO, half), HALO), ((0, end), HALO)),
+            (((half, 0), piece), ((half - HALO, half), HALO)),
             (((half + piece, piece), PIECES[1]),),
         ),
     )
+    halo_own = lax.ppermute(edge_own, both, outer_own)
+    halo_partner = lax.ppermute(edge_partner, both, outer_partner)
+    rest, halo_own, halo_partner = lax.optimization_barrier(
+        (rest, halo_own, halo_partner)
+    )
     partner = [lax.ppermute(part, "image", across) for part in (lead, rest)]
     beyond_own = lax.ppermute(own, "image", own_out)
-    edges = jnp.concatenate([edge_own, partner[0][:, piece + HALO :]], axis=1)
-    halo = lax.ppermute(edges, both, outward)
     beyond_partner = [lax.ppermute(part, "image", partner_out) for part in partner]
     own_source = (
         (own, None, 0, half, (HALO, HALO)),
-        (halo, None, 0, HALO, outer),
+        (halo_own, None, 0, HALO, outer),
         (near_inner, None, 0, HALO, inner),
     )
     partner_source = (
         (partner[0], None, 0, piece, (HALO, HALO)),
         (partner[0], None, piece, HALO, inner),
         (partner[1], None, 0, PIECES[1], (HALO + piece,) * 2),
-        (halo, None, HALO, HALO, outer),
+        (halo_partner, None, 0, HALO, outer),
     )
     forces, energies = image_forces(side_arg, half, (own_source, partner_source))
     far_speed, slab_sq = cut(side_arg, slab_speed, ((((half, 0), half),),), True)
-    far_speed, *_ = lax.optimization_barrier((far_speed, halo, beyond_partner[0], beyond_own))
+    far_speed, *_ = lax.optimization_barrier((far_speed, partner[0]))
     partner_speed = lax.ppermute(far_speed, "image", across)
 
     path = (beyond_partner, [own], partner, [beyond_own])

time: 112 us -> 109 us (0.973)
  waiting for transfers between devices: 27.3 us -> 15.9 us
  starting transfers between devices: 25.3 us -> 32.1 us
  blocking collectives: 36.5 us -> 38 us
    ppermute x1 -> x2, waiting for transfers between devices: 6.91 us -> 0.6 us  [the longest x1 0.6 us: local(): halo_own = lax.ppermute(edge_own, both, outer_own)]
    ppermute x1 -> x2, starting transfers between devices: 0.07 us -> 5.09 us  [the longest x1 5.09 us: local(): halo_partner = lax.ppermute(edge_partner, both, outer_partner)]
    ppermute x2, waiting for transfers between devices: 6.73 us -> 2.75 us  [local(): partner = [lax.ppermute(part, 'image', across) for part in (lead, rest)]]
    ppermute x2, starting transfers between devices: 6.48 us -> 8.06 us  [local(): lax.ppermute(part, 'image', partner_out)]
    all_to_all x2, blocking collectives: 36.5 us -> 38 us  [local(): gathered = lax.all_to_all(payload, both, 0, 0, tiled=True)]
  transfers between devices with their start and end apart: 14 -> 15, of which waited for: 6 -> 6; matrix products, arithmetic and copies ran while one was open for 0% -> 0% of each run, Pallas kernels for 16% -> 17%
where the time goes in v7:
time: 109 us
  blocking collectives  38 us (35%)
  starting transfers between devices  32.1 us (29%)
  Pallas kernels  20.4 us (19%)
  waiting for transfers between devices  15.9 us (15%)
  local copies, waits for them, and re-layouts  1.36 us (1%)
    all_to_all x2, blocking collectives, local(): gathered = lax.all_to_all(payload, both, 0, 0, tiled=True)  38 us
    pallas_call x2, Pallas kernels, image_forces(): pl.pallas_call(functools.partial(force_kernel, layouts), out_shape=(jax.S...  13.5 us
    ppermute x2, waiting for transfers between devices, local(): last_speeds = [lax.ppermute(part, 'image', across) for part in last_speeds]  10.3 us
    ppermute x2, starting transfers between devices, local(): lax.ppermute(part, 'image', partner_out)  8.06 us
    ppermute x1, starting transfers between devices, local(): halo_partner = lax.ppermute(edge_partner, both, outer_partner)  5.09 us
    ppermute x1, starting transfers between devices, local(): high = lax.ppermute(bottoms, both, downward)  5.05 us
    ppermute x1, starting transfers between devices, local(): lax.ppermute(moved[1], 'image', partner_out)  4.58 us
    ppermute x2, starting transfers between devices, local(): partner = [lax.ppermute(part, 'image', across) for part in (lead, rest)]  4.28 us
  transfers between devices with their start and end apart: 15, of which 6 were waited for; matrix products, arithmetic and copies ran while one was open for 0% of the time, Pallas kernels for 17%

profile of v7, /device:TPU:0, one launch (start us, length us, event | category | flops | bytes accessed | tf_op | source)
XLA Modules:
  0.0 108.6 jit_solution(10553471177121096882)
XLA Ops:
  0.6 0.0 copy-start
  0.7 0.0 copy-start.1
  0.7 1.4 %copy-done.1 = f32[1,3,98304]{2,0,1:T(1,128)S(1)} copy-done((f32[1,3,98304]{2,0,1:T(1,128)S(1)}, f32[1,3,98304]{2,0,1:T(1,128)}, u32[]{:S(2)}) %copy-start.1) | copy-done | bytes 1179672
  2.0 0.2 cut.2
  2.2 2.1 %collective-permute-start = (f32[3,26,8,128]{3,2,1,0:T(8,128)S(1)}, f32[3,26,8,128]{3,2,1,0:T(8,128)S(1)}, u32[]{:S(2)}, u32[]{:S(2)}) collective-permute-start(f32[3,26,8,128]{3,2,1,0:T(8,128)S(1)} %get-tuple-element.40), channel_id=1, source_target_pairs={{0,16},{16,0},{32,48},{48,32},{64,80},{80,64},{96,112},{112,96},{1... | collective-permute-start | bytes 958472 | tf_op jit(solution)/shard_map/ppermute | solution.py:713
  4.3 0.0 collective-permute-start.2
  4.3 5.1 %collective-permute-start.3 = (f32[3,2,8,128]{3,2,1,0:T(8,128)S(1)}, f32[3,2,8,128]{3,2,1,0:T(8,128)S(1)}, u32[]{:S(2)}, u32[]{:S(2)}) collective-permute-start(f32[3,2,8,128]{3,2,1,0:T(8,128)S(1)} %get-tuple-element.43), channel_id=1, source_target_pairs={{0,31},{1,16},{2,17},{3,18},{4,19},{5,20},{6,21},{7,22},{8,23},{9,... | collective-permute-start | bytes 73736 | tf_op jit(solution)/shard_map/ppermute | solution.py:709
  9.4 1.3 %collective-permute-start.6 = (f32[3,48,8,128]{3,2,1,0:T(8,128)S(1)}, f32[3,48,8,128]{3,2,1,0:T(8,128)S(1)}, u32[]{:S(2)}, u32[]{:S(2)}) collective-permute-start(f32[3,48,8,128]{3,2,1,0:T(8,128)S(1)} %get-tuple-element.45.refs_0_.refs_2_), channel_id=1, source_target_pairs={{16,48},{32,0},{48,80},{64,32},{80,112},{96,64},{17,49},{33,1},{49... | collective-permute-start | bytes 1769480 | tf_op jit(solution)/shard_map/ppermute | solution.py:714
  10.7 0.6 collective-permute-done.2.refs_1_
  11.3 0.0 collective-permute-done.3.refs_6_
  11.3 2.2 %collective-permute-start.4 = (f32[3,24,8,128]{3,2,1,0:T(8,128)S(1)}, f32[3,24,8,128]{3,2,1,0:T(8,128)S(1)}, u32[]{:S(2)}, u32[]{:S(2)}) collective-permute-start(f32[3,24,8,128]{3,2,1,0:T(8,128)S(1)} %get-tuple-element.44), channel_id=1, source_target_pairs={{0,16},{16,0},{32,48},{48,32},{64,80},{80,64},{96,112},{112,96},{1... | collective-permute-start | bytes 884744 | tf_op jit(solution)/shard_map/ppermute | solution.py:713
  13.5 0.0 copy-done
  13.5 0.3 cut.3
  13.8 0.0 collective-permute-done.refs_3_.refs_4_
  13.8 0.3 collective-permute-start.7
  14.1 3.6 %collective-permute-start.1 = (f32[3,26,8,128]{3,2,1,0:T(8,128)S(1)}, f32[3,26,8,128]{3,2,1,0:T(8,128)S(1)}, u32[]{:S(2)}, u32[]{:S(2)}) collective-permute-start(f32[3,26,8,128]{3,2,1,0:T(8,128)S(1)} %collective-permute-done.refs_3_.refs_4_), channel_id=1, source_target_pairs={{48,16},{0,32},{80,48},{32,64},{112,80},{64,96},{49,17},{1,33},{81... | collective-permute-start | bytes 958472 | tf_op jit(solution)/shard_map/ppermute | solution.py:715
  17.7 2.8 %collective-permute-done.4.refs_5_.refs_4_ = f32[3,24,8,128]{3,2,1,0:T(8,128)S(1)} collective-permute-done((f32[3,24,8,128]{3,2,1,0:T(8,128)S(1)}, f32[3,24,8,128]{3,2,1,0:T(8,128)S(1)}, u32[]{:S(2)}, u32[]{:S(2)}) %collective-permute-start.4) | collective-permute-done | bytes 294944 | tf_op jit(solution)/shard_map/ppermute | solution.py:713
  20.5 4.4 %collective-permute-start.5 = (f32[3,24,8,128]{3,2,1,0:T(8,128)S(1)}, f32[3,24,8,128]{3,2,1,0:T(8,128)S(1)}, u32[]{:S(2)}, u32[]{:S(2)}) collective-permute-start(f32[3,24,8,128]{3,2,1,0:T(8,128)S(1)} %collective-permute-done.4.refs_5_.refs_4_), channel_id=1, source_target_pairs={{48,16},{0,32},{80,48},{32,64},{112,80},{64,96},{49,17},{1,33},{81... | collective-permute-start | bytes 884744 | tf_op jit(solution)/shard_map/ppermute | solution.py:715
  24.9 6.7 %slab_forces.2 = (f32[3,48,8,128]{3,2,1,0:T(8,128)S(1)}, f32[8,128]{1,0:T(8,128)S(1)}, f32[3,48,8,128]{3,2,1,0:T(8,128)S(1)}, f32[8,128]{1,0:T(8,128)S(1)}) custom-call(s32[1]{0:T(128)} %bitcast.side_ref, f32[3,48,8,128]{3,2,1,0:T(8,128)S(1)} %get-tuple-element.45.refs_0_.refs_2_, f32[3,2,8,128]{3,2,1,0:T(8,128)S(1)} %collective-permute-done.2.refs_1_, ...), custom_call_target="tpu_custom_call" | custom-call | flops 40000000 | bytes 30000000 | tf_op jit(solution)/shard_map/slab_forces/pallas_call | solution.py:268
  31.6 0.0 collective-permute-done.6.refs_5_
  31.6 0.4 collective-permute-done.5.refs_1_
  32.0 0.0 collective-permute-done.1.refs_0_
  32.0 0.7 path_moments.2
  32.7 20.2 %all_to_all.22 = f32[128,1,128]{2,1,0:T(1,128)S(1)} all-to-all(f32[128,1,128]{2,1,0:T(1,128)S(1)} %bitcast.18), channel_id=1, replica_groups=mesh['image'=8,'domain'=16] {'image','domain'}, dimensions={0} | all-to-all | bytes 131072 | tf_op jit(solution)/shard_map/all_to_all | solution.py:739
  53.0 0.0 collective-permute-done.7.refs_8_
  53.0 1.0 fire_update.1
  54.0 1.3 %collective-permute-start.12 = (f32[3,48,8,128]{3,2,1,0:T(8,128)S(1)}, f32[3,48,8,128]{3,2,1,0:T(8,128)S(1)}, u32[]{:S(2)}, u32[]{:S(2)}) collective-permute-start(f32[3,48,8,128]{3,2,1,0:T(8,128)S(1)} %get-tuple-element.60.refs_0_.refs_1_.before.here), channel_id=1, source_target_pairs={{16,48},{32,0},{48,80},{64,32},{80,112},{96,64},{17,49},{33,1},{49... | collective-permute-start | bytes 1769480 | tf_op jit(solution)/shard_map/ppermute | solution.py:759
  55.3 4.6 %collective-permute-start.11 = (f32[3,48,8,128]{3,2,1,0:T(8,128)S(1)}, f32[3,48,8,128]{3,2,1,0:T(8,128)S(1)}, u32[]{:S(2)}, u32[]{:S(2)}) collective-permute-start(f32[3,48,8,128]{3,2,1,0:T(8,128)S(1)} %get-tuple-element.59.refs_3_.refs_2_.here.after), channel_id=1, source_target_pairs={{48,16},{0,32},{80,48},{32,64},{112,80},{64,96},{49,17},{1,33},{81... | collective-permute-start | bytes 1769480 | tf_op jit(solution)/shard_map/ppermute | solution.py:756
  59.9 0.1 collective-permute-start.8
  60.0 5.1 %collective-permute-start.9 = (f32[2,3,2,8,128]{4,3,2,1,0:T(8,128)S(1)}, f32[2,3,2,8,128]{4,3,2,1,0:T(8,128)S(1)}, u32[]{:S(2)}, u32[]{:S(2)}) collective-permute-start(f32[2,3,2,8,128]{4,3,2,1,0:T(8,128)S(1)} %get-tuple-element.58), channel_id=1, source_target_pairs={{16,0},{17,1},{18,2},{19,3},{20,4},{21,5},{22,6},{23,7},{24,8},{25... | collective-permute-start | bytes 147464 | tf_op jit(solution)/shard_map/ppermute | solution.py:746
  65.0 1.8 %collective-permute-done.8.refs_1_.refs_4_ = f32[2,3,2,8,128]{4,3,2,1,0:T(8,128)S(1)} collective-permute-done((f32[2,3,2,8,128]{4,3,2,1,0:T(8,128)S(1)}, f32[2,3,2,8,128]{4,3,2,1,0:T(8,128)S(1)}, u32[]{:S(2)}, u32[]{:S(2)}) %collective-permute-start.8) | collective-permute-done | bytes 49184 | tf_op jit(solution)/shard_map/ppermute | solution.py:745
  66.8 0.0 collective-permute-done.9.refs_2_.refs_5_
  66.8 0.0 collective-permute-start.10
  66.8 6.8 %slab_forces.3 = (f32[3,48,8,128]{3,2,1,0:T(8,128)S(1)}, f32[8,128]{1,0:T(8,128)S(1)}, f32[3,48,8,128]{3,2,1,0:T(8,128)S(1)}, f32[8,128]{1,0:T(8,128)S(1)}) custom-call(s32[1]{0:T(128)} %bitcast.side_ref, f32[3,48,8,128]{3,2,1,0:T(8,128)S(1)} %get-tuple-element.60.refs_0_.refs_1_.before.here, ...), custom_call_target="tpu_custom_call" | custom-call | flops 40000000 | bytes 30000000 | tf_op jit(solution)/shard_map/slab_forces/pallas_call | solution.py:268
  73.6 0.0 collective-permute-done.12.refs_3_.after
  73.6 0.0 collective-permute-done.11.refs_0_.before
  73.6 0.7 path_moments.3
  74.3 17.8 %all_to_all.23 = f32[128,1,128]{2,1,0:T(1,128)S(1)} all-to-all(f32[128,1,128]{2,1,0:T(1,128)S(1)} %bitcast.19), channel_id=1, replica_groups=mesh['image'=8,'domain'=16] {'image','domain'}, dimensions={0} | all-to-all | bytes 131072 | tf_op jit(solution)/shard_map/all_to_all | solution.py:739
  92.1 0.6 last_partner.1
  92.7 0.9 collective-permute-start.14
  93.7 1.2 %collective-permute-start.13 = (f32[3,24,8,128]{3,2,1,0:T(8,128)S(1)}, f32[3,24,8,128]{3,2,1,0:T(8,128)S(1)}, u32[]{:S(2)}, u32[]{:S(2)}) collective-permute-start(f32[3,24,8,128]{3,2,1,0:T(8,128)S(1)} %get-tuple-element.68), channel_id=1, source_target_pairs={{0,16},{16,0},{32,48},{48,32},{64,80},{80,64},{96,112},{112,96},{1... | collective-permute-start | bytes 884744 | tf_op jit(solution)/shard_map/ppermute | solution.py:767
  94.8 1.6 %last_own.1 = (f32[3,96,8,128]{3,2,1,0:T(8,128)}, f32[3,96,8,128]{3,2,1,0:T(8,128)}) custom-call(s32[1]{0:T(128)} %bitcast.side_ref, f32[2,4,8,128]{3,2,1,0:T(8,128)S(1)} %get-tuple-element.70.terms, f32[3,48,8,128]{3,2,1,0:T(8,128)S(1)} %collective-permute-done.11.refs_0_.before, f32[3,48,8,128]{3,2,1,0:T(8,128)S(1)} %get-tuple-element.60.refs_0_.refs_1_.before.here, ...), custom_call_target="tpu_custom_call" | custom-call | tf_op jit(solution)/shard_map/last_own/pallas_call | solution.py:573
  96.4 0.0 collective-permute-done.10.here
  96.4 6.3 %collective-permute-done.14.speed = f32[3,24,8,128]{3,2,1,0:T(8,128)S(1)} collective-permute-done((f32[3,24,8,128]{3,2,1,0:T(8,128)S(1)}, f32[3,24,8,128]{3,2,1,0:T(8,128)S(1)}, u32[]{:S(2)}, u32[]{:S(2)}) %collective-permute-start.14) | collective-permute-done | bytes 294944 | tf_op jit(solution)/shard_map/ppermute | solution.py:767
  102.8 0.9 last_join.2
  103.7 4.0 %collective-permute-done.13.speed = f32[3,24,8,128]{3,2,1,0:T(8,128)S(1)} collective-permute-done((f32[3,24,8,128]{3,2,1,0:T(8,128)S(1)}, f32[3,24,8,128]{3,2,1,0:T(8,128)S(1)}, u32[]{:S(2)}, u32[]{:S(2)}) %collective-permute-start.13) | collective-permute-done | bytes 294944 | tf_op jit(solution)/shard_map/ppermute | solution.py:767
  107.7 0.9 last_join.3
  (1 shorter events, 0.0 us)
Async XLA Ops:
  0.6 12.8 %copy-start = (f32[1,3,98304]{2,0,1:T(1,128)S(1)}, f32[1,3,98304]{2,0,1:T(1,128)}, u32[]{:S(2)}) copy-start(f32[1,3,98304]{2,0,1:T(1,128)} %param.3) | copy-start | bytes 3538948
  0.7 1.4 %copy-start.1 = (f32[1,3,98304]{2,0,1:T(1,128)S(1)}, f32[1,3,98304]{2,0,1:T(1,128)}, u32[]{:S(2)}) copy-start(f32[1,3,98304]{2,0,1:T(1,128)} %param.2) | copy-start | bytes 3538948
  2.2 11.6 %collective-permute-start = (f32[3,26,8,128]{3,2,1,0:T(8,128)S(1)}, f32[3,26,8,128]{3,2,1,0:T(8,128)S(1)}, u32[]{:S(2)}, u32[]{:S(2)}) collective-permute-start(f32[3,26,8,128]{3,2,1,0:T(8,128)S(1)} %get-tuple-element.40), channel_id=1, source_target_pairs={{0,16},{16,0},{32,48},{48,32},{64,80},{80,64},{96,112},{112,96},{1... | collective-permute-start | bytes 958472 | tf_op jit(solution)/shard_map/ppermute | solution.py:713
  4.3 7.0 %collective-permute-start.2 = (f32[3,2,8,128]{3,2,1,0:T(8,128)S(1)}, f32[3,2,8,128]{3,2,1,0:T(8,128)S(1)}, u32[]{:S(2)}, u32[]{:S(2)}) collective-permute-start(f32[3,2,8,128]{3,2,1,0:T(8,128)S(1)} %get-tuple-element.42), channel_id=1, source_target_pairs={{0,1},{1,2},{2,3},{3,4},{4,5},{5,6},{6,7},{7,8},{8,9},{9,10},{10,1... | collective-permute-start | bytes 73736 | tf_op jit(solution)/shard_map/ppermute | solution.py:708
  4.3 7.0 %collective-permute-start.3 = (f32[3,2,8,128]{3,2,1,0:T(8,128)S(1)}, f32[3,2,8,128]{3,2,1,0:T(8,128)S(1)}, u32[]{:S(2)}, u32[]{:S(2)}) collective-permute-start(f32[3,2,8,128]{3,2,1,0:T(8,128)S(1)} %get-tuple-element.43), channel_id=1, source_target_pairs={{0,31},{1,16},{2,17},{3,18},{4,19},{5,20},{6,21},{7,22},{8,23},{9,... | collective-permute-start | bytes 73736 | tf_op jit(solution)/shard_map/ppermute | solution.py:709
  9.4 22.2 %collective-permute-start.6 = (f32[3,48,8,128]{3,2,1,0:T(8,128)S(1)}, f32[3,48,8,128]{3,2,1,0:T(8,128)S(1)}, u32[]{:S(2)}, u32[]{:S(2)}) collective-permute-start(f32[3,48,8,128]{3,2,1,0:T(8,128)S(1)} %get-tuple-element.45.refs_0_.refs_2_), channel_id=1, source_target_pairs={{16,48},{32,0},{48,80},{64,32},{80,112},{96,64},{17,49},{33,1},{49... | collective-permute-start | bytes 1769480 | tf_op jit(solution)/shard_map/ppermute | solution.py:714
  11.3 9.2 %collective-permute-start.4 = (f32[3,24,8,128]{3,2,1,0:T(8,128)S(1)}, f32[3,24,8,128]{3,2,1,0:T(8,128)S(1)}, u32[]{:S(2)}, u32[]{:S(2)}) collective-permute-start(f32[3,24,8,128]{3,2,1,0:T(8,128)S(1)} %get-tuple-element.44), channel_id=1, source_target_pairs={{0,16},{16,0},{32,48},{48,32},{64,80},{80,64},{96,112},{112,96},{1... | collective-permute-start | bytes 884744 | tf_op jit(solution)/shard_map/ppermute | solution.py:713
  13.8 39.2 %collective-permute-start.7 = (f32[3,48,8,128]{3,2,1,0:T(8,128)S(1)}, f32[3,48,8,128]{3,2,1,0:T(8,128)S(1)}, u32[]{:S(2)}, u32[]{:S(2)}) collective-permute-start(f32[3,48,8,128]{3,2,1,0:T(8,128)S(1)} %get-tuple-element.55), channel_id=1, source_target_pairs={{0,16},{16,0},{32,48},{48,32},{64,80},{80,64},{96,112},{112,96},{1... | collective-permute-start | bytes 1769480 | tf_op jit(solution)/shard_map/ppermute | solution.py:730
  14.1 17.9 %collective-permute-start.1 = (f32[3,26,8,128]{3,2,1,0:T(8,128)S(1)}, f32[3,26,8,128]{3,2,1,0:T(8,128)S(1)}, u32[]{:S(2)}, u32[]{:S(2)}) collective-permute-start(f32[3,26,8,128]{3,2,1,0:T(8,128)S(1)} %collective-permute-done.refs_3_.refs_4_), channel_id=1, source_target_pairs={{48,16},{0,32},{80,48},{32,64},{112,80},{64,96},{49,17},{1,33},{81... | collective-permute-start | bytes 958472 | tf_op jit(solution)/shard_map/ppermute | solution.py:715
  20.5 11.5 %collective-permute-start.5 = (f32[3,24,8,128]{3,2,1,0:T(8,128)S(1)}, f32[3,24,8,128]{3,2,1,0:T(8,128)S(1)}, u32[]{:S(2)}, u32[]{:S(2)}) collective-permute-start(f32[3,24,8,128]{3,2,1,0:T(8,128)S(1)} %collective-permute-done.4.refs_5_.refs_4_), channel_id=1, source_target_pairs={{48,16},{0,32},{80,48},{32,64},{112,80},{64,96},{49,17},{1,33},{81... | collective-permute-start | bytes 884744 | tf_op jit(solution)/shard_map/ppermute | solution.py:715
  54.0 19.6 %collective-permute-start.12 = (f32[3,48,8,128]{3,2,1,0:T(8,128)S(1)}, f32[3,48,8,128]{3,2,1,0:T(8,128)S(1)}, u32[]{:S(2)}, u32[]{:S(2)}) collective-permute-start(f32[3,48,8,128]{3,2,1,0:T(8,128)S(1)} %get-tuple-element.60.refs_0_.refs_1_.before.here), channel_id=1, source_target_pairs={{16,48},{32,0},{48,80},{64,32},{80,112},{96,64},{17,49},{33,1},{49... | collective-permute-start | bytes 1769480 | tf_op jit(solution)/shard_map/ppermute | solution.py:759
  55.3 18.3 %collective-permute-start.11 = (f32[3,48,8,128]{3,2,1,0:T(8,128)S(1)}, f32[3,48,8,128]{3,2,1,0:T(8,128)S(1)}, u32[]{:S(2)}, u32[]{:S(2)}) collective-permute-start(f32[3,48,8,128]{3,2,1,0:T(8,128)S(1)} %get-tuple-element.59.refs_3_.refs_2_.here.after), channel_id=1, source_target_pairs={{48,16},{0,32},{80,48},{32,64},{112,80},{64,96},{49,17},{1,33},{81... | collective-permute-start | bytes 1769480 | tf_op jit(solution)/shard_map/ppermute | solution.py:756
  59.9 6.9 %collective-permute-start.8 = (f32[2,3,2,8,128]{4,3,2,1,0:T(8,128)S(1)}, f32[2,3,2,8,128]{4,3,2,1,0:T(8,128)S(1)}, u32[]{:S(2)}, u32[]{:S(2)}) collective-permute-start(f32[2,3,2,8,128]{4,3,2,1,0:T(8,128)S(1)} %get-tuple-element.57), channel_id=1, source_target_pairs={{0,16},{1,17},{2,18},{3,19},{4,20},{5,21},{6,22},{7,23},{8,24},{9,... | collective-permute-start | bytes 147464 | tf_op jit(solution)/shard_map/ppermute | solution.py:745
  60.0 6.8 %collective-permute-start.9 = (f32[2,3,2,8,128]{4,3,2,1,0:T(8,128)S(1)}, f32[2,3,2,8,128]{4,3,2,1,0:T(8,128)S(1)}, u32[]{:S(2)}, u32[]{:S(2)}) collective-permute-start(f32[2,3,2,8,128]{4,3,2,1,0:T(8,128)S(1)} %get-tuple-element.58), channel_id=1, source_target_pairs={{16,0},{17,1},{18,2},{19,3},{20,4},{21,5},{22,6},{23,7},{24,8},{25... | collective-permute-start | bytes 147464 | tf_op jit(solution)/shard_map/ppermute | solution.py:746
  66.8 29.6 %collective-permute-start.10 = (f32[3,48,8,128]{3,2,1,0:T(8,128)S(1)}, f32[3,48,8,128]{3,2,1,0:T(8,128)S(1)}, u32[]{:S(2)}, u32[]{:S(2)}) collective-permute-start(f32[3,48,8,128]{3,2,1,0:T(8,128)S(1)} %get-tuple-element.59.refs_3_.refs_2_.here.after), channel_id=1, source_target_pairs={{0,16},{16,0},{32,48},{48,32},{64,80},{80,64},{96,112},{112,96},{1... | collective-permute-start | bytes 1769480 | tf_op jit(solution)/shard_map/ppermute | solution.py:762
  92.7 10.0 %collective-permute-start.14 = (f32[3,24,8,128]{3,2,1,0:T(8,128)S(1)}, f32[3,24,8,128]{3,2,1,0:T(8,128)S(1)}, u32[]{:S(2)}, u32[]{:S(2)}) collective-permute-start(f32[3,24,8,128]{3,2,1,0:T(8,128)S(1)} %get-tuple-element.69), channel_id=1, source_target_pairs={{0,16},{16,0},{32,48},{48,32},{64,80},{80,64},{96,112},{112,96},{1... | collective-permute-start | bytes 884744 | tf_op jit(solution)/shard_map/ppermute | solution.py:767
  93.7 14.0 %collective-permute-start.13 = (f32[3,24,8,128]{3,2,1,0:T(8,128)S(1)}, f32[3,24,8,128]{3,2,1,0:T(8,128)S(1)}, u32[]{:S(2)}, u32[]{:S(2)}) collective-permute-start(f32[3,24,8,128]{3,2,1,0:T(8,128)S(1)} %get-tuple-element.68), channel_id=1, source_target_pairs={{0,16},{16,0},{32,48},{48,32},{64,80},{80,64},{96,112},{112,96},{1... | collective-permute-start | bytes 884744 | tf_op jit(solution)/shard_map/ppermute | solution.py:767

commit v8 on v7

--- a/solution.py
+++ b/solution.py
@@ -12,8 +12,6 @@
 FIRE_STEPS = 2
 QUANTITIES = 8
 HALO = 2
-EMBED_UNROLL = 48
-FINISH_UNROLL = 16
 REGIONS = 2
 PIECES = (24, 24)
 JOIN_STEPS = 2
@@ -174,22 +172,18 @@
         back[0, e + 1] = dens[1] + dens[4]
         back[1, e + 1] = dens[2] + dens[5]
         back[2, e + 1] = dens[3]
-        weight = jnp.where((e >= 1) & (e <= planes), 1.0, 0.0).astype(f32)
-        sum_f = sum_f + weight * (cross + inside)
-        sum_c = sum_c + weight * (
-            ((cubes[0] + cubes[1]) + (cubes[2] + cubes[3])) + (cubes[4] + cubes[5])
-        )
+        if 1 <= e <= planes:
+            sum_f = sum_f + (cross + inside)
+            sum_c = sum_c + (((cubes[0] + cubes[1]) + (cubes[2] + cubes[3])) + (cubes[4] + cubes[5]))
         return (dens[0] + inside, sum_f, sum_c)
 
     down = limits(-1, site_u, site_v)
     up = limits(1, site_u, site_v)
 
-    def density_pair(t, carry):
-        carry = density(2 * t, -1, down, carry)
-        return density(2 * t + 1, 1, up, carry)
-
-    carry = lax.fori_loop(0, planes // 2 + 1, density_pair, (zero, zero, zero))
-    _, sum_f, sum_c = density(planes + 2, -1, down, carry)
+    carry = (zero, zero, zero)
+    for e in range(planes + 2 * HALO - 1):
+        carry = density(e, (-1, 1)[e % 2], (down, up)[e % 2], carry)
+    _, sum_f, sum_c = carry
 
     def embedding(q, side):
         total = rho[q] + gather_back(back[0, q], back[1, q], back[2, q], side, lanes)
@@ -201,12 +195,9 @@
     embedding(1, side_of(1))
     embedding(planes + HALO, side_of(0))
 
-    def embed_some(t, total):
-        for j in range(EMBED_UNROLL):
-            total = total + embedding(HALO + t * EMBED_UNROLL + j, side_of(j))
-        return total
-
-    roots = lax.fori_loop(0, planes // EMBED_UNROLL, embed_some, zero)
+    roots = zero
+    for q in range(HALO, HALO + planes):
+        roots = roots + embedding(q, side_of(q))
     energy_ref[...] = f32(-embed_scale) * roots + f32(pair_energy_scale) * (
         sum_f + f32(pair_shift - dens_shift) * sum_c
     )
@@ -215,14 +206,8 @@
         for k, seen in enumerate(partners(embed[0, q], side, lanes)):
             embed[1 + k, q] = seen
 
-    see(planes + HALO, side_of(0))
-
-    def see_some(t, carry):
-        for j in range(EMBED_UNROLL):
-            see(HALO + t * EMBED_UNROLL + j, side_of(j))
-        return carry
-
-    lax.fori_loop(0, planes // EMBED_UNROLL, see_some, 0)
+    for q in range(HALO, HALO + planes + 1):
+        see(q, side_of(q))
 
     def force(e, keep, carry):
         own = embed[0, e]
@@ -241,23 +226,16 @@
             out.append((g[4] + g[5]) - g[0])
         return tuple(out)
 
-    def force_pair(t, carry):
-        carry = force(HALO + 2 * t, True, carry)
-        return force(HALO + 2 * t + 1, True, carry)
-
-    lax.fori_loop(0, planes // 2, force_pair, force(1, False, (zero, zero, zero)))
-
-    def finish(t, carry):
-        for j in range(FINISH_UNROLL):
-            p = t * FINISH_UNROLL + j
-            for axis in range(3):
-                parts = [force_back[axis, k, p + HALO] for k in range(3)]
-                force_ref[axis, p] = f32(force_scale) * (
-                    force_ref[axis, p] - gather_back(*parts, side_of(j), lanes)
-                )
-        return carry
-
-    lax.fori_loop(0, planes // FINISH_UNROLL, finish, 0)
+    carry = force(1, False, (zero, zero, zero))
+    for e in range(HALO, HALO + planes):
+        carry = force(e, True, carry)
+
+    for p in range(planes):
+        for axis in range(3):
+            parts = [force_back[axis, k, p + HALO] for k in range(3)]
+            force_ref[axis, p] = f32(force_scale) * (
+                force_ref[axis, p] - gather_back(*parts, side_of(p), lanes)
+            )
 
 
 def image_forces(side, planes, images):
@@ -707,8 +685,8 @@
     )
     halo_own = lax.ppermute(edge_own, both, outer_own)
     halo_partner = lax.ppermute(edge_partner, both, outer_partner)
-    rest, halo_own, halo_partner = lax.optimization_barrier(
-        (rest, halo_own, halo_partner)
+    own, halo_own, halo_partner = lax.optimization_barrier(
+        (own, halo_own, halo_partner)
     )
     partner = [lax.ppermute(part, "image", across) for part in (lead, rest)]
     beyond_own = lax.ppermute(own, "image", own_out)

time: 109 us -> 109 us (level)
  Pallas kernels: 20.4 us -> 16.1 us
  waiting for transfers between devices: 15.9 us -> 19.4 us
    ppermute x2, waiting for transfers between devices: 0.4 us -> 5.11 us  [local(): lax.ppermute(part, 'image', partner_out)]
    pallas_call x2, Pallas kernels: 13.5 us -> 9.11 us  [image_forces(): pl.pallas_call(functools.partial(force_kernel, layouts), out_shape=(jax.S...]
    ppermute x1, starting transfers between devices: 0.32 us -> 4.42 us  [local(): partner_speed = lax.ppermute(far_speed, 'image', across)]
    ppermute x2, waiting for transfers between devices: 2.75 us -> 0.01 us  [local(): partner = [lax.ppermute(part, 'image', across) for part in (lead, rest)]]
    ppermute x2, starting transfers between devices: 4.28 us -> 2.32 us  [local(): partner = [lax.ppermute(part, 'image', across) for part in (lead, rest)]]
    ppermute x2, starting transfers between devices: 8.06 us -> 6.47 us  [local(): lax.ppermute(part, 'image', partner_out)]
  transfers between devices with their start and end apart: 15 -> 15, of which waited for: 6 -> 6; matrix products, arithmetic and copies ran while one was open for 0% -> 0% of each run, Pallas kernels for 17% -> 13%
where the time goes in v8:
time: 109 us; the launch traced here: 108 us
  blocking collectives  38.1 us (35%)
  starting transfers between devices  32.7 us (30%)
  waiting for transfers between devices  19.4 us (18%)
  Pallas kernels  16.1 us (15%)
  local copies, waits for them, and re-layouts  1.36 us (1%)
    all_to_all x2, blocking collectives, local(): gathered = lax.all_to_all(payload, both, 0, 0, tiled=True)  38.1 us
    ppermute x2, waiting for transfers between devices, local(): last_speeds = [lax.ppermute(part, 'image', across) for part in last_speeds]  10.3 us
    pallas_call x2, Pallas kernels, image_forces(): pl.pallas_call(functools.partial(force_kernel, layouts), out_shape=(jax.S...  9.11 us
    ppermute x2, starting transfers between devices, local(): lax.ppermute(part, 'image', partner_out)  6.47 us
    ppermute x2, waiting for transfers between devices, local(): lax.ppermute(part, 'image', partner_out)  5.11 us
    ppermute x1, starting transfers between devices, local(): halo_partner = lax.ppermute(edge_partner, both, outer_partner)  5.09 us
    ppermute x1, starting transfers between devices, local(): high = lax.ppermute(bottoms, both, downward)  5.05 us
    ppermute x1, starting transfers between devices, local(): lax.ppermute(moved[1], 'image', partner_out)  4.58 us
  transfers between devices with their start and end apart: 15, of which 6 were waited for; matrix products, arithmetic and copies ran while one was open for 0% of the time, Pallas kernels for 13%

profile of v8, /device:TPU:0, one launch (start us, length us, event | category | flops | bytes accessed | tf_op | source)
XLA Modules:
  0.0 108.4 jit_solution(1677280263945868028)
XLA Ops:
  0.6 0.0 copy-start
  0.7 0.0 copy-start.1
  0.7 1.4 %copy-done.1 = f32[1,3,98304]{2,0,1:T(1,128)S(1)} copy-done((f32[1,3,98304]{2,0,1:T(1,128)S(1)}, f32[1,3,98304]{2,0,1:T(1,128)}, u32[]{:S(2)}) %copy-start.1) | copy-done | bytes 1179672
  2.0 0.2 cut.2
  2.2 2.1 %collective-permute-start = (f32[3,26,8,128]{3,2,1,0:T(8,128)S(1)}, f32[3,26,8,128]{3,2,1,0:T(8,128)S(1)}, u32[]{:S(2)}, u32[]{:S(2)}) collective-permute-start(f32[3,26,8,128]{3,2,1,0:T(8,128)S(1)} %get-tuple-element.40), channel_id=1, source_target_pairs={{0,16},{16,0},{32,48},{48,32},{64,80},{80,64},{96,112},{112,96},{1... | collective-permute-start | bytes 958472 | tf_op jit(solution)/shard_map/ppermute | solution.py:691
  4.3 0.0 collective-permute-start.4
  4.3 5.1 %collective-permute-start.5 = (f32[3,2,8,128]{3,2,1,0:T(8,128)S(1)}, f32[3,2,8,128]{3,2,1,0:T(8,128)S(1)}, u32[]{:S(2)}, u32[]{:S(2)}) collective-permute-start(f32[3,2,8,128]{3,2,1,0:T(8,128)S(1)} %get-tuple-element.44), channel_id=1, source_target_pairs={{0,31},{1,16},{2,17},{3,18},{4,19},{5,20},{6,21},{7,22},{8,23},{9,... | collective-permute-start | bytes 73736 | tf_op jit(solution)/shard_map/ppermute | solution.py:687
  9.4 0.2 collective-permute-start.2
  9.6 1.6 %collective-permute-done.4.refs_1_ = f32[3,2,8,128]{3,2,1,0:T(8,128)S(1)} collective-permute-done((f32[3,2,8,128]{3,2,1,0:T(8,128)S(1)}, f32[3,2,8,128]{3,2,1,0:T(8,128)S(1)}, u32[]{:S(2)}, u32[]{:S(2)}) %collective-permute-start.4) | collective-permute-done | bytes 24608 | tf_op jit(solution)/shard_map/ppermute | solution.py:686
  11.3 0.0 collective-permute-done.5.refs_6_
  11.3 1.3 %collective-permute-start.6 = (f32[3,48,8,128]{3,2,1,0:T(8,128)S(1)}, f32[3,48,8,128]{3,2,1,0:T(8,128)S(1)}, u32[]{:S(2)}, u32[]{:S(2)}) collective-permute-start(f32[3,48,8,128]{3,2,1,0:T(8,128)S(1)} %get-tuple-element.45.refs_0_.refs_2_), channel_id=1, source_target_pairs={{16,48},{32,0},{48,80},{64,32},{80,112},{96,64},{17,49},{33,1},{49... | collective-permute-start | bytes 1769480 | tf_op jit(solution)/shard_map/ppermute | solution.py:692
  12.6 0.0 copy-done
  12.6 0.3 cut.3
  12.9 0.0 collective-permute-done.refs_3_.refs_4_
  12.9 4.4 %collective-permute-start.7 = (f32[3,48,8,128]{3,2,1,0:T(8,128)S(1)}, f32[3,48,8,128]{3,2,1,0:T(8,128)S(1)}, u32[]{:S(2)}, u32[]{:S(2)}) collective-permute-start(f32[3,48,8,128]{3,2,1,0:T(8,128)S(1)} %get-tuple-element.55), channel_id=1, source_target_pairs={{0,16},{16,0},{32,48},{48,32},{64,80},{80,64},{96,112},{112,96},{1... | collective-permute-start | bytes 1769480 | tf_op jit(solution)/shard_map/ppermute | solution.py:708
  17.3 3.4 %collective-permute-start.1 = (f32[3,26,8,128]{3,2,1,0:T(8,128)S(1)}, f32[3,26,8,128]{3,2,1,0:T(8,128)S(1)}, u32[]{:S(2)}, u32[]{:S(2)}) collective-permute-start(f32[3,26,8,128]{3,2,1,0:T(8,128)S(1)} %collective-permute-done.refs_3_.refs_4_), channel_id=1, source_target_pairs={{48,16},{0,32},{80,48},{32,64},{112,80},{64,96},{49,17},{1,33},{81... | collective-permute-start | bytes 958472 | tf_op jit(solution)/shard_map/ppermute | solution.py:693
  20.7 0.0 collective-permute-done.2.refs_5_.refs_4_
  20.7 3.1 %collective-permute-start.3 = (f32[3,24,8,128]{3,2,1,0:T(8,128)S(1)}, f32[3,24,8,128]{3,2,1,0:T(8,128)S(1)}, u32[]{:S(2)}, u32[]{:S(2)}) collective-permute-start(f32[3,24,8,128]{3,2,1,0:T(8,128)S(1)} %collective-permute-done.2.refs_5_.refs_4_), channel_id=1, source_target_pairs={{48,16},{0,32},{80,48},{32,64},{112,80},{64,96},{49,17},{1,33},{81... | collective-permute-start | bytes 884744 | tf_op jit(solution)/shard_map/ppermute | solution.py:693
  23.8 4.5 %slab_forces.2 = (f32[3,48,8,128]{3,2,1,0:T(8,128)S(1)}, f32[8,128]{1,0:T(8,128)S(1)}, f32[3,48,8,128]{3,2,1,0:T(8,128)S(1)}, f32[8,128]{1,0:T(8,128)S(1)}) custom-call(s32[1]{0:T(128)} %bitcast.side_ref, f32[3,48,8,128]{3,2,1,0:T(8,128)S(1)} %get-tuple-element.45.refs_0_.refs_2_, f32[3,2,8,128]{3,2,1,0:T(8,128)S(1)} %collective-permute-done.4.refs_1_, ...), custom_call_target="tpu_custom_call" | custom-call | flops 40000000 | bytes 30000000 | tf_op jit(solution)/shard_map/slab_forces/pallas_call | solution.py:246
  28.3 5.1 %collective-permute-done.3.refs_1_ = f32[3,24,8,128]{3,2,1,0:T(8,128)S(1)} collective-permute-done((f32[3,24,8,128]{3,2,1,0:T(8,128)S(1)}, f32[3,24,8,128]{3,2,1,0:T(8,128)S(1)}, u32[]{:S(2)}, u32[]{:S(2)}) %collective-permute-start.3) | collective-permute-done | bytes 294944 | tf_op jit(solution)/shard_map/ppermute | solution.py:693
  33.4 0.0 collective-permute-done.6.refs_5_
  33.4 0.0 collective-permute-done.1.refs_0_
  33.4 0.7 path_moments.2
  34.1 20.8 %all_to_all.22 = f32[128,1,128]{2,1,0:T(1,128)S(1)} all-to-all(f32[128,1,128]{2,1,0:T(1,128)S(1)} %bitcast.18), channel_id=1, replica_groups=mesh['image'=8,'domain'=16] {'image','domain'}, dimensions={0} | all-to-all | bytes 131072 | tf_op jit(solution)/shard_map/all_to_all | solution.py:717
  54.9 0.0 collective-permute-done.7.refs_8_
  54.9 1.0 fire_update.1
  56.0 1.3 %collective-permute-start.12 = (f32[3,48,8,128]{3,2,1,0:T(8,128)S(1)}, f32[3,48,8,128]{3,2,1,0:T(8,128)S(1)}, u32[]{:S(2)}, u32[]{:S(2)}) collective-permute-start(f32[3,48,8,128]{3,2,1,0:T(8,128)S(1)} %get-tuple-element.60.refs_0_.refs_1_.before.here), channel_id=1, source_target_pairs={{16,48},{32,0},{48,80},{64,32},{80,112},{96,64},{17,49},{33,1},{49... | collective-permute-start | bytes 1769480 | tf_op jit(solution)/shard_map/ppermute | solution.py:737
  57.2 4.6 %collective-permute-start.11 = (f32[3,48,8,128]{3,2,1,0:T(8,128)S(1)}, f32[3,48,8,128]{3,2,1,0:T(8,128)S(1)}, u32[]{:S(2)}, u32[]{:S(2)}) collective-permute-start(f32[3,48,8,128]{3,2,1,0:T(8,128)S(1)} %get-tuple-element.59.refs_3_.refs_2_.here.after), channel_id=1, source_target_pairs={{48,16},{0,32},{80,48},{32,64},{112,80},{64,96},{49,17},{1,33},{81... | collective-permute-start | bytes 1769480 | tf_op jit(solution)/shard_map/ppermute | solution.py:734
  61.8 0.1 collective-permute-start.8
  61.9 5.1 %collective-permute-start.9 = (f32[2,3,2,8,128]{4,3,2,1,0:T(8,128)S(1)}, f32[2,3,2,8,128]{4,3,2,1,0:T(8,128)S(1)}, u32[]{:S(2)}, u32[]{:S(2)}) collective-permute-start(f32[2,3,2,8,128]{4,3,2,1,0:T(8,128)S(1)} %get-tuple-element.58), channel_id=1, source_target_pairs={{16,0},{17,1},{18,2},{19,3},{20,4},{21,5},{22,6},{23,7},{24,8},{25... | collective-permute-start | bytes 147464 | tf_op jit(solution)/shard_map/ppermute | solution.py:724
  67.0 1.8 %collective-permute-done.8.refs_1_.refs_4_ = f32[2,3,2,8,128]{4,3,2,1,0:T(8,128)S(1)} collective-permute-done((f32[2,3,2,8,128]{4,3,2,1,0:T(8,128)S(1)}, f32[2,3,2,8,128]{4,3,2,1,0:T(8,128)S(1)}, u32[]{:S(2)}, u32[]{:S(2)}) %collective-permute-start.8) | collective-permute-done | bytes 49184 | tf_op jit(solution)/shard_map/ppermute | solution.py:723
  68.8 0.0 collective-permute-done.9.refs_2_.refs_5_
  68.8 0.0 collective-permute-start.10
  68.8 4.6 %slab_forces.3 = (f32[3,48,8,128]{3,2,1,0:T(8,128)S(1)}, f32[8,128]{1,0:T(8,128)S(1)}, f32[3,48,8,128]{3,2,1,0:T(8,128)S(1)}, f32[8,128]{1,0:T(8,128)S(1)}) custom-call(s32[1]{0:T(128)} %bitcast.side_ref, f32[3,48,8,128]{3,2,1,0:T(8,128)S(1)} %get-tuple-element.60.refs_0_.refs_1_.before.here, ...), custom_call_target="tpu_custom_call" | custom-call | flops 40000000 | bytes 30000000 | tf_op jit(solution)/shard_map/slab_forces/pallas_call | solution.py:246
  73.4 0.0 collective-permute-done.12.refs_3_.after
  73.4 0.5 collective-permute-done.11.refs_0_.before
  73.9 0.7 path_moments.3
  74.6 17.3 %all_to_all.23 = f32[128,1,128]{2,1,0:T(1,128)S(1)} all-to-all(f32[128,1,128]{2,1,0:T(1,128)S(1)} %bitcast.19), channel_id=1, replica_groups=mesh['image'=8,'domain'=16] {'image','domain'}, dimensions={0} | all-to-all | bytes 131072 | tf_op jit(solution)/shard_map/all_to_all | solution.py:717
  91.9 0.6 last_partner.1
  92.5 0.9 collective-permute-start.14
  93.5 1.2 %collective-permute-start.13 = (f32[3,24,8,128]{3,2,1,0:T(8,128)S(1)}, f32[3,24,8,128]{3,2,1,0:T(8,128)S(1)}, u32[]{:S(2)}, u32[]{:S(2)}) collective-permute-start(f32[3,24,8,128]{3,2,1,0:T(8,128)S(1)} %get-tuple-element.68), channel_id=1, source_target_pairs={{0,16},{16,0},{32,48},{48,32},{64,80},{80,64},{96,112},{112,96},{1... | collective-permute-start | bytes 884744 | tf_op jit(solution)/shard_map/ppermute | solution.py:745
  94.7 1.6 %last_own.1 = (f32[3,96,8,128]{3,2,1,0:T(8,128)}, f32[3,96,8,128]{3,2,1,0:T(8,128)}) custom-call(s32[1]{0:T(128)} %bitcast.side_ref, f32[2,4,8,128]{3,2,1,0:T(8,128)S(1)} %get-tuple-element.70.terms, f32[3,48,8,128]{3,2,1,0:T(8,128)S(1)} %collective-permute-done.11.refs_0_.before, f32[3,48,8,128]{3,2,1,0:T(8,128)S(1)} %get-tuple-element.60.refs_0_.refs_1_.before.here, ...), custom_call_target="tpu_custom_call" | custom-call | tf_op jit(solution)/shard_map/last_own/pallas_call | solution.py:551
  96.2 0.0 collective-permute-done.10.here
  96.2 6.3 %collective-permute-done.14.speed = f32[3,24,8,128]{3,2,1,0:T(8,128)S(1)} collective-permute-done((f32[3,24,8,128]{3,2,1,0:T(8,128)S(1)}, f32[3,24,8,128]{3,2,1,0:T(8,128)S(1)}, u32[]{:S(2)}, u32[]{:S(2)}) %collective-permute-start.14) | collective-permute-done | bytes 294944 | tf_op jit(solution)/shard_map/ppermute | solution.py:745
  102.6 0.9 last_join.2
  103.5 4.0 %collective-permute-done.13.speed = f32[3,24,8,128]{3,2,1,0:T(8,128)S(1)} collective-permute-done((f32[3,24,8,128]{3,2,1,0:T(8,128)S(1)}, f32[3,24,8,128]{3,2,1,0:T(8,128)S(1)}, u32[]{:S(2)}, u32[]{:S(2)}) %collective-permute-start.13) | collective-permute-done | bytes 294944 | tf_op jit(solution)/shard_map/ppermute | solution.py:745
  107.5 0.9 last_join.3
  (1 shorter events, 0.0 us)
Async XLA Ops:
  0.6 11.9 %copy-start = (f32[1,3,98304]{2,0,1:T(1,128)S(1)}, f32[1,3,98304]{2,0,1:T(1,128)}, u32[]{:S(2)}) copy-start(f32[1,3,98304]{2,0,1:T(1,128)} %param.3) | copy-start | bytes 3538948
  0.7 1.4 %copy-start.1 = (f32[1,3,98304]{2,0,1:T(1,128)S(1)}, f32[1,3,98304]{2,0,1:T(1,128)}, u32[]{:S(2)}) copy-start(f32[1,3,98304]{2,0,1:T(1,128)} %param.2) | copy-start | bytes 3538948
  2.2 10.7 %collective-permute-start = (f32[3,26,8,128]{3,2,1,0:T(8,128)S(1)}, f32[3,26,8,128]{3,2,1,0:T(8,128)S(1)}, u32[]{:S(2)}, u32[]{:S(2)}) collective-permute-start(f32[3,26,8,128]{3,2,1,0:T(8,128)S(1)} %get-tuple-element.40), channel_id=1, source_target_pairs={{0,16},{16,0},{32,48},{48,32},{64,80},{80,64},{96,112},{112,96},{1... | collective-permute-start | bytes 958472 | tf_op jit(solution)/shard_map/ppermute | solution.py:691
  4.3 7.0 %collective-permute-start.4 = (f32[3,2,8,128]{3,2,1,0:T(8,128)S(1)}, f32[3,2,8,128]{3,2,1,0:T(8,128)S(1)}, u32[]{:S(2)}, u32[]{:S(2)}) collective-permute-start(f32[3,2,8,128]{3,2,1,0:T(8,128)S(1)} %get-tuple-element.43), channel_id=1, source_target_pairs={{0,1},{1,2},{2,3},{3,4},{4,5},{5,6},{6,7},{7,8},{8,9},{9,10},{10,1... | collective-permute-start | bytes 73736 | tf_op jit(solution)/shard_map/ppermute | solution.py:686
  4.3 7.0 %collective-permute-start.5 = (f32[3,2,8,128]{3,2,1,0:T(8,128)S(1)}, f32[3,2,8,128]{3,2,1,0:T(8,128)S(1)}, u32[]{:S(2)}, u32[]{:S(2)}) collective-permute-start(f32[3,2,8,128]{3,2,1,0:T(8,128)S(1)} %get-tuple-element.44), channel_id=1, source_target_pairs={{0,31},{1,16},{2,17},{3,18},{4,19},{5,20},{6,21},{7,22},{8,23},{9,... | collective-permute-start | bytes 73736 | tf_op jit(solution)/shard_map/ppermute | solution.py:687
  9.4 11.3 %collective-permute-start.2 = (f32[3,24,8,128]{3,2,1,0:T(8,128)S(1)}, f32[3,24,8,128]{3,2,1,0:T(8,128)S(1)}, u32[]{:S(2)}, u32[]{:S(2)}) collective-permute-start(f32[3,24,8,128]{3,2,1,0:T(8,128)S(1)} %get-tuple-element.41), channel_id=1, source_target_pairs={{0,16},{16,0},{32,48},{48,32},{64,80},{80,64},{96,112},{112,96},{1... | collective-permute-start | bytes 884744 | tf_op jit(solution)/shard_map/ppermute | solution.py:691
  11.3 22.1 %collective-permute-start.6 = (f32[3,48,8,128]{3,2,1,0:T(8,128)S(1)}, f32[3,48,8,128]{3,2,1,0:T(8,128)S(1)}, u32[]{:S(2)}, u32[]{:S(2)}) collective-permute-start(f32[3,48,8,128]{3,2,1,0:T(8,128)S(1)} %get-tuple-element.45.refs_0_.refs_2_), channel_id=1, source_target_pairs={{16,48},{32,0},{48,80},{64,32},{80,112},{96,64},{17,49},{33,1},{49... | collective-permute-start | bytes 1769480 | tf_op jit(solution)/shard_map/ppermute | solution.py:692
  12.9 42.0 %collective-permute-start.7 = (f32[3,48,8,128]{3,2,1,0:T(8,128)S(1)}, f32[3,48,8,128]{3,2,1,0:T(8,128)S(1)}, u32[]{:S(2)}, u32[]{:S(2)}) collective-permute-start(f32[3,48,8,128]{3,2,1,0:T(8,128)S(1)} %get-tuple-element.55), channel_id=1, source_target_pairs={{0,16},{16,0},{32,48},{48,32},{64,80},{80,64},{96,112},{112,96},{1... | collective-permute-start | bytes 1769480 | tf_op jit(solution)/shard_map/ppermute | solution.py:708
  17.3 16.1 %collective-permute-start.1 = (f32[3,26,8,128]{3,2,1,0:T(8,128)S(1)}, f32[3,26,8,128]{3,2,1,0:T(8,128)S(1)}, u32[]{:S(2)}, u32[]{:S(2)}) collective-permute-start(f32[3,26,8,128]{3,2,1,0:T(8,128)S(1)} %collective-permute-done.refs_3_.refs_4_), channel_id=1, source_target_pairs={{48,16},{0,32},{80,48},{32,64},{112,80},{64,96},{49,17},{1,33},{81... | collective-permute-start | bytes 958472 | tf_op jit(solution)/shard_map/ppermute | solution.py:693
  20.7 12.7 %collective-permute-start.3 = (f32[3,24,8,128]{3,2,1,0:T(8,128)S(1)}, f32[3,24,8,128]{3,2,1,0:T(8,128)S(1)}, u32[]{:S(2)}, u32[]{:S(2)}) collective-permute-start(f32[3,24,8,128]{3,2,1,0:T(8,128)S(1)} %collective-permute-done.2.refs_5_.refs_4_), channel_id=1, source_target_pairs={{48,16},{0,32},{80,48},{32,64},{112,80},{64,96},{49,17},{1,33},{81... | collective-permute-start | bytes 884744 | tf_op jit(solution)/shard_map/ppermute | solution.py:693
  56.0 17.4 %collective-permute-start.12 = (f32[3,48,8,128]{3,2,1,0:T(8,128)S(1)}, f32[3,48,8,128]{3,2,1,0:T(8,128)S(1)}, u32[]{:S(2)}, u32[]{:S(2)}) collective-permute-start(f32[3,48,8,128]{3,2,1,0:T(8,128)S(1)} %get-tuple-element.60.refs_0_.refs_1_.before.here), channel_id=1, source_target_pairs={{16,48},{32,0},{48,80},{64,32},{80,112},{96,64},{17,49},{33,1},{49... | collective-permute-start | bytes 1769480 | tf_op jit(solution)/shard_map/ppermute | solution.py:737
  57.2 16.6 %collective-permute-start.11 = (f32[3,48,8,128]{3,2,1,0:T(8,128)S(1)}, f32[3,48,8,128]{3,2,1,0:T(8,128)S(1)}, u32[]{:S(2)}, u32[]{:S(2)}) collective-permute-start(f32[3,48,8,128]{3,2,1,0:T(8,128)S(1)} %get-tuple-element.59.refs_3_.refs_2_.here.after), channel_id=1, source_target_pairs={{48,16},{0,32},{80,48},{32,64},{112,80},{64,96},{49,17},{1,33},{81... | collective-permute-start | bytes 1769480 | tf_op jit(solution)/shard_map/ppermute | solution.py:734
  61.8 6.9 %collective-permute-start.8 = (f32[2,3,2,8,128]{4,3,2,1,0:T(8,128)S(1)}, f32[2,3,2,8,128]{4,3,2,1,0:T(8,128)S(1)}, u32[]{:S(2)}, u32[]{:S(2)}) collective-permute-start(f32[2,3,2,8,128]{4,3,2,1,0:T(8,128)S(1)} %get-tuple-element.57), channel_id=1, source_target_pairs={{0,16},{1,17},{2,18},{3,19},{4,20},{5,21},{6,22},{7,23},{8,24},{9,... | collective-permute-start | bytes 147464 | tf_op jit(solution)/shard_map/ppermute | solution.py:723
  61.9 6.8 %collective-permute-start.9 = (f32[2,3,2,8,128]{4,3,2,1,0:T(8,128)S(1)}, f32[2,3,2,8,128]{4,3,2,1,0:T(8,128)S(1)}, u32[]{:S(2)}, u32[]{:S(2)}) collective-permute-start(f32[2,3,2,8,128]{4,3,2,1,0:T(8,128)S(1)} %get-tuple-element.58), channel_id=1, source_target_pairs={{16,0},{17,1},{18,2},{19,3},{20,4},{21,5},{22,6},{23,7},{24,8},{25... | collective-permute-start | bytes 147464 | tf_op jit(solution)/shard_map/ppermute | solution.py:724
  68.8 27.5 %collective-permute-start.10 = (f32[3,48,8,128]{3,2,1,0:T(8,128)S(1)}, f32[3,48,8,128]{3,2,1,0:T(8,128)S(1)}, u32[]{:S(2)}, u32[]{:S(2)}) collective-permute-start(f32[3,48,8,128]{3,2,1,0:T(8,128)S(1)} %get-tuple-element.59.refs_3_.refs_2_.here.after), channel_id=1, source_target_pairs={{0,16},{16,0},{32,48},{48,32},{64,80},{80,64},{96,112},{112,96},{1... | collective-permute-start | bytes 1769480 | tf_op jit(solution)/shard_map/ppermute | solution.py:740
  92.5 10.0 %collective-permute-start.14 = (f32[3,24,8,128]{3,2,1,0:T(8,128)S(1)}, f32[3,24,8,128]{3,2,1,0:T(8,128)S(1)}, u32[]{:S(2)}, u32[]{:S(2)}) collective-permute-start(f32[3,24,8,128]{3,2,1,0:T(8,128)S(1)} %get-tuple-element.69), channel_id=1, source_target_pairs={{0,16},{16,0},{32,48},{48,32},{64,80},{80,64},{96,112},{112,96},{1... | collective-permute-start | bytes 884744 | tf_op jit(solution)/shard_map/ppermute | solution.py:745
  93.5 14.0 %collective-permute-start.13 = (f32[3,24,8,128]{3,2,1,0:T(8,128)S(1)}, f32[3,24,8,128]{3,2,1,0:T(8,128)S(1)}, u32[]{:S(2)}, u32[]{:S(2)}) collective-permute-start(f32[3,24,8,128]{3,2,1,0:T(8,128)S(1)} %get-tuple-element.68), channel_id=1, source_target_pairs={{0,16},{16,0},{32,48},{48,32},{64,80},{80,64},{96,112},{112,96},{1... | collective-permute-start | bytes 884744 | tf_op jit(solution)/shard_map/ppermute | solution.py:745

commit v9 on v8

--- a/solution.py
+++ b/solution.py
@@ -685,8 +685,8 @@
     )
     halo_own = lax.ppermute(edge_own, both, outer_own)
     halo_partner = lax.ppermute(edge_partner, both, outer_partner)
-    own, halo_own, halo_partner = lax.optimization_barrier(
-        (own, halo_own, halo_partner)
+    rest, halo_own, halo_partner = lax.optimization_barrier(
+        (rest, halo_own, halo_partner)
     )
     partner = [lax.ppermute(part, "image", across) for part in (lead, rest)]
     beyond_own = lax.ppermute(own, "image", own_out)
@@ -704,7 +704,7 @@
     )
     forces, energies = image_forces(side_arg, half, (own_source, partner_source))
     far_speed, slab_sq = cut(side_arg, slab_speed, ((((half, 0), half),),), True)
-    far_speed, *_ = lax.optimization_barrier((far_speed, partner[0]))
+    far_speed, *_ = lax.optimization_barrier((far_speed, beyond_partner[0], partner[1]))
     partner_speed = lax.ppermute(far_speed, "image", across)
 
     path = (beyond_partner, [own], partner, [beyond_own])

time: 109 us -> 107 us (0.982)
  starting transfers between devices: 32.7 us -> 29 us
  waiting for transfers between devices: 19.4 us -> 21.5 us
    ppermute x2, waiting for transfers between devices: 0.01 us -> 8.88 us  [local(): partner = [lax.ppermute(part, 'image', across) for part in (lead, rest)]]
    ppermute x2, waiting for transfers between devices: 5.11 us -> 0.01 us  [local(): lax.ppermute(part, 'image', partner_out)]
    ppermute x1, starting transfers between devices: 4.42 us -> 0.53 us  [local(): partner_speed = lax.ppermute(far_speed, 'image', across)]
    ppermute x1, waiting for transfers between devices: 1.64 us -> 0.01 us  [local(): halo_own = lax.ppermute(edge_own, both, outer_own)]
where the time goes in v9:
time: 107 us
  blocking collectives  38.1 us (36%)
  starting transfers between devices  29 us (27%)
  waiting for transfers between devices  21.5 us (20%)
  Pallas kernels  16.1 us (15%)
  local copies, waits for them, and re-layouts  1.36 us (1%)
    all_to_all x2, blocking collectives, local(): gathered = lax.all_to_all(payload, both, 0, 0, tiled=True)  38.1 us
    ppermute x2, waiting for transfers between devices, local(): last_speeds = [lax.ppermute(part, 'image', across) for part in last_speeds]  10.3 us
    pallas_call x2, Pallas kernels, image_forces(): pl.pallas_call(functools.partial(force_kernel, layouts), out_shape=(jax.S...  9.11 us
    ppermute x2, waiting for transfers between devices, local(): partner = [lax.ppermute(part, 'image', across) for part in (lead, rest)]  8.88 us
    ppermute x2, starting transfers between devices, local(): lax.ppermute(part, 'image', partner_out)  6.8 us
    ppermute x1, starting transfers between devices, local(): halo_partner = lax.ppermute(edge_partner, both, outer_partner)  5.09 us
    ppermute x1, starting transfers between devices, local(): high = lax.ppermute(bottoms, both, downward)  5.05 us
    ppermute x1, starting transfers between devices, local(): lax.ppermute(moved[1], 'image', partner_out)  4.58 us
  transfers between devices with their start and end apart: 15, of which 6 were waited for; matrix products, arithmetic and copies ran while one was open for 0% of the time, Pallas kernels for 13%

profile of v9, /device:TPU:0, one launch (start us, length us, event | category | flops | bytes accessed | tf_op | source)
XLA Modules:
  0.0 106.8 jit_solution(17917832412859240129)
XLA Ops:
  0.6 0.0 copy-start
  0.7 0.0 copy-start.1
  0.7 1.4 %copy-done.1 = f32[1,3,98304]{2,0,1:T(1,128)S(1)} copy-done((f32[1,3,98304]{2,0,1:T(1,128)S(1)}, f32[1,3,98304]{2,0,1:T(1,128)}, u32[]{:S(2)}) %copy-start.1) | copy-done | bytes 1179672
  2.0 0.2 cut.2
  2.2 2.1 %collective-permute-start = (f32[3,26,8,128]{3,2,1,0:T(8,128)S(1)}, f32[3,26,8,128]{3,2,1,0:T(8,128)S(1)}, u32[]{:S(2)}, u32[]{:S(2)}) collective-permute-start(f32[3,26,8,128]{3,2,1,0:T(8,128)S(1)} %get-tuple-element.40), channel_id=1, source_target_pairs={{0,16},{16,0},{32,48},{48,32},{64,80},{80,64},{96,112},{112,96},{1... | collective-permute-start | bytes 958472 | tf_op jit(solution)/shard_map/ppermute | solution.py:691
  4.3 0.0 collective-permute-start.2
  4.3 5.1 %collective-permute-start.3 = (f32[3,2,8,128]{3,2,1,0:T(8,128)S(1)}, f32[3,2,8,128]{3,2,1,0:T(8,128)S(1)}, u32[]{:S(2)}, u32[]{:S(2)}) collective-permute-start(f32[3,2,8,128]{3,2,1,0:T(8,128)S(1)} %get-tuple-element.43), channel_id=1, source_target_pairs={{0,31},{1,16},{2,17},{3,18},{4,19},{5,20},{6,21},{7,22},{8,23},{9,... | collective-permute-start | bytes 73736 | tf_op jit(solution)/shard_map/ppermute | solution.py:687
  9.4 2.7 %collective-permute-done.refs_3_.refs_4_ = f32[3,26,8,128]{3,2,1,0:T(8,128)S(1)} collective-permute-done((f32[3,26,8,128]{3,2,1,0:T(8,128)S(1)}, f32[3,26,8,128]{3,2,1,0:T(8,128)S(1)}, u32[]{:S(2)}, u32[]{:S(2)}) %collective-permute-start) | collective-permute-done | bytes 319520 | tf_op jit(solution)/shard_map/ppermute | solution.py:691
  12.1 3.4 %collective-permute-start.1 = (f32[3,26,8,128]{3,2,1,0:T(8,128)S(1)}, f32[3,26,8,128]{3,2,1,0:T(8,128)S(1)}, u32[]{:S(2)}, u32[]{:S(2)}) collective-permute-start(f32[3,26,8,128]{3,2,1,0:T(8,128)S(1)} %collective-permute-done.refs_3_.refs_4_), channel_id=1, source_target_pairs={{48,16},{0,32},{80,48},{32,64},{112,80},{64,96},{49,17},{1,33},{81... | collective-permute-start | bytes 958472 | tf_op jit(solution)/shard_map/ppermute | solution.py:693
  15.5 0.0 collective-permute-done.2.refs_1_
  15.5 0.0 collective-permute-done.3.refs_6_
  15.5 0.1 collective-permute-start.4
  15.6 1.3 %collective-permute-start.6 = (f32[3,48,8,128]{3,2,1,0:T(8,128)S(1)}, f32[3,48,8,128]{3,2,1,0:T(8,128)S(1)}, u32[]{:S(2)}, u32[]{:S(2)}) collective-permute-start(f32[3,48,8,128]{3,2,1,0:T(8,128)S(1)} %get-tuple-element.45.refs_0_.refs_2_), channel_id=1, source_target_pairs={{16,48},{32,0},{48,80},{64,32},{80,112},{96,64},{17,49},{33,1},{49... | collective-permute-start | bytes 1769480 | tf_op jit(solution)/shard_map/ppermute | solution.py:692
  16.9 0.0 copy-done
  16.9 0.3 cut.3
  17.2 6.2 %collective-permute-done.4.refs_5_.refs_4_ = f32[3,24,8,128]{3,2,1,0:T(8,128)S(1)} collective-permute-done((f32[3,24,8,128]{3,2,1,0:T(8,128)S(1)}, f32[3,24,8,128]{3,2,1,0:T(8,128)S(1)}, u32[]{:S(2)}, u32[]{:S(2)}) %collective-permute-start.4) | collective-permute-done | bytes 294944 | tf_op jit(solution)/shard_map/ppermute | solution.py:691
  23.4 0.0 collective-permute-done.1.refs_0_
  23.4 0.5 collective-permute-start.7
  23.9 3.4 %collective-permute-start.5 = (f32[3,24,8,128]{3,2,1,0:T(8,128)S(1)}, f32[3,24,8,128]{3,2,1,0:T(8,128)S(1)}, u32[]{:S(2)}, u32[]{:S(2)}) collective-permute-start(f32[3,24,8,128]{3,2,1,0:T(8,128)S(1)} %collective-permute-done.4.refs_5_.refs_4_), channel_id=1, source_target_pairs={{48,16},{0,32},{80,48},{32,64},{112,80},{64,96},{49,17},{1,33},{81... | collective-permute-start | bytes 884744 | tf_op jit(solution)/shard_map/ppermute | solution.py:693
  27.3 4.5 %slab_forces.2 = (f32[3,48,8,128]{3,2,1,0:T(8,128)S(1)}, f32[8,128]{1,0:T(8,128)S(1)}, f32[3,48,8,128]{3,2,1,0:T(8,128)S(1)}, f32[8,128]{1,0:T(8,128)S(1)}) custom-call(s32[1]{0:T(128)} %bitcast.side_ref, f32[3,48,8,128]{3,2,1,0:T(8,128)S(1)} %get-tuple-element.45.refs_0_.refs_2_, f32[3,2,8,128]{3,2,1,0:T(8,128)S(1)} %collective-permute-done.2.refs_1_, ...), custom_call_target="tpu_custom_call" | custom-call | flops 40000000 | bytes 30000000 | tf_op jit(solution)/shard_map/slab_forces/pallas_call | solution.py:246
  31.8 0.0 collective-permute-done.6.refs_5_
  31.8 0.0 collective-permute-done.5.refs_1_
  31.9 0.7 path_moments.2
  32.6 20.7 %all_to_all.22 = f32[128,1,128]{2,1,0:T(1,128)S(1)} all-to-all(f32[128,1,128]{2,1,0:T(1,128)S(1)} %bitcast.18), channel_id=1, replica_groups=mesh['image'=8,'domain'=16] {'image','domain'}, dimensions={0} | all-to-all | bytes 131072 | tf_op jit(solution)/shard_map/all_to_all | solution.py:717
  53.3 0.0 collective-permute-done.7.refs_8_
  53.3 1.0 fire_update.1
  54.4 1.3 %collective-permute-start.12 = (f32[3,48,8,128]{3,2,1,0:T(8,128)S(1)}, f32[3,48,8,128]{3,2,1,0:T(8,128)S(1)}, u32[]{:S(2)}, u32[]{:S(2)}) collective-permute-start(f32[3,48,8,128]{3,2,1,0:T(8,128)S(1)} %get-tuple-element.60.refs_0_.refs_1_.before.here), channel_id=1, source_target_pairs={{16,48},{32,0},{48,80},{64,32},{80,112},{96,64},{17,49},{33,1},{49... | collective-permute-start | bytes 1769480 | tf_op jit(solution)/shard_map/ppermute | solution.py:737
  55.7 4.6 %collective-permute-start.11 = (f32[3,48,8,128]{3,2,1,0:T(8,128)S(1)}, f32[3,48,8,128]{3,2,1,0:T(8,128)S(1)}, u32[]{:S(2)}, u32[]{:S(2)}) collective-permute-start(f32[3,48,8,128]{3,2,1,0:T(8,128)S(1)} %get-tuple-element.59.refs_3_.refs_2_.here.after), channel_id=1, source_target_pairs={{48,16},{0,32},{80,48},{32,64},{112,80},{64,96},{49,17},{1,33},{81... | collective-permute-start | bytes 1769480 | tf_op jit(solution)/shard_map/ppermute | solution.py:734
  60.3 0.1 collective-permute-start.8
  60.4 5.1 %collective-permute-start.9 = (f32[2,3,2,8,128]{4,3,2,1,0:T(8,128)S(1)}, f32[2,3,2,8,128]{4,3,2,1,0:T(8,128)S(1)}, u32[]{:S(2)}, u32[]{:S(2)}) collective-permute-start(f32[2,3,2,8,128]{4,3,2,1,0:T(8,128)S(1)} %get-tuple-element.58), channel_id=1, source_target_pairs={{16,0},{17,1},{18,2},{19,3},{20,4},{21,5},{22,6},{23,7},{24,8},{25... | collective-permute-start | bytes 147464 | tf_op jit(solution)/shard_map/ppermute | solution.py:724
  65.4 1.8 %collective-permute-done.8.refs_1_.refs_4_ = f32[2,3,2,8,128]{4,3,2,1,0:T(8,128)S(1)} collective-permute-done((f32[2,3,2,8,128]{4,3,2,1,0:T(8,128)S(1)}, f32[2,3,2,8,128]{4,3,2,1,0:T(8,128)S(1)}, u32[]{:S(2)}, u32[]{:S(2)}) %collective-permute-start.8) | collective-permute-done | bytes 49184 | tf_op jit(solution)/shard_map/ppermute | solution.py:723
  67.2 0.0 collective-permute-done.9.refs_2_.refs_5_
  67.2 0.0 collective-permute-start.10
  67.2 4.6 %slab_forces.3 = (f32[3,48,8,128]{3,2,1,0:T(8,128)S(1)}, f32[8,128]{1,0:T(8,128)S(1)}, f32[3,48,8,128]{3,2,1,0:T(8,128)S(1)}, f32[8,128]{1,0:T(8,128)S(1)}) custom-call(s32[1]{0:T(128)} %bitcast.side_ref, f32[3,48,8,128]{3,2,1,0:T(8,128)S(1)} %get-tuple-element.60.refs_0_.refs_1_.before.here, ...), custom_call_target="tpu_custom_call" | custom-call | flops 40000000 | bytes 30000000 | tf_op jit(solution)/shard_map/slab_forces/pallas_call | solution.py:246
  71.8 0.0 collective-permute-done.12.refs_3_.after
  71.8 0.5 collective-permute-done.11.refs_0_.before
  72.3 0.7 path_moments.3
  73.0 17.3 %all_to_all.23 = f32[128,1,128]{2,1,0:T(1,128)S(1)} all-to-all(f32[128,1,128]{2,1,0:T(1,128)S(1)} %bitcast.19), channel_id=1, replica_groups=mesh['image'=8,'domain'=16] {'image','domain'}, dimensions={0} | all-to-all | bytes 131072 | tf_op jit(solution)/shard_map/all_to_all | solution.py:717
  90.3 0.6 last_partner.1
  91.0 0.9 collective-permute-start.14
  91.9 1.2 %collective-permute-start.13 = (f32[3,24,8,128]{3,2,1,0:T(8,128)S(1)}, f32[3,24,8,128]{3,2,1,0:T(8,128)S(1)}, u32[]{:S(2)}, u32[]{:S(2)}) collective-permute-start(f32[3,24,8,128]{3,2,1,0:T(8,128)S(1)} %get-tuple-element.68), channel_id=1, source_target_pairs={{0,16},{16,0},{32,48},{48,32},{64,80},{80,64},{96,112},{112,96},{1... | collective-permute-start | bytes 884744 | tf_op jit(solution)/shard_map/ppermute | solution.py:745
  93.1 1.6 %last_own.1 = (f32[3,96,8,128]{3,2,1,0:T(8,128)}, f32[3,96,8,128]{3,2,1,0:T(8,128)}) custom-call(s32[1]{0:T(128)} %bitcast.side_ref, f32[2,4,8,128]{3,2,1,0:T(8,128)S(1)} %get-tuple-element.70.terms, f32[3,48,8,128]{3,2,1,0:T(8,128)S(1)} %collective-permute-done.11.refs_0_.before, f32[3,48,8,128]{3,2,1,0:T(8,128)S(1)} %get-tuple-element.60.refs_0_.refs_1_.before.here, ...), custom_call_target="tpu_custom_call" | custom-call | tf_op jit(solution)/shard_map/last_own/pallas_call | solution.py:551
  94.6 0.0 collective-permute-done.10.here
  94.6 6.3 %collective-permute-done.14.speed = f32[3,24,8,128]{3,2,1,0:T(8,128)S(1)} collective-permute-done((f32[3,24,8,128]{3,2,1,0:T(8,128)S(1)}, f32[3,24,8,128]{3,2,1,0:T(8,128)S(1)}, u32[]{:S(2)}, u32[]{:S(2)}) %collective-permute-start.14) | collective-permute-done | bytes 294944 | tf_op jit(solution)/shard_map/ppermute | solution.py:745
  101.0 0.9 last_join.2
  101.9 4.0 %collective-permute-done.13.speed = f32[3,24,8,128]{3,2,1,0:T(8,128)S(1)} collective-permute-done((f32[3,24,8,128]{3,2,1,0:T(8,128)S(1)}, f32[3,24,8,128]{3,2,1,0:T(8,128)S(1)}, u32[]{:S(2)}, u32[]{:S(2)}) %collective-permute-start.13) | collective-permute-done | bytes 294944 | tf_op jit(solution)/shard_map/ppermute | solution.py:745
  105.9 0.9 last_join.3
  (1 shorter events, 0.0 us)
Async XLA Ops:
  0.6 16.3 %copy-start = (f32[1,3,98304]{2,0,1:T(1,128)S(1)}, f32[1,3,98304]{2,0,1:T(1,128)}, u32[]{:S(2)}) copy-start(f32[1,3,98304]{2,0,1:T(1,128)} %param.3) | copy-start | bytes 3538948
  0.7 1.4 %copy-start.1 = (f32[1,3,98304]{2,0,1:T(1,128)S(1)}, f32[1,3,98304]{2,0,1:T(1,128)}, u32[]{:S(2)}) copy-start(f32[1,3,98304]{2,0,1:T(1,128)} %param.2) | copy-start | bytes 3538948
  2.2 9.9 %collective-permute-start = (f32[3,26,8,128]{3,2,1,0:T(8,128)S(1)}, f32[3,26,8,128]{3,2,1,0:T(8,128)S(1)}, u32[]{:S(2)}, u32[]{:S(2)}) collective-permute-start(f32[3,26,8,128]{3,2,1,0:T(8,128)S(1)} %get-tuple-element.40), channel_id=1, source_target_pairs={{0,16},{16,0},{32,48},{48,32},{64,80},{80,64},{96,112},{112,96},{1... | collective-permute-start | bytes 958472 | tf_op jit(solution)/shard_map/ppermute | solution.py:691
  4.3 11.2 %collective-permute-start.2 = (f32[3,2,8,128]{3,2,1,0:T(8,128)S(1)}, f32[3,2,8,128]{3,2,1,0:T(8,128)S(1)}, u32[]{:S(2)}, u32[]{:S(2)}) collective-permute-start(f32[3,2,8,128]{3,2,1,0:T(8,128)S(1)} %get-tuple-element.42), channel_id=1, source_target_pairs={{0,1},{1,2},{2,3},{3,4},{4,5},{5,6},{6,7},{7,8},{8,9},{9,10},{10,1... | collective-permute-start | bytes 73736 | tf_op jit(solution)/shard_map/ppermute | solution.py:686
  4.3 11.2 %collective-permute-start.3 = (f32[3,2,8,128]{3,2,1,0:T(8,128)S(1)}, f32[3,2,8,128]{3,2,1,0:T(8,128)S(1)}, u32[]{:S(2)}, u32[]{:S(2)}) collective-permute-start(f32[3,2,8,128]{3,2,1,0:T(8,128)S(1)} %get-tuple-element.43), channel_id=1, source_target_pairs={{0,31},{1,16},{2,17},{3,18},{4,19},{5,20},{6,21},{7,22},{8,23},{9,... | collective-permute-start | bytes 73736 | tf_op jit(solution)/shard_map/ppermute | solution.py:687
  12.1 11.3 %collective-permute-start.1 = (f32[3,26,8,128]{3,2,1,0:T(8,128)S(1)}, f32[3,26,8,128]{3,2,1,0:T(8,128)S(1)}, u32[]{:S(2)}, u32[]{:S(2)}) collective-permute-start(f32[3,26,8,128]{3,2,1,0:T(8,128)S(1)} %collective-permute-done.refs_3_.refs_4_), channel_id=1, source_target_pairs={{48,16},{0,32},{80,48},{32,64},{112,80},{64,96},{49,17},{1,33},{81... | collective-permute-start | bytes 958472 | tf_op jit(solution)/shard_map/ppermute | solution.py:693
  15.5 7.9 %collective-permute-start.4 = (f32[3,24,8,128]{3,2,1,0:T(8,128)S(1)}, f32[3,24,8,128]{3,2,1,0:T(8,128)S(1)}, u32[]{:S(2)}, u32[]{:S(2)}) collective-permute-start(f32[3,24,8,128]{3,2,1,0:T(8,128)S(1)} %get-tuple-element.44), channel_id=1, source_target_pairs={{0,16},{16,0},{32,48},{48,32},{64,80},{80,64},{96,112},{112,96},{1... | collective-permute-start | bytes 884744 | tf_op jit(solution)/shard_map/ppermute | solution.py:691
  15.6 16.2 %collective-permute-start.6 = (f32[3,48,8,128]{3,2,1,0:T(8,128)S(1)}, f32[3,48,8,128]{3,2,1,0:T(8,128)S(1)}, u32[]{:S(2)}, u32[]{:S(2)}) collective-permute-start(f32[3,48,8,128]{3,2,1,0:T(8,128)S(1)} %get-tuple-element.45.refs_0_.refs_2_), channel_id=1, source_target_pairs={{16,48},{32,0},{48,80},{64,32},{80,112},{96,64},{17,49},{33,1},{49... | collective-permute-start | bytes 1769480 | tf_op jit(solution)/shard_map/ppermute | solution.py:692
  23.4 29.9 %collective-permute-start.7 = (f32[3,48,8,128]{3,2,1,0:T(8,128)S(1)}, f32[3,48,8,128]{3,2,1,0:T(8,128)S(1)}, u32[]{:S(2)}, u32[]{:S(2)}) collective-permute-start(f32[3,48,8,128]{3,2,1,0:T(8,128)S(1)} %get-tuple-element.55), channel_id=1, source_target_pairs={{0,16},{16,0},{32,48},{48,32},{64,80},{80,64},{96,112},{112,96},{1... | collective-permute-start | bytes 1769480 | tf_op jit(solution)/shard_map/ppermute | solution.py:708
  23.9 7.9 %collective-permute-start.5 = (f32[3,24,8,128]{3,2,1,0:T(8,128)S(1)}, f32[3,24,8,128]{3,2,1,0:T(8,128)S(1)}, u32[]{:S(2)}, u32[]{:S(2)}) collective-permute-start(f32[3,24,8,128]{3,2,1,0:T(8,128)S(1)} %collective-permute-done.4.refs_5_.refs_4_), channel_id=1, source_target_pairs={{48,16},{0,32},{80,48},{32,64},{112,80},{64,96},{49,17},{1,33},{81... | collective-permute-start | bytes 884744 | tf_op jit(solution)/shard_map/ppermute | solution.py:693
  54.4 17.4 %collective-permute-start.12 = (f32[3,48,8,128]{3,2,1,0:T(8,128)S(1)}, f32[3,48,8,128]{3,2,1,0:T(8,128)S(1)}, u32[]{:S(2)}, u32[]{:S(2)}) collective-permute-start(f32[3,48,8,128]{3,2,1,0:T(8,128)S(1)} %get-tuple-element.60.refs_0_.refs_1_.before.here), channel_id=1, source_target_pairs={{16,48},{32,0},{48,80},{64,32},{80,112},{96,64},{17,49},{33,1},{49... | collective-permute-start | bytes 1769480 | tf_op jit(solution)/shard_map/ppermute | solution.py:737
  55.7 16.6 %collective-permute-start.11 = (f32[3,48,8,128]{3,2,1,0:T(8,128)S(1)}, f32[3,48,8,128]{3,2,1,0:T(8,128)S(1)}, u32[]{:S(2)}, u32[]{:S(2)}) collective-permute-start(f32[3,48,8,128]{3,2,1,0:T(8,128)S(1)} %get-tuple-element.59.refs_3_.refs_2_.here.after), channel_id=1, source_target_pairs={{48,16},{0,32},{80,48},{32,64},{112,80},{64,96},{49,17},{1,33},{81... | collective-permute-start | bytes 1769480 | tf_op jit(solution)/shard_map/ppermute | solution.py:734
  60.3 6.9 %collective-permute-start.8 = (f32[2,3,2,8,128]{4,3,2,1,0:T(8,128)S(1)}, f32[2,3,2,8,128]{4,3,2,1,0:T(8,128)S(1)}, u32[]{:S(2)}, u32[]{:S(2)}) collective-permute-start(f32[2,3,2,8,128]{4,3,2,1,0:T(8,128)S(1)} %get-tuple-element.57), channel_id=1, source_target_pairs={{0,16},{1,17},{2,18},{3,19},{4,20},{5,21},{6,22},{7,23},{8,24},{9,... | collective-permute-start | bytes 147464 | tf_op jit(solution)/shard_map/ppermute | solution.py:723
  60.4 6.8 %collective-permute-start.9 = (f32[2,3,2,8,128]{4,3,2,1,0:T(8,128)S(1)}, f32[2,3,2,8,128]{4,3,2,1,0:T(8,128)S(1)}, u32[]{:S(2)}, u32[]{:S(2)}) collective-permute-start(f32[2,3,2,8,128]{4,3,2,1,0:T(8,128)S(1)} %get-tuple-element.58), channel_id=1, source_target_pairs={{16,0},{17,1},{18,2},{19,3},{20,4},{21,5},{22,6},{23,7},{24,8},{25... | collective-permute-start | bytes 147464 | tf_op jit(solution)/shard_map/ppermute | solution.py:724
  67.2 27.5 %collective-permute-start.10 = (f32[3,48,8,128]{3,2,1,0:T(8,128)S(1)}, f32[3,48,8,128]{3,2,1,0:T(8,128)S(1)}, u32[]{:S(2)}, u32[]{:S(2)}) collective-permute-start(f32[3,48,8,128]{3,2,1,0:T(8,128)S(1)} %get-tuple-element.59.refs_3_.refs_2_.here.after), channel_id=1, source_target_pairs={{0,16},{16,0},{32,48},{48,32},{64,80},{80,64},{96,112},{112,96},{1... | collective-permute-start | bytes 1769480 | tf_op jit(solution)/shard_map/ppermute | solution.py:740
  91.0 10.0 %collective-permute-start.14 = (f32[3,24,8,128]{3,2,1,0:T(8,128)S(1)}, f32[3,24,8,128]{3,2,1,0:T(8,128)S(1)}, u32[]{:S(2)}, u32[]{:S(2)}) collective-permute-start(f32[3,24,8,128]{3,2,1,0:T(8,128)S(1)} %get-tuple-element.69), channel_id=1, source_target_pairs={{0,16},{16,0},{32,48},{48,32},{64,80},{80,64},{96,112},{112,96},{1... | collective-permute-start | bytes 884744 | tf_op jit(solution)/shard_map/ppermute | solution.py:745
  91.9 14.0 %collective-permute-start.13 = (f32[3,24,8,128]{3,2,1,0:T(8,128)S(1)}, f32[3,24,8,128]{3,2,1,0:T(8,128)S(1)}, u32[]{:S(2)}, u32[]{:S(2)}) collective-permute-start(f32[3,24,8,128]{3,2,1,0:T(8,128)S(1)} %get-tuple-element.68), channel_id=1, source_target_pairs={{0,16},{16,0},{32,48},{48,32},{64,80},{80,64},{96,112},{112,96},{1... | collective-permute-start | bytes 884744 | tf_op jit(solution)/shard_map/ppermute | solution.py:745

commit v10 on v9

--- a/solution.py
+++ b/solution.py
@@ -704,7 +704,7 @@
     )
     forces, energies = image_forces(side_arg, half, (own_source, partner_source))
     far_speed, slab_sq = cut(side_arg, slab_speed, ((((half, 0), half),),), True)
-    far_speed, *_ = lax.optimization_barrier((far_speed, beyond_partner[0], partner[1]))
+    far_speed, *_ = lax.optimization_barrier((far_speed, partner[0], halo_own, halo_partner))
     partner_speed = lax.ppermute(far_speed, "image", across)
 
     path = (beyond_partner, [own], partner, [beyond_own])

time: 107 us -> 107 us (level)
  starting transfers between devices: 29 us -> 32.1 us
  waiting for transfers between devices: 21.5 us -> 18.5 us
    ppermute x2, waiting for transfers between devices: 8.88 us -> 2.75 us  [local(): partner = [lax.ppermute(part, 'image', across) for part in (lead, rest)]]
    ppermute x2, waiting for transfers between devices: 0.01 us -> 2.58 us  [local(): lax.ppermute(part, 'image', partner_out)]
    ppermute x2, starting transfers between devices: 2.17 us -> 4.28 us  [local(): partner = [lax.ppermute(part, 'image', across) for part in (lead, rest)]]
    ppermute x2, starting transfers between devices: 6.8 us -> 8.06 us  [local(): lax.ppermute(part, 'image', partner_out)]
  transfers between devices with their start and end apart: 15 -> 15, of which waited for: 6 -> 7; matrix products, arithmetic and copies ran while one was open for 0% -> 0% of each run, Pallas kernels for 13% -> 13%
where the time goes in v10:
time: 107 us; the launch traced here: 106 us
  blocking collectives  37.5 us (35%)
  starting transfers between devices  32.1 us (30%)
  waiting for transfers between devices  18.5 us (17%)
  Pallas kernels  16.1 us (15%)
  local copies, waits for them, and re-layouts  1.36 us (1%)
    all_to_all x2, blocking collectives, local(): gathered = lax.all_to_all(payload, both, 0, 0, tiled=True)  37.5 us
    ppermute x2, waiting for transfers between devices, local(): last_speeds = [lax.ppermute(part, 'image', across) for part in last_speeds]  10.3 us
    pallas_call x2, Pallas kernels, image_forces(): pl.pallas_call(functools.partial(force_kernel, layouts), out_shape=(jax.S...  9.11 us
    ppermute x2, starting transfers between devices, local(): lax.ppermute(part, 'image', partner_out)  8.06 us
    ppermute x1, starting transfers between devices, local(): halo_partner = lax.ppermute(edge_partner, both, outer_partner)  5.09 us
    ppermute x1, starting transfers between devices, local(): high = lax.ppermute(bottoms, both, downward)  5.05 us
    ppermute x1, starting transfers between devices, local(): lax.ppermute(moved[1], 'image', partner_out)  4.58 us
    ppermute x2, starting transfers between devices, local(): partner = [lax.ppermute(part, 'image', across) for part in (lead, rest)]  4.28 us
  transfers between devices with their start and end apart: 15, of which 7 were waited for; matrix products, arithmetic and copies ran while one was open for 0% of the time, Pallas kernels for 13%

profile of v10, /device:TPU:0, one launch (start us, length us, event | category | flops | bytes accessed | tf_op | source)
XLA Modules:
  0.0 106.4 jit_solution(3499186318139466595)
XLA Ops:
  0.6 0.0 copy-start
  0.7 0.0 copy-start.1
  0.7 1.4 %copy-done.1 = f32[1,3,98304]{2,0,1:T(1,128)S(1)} copy-done((f32[1,3,98304]{2,0,1:T(1,128)S(1)}, f32[1,3,98304]{2,0,1:T(1,128)}, u32[]{:S(2)}) %copy-start.1) | copy-done | bytes 1179672
  2.0 0.2 cut.2
  2.2 2.1 %collective-permute-start = (f32[3,26,8,128]{3,2,1,0:T(8,128)S(1)}, f32[3,26,8,128]{3,2,1,0:T(8,128)S(1)}, u32[]{:S(2)}, u32[]{:S(2)}) collective-permute-start(f32[3,26,8,128]{3,2,1,0:T(8,128)S(1)} %get-tuple-element.40), channel_id=1, source_target_pairs={{0,16},{16,0},{32,48},{48,32},{64,80},{80,64},{96,112},{112,96},{1... | collective-permute-start | bytes 958472 | tf_op jit(solution)/shard_map/ppermute | solution.py:691
  4.3 0.0 collective-permute-start.2
  4.3 5.1 %collective-permute-start.3 = (f32[3,2,8,128]{3,2,1,0:T(8,128)S(1)}, f32[3,2,8,128]{3,2,1,0:T(8,128)S(1)}, u32[]{:S(2)}, u32[]{:S(2)}) collective-permute-start(f32[3,2,8,128]{3,2,1,0:T(8,128)S(1)} %get-tuple-element.43), channel_id=1, source_target_pairs={{0,31},{1,16},{2,17},{3,18},{4,19},{5,20},{6,21},{7,22},{8,23},{9,... | collective-permute-start | bytes 73736 | tf_op jit(solution)/shard_map/ppermute | solution.py:687
  9.4 1.3 %collective-permute-start.6 = (f32[3,48,8,128]{3,2,1,0:T(8,128)S(1)}, f32[3,48,8,128]{3,2,1,0:T(8,128)S(1)}, u32[]{:S(2)}, u32[]{:S(2)}) collective-permute-start(f32[3,48,8,128]{3,2,1,0:T(8,128)S(1)} %get-tuple-element.45.refs_0_.refs_2_), channel_id=1, source_target_pairs={{16,48},{32,0},{48,80},{64,32},{80,112},{96,64},{17,49},{33,1},{49... | collective-permute-start | bytes 1769480 | tf_op jit(solution)/shard_map/ppermute | solution.py:692
  10.7 0.6 collective-permute-done.2.refs_1_
  11.3 0.0 collective-permute-done.3.refs_6_
  11.3 2.2 %collective-permute-start.4 = (f32[3,24,8,128]{3,2,1,0:T(8,128)S(1)}, f32[3,24,8,128]{3,2,1,0:T(8,128)S(1)}, u32[]{:S(2)}, u32[]{:S(2)}) collective-permute-start(f32[3,24,8,128]{3,2,1,0:T(8,128)S(1)} %get-tuple-element.44), channel_id=1, source_target_pairs={{0,16},{16,0},{32,48},{48,32},{64,80},{80,64},{96,112},{112,96},{1... | collective-permute-start | bytes 884744 | tf_op jit(solution)/shard_map/ppermute | solution.py:691
  13.5 0.0 copy-done
  13.5 0.3 cut.3
  13.8 0.0 collective-permute-done.refs_3_.refs_4_
  13.8 0.3 collective-permute-start.7
  14.1 3.6 %collective-permute-start.1 = (f32[3,26,8,128]{3,2,1,0:T(8,128)S(1)}, f32[3,26,8,128]{3,2,1,0:T(8,128)S(1)}, u32[]{:S(2)}, u32[]{:S(2)}) collective-permute-start(f32[3,26,8,128]{3,2,1,0:T(8,128)S(1)} %collective-permute-done.refs_3_.refs_4_), channel_id=1, source_target_pairs={{48,16},{0,32},{80,48},{32,64},{112,80},{64,96},{49,17},{1,33},{81... | collective-permute-start | bytes 958472 | tf_op jit(solution)/shard_map/ppermute | solution.py:693
  17.7 2.8 %collective-permute-done.4.refs_5_.refs_4_ = f32[3,24,8,128]{3,2,1,0:T(8,128)S(1)} collective-permute-done((f32[3,24,8,128]{3,2,1,0:T(8,128)S(1)}, f32[3,24,8,128]{3,2,1,0:T(8,128)S(1)}, u32[]{:S(2)}, u32[]{:S(2)}) %collective-permute-start.4) | collective-permute-done | bytes 294944 | tf_op jit(solution)/shard_map/ppermute | solution.py:691
  20.5 4.4 %collective-permute-start.5 = (f32[3,24,8,128]{3,2,1,0:T(8,128)S(1)}, f32[3,24,8,128]{3,2,1,0:T(8,128)S(1)}, u32[]{:S(2)}, u32[]{:S(2)}) collective-permute-start(f32[3,24,8,128]{3,2,1,0:T(8,128)S(1)} %collective-permute-done.4.refs_5_.refs_4_), channel_id=1, source_target_pairs={{48,16},{0,32},{80,48},{32,64},{112,80},{64,96},{49,17},{1,33},{81... | collective-permute-start | bytes 884744 | tf_op jit(solution)/shard_map/ppermute | solution.py:693
  24.9 4.5 %slab_forces.2 = (f32[3,48,8,128]{3,2,1,0:T(8,128)S(1)}, f32[8,128]{1,0:T(8,128)S(1)}, f32[3,48,8,128]{3,2,1,0:T(8,128)S(1)}, f32[8,128]{1,0:T(8,128)S(1)}) custom-call(s32[1]{0:T(128)} %bitcast.side_ref, f32[3,48,8,128]{3,2,1,0:T(8,128)S(1)} %get-tuple-element.45.refs_0_.refs_2_, f32[3,2,8,128]{3,2,1,0:T(8,128)S(1)} %collective-permute-done.2.refs_1_, ...), custom_call_target="tpu_custom_call" | custom-call | flops 40000000 | bytes 30000000 | tf_op jit(solution)/shard_map/slab_forces/pallas_call | solution.py:246
  29.4 0.0 collective-permute-done.6.refs_5_
  29.4 2.6 %collective-permute-done.5.refs_1_ = f32[3,24,8,128]{3,2,1,0:T(8,128)S(1)} collective-permute-done((f32[3,24,8,128]{3,2,1,0:T(8,128)S(1)}, f32[3,24,8,128]{3,2,1,0:T(8,128)S(1)}, u32[]{:S(2)}, u32[]{:S(2)}) %collective-permute-start.5) | collective-permute-done | bytes 294944 | tf_op jit(solution)/shard_map/ppermute | solution.py:693
  32.0 0.0 collective-permute-done.1.refs_0_
  32.0 0.7 path_moments.2
  32.7 20.2 %all_to_all.22 = f32[128,1,128]{2,1,0:T(1,128)S(1)} all-to-all(f32[128,1,128]{2,1,0:T(1,128)S(1)} %bitcast.18), channel_id=1, replica_groups=mesh['image'=8,'domain'=16] {'image','domain'}, dimensions={0} | all-to-all | bytes 131072 | tf_op jit(solution)/shard_map/all_to_all | solution.py:717
  53.0 0.0 collective-permute-done.7.refs_8_
  53.0 1.0 fire_update.1
  54.0 1.3 %collective-permute-start.12 = (f32[3,48,8,128]{3,2,1,0:T(8,128)S(1)}, f32[3,48,8,128]{3,2,1,0:T(8,128)S(1)}, u32[]{:S(2)}, u32[]{:S(2)}) collective-permute-start(f32[3,48,8,128]{3,2,1,0:T(8,128)S(1)} %get-tuple-element.60.refs_0_.refs_1_.before.here), channel_id=1, source_target_pairs={{16,48},{32,0},{48,80},{64,32},{80,112},{96,64},{17,49},{33,1},{49... | collective-permute-start | bytes 1769480 | tf_op jit(solution)/shard_map/ppermute | solution.py:737
  55.3 4.6 %collective-permute-start.11 = (f32[3,48,8,128]{3,2,1,0:T(8,128)S(1)}, f32[3,48,8,128]{3,2,1,0:T(8,128)S(1)}, u32[]{:S(2)}, u32[]{:S(2)}) collective-permute-start(f32[3,48,8,128]{3,2,1,0:T(8,128)S(1)} %get-tuple-element.59.refs_3_.refs_2_.here.after), channel_id=1, source_target_pairs={{48,16},{0,32},{80,48},{32,64},{112,80},{64,96},{49,17},{1,33},{81... | collective-permute-start | bytes 1769480 | tf_op jit(solution)/shard_map/ppermute | solution.py:734
  59.9 0.1 collective-permute-start.8
  60.0 5.1 %collective-permute-start.9 = (f32[2,3,2,8,128]{4,3,2,1,0:T(8,128)S(1)}, f32[2,3,2,8,128]{4,3,2,1,0:T(8,128)S(1)}, u32[]{:S(2)}, u32[]{:S(2)}) collective-permute-start(f32[2,3,2,8,128]{4,3,2,1,0:T(8,128)S(1)} %get-tuple-element.58), channel_id=1, source_target_pairs={{16,0},{17,1},{18,2},{19,3},{20,4},{21,5},{22,6},{23,7},{24,8},{25... | collective-permute-start | bytes 147464 | tf_op jit(solution)/shard_map/ppermute | solution.py:724
  65.0 1.8 %collective-permute-done.8.refs_1_.refs_4_ = f32[2,3,2,8,128]{4,3,2,1,0:T(8,128)S(1)} collective-permute-done((f32[2,3,2,8,128]{4,3,2,1,0:T(8,128)S(1)}, f32[2,3,2,8,128]{4,3,2,1,0:T(8,128)S(1)}, u32[]{:S(2)}, u32[]{:S(2)}) %collective-permute-start.8) | collective-permute-done | bytes 49184 | tf_op jit(solution)/shard_map/ppermute | solution.py:723
  66.8 0.0 collective-permute-done.9.refs_2_.refs_5_
  66.8 0.0 collective-permute-start.10
  66.8 4.6 %slab_forces.3 = (f32[3,48,8,128]{3,2,1,0:T(8,128)S(1)}, f32[8,128]{1,0:T(8,128)S(1)}, f32[3,48,8,128]{3,2,1,0:T(8,128)S(1)}, f32[8,128]{1,0:T(8,128)S(1)}) custom-call(s32[1]{0:T(128)} %bitcast.side_ref, f32[3,48,8,128]{3,2,1,0:T(8,128)S(1)} %get-tuple-element.60.refs_0_.refs_1_.before.here, ...), custom_call_target="tpu_custom_call" | custom-call | flops 40000000 | bytes 30000000 | tf_op jit(solution)/shard_map/slab_forces/pallas_call | solution.py:246
  71.4 0.0 collective-permute-done.12.refs_3_.after
  71.4 0.5 collective-permute-done.11.refs_0_.before
  71.9 0.7 path_moments.3
  72.6 17.3 %all_to_all.23 = f32[128,1,128]{2,1,0:T(1,128)S(1)} all-to-all(f32[128,1,128]{2,1,0:T(1,128)S(1)} %bitcast.19), channel_id=1, replica_groups=mesh['image'=8,'domain'=16] {'image','domain'}, dimensions={0} | all-to-all | bytes 131072 | tf_op jit(solution)/shard_map/all_to_all | solution.py:717
  90.0 0.6 last_partner.1
  90.6 0.9 collective-permute-start.14
  91.5 1.2 %collective-permute-start.13 = (f32[3,24,8,128]{3,2,1,0:T(8,128)S(1)}, f32[3,24,8,128]{3,2,1,0:T(8,128)S(1)}, u32[]{:S(2)}, u32[]{:S(2)}) collective-permute-start(f32[3,24,8,128]{3,2,1,0:T(8,128)S(1)} %get-tuple-element.68), channel_id=1, source_target_pairs={{0,16},{16,0},{32,48},{48,32},{64,80},{80,64},{96,112},{112,96},{1... | collective-permute-start | bytes 884744 | tf_op jit(solution)/shard_map/ppermute | solution.py:745
  92.7 1.6 %last_own.1 = (f32[3,96,8,128]{3,2,1,0:T(8,128)}, f32[3,96,8,128]{3,2,1,0:T(8,128)}) custom-call(s32[1]{0:T(128)} %bitcast.side_ref, f32[2,4,8,128]{3,2,1,0:T(8,128)S(1)} %get-tuple-element.70.terms, f32[3,48,8,128]{3,2,1,0:T(8,128)S(1)} %collective-permute-done.11.refs_0_.before, f32[3,48,8,128]{3,2,1,0:T(8,128)S(1)} %get-tuple-element.60.refs_0_.refs_1_.before.here, ...), custom_call_target="tpu_custom_call" | custom-call | tf_op jit(solution)/shard_map/last_own/pallas_call | solution.py:551
  94.2 0.0 collective-permute-done.10.here
  94.2 6.3 %collective-permute-done.14.speed = f32[3,24,8,128]{3,2,1,0:T(8,128)S(1)} collective-permute-done((f32[3,24,8,128]{3,2,1,0:T(8,128)S(1)}, f32[3,24,8,128]{3,2,1,0:T(8,128)S(1)}, u32[]{:S(2)}, u32[]{:S(2)}) %collective-permute-start.14) | collective-permute-done | bytes 294944 | tf_op jit(solution)/shard_map/ppermute | solution.py:745
  100.6 0.9 last_join.2
  101.5 4.0 %collective-permute-done.13.speed = f32[3,24,8,128]{3,2,1,0:T(8,128)S(1)} collective-permute-done((f32[3,24,8,128]{3,2,1,0:T(8,128)S(1)}, f32[3,24,8,128]{3,2,1,0:T(8,128)S(1)}, u32[]{:S(2)}, u32[]{:S(2)}) %collective-permute-start.13) | collective-permute-done | bytes 294944 | tf_op jit(solution)/shard_map/ppermute | solution.py:745
  105.5 0.9 last_join.3
  (1 shorter events, 0.0 us)
Async XLA Ops:
  0.6 12.8 %copy-start = (f32[1,3,98304]{2,0,1:T(1,128)S(1)}, f32[1,3,98304]{2,0,1:T(1,128)}, u32[]{:S(2)}) copy-start(f32[1,3,98304]{2,0,1:T(1,128)} %param.3) | copy-start | bytes 3538948
  0.7 1.4 %copy-start.1 = (f32[1,3,98304]{2,0,1:T(1,128)S(1)}, f32[1,3,98304]{2,0,1:T(1,128)}, u32[]{:S(2)}) copy-start(f32[1,3,98304]{2,0,1:T(1,128)} %param.2) | copy-start | bytes 3538948
  2.2 11.6 %collective-permute-start = (f32[3,26,8,128]{3,2,1,0:T(8,128)S(1)}, f32[3,26,8,128]{3,2,1,0:T(8,128)S(1)}, u32[]{:S(2)}, u32[]{:S(2)}) collective-permute-start(f32[3,26,8,128]{3,2,1,0:T(8,128)S(1)} %get-tuple-element.40), channel_id=1, source_target_pairs={{0,16},{16,0},{32,48},{48,32},{64,80},{80,64},{96,112},{112,96},{1... | collective-permute-start | bytes 958472 | tf_op jit(solution)/shard_map/ppermute | solution.py:691
  4.3 7.0 %collective-permute-start.2 = (f32[3,2,8,128]{3,2,1,0:T(8,128)S(1)}, f32[3,2,8,128]{3,2,1,0:T(8,128)S(1)}, u32[]{:S(2)}, u32[]{:S(2)}) collective-permute-start(f32[3,2,8,128]{3,2,1,0:T(8,128)S(1)} %get-tuple-element.42), channel_id=1, source_target_pairs={{0,1},{1,2},{2,3},{3,4},{4,5},{5,6},{6,7},{7,8},{8,9},{9,10},{10,1... | collective-permute-start | bytes 73736 | tf_op jit(solution)/shard_map/ppermute | solution.py:686
  4.3 7.0 %collective-permute-start.3 = (f32[3,2,8,128]{3,2,1,0:T(8,128)S(1)}, f32[3,2,8,128]{3,2,1,0:T(8,128)S(1)}, u32[]{:S(2)}, u32[]{:S(2)}) collective-permute-start(f32[3,2,8,128]{3,2,1,0:T(8,128)S(1)} %get-tuple-element.43), channel_id=1, source_target_pairs={{0,31},{1,16},{2,17},{3,18},{4,19},{5,20},{6,21},{7,22},{8,23},{9,... | collective-permute-start | bytes 73736 | tf_op jit(solution)/shard_map/ppermute | solution.py:687
  9.4 20.0 %collective-permute-start.6 = (f32[3,48,8,128]{3,2,1,0:T(8,128)S(1)}, f32[3,48,8,128]{3,2,1,0:T(8,128)S(1)}, u32[]{:S(2)}, u32[]{:S(2)}) collective-permute-start(f32[3,48,8,128]{3,2,1,0:T(8,128)S(1)} %get-tuple-element.45.refs_0_.refs_2_), channel_id=1, source_target_pairs={{16,48},{32,0},{48,80},{64,32},{80,112},{96,64},{17,49},{33,1},{49... | collective-permute-start | bytes 1769480 | tf_op jit(solution)/shard_map/ppermute | solution.py:692
  11.3 9.2 %collective-permute-start.4 = (f32[3,24,8,128]{3,2,1,0:T(8,128)S(1)}, f32[3,24,8,128]{3,2,1,0:T(8,128)S(1)}, u32[]{:S(2)}, u32[]{:S(2)}) collective-permute-start(f32[3,24,8,128]{3,2,1,0:T(8,128)S(1)} %get-tuple-element.44), channel_id=1, source_target_pairs={{0,16},{16,0},{32,48},{48,32},{64,80},{80,64},{96,112},{112,96},{1... | collective-permute-start | bytes 884744 | tf_op jit(solution)/shard_map/ppermute | solution.py:691
  13.8 39.2 %collective-permute-start.7 = (f32[3,48,8,128]{3,2,1,0:T(8,128)S(1)}, f32[3,48,8,128]{3,2,1,0:T(8,128)S(1)}, u32[]{:S(2)}, u32[]{:S(2)}) collective-permute-start(f32[3,48,8,128]{3,2,1,0:T(8,128)S(1)} %get-tuple-element.55), channel_id=1, source_target_pairs={{0,16},{16,0},{32,48},{48,32},{64,80},{80,64},{96,112},{112,96},{1... | collective-permute-start | bytes 1769480 | tf_op jit(solution)/shard_map/ppermute | solution.py:708
  14.1 17.9 %collective-permute-start.1 = (f32[3,26,8,128]{3,2,1,0:T(8,128)S(1)}, f32[3,26,8,128]{3,2,1,0:T(8,128)S(1)}, u32[]{:S(2)}, u32[]{:S(2)}) collective-permute-start(f32[3,26,8,128]{3,2,1,0:T(8,128)S(1)} %collective-permute-done.refs_3_.refs_4_), channel_id=1, source_target_pairs={{48,16},{0,32},{80,48},{32,64},{112,80},{64,96},{49,17},{1,33},{81... | collective-permute-start | bytes 958472 | tf_op jit(solution)/shard_map/ppermute | solution.py:693
  20.5 11.5 %collective-permute-start.5 = (f32[3,24,8,128]{3,2,1,0:T(8,128)S(1)}, f32[3,24,8,128]{3,2,1,0:T(8,128)S(1)}, u32[]{:S(2)}, u32[]{:S(2)}) collective-permute-start(f32[3,24,8,128]{3,2,1,0:T(8,128)S(1)} %collective-permute-done.4.refs_5_.refs_4_), channel_id=1, source_target_pairs={{48,16},{0,32},{80,48},{32,64},{112,80},{64,96},{49,17},{1,33},{81... | collective-permute-start | bytes 884744 | tf_op jit(solution)/shard_map/ppermute | solution.py:693
  54.0 17.4 %collective-permute-start.12 = (f32[3,48,8,128]{3,2,1,0:T(8,128)S(1)}, f32[3,48,8,128]{3,2,1,0:T(8,128)S(1)}, u32[]{:S(2)}, u32[]{:S(2)}) collective-permute-start(f32[3,48,8,128]{3,2,1,0:T(8,128)S(1)} %get-tuple-element.60.refs_0_.refs_1_.before.here), channel_id=1, source_target_pairs={{16,48},{32,0},{48,80},{64,32},{80,112},{96,64},{17,49},{33,1},{49... | collective-permute-start | bytes 1769480 | tf_op jit(solution)/shard_map/ppermute | solution.py:737
  55.3 16.6 %collective-permute-start.11 = (f32[3,48,8,128]{3,2,1,0:T(8,128)S(1)}, f32[3,48,8,128]{3,2,1,0:T(8,128)S(1)}, u32[]{:S(2)}, u32[]{:S(2)}) collective-permute-start(f32[3,48,8,128]{3,2,1,0:T(8,128)S(1)} %get-tuple-element.59.refs_3_.refs_2_.here.after), channel_id=1, source_target_pairs={{48,16},{0,32},{80,48},{32,64},{112,80},{64,96},{49,17},{1,33},{81... | collective-permute-start | bytes 1769480 | tf_op jit(solution)/shard_map/ppermute | solution.py:734
  59.9 6.9 %collective-permute-start.8 = (f32[2,3,2,8,128]{4,3,2,1,0:T(8,128)S(1)}, f32[2,3,2,8,128]{4,3,2,1,0:T(8,128)S(1)}, u32[]{:S(2)}, u32[]{:S(2)}) collective-permute-start(f32[2,3,2,8,128]{4,3,2,1,0:T(8,128)S(1)} %get-tuple-element.57), channel_id=1, source_target_pairs={{0,16},{1,17},{2,18},{3,19},{4,20},{5,21},{6,22},{7,23},{8,24},{9,... | collective-permute-start | bytes 147464 | tf_op jit(solution)/shard_map/ppermute | solution.py:723
  60.0 6.8 %collective-permute-start.9 = (f32[2,3,2,8,128]{4,3,2,1,0:T(8,128)S(1)}, f32[2,3,2,8,128]{4,3,2,1,0:T(8,128)S(1)}, u32[]{:S(2)}, u32[]{:S(2)}) collective-permute-start(f32[2,3,2,8,128]{4,3,2,1,0:T(8,128)S(1)} %get-tuple-element.58), channel_id=1, source_target_pairs={{16,0},{17,1},{18,2},{19,3},{20,4},{21,5},{22,6},{23,7},{24,8},{25... | collective-permute-start | bytes 147464 | tf_op jit(solution)/shard_map/ppermute | solution.py:724
  66.8 27.5 %collective-permute-start.10 = (f32[3,48,8,128]{3,2,1,0:T(8,128)S(1)}, f32[3,48,8,128]{3,2,1,0:T(8,128)S(1)}, u32[]{:S(2)}, u32[]{:S(2)}) collective-permute-start(f32[3,48,8,128]{3,2,1,0:T(8,128)S(1)} %get-tuple-element.59.refs_3_.refs_2_.here.after), channel_id=1, source_target_pairs={{0,16},{16,0},{32,48},{48,32},{64,80},{80,64},{96,112},{112,96},{1... | collective-permute-start | bytes 1769480 | tf_op jit(solution)/shard_map/ppermute | solution.py:740
  90.6 10.0 %collective-permute-start.14 = (f32[3,24,8,128]{3,2,1,0:T(8,128)S(1)}, f32[3,24,8,128]{3,2,1,0:T(8,128)S(1)}, u32[]{:S(2)}, u32[]{:S(2)}) collective-permute-start(f32[3,24,8,128]{3,2,1,0:T(8,128)S(1)} %get-tuple-element.69), channel_id=1, source_target_pairs={{0,16},{16,0},{32,48},{48,32},{64,80},{80,64},{96,112},{112,96},{1... | collective-permute-start | bytes 884744 | tf_op jit(solution)/shard_map/ppermute | solution.py:745
  91.5 14.0 %collective-permute-start.13 = (f32[3,24,8,128]{3,2,1,0:T(8,128)S(1)}, f32[3,24,8,128]{3,2,1,0:T(8,128)S(1)}, u32[]{:S(2)}, u32[]{:S(2)}) collective-permute-start(f32[3,24,8,128]{3,2,1,0:T(8,128)S(1)} %get-tuple-element.68), channel_id=1, source_target_pairs={{0,16},{16,0},{32,48},{48,32},{64,80},{80,64},{96,112},{112,96},{1... | collective-permute-start | bytes 884744 | tf_op jit(solution)/shard_map/ppermute | solution.py:745
